TPU v7x, 32 devices: a whole 2x2x4 slice. The times are simulated.
32 devices in a mesh: dom: 4 (over z), src: 4 (over y, x), rel: 2 (over core).
Axes of the slice: x: 2, y: 2, z: 4, core: 2. Of those that a mesh axis runs over, the one named last changes fastest.
Arguments:
- source_feats: bfloat16 [8192, 256], P(('dom', 'src', 'rel')), may hold values from -6 to 6
- rel_weight: bfloat16 [12, 256, 256], P('rel'), may hold values from -0.375 to 0.375
- halo_pick: int32 [4, 4, 2, 4], P('dom', 'src', 'rel'), may hold values from 0 to 1
- entry_index: int32 [4, 4, 2, 3, 64], P('dom', 'src', 'rel'), may hold values from 0 to 15, as said below
- entry_count: int32 [4, 4, 2], P('dom', 'src', 'rel'), may hold values from 1 to 64, as said below
- entry_values: bfloat16 [4, 4, 2, 64, 128, 128], P('dom', 'src', 'rel'), may hold values from -0.125 to 0.125
- cotangent: bfloat16 [8192, 256], P(('dom', 'src', 'rel')), may hold values from -0.21875 to 0.21875
Outputs:
- out_feats: bfloat16 [8192, 256], P(('dom', 'src', 'rel'))
- grad_rel: float32 [12, 256, 256], P('rel')
Inputs may be any that keep to these rules, and one draw needn't show every extreme that they name: `entry_index`: row 0 of an entry is a target block below 16, row 1 a partition below 4, row 2 a relation below 6. Over all 64 entries of one (p,s,g), every partition is named 64 // 4 times or once more. `entry_count`: live entries come first; some (p,s,g) has all 64 entries live in every draw.
All inputs are finite; a program needn't handle non-finite values.
Results may differ from a plain program's by a relative error of at most 0.0057.
Values may be sent and summed in bfloat16 or wider, within the bound.
No kernel may reach another device: no remote copies, remote signals or barrier semaphores. Data moves between devices by JAX's collectives and lax.ppermute only.
A program may use at most 64 MiB of HBM per device.

v0:
```python
import jax
import jax.numpy as jnp
from jax import lax
from jax.sharding import PartitionSpec as P


def silu_slope(pre_values):
    logistic = jax.nn.sigmoid(pre_values)
    return logistic * (1.0 + pre_values * (1.0 - logistic))


def local(source_feats, rel_weight, halo_pick, entry_index, entry_count, entry_values, cotangent):
    partitions = lax.axis_size("dom")
    tile_rows = entry_values.shape[-1]
    features = source_feats.shape[1]
    chosen = halo_pick.reshape(-1)
    everyone = lax.all_gather(source_feats, "dom", axis=0, tiled=True)
    everyone = everyone.reshape(partitions, -1, tile_rows, features)
    halo_blocks = everyone[jnp.arange(partitions, dtype=jnp.int32), chosen]
    own_rows = cotangent.shape[0]
    tgt_blocks = own_rows * lax.axis_size("src") * lax.axis_size("rel") // tile_rows
    rel_local = rel_weight.shape[0]
    entry_table = entry_index.reshape(3, -1)
    slot_total = entry_table.shape[1]
    values = entry_values.reshape(-1, tile_rows, tile_rows)
    picked = halo_blocks[entry_table[1]]
    messages = jnp.einsum("eij,ejd->eid", values, picked, preferred_element_type=jnp.float32)
    live_mask = jnp.arange(slot_total, dtype=jnp.int32) < entry_count.reshape(())
    target_slot = entry_table[2] * tgt_blocks + entry_table[0]
    slot_numbers = jnp.arange(rel_local * tgt_blocks, dtype=jnp.int32)
    placement = ((slot_numbers[:, None] == target_slot[None, :]) & live_mask[None, :]).astype(
        jnp.float32
    )
    totals = jnp.einsum(
        "se,eid->sid",
        placement,
        messages,
        precision=lax.Precision.HIGHEST,
        preferred_element_type=jnp.float32,
    )
    relation_terms = totals.astype(jnp.bfloat16).reshape(
        rel_local, tgt_blocks * tile_rows, features
    )
    summed = lax.psum_scatter(
        jnp.einsum("rtd,rde->te", relation_terms, rel_weight, preferred_element_type=jnp.float32),
        ("src", "rel"),
        scatter_dimension=0,
        tiled=True,
    )
    out_feats = jax.nn.silu(summed).astype(jnp.bfloat16)
    local_grad = (cotangent.astype(jnp.float32) * silu_slope(summed)).astype(jnp.bfloat16)
    grad_rows = lax.all_gather(local_grad, ("src", "rel"), axis=0, tiled=True)
    weight_terms = jnp.einsum(
        "rtd,te->rde", relation_terms, grad_rows, preferred_element_type=jnp.float32
    )
    grad_rel = lax.psum(weight_terms, ("dom", "src"))
    return (out_feats, grad_rel)


def solution(mesh):
    return jax.shard_map(
        local,
        mesh=mesh,
        in_specs=(
            P(("dom", "src", "rel"), None),
            P("rel", None, None),
            P("dom", "src", "rel", None),
            P("dom", "src", "rel", None, None),
            P("dom", "src", "rel"),
            P("dom", "src", "rel", None, None, None),
            P(("dom", "src", "rel"), None),
        ),
        out_specs=(P(("dom", "src", "rel"), None), P("rel", None, None)),
        check_vma=False,
    )
```

profile of v0, /device:TPU:0, one launch (start us, length us, event | category | flops | bytes accessed | tf_op | source)
XLA Modules:
  0.0 267.8 jit_solution(13819446079555441794)
XLA Ops:
  7.2 0.0 reduce-scatter.2.cloned.1.call-start
  7.2 0.8 fusion.17
  8.0 0.7 add_bitcast_fusion
  8.7 17.6 %all_gather.6 = bf16[1024,256]{1,0:T(8,128)(2,1)S(1)} all-gather(bf16[256,256]{1,0:T(8,128)(2,1)} %param.7), channel_id=1, replica_groups=mesh['dom'=4,'src'=4,'rel'=2] {'dom'}, dimensions={0}, use_global_device_ids=true | all-gather | bytes 655360 | tf_op jit(solution)/shard_map/all_gather | solution.py:17
  26.3 0.7 fusion.18
  26.9 0.6 gather_fusion
  27.5 2.8 %gather_fusion.1 = bf16[64,128,256]{2,1,0:T(8,128)(2,1)} fusion(bf16[4,128,256]{2,1,0:T(8,128)(2,1)S(1)} %gather_fusion, s32[1024]{0:T(1024)S(1)} %pad_clamp_fusion), kind=kCustom, calls=%fused_computation.1 | custom fusion | bytes 8388864 | tf_op jit(solution)/shard_map/gather | solution.py:26
  30.3 6.7 %fusion.5 = f32[64,256,128]{2,1,0:T(8,128)} fusion(bf16[64,128,256]{2,1,0:T(8,128)(2,1)} %gather_fusion.1, bf16[1,1,1,64,128,128]{5,4,3,2,1,0:T(8,128)(2,1)S(1)} %copy-done), kind=kOutput, calls=%fused_computation.6 | convolution fusion | flops 536870912 | bytes 14680064 | tf_op jit(solution)/shard_map/eij,ejd->eid/dot_general | solution.py:27
  37.0 9.2 %copy.12 = f32[64,256,128]{1,0,2:T(8,128)} copy(f32[64,256,128]{2,1,0:T(8,128)} %fusion.5) | data formatting | bytes 16777216 | tf_op jit(solution)/shard_map/eij,ejd->eid/dot_general | solution.py:27
  46.9 8.5 %fusion.2 = bf16[96,128,256]{2,0,1:T(8,128)(2,1)S(1)} fusion(f32[64,256,128]{1,0,2:T(8,128)} %copy.12, s32[64]{0:T(128)S(1)} %add_bitcast_fusion, pred[64]{0:T(512)(128)(4,1)S(1)} %iota_compare_fusion.1), kind=kOutput, calls=%fused_computation.4 | convolution fusion | flops 2419077120 | bytes 14680384 | tf_op jit(solution)/shard_map/se,eid->sid/dot_general | solution.py:34
  55.4 3.7 %copy.10 = bf16[96,128,256]{2,1,0:T(8,128)(2,1)S(1)} copy(bf16[96,128,256]{2,0,1:T(8,128)(2,1)S(1)} %fusion.2) | data formatting | bytes 12582912 | tf_op jit(solution)/shard_map/convert_element_type | solution.py:41
  59.0 2.7 copy-done.1
  61.7 3.3 %convolution_bitcast_fusion = f32[2048,256]{1,0:T(8,128)} fusion(bf16[6,2048,256]{2,1,0:T(8,128)(2,1)S(1)} %bitcast.36, bf16[6,256,256]{2,1,0:T(8,128)(2,1)S(1)} %copy-done.3), kind=kOutput, calls=%fused_computation.5 | convolution fusion | flops 1610612736 | bytes 9175040 | tf_op jit(solution)/shard_map/rtd,rde->te/dot_general | solution.py:45
  65.0 0.0 reduce-scatter.2.cloned.1.call-update
  65.0 0.0 all-gather.2.cloned.1.call-start
  65.1 43.1 %reduce-scatter.2.cloned.1.call-done = f32[256,256]{1,0:T(8,128)} async-done(((f32[2048,256]{1,0:T(8,128)}), f32[256,256]{1,0:T(8,128)}) %reduce-scatter.2.cloned.1.call-update) | async-done | bytes 262160 | tf_op jit(solution)/shard_map/reduce_scatter | solution.py:44
  108.2 1.8 multiply_convert_fusion
  109.9 0.0 all-gather.2.cloned.1.call-update
  110.0 0.0 all-reduce.2.cloned.1.call-start
  110.0 24.3 %all-gather.2.cloned.1.call-done = bf16[2048,256]{1,0:T(8,128)(2,1)} async-done(((bf16[256,256]{1,0:T(8,128)(2,1)}), bf16[2048,256]{1,0:T(8,128)(2,1)}) %all-gather.2.cloned.1.call-update) | async-done | bytes 1048592 | tf_op jit(solution)/shard_map/all_gather | solution.py:52
  134.3 6.0 %fusion.7 = f32[6,256,256]{2,1,0:T(8,128)} fusion(bf16[6,2048,256]{2,1,0:T(8,128)(2,1)} %bitcast.37, bf16[2048,256]{1,0:T(8,128)(2,1)} %all-gather.2.cloned.1.call-done), kind=kOutput, calls=%fused_computation.8 | convolution fusion | flops 1610612736 | bytes 8912896 | tf_op jit(solution)/shard_map/rtd,te->rde/dot_general | solution.py:53
  140.3 0.0 all-reduce.2.cloned.1.call-update
  140.3 118.2 %all-reduce.2.cloned.1.call-done = f32[6,256,256]{2,1,0:T(8,128)} async-done(((f32[6,256,256]{2,1,0:T(8,128)}), f32[6,256,256]{2,1,0:T(8,128)}) %all-reduce.2.cloned.1.call-update) | async-done | bytes 1572880 | tf_op jit(solution)/shard_map/psum | solution.py:56
  258.5 2.7 %copy.16 = f32[6,256,256]{2,1,0:T(8,128)} copy(f32[6,256,256]{2,1,0:T(8,128)} %all-reduce.2.cloned.1.call-done) | data formatting | bytes 3145728
  (9 shorter events, 0.0 us)
Async XLA Ops:
  7.2 23.1 %copy-start = (bf16[1,1,1,64,128,128]{5,4,3,2,1,0:T(8,128)(2,1)S(1)}, bf16[1,1,1,64,128,128]{5,4,3,2,1,0:T(8,128)(2,1)}, u32[]{:S(2)}) copy-start(bf16[1,1,1,64,128,128]{5,4,3,2,1,0:T(8,128)(2,1)} %param.12) | copy-start | bytes 6291460
  7.2 101.0 %reduce-scatter.2.cloned.1.call-start = ((), (), s32[]{:S(2)}) async-start(), calls=%async_computation.1 | async-start | bytes 2359296 | tf_op jit(solution)/shard_map/reduce_scatter | solution.py:44
  55.4 6.3 %copy-start.3 = (bf16[6,256,256]{2,1,0:T(8,128)(2,1)S(1)}, bf16[6,256,256]{2,1,0:T(8,128)(2,1)}, u32[]{:S(2)}) copy-start(bf16[6,256,256]{2,1,0:T(8,128)(2,1)} %param.8) | copy-start | bytes 2359300
  59.0 2.7 copy-start.1
  61.7 46.4 %copy-start.2 = (bf16[256,256]{1,0:T(8,128)(2,1)S(1)}, bf16[256,256]{1,0:T(8,128)(2,1)}, u32[]{:S(2)}) copy-start(bf16[256,256]{1,0:T(8,128)(2,1)} %param.13) | copy-start | bytes 393220
  65.0 69.3 %all-gather.2.cloned.1.call-start = ((), (), s32[]{:S(2)}) async-start(), calls=%async_computation.2 | async-start | bytes 1179648 | tf_op jit(solution)/shard_map/all_gather | solution.py:52
  110.0 148.6 %all-reduce.2.cloned.1.call-start = ((), (), s32[]{:S(2)}) async-start(), calls=%async_computation.3 | async-start | bytes 3145728 | tf_op jit(solution)/shard_map/psum | solution.py:56
Sparse Core Ops, SparseCore 0:
  65.1 42.9 reduce-scatter.1
  110.8 23.4 all-gather.1
  141.2 117.3 all-reduce.1
where the time goes:
time: 268 us
  waiting for transfers between devices  186 us (69%)
  matrix products  24.5 us (9%)
  local copies, waits for them, and re-layouts  21.7 us (8%)
  blocking collectives  17.6 us (7%)
  between operations  14.5 us (5%)
  other arithmetic  3.91 us (1%)
    psum x1, waiting for transfers between devices, local(): grad_rel = lax.psum(weight_terms, ('dom', 'src'))  118 us
    reduce_scatter x1, waiting for transfers between devices, local(): lax.psum_scatter(jnp.einsum('rtd,rde->te', relation_terms, rel_weight, pr...  43.1 us
    all_gather x1, waiting for transfers between devices, local(): grad_rows = lax.all_gather(local_grad, ('src', 'rel'), axis=0, tiled=True)  24.3 us
    all_gather x1, blocking collectives, local(): everyone = lax.all_gather(source_feats, 'dom', axis=0, tiled=True)  17.6 us
    dot_general x1, local copies, waits for them, and re-layouts, local(): jnp.einsum('eij,ejd->eid', values, picked, preferred_element_type=jnp.flo...  9.24 us
    dot_general x1, matrix products, local(): jnp.einsum('se,eid->sid', placement, messages, precision=lax.Precision.HI...  8.46 us
    dot_general x1, matrix products, local(): jnp.einsum('eij,ejd->eid', values, picked, preferred_element_type=jnp.flo...  6.72 us
    dot_general x1, matrix products, local(): jnp.einsum('rtd,te->rde', relation_terms, grad_rows, preferred_element_ty...  6.02 us
  transfers between devices with their start and end apart: 3, of which 3 were waited for; matrix products, arithmetic and copies ran while one was open for 0% of the time, Pallas kernels for 0%

commit v1 on v0

v1 whole, which is shorter than its diff:
```python
import functools

import jax
import jax.numpy as jnp
from jax import lax
from jax.experimental import pallas as pl
from jax.experimental.pallas import tpu as pltpu
from jax.sharding import PartitionSpec as P

F32, BF16 = jnp.float32, jnp.bfloat16
VMEM_BYTES = 56 * 1024 * 1024
WHOLE = pl.BlockSpec(memory_space=pltpu.VMEM)
SCALARS = pl.BlockSpec(memory_space=pltpu.SMEM)


def partner_pairs(size, mask):
    return [(i, i ^ mask) for i in range(size)]


def swap(value, axis, mask):
    return lax.ppermute(value, axis, partner_pairs(lax.axis_size(axis), mask))


def halo_slot(places, partition, masked):
    return partition ^ places[0] if masked else partition


def forward_kernel(masked, tile, halo_count, places, chosen, table, count, *refs):
    halo_refs, (weight, values, keep, send, projected, pre) = refs[:halo_count], refs[halo_count:]
    relations, features = weight.shape[0], weight.shape[1]
    per_call = halo_refs[0].shape[0]
    slots = halo_count * per_call
    for slot in range(slots):
        partition = halo_slot(places, slot, masked)
        first = pl.multiple_of(chosen[partition] * tile, tile)
        block = halo_refs[slot // per_call][slot % per_call, pl.ds(first, tile), :]
        for r in range(relations):
            projected[slot * relations + r] = jnp.dot(
                block, weight[r], preferred_element_type=F32
            ).astype(BF16)
    pre[...] = jnp.zeros_like(pre)

    def entry(e, carry):
        slot = halo_slot(places, table[1, e], masked)
        term = jnp.dot(
            values[e], projected[slot * relations + table[2, e]], preferred_element_type=F32
        )
        target = table[0, e]
        pre[target] = pre[target] + term
        return carry

    lax.fori_loop(0, count[0], entry, 0)
    panels, per_owner = keep.shape[0], keep.shape[1] // tile
    groups = pre.shape[0] // (panels * per_owner)
    for distance in range(panels):
        panel = places[1] ^ distance
        for part in range(per_owner):
            rows = pl.ds(part * tile, tile)
            mine = (panel * groups + places[2]) * per_owner + part
            keep[distance, rows, :] = pre[mine]
            other = (panel * groups + (places[2] ^ 1)) * per_owner + part
            send[distance, rows, :] = pre[other].astype(BF16)


def terms_kernel(masked, tile, halo_count, places, chosen, table, count, *refs):
    halo_refs, (values, terms, turned, total) = refs[:halo_count], refs[halo_count:]
    per_call = halo_refs[0].shape[0]
    targets = terms.shape[2] // tile
    for slot in range(halo_count * per_call):
        partition = halo_slot(places, slot, masked)
        first = pl.multiple_of(chosen[partition] * tile, tile)
        block = halo_refs[slot // per_call][slot % per_call, pl.ds(first, tile), :]
        turned[slot] = block.astype(F32).T.astype(BF16)
    total[...] = jnp.zeros_like(total)

    def entry(e, carry):
        slot = halo_slot(places, table[1, e], masked)
        message = lax.dot_general(
            turned[slot], values[e], (((1,), (1,)), ((), ())), preferred_element_type=F32
        )
        columns = pl.ds(pl.multiple_of(table[0, e] * tile, tile), tile)
        relation = table[2, e]
        total[relation, :, columns] = total[relation, :, columns] + message
        return carry

    lax.fori_loop(0, count[0], entry, 0)
    terms[...] = total[...].astype(BF16)


def weight_kernel(terms, grads, out):
    out[0] = jnp.dot(terms[0], grads[...], preferred_element_type=F32).astype(BF16)


def silu_slope(pre_values):
    logistic = jax.nn.sigmoid(pre_values)
    return logistic * (1.0 + pre_values * (1.0 - logistic))


def reduce_scatter(pieces, axis):
    arrived = [swap(pieces[m].astype(BF16), axis, m) for m in range(len(pieces) - 1, 0, -1)]
    total = pieces[0].astype(F32)
    for value in arrived:
        total = total + value.astype(F32)
    return total


def gather(value, axis):
    return [value] + [swap(value, axis, m) for m in range(1, lax.axis_size(axis))]


def in_axis_order(pieces, axis):
    me = lax.axis_index(axis)
    stacked = jnp.stack(pieces)
    return stacked[me ^ jnp.arange(len(pieces), dtype=jnp.int32)]


def local(source_feats, rel_weight, halo_pick, entry_index, entry_count, entry_values, cotangent):
    partitions, panels = lax.axis_size("dom"), lax.axis_size("src")
    groups = lax.axis_size("rel")
    tile = entry_values.shape[-1]
    own_rows, features = cotangent.shape
    relations = rel_weight.shape[0]
    values = entry_values.reshape(-1, tile, tile)
    table = entry_index.reshape(3, -1)
    count = entry_count.reshape(1)
    chosen = halo_pick.reshape(-1)
    places = jnp.stack(
        [lax.axis_index("dom"), lax.axis_index("src"), lax.axis_index("rel")]
    ).astype(jnp.int32)
    target_rows = own_rows * panels * groups
    direct = partitions <= 8

    if direct:
        halo = [source_feats[None]] + [
            swap(source_feats, "dom", m)[None] for m in range(1, partitions)
        ]
    else:
        halo = [lax.all_gather(source_feats, "dom", axis=0)]
    slots = sum(h.shape[0] for h in halo)

    keep, send = pl.pallas_call(
        functools.partial(forward_kernel, direct, tile, len(halo)),
        out_shape=(
            jax.ShapeDtypeStruct((panels, own_rows, features), F32),
            jax.ShapeDtypeStruct((panels, own_rows, features), BF16),
        ),
        in_specs=[SCALARS] * 4 + [WHOLE] * (len(halo) + 2),
        out_specs=(WHOLE, WHOLE),
        scratch_shapes=[
            pltpu.VMEM((slots * relations, tile, features), BF16),
            pltpu.VMEM((target_rows // tile, tile, features), F32),
        ],
        compiler_params=pltpu.CompilerParams(vmem_limit_bytes=VMEM_BYTES),
        name="forward",
    )(places, chosen, table, count, *halo, rel_weight, values)

    chip_sum = keep + swap(send, "rel", 1).astype(F32)
    pre = reduce_scatter([chip_sum[m] for m in range(panels)], "src")

    terms = pl.pallas_call(
        functools.partial(terms_kernel, direct, tile, len(halo)),
        out_shape=jax.ShapeDtypeStruct((relations, features, target_rows), BF16),
        in_specs=[SCALARS] * 4 + [WHOLE] * (len(halo) + 1),
        out_specs=WHOLE,
        scratch_shapes=[
            pltpu.VMEM((slots, features, tile), BF16),
            pltpu.VMEM((relations, features, target_rows), F32),
        ],
        compiler_params=pltpu.CompilerParams(vmem_limit_bytes=VMEM_BYTES),
        cost_estimate=pl.CostEstimate(
            flops=2 * values.shape[0] * tile * tile * features,
            bytes_accessed=2 * relations * target_rows * features,
            transcendentals=0,
        ),
        name="terms",
    )(places, chosen, table, count, *halo, values)

    out_feats = jax.nn.silu(pre).astype(BF16)
    local_grad = (cotangent.astype(F32) * silu_slope(pre)).astype(BF16)

    chip_grads = in_axis_order(gather(local_grad, "src"), "src")
    both = in_axis_order([chip_grads, swap(chip_grads, "rel", 1)], "rel")
    grad_rows = both.transpose(1, 0, 2, 3).reshape(target_rows, features)

    weight_terms = pl.pallas_call(
        weight_kernel,
        grid=(relations,),
        out_shape=jax.ShapeDtypeStruct((relations, features, features), BF16),
        in_specs=[
            pl.BlockSpec((1, features, target_rows), lambda r: (r, 0, 0)),
            pl.BlockSpec((target_rows, features), lambda r: (0, 0)),
        ],
        out_specs=pl.BlockSpec((1, features, features), lambda r: (r, 0, 0)),
        compiler_params=pltpu.CompilerParams(vmem_limit_bytes=VMEM_BYTES),
        name="weight_terms",
    )(terms, grad_rows)

    flat = weight_terms.reshape(panels, -1, features)
    panel = lax.axis_index("src")
    pieces = [
        lax.dynamic_index_in_dim(flat, panel ^ m, 0, keepdims=False) for m in range(panels)
    ]
    panel_sum = reduce_scatter(pieces, "src").astype(BF16)
    if direct:
        parts = panel_sum.reshape(partitions, -1, features)
        part = lax.axis_index("dom")
        pieces = [
            lax.dynamic_index_in_dim(parts, part ^ m, 0, keepdims=False)
            for m in range(partitions)
        ]
        whole_sum = reduce_scatter(pieces, "dom").astype(BF16)
        dom_sum = in_axis_order(gather(whole_sum, "dom"), "dom").reshape(panel_sum.shape)
    else:
        dom_sum = lax.psum(panel_sum.astype(F32), "dom").astype(BF16)
    grad_rel = in_axis_order(gather(dom_sum, "src"), "src")
    grad_rel = grad_rel.reshape(relations, features, features).astype(F32)
    return (out_feats, grad_rel)


def solution(mesh):
    return jax.shard_map(
        local,
        mesh=mesh,
        in_specs=(
            P(("dom", "src", "rel"), None),
            P("rel", None, None),
            P("dom", "src", "rel", None),
            P("dom", "src", "rel", None, None),
            P("dom", "src", "rel"),
            P("dom", "src", "rel", None, None, None),
            P(("dom", "src", "rel"), None),
        ),
        out_specs=(P(("dom", "src", "rel"), None), P("rel", None, None)),
        check_vma=False,
    )
```

time: 268 us -> 121 us (0.45)
  waiting for transfers between devices: 186 us -> 43.6 us
  Pallas kernels: 0 us -> 32.9 us
  starting transfers between devices: 0.12 us -> 31 us
  matrix products: 24.5 us -> 0 us
  blocking collectives: 17.6 us -> 0 us
  local copies, waits for them, and re-layouts: 21.7 us -> 6.57 us
  between operations: 14.5 us -> 1.45 us
    psum x1 -> x0, waiting for transfers between devices: 118 us -> none  [local(): grad_rel = lax.psum(weight_terms, ('dom', 'src'))]
    ppermute x0 -> x23, waiting for transfers between devices: none -> 43.6 us  [swap(): return lax.ppermute(value, axis, partner_pairs(lax.axis_size(axis), mask))]
    reduce_scatter x1 -> x0, waiting for transfers between devices: 43.1 us -> none  [local(): lax.psum_scatter(jnp.einsum('rtd,rde->te', relation_terms, rel_weight, pr...]
    pallas_call x0 -> x3, Pallas kernels: none -> 32.9 us  [the longest x1 14.4 us: local(): pl.pallas_call(functools.partial(terms_kernel, direct, tile, len(halo)),...]
    ppermute x0 -> x23, starting transfers between devices: none -> 31 us  [swap(): return lax.ppermute(value, axis, partner_pairs(lax.axis_size(axis), mask))]
    dot_general x4 -> x0, matrix products: 24.5 us -> none  [the longest x1 8.46 us: local(): jnp.einsum('se,eid->sid', placement, messages, precision=lax.Precision.HI...]
    all_gather x1 -> x0, waiting for transfers between devices: 24.3 us -> none  [local(): grad_rows = lax.all_gather(local_grad, ('src', 'rel'), axis=0, tiled=True)]
    all_gather x1 -> x0, blocking collectives: 17.6 us -> none  [local(): everyone = lax.all_gather(source_feats, 'dom', axis=0, tiled=True)]
  transfers between devices with their start and end apart: 3 -> 23, of which waited for: 3 -> 17; matrix products, arithmetic and copies ran while one was open for 0% -> 2% of each run, Pallas kernels for 0% -> 12%
where the time goes in v1:
time: 121 us
  waiting for transfers between devices  43.6 us (36%)
  Pallas kernels  32.9 us (27%)
  starting transfers between devices  31 us (26%)
  local copies, waits for them, and re-layouts  6.57 us (5%)
  other arithmetic  5.47 us (5%)
  between operations  1.45 us (1%)
    ppermute x23, waiting for transfers between devices, swap(): return lax.ppermute(value, axis, partner_pairs(lax.axis_size(axis), mask))  43.6 us
    ppermute x23, starting transfers between devices, swap(): return lax.ppermute(value, axis, partner_pairs(lax.axis_size(axis), mask))  31 us
    pallas_call x1, Pallas kernels, local(): pl.pallas_call(functools.partial(terms_kernel, direct, tile, len(halo)),...  14.4 us
    pallas_call x1, Pallas kernels, local(): pl.pallas_call(functools.partial(forward_kernel, direct, tile, len(halo))...  11.6 us
    pallas_call x1, Pallas kernels, local(): pl.pallas_call(weight_kernel, grid=(relations,), out_shape=jax.ShapeDtype...  6.84 us
  transfers between devices with their start and end apart: 23, of which 17 were waited for; matrix products, arithmetic and copies ran while one was open for 2% of the time, Pallas kernels for 12%

profile of v1, /device:TPU:0, one launch (start us, length us, event | category | flops | bytes accessed | tf_op | source)
XLA Modules:
  0.0 121.0 jit_solution(10021476247329757121)
XLA Ops:
  0.6 3.1 %collective-permute-start = (bf16[256,256]{1,0:T(8,128)(2,1)}, bf16[256,256]{1,0:T(8,128)(2,1)S(1)}, u32[]{:S(2)}, u32[]{:S(2)}) collective-permute-start(bf16[256,256]{1,0:T(8,128)(2,1)} %param.7), channel_id=1, source_target_pairs={{0,8},{8,0},{16,24},{24,16},{1,9},{9,1},{17,25},{25,17},{2,10},{10... | collective-permute-start | bytes 393224 | tf_op jit(solution)/shard_map/ppermute | solution.py:21
  3.7 2.6 %collective-permute-start.1 = (bf16[256,256]{1,0:T(8,128)(2,1)}, bf16[256,256]{1,0:T(8,128)(2,1)S(1)}, u32[]{:S(2)}, u32[]{:S(2)}) collective-permute-start(bf16[256,256]{1,0:T(8,128)(2,1)} %param.7), channel_id=1, source_target_pairs={{0,16},{8,24},{16,0},{24,8},{1,17},{9,25},{17,1},{25,9},{2,18},{10... | collective-permute-start | bytes 393224 | tf_op jit(solution)/shard_map/ppermute | solution.py:21
  9.0 7.9 %collective-permute-done.1 = bf16[256,256]{1,0:T(8,128)(2,1)S(1)} collective-permute-done((bf16[256,256]{1,0:T(8,128)(2,1)}, bf16[256,256]{1,0:T(8,128)(2,1)S(1)}, u32[]{:S(2)}, u32[]{:S(2)}) %collective-permute-start.1) | collective-permute-done | bytes 131104 | tf_op jit(solution)/shard_map/ppermute | solution.py:21
  17.6 11.6 %forward.1 = (f32[4,256,256]{2,1,0:T(8,128)}, bf16[4,256,256]{2,1,0:T(8,128)(2,1)}) custom-call(s32[3]{0:T(128)} %pad_add_fusion.places, s32[4]{0:T(128)} %bitcast.114, s32[3,64]{1,0:T(4,128)} %bitcast.112, s32[1]{0:T(128)} %bitcast.76.count, bf16[1,256,256]{2,1,0:T(8,128)(2,1)} %bitcast.92, bf16[1,256,256]{2,1,0:T(8,128)(2,1)} %bitcast.94, ...), custom_call_target="tpu_custom_call" | custom-call | tf_op jit(solution)/shard_map/forward/pallas_call | solution.py:141
  29.2 2.1 %collective-permute-done.3 = bf16[4,256,256]{2,1,0:T(8,128)(2,1)S(1)} collective-permute-done((bf16[4,256,256]{2,1,0:T(8,128)(2,1)}, bf16[4,256,256]{2,1,0:T(8,128)(2,1)S(1)}, u32[]{:S(2)}, u32[]{:S(2)}) %collective-permute-start.3) | collective-permute-done | bytes 524320 | tf_op jit(solution)/shard_map/ppermute | solution.py:21
  31.3 1.4 %fusion.12 = (bf16[4,256,256]{2,1,0:T(8,128)(2,1)S(1)}, f32[4,256,256]{2,1,0:T(8,128)S(1)}) fusion(f32[4,256,256]{2,1,0:T(8,128)} %get-tuple-element.4, bf16[4,256,256]{2,1,0:T(8,128)(2,1)S(1)} %collective-permute-done.3), kind=kLoop, calls=%fused_computation.44 | loop fusion | flops 786432 | bytes 3145728 | tf_op jit(solution)/shard_map/convert.5
  32.7 4.5 %collective-permute-start.4 = (bf16[256,256]{1,0:T(8,128)(2,1)S(1)}, bf16[256,256]{1,0:T(8,128)(2,1)S(1)}, u32[]{:S(2)}, u32[]{:S(2)}) collective-permute-start(bf16[256,256]{1,0:T(8,128)(2,1)S(1)} %get-tuple-element.13), channel_id=1, source_target_pairs={{0,6},{2,4},{4,2},{6,0},{1,7},{3,5},{5,3},{7,1},{8,14},{10,12},{12... | collective-permute-start | bytes 393224 | tf_op jit(solution)/shard_map/ppermute | solution.py:21
  37.9 3.3 %collective-permute-done.4 = bf16[256,256]{1,0:T(8,128)(2,1)S(1)} collective-permute-done((bf16[256,256]{1,0:T(8,128)(2,1)S(1)}, bf16[256,256]{1,0:T(8,128)(2,1)S(1)}, u32[]{:S(2)}, u32[]{:S(2)}) %collective-permute-start.4) | collective-permute-done | bytes 131104 | tf_op jit(solution)/shard_map/ppermute | solution.py:21
  41.1 2.7 %collective-permute-done.5 = bf16[256,256]{1,0:T(8,128)(2,1)S(1)} collective-permute-done((bf16[256,256]{1,0:T(8,128)(2,1)S(1)}, bf16[256,256]{1,0:T(8,128)(2,1)S(1)}, u32[]{:S(2)}, u32[]{:S(2)}) %collective-permute-start.5) | collective-permute-done | bytes 131104 | tf_op jit(solution)/shard_map/ppermute | solution.py:21
  44.7 1.8 %collective-permute-start.7 = (bf16[256,256]{1,0:T(8,128)(2,1)S(1)}, bf16[256,256]{1,0:T(8,128)(2,1)S(1)}, u32[]{:S(2)}, u32[]{:S(2)}) collective-permute-start(bf16[256,256]{1,0:T(8,128)(2,1)S(1)} %get-tuple-element.8), channel_id=1, source_target_pairs={{0,2},{2,0},{4,6},{6,4},{1,3},{3,1},{5,7},{7,5},{8,10},{10,8},{12,... | collective-permute-start | bytes 393224 | tf_op jit(solution)/shard_map/ppermute | solution.py:21
  48.2 2.7 %collective-permute-done.7 = bf16[256,256]{1,0:T(8,128)(2,1)S(1)} collective-permute-done((bf16[256,256]{1,0:T(8,128)(2,1)S(1)}, bf16[256,256]{1,0:T(8,128)(2,1)S(1)}, u32[]{:S(2)}, u32[]{:S(2)}) %collective-permute-start.7) | collective-permute-done | bytes 131104 | tf_op jit(solution)/shard_map/ppermute | solution.py:21
  50.9 2.9 %collective-permute-done.8 = bf16[256,256]{1,0:T(8,128)(2,1)S(1)} collective-permute-done((bf16[256,256]{1,0:T(8,128)(2,1)S(1)}, bf16[256,256]{1,0:T(8,128)(2,1)S(1)}, u32[]{:S(2)}, u32[]{:S(2)}) %collective-permute-start.8) | collective-permute-done | bytes 131104 | tf_op jit(solution)/shard_map/ppermute | solution.py:21
  54.6 14.4 %terms.1 = bf16[6,256,2048]{2,1,0:T(8,128)(2,1)} custom-call(s32[3]{0:T(128)} %pad_add_fusion.places, s32[4]{0:T(128)} %bitcast.115, s32[3,64]{1,0:T(4,128)} %bitcast.113, s32[1]{0:T(128)} %bitcast.77.count, bf16[1,256,256]{2,1,0:T(8,128)(2,1)} %bitcast.93, bf16[1,256,256]{2,1,0:T(8,128)(2,1)} %bitcast.95, bf16[1,256,256]{2,1,0:T(8,128)(2,1)} %bitcast.97, ...), custom_call_target="tpu_custom_call" | custom-call | flops 536870912 | bytes 6291456 | tf_op jit(solution)/shard_map/terms/pallas_call | solution.py:160
  70.8 6.8 %weight_terms.1 = bf16[6,256,256]{2,1,0:T(8,128)(2,1)} custom-call(bf16[6,256,2048]{2,1,0:T(8,128)(2,1)} %terms.1, bf16[2048,256]{1,0:T(8,128)(2,1)} %bitcast.81), custom_call_target="tpu_custom_call" | custom-call | tf_op jit(solution)/shard_map/weight_terms/pallas_call | solution.py:185
  78.8 3.5 %collective-permute-start.11 = (bf16[384,256]{1,0:T(8,128)(2,1)S(1)}, bf16[384,256]{1,0:T(8,128)(2,1)S(1)}, u32[]{:S(2)}, u32[]{:S(2)}) collective-permute-start(bf16[384,256]{1,0:T(8,128)(2,1)S(1)} %get-tuple-element.10), channel_id=1, source_target_pairs={{0,6},{2,4},{4,2},{6,0},{1,7},{3,5},{5,3},{7,1},{8,14},{10,12},{12... | collective-permute-start | bytes 589832 | tf_op jit(solution)/shard_map/ppermute | solution.py:21
  83.0 4.7 %collective-permute-done.11 = bf16[384,256]{1,0:T(8,128)(2,1)S(1)} collective-permute-done((bf16[384,256]{1,0:T(8,128)(2,1)S(1)}, bf16[384,256]{1,0:T(8,128)(2,1)S(1)}, u32[]{:S(2)}, u32[]{:S(2)}) %collective-permute-start.11) | collective-permute-done | bytes 196640 | tf_op jit(solution)/shard_map/ppermute | solution.py:21
  87.7 4.6 %collective-permute-done.12 = bf16[384,256]{1,0:T(8,128)(2,1)S(1)} collective-permute-done((bf16[384,256]{1,0:T(8,128)(2,1)S(1)}, bf16[384,256]{1,0:T(8,128)(2,1)S(1)}, u32[]{:S(2)}, u32[]{:S(2)}) %collective-permute-start.12) | collective-permute-done | bytes 196640 | tf_op jit(solution)/shard_map/ppermute | solution.py:21
  93.5 3.4 %collective-permute-start.15 = (bf16[96,256]{1,0:T(8,128)(2,1)S(1)}, bf16[96,256]{1,0:T(8,128)(2,1)S(1)}, u32[]{:S(2)}, u32[]{:S(2)}) collective-permute-start(bf16[96,256]{1,0:T(8,128)(2,1)S(1)} %get-tuple-element.18), channel_id=1, source_target_pairs={{0,16},{8,24},{16,0},{24,8},{1,17},{9,25},{17,1},{25,9},{2,18},{10... | collective-permute-start | bytes 147464 | tf_op jit(solution)/shard_map/ppermute | solution.py:21
  97.8 2.0 %collective-permute-done.14 = bf16[96,256]{1,0:T(8,128)(2,1)S(1)} collective-permute-done((bf16[96,256]{1,0:T(8,128)(2,1)S(1)}, bf16[96,256]{1,0:T(8,128)(2,1)S(1)}, u32[]{:S(2)}, u32[]{:S(2)}) %collective-permute-start.14) | collective-permute-done | bytes 49184 | tf_op jit(solution)/shard_map/ppermute | solution.py:21
  103.1 2.8 %collective-permute-start.19 = (bf16[96,256]{1,0:T(8,128)(2,1)S(1)}, bf16[96,256]{1,0:T(8,128)(2,1)S(1)}, u32[]{:S(2)}, u32[]{:S(2)}) collective-permute-start(bf16[96,256]{1,0:T(8,128)(2,1)S(1)} %fusion.8), channel_id=1, source_target_pairs={{0,24},{8,16},{16,8},{24,0},{1,25},{9,17},{17,9},{25,1},{2,26},{10... | collective-permute-start | bytes 147464 | tf_op jit(solution)/shard_map/ppermute | solution.py:21
  107.0 2.0 %collective-permute-done.19 = bf16[96,256]{1,0:T(8,128)(2,1)S(1)} collective-permute-done((bf16[96,256]{1,0:T(8,128)(2,1)S(1)}, bf16[96,256]{1,0:T(8,128)(2,1)S(1)}, u32[]{:S(2)}, u32[]{:S(2)}) %collective-permute-start.19) | collective-permute-done | bytes 49184 | tf_op jit(solution)/shard_map/ppermute | solution.py:21
  111.5 1.6 %collective-permute-start.22 = (bf16[384,256]{1,0:T(8,128)(2,1)S(1)}, bf16[384,256]{1,0:T(8,128)(2,1)S(1)}, u32[]{:S(2)}, u32[]{:S(2)}) collective-permute-start(bf16[384,256]{1,0:T(8,128)(2,1)S(1)} %bitcast.88), channel_id=1, source_target_pairs={{0,6},{2,4},{4,2},{6,0},{1,7},{3,5},{5,3},{7,1},{8,14},{10,12},{12... | collective-permute-start | bytes 589832 | tf_op jit(solution)/shard_map/ppermute | solution.py:21
  113.2 2.5 %collective-permute-done.20 = bf16[384,256]{1,0:T(8,128)(2,1)S(1)} collective-permute-done((bf16[384,256]{1,0:T(8,128)(2,1)S(1)}, bf16[384,256]{1,0:T(8,128)(2,1)S(1)}, u32[]{:S(2)}, u32[]{:S(2)}) %collective-permute-start.20) | collective-permute-done | bytes 196640 | tf_op jit(solution)/shard_map/ppermute | solution.py:21
  115.7 3.3 %collective-permute-done.21 = bf16[384,256]{1,0:T(8,128)(2,1)S(1)} collective-permute-done((bf16[384,256]{1,0:T(8,128)(2,1)S(1)}, bf16[384,256]{1,0:T(8,128)(2,1)S(1)}, u32[]{:S(2)}, u32[]{:S(2)}) %collective-permute-start.21) | collective-permute-done | bytes 196640 | tf_op jit(solution)/shard_map/ppermute | solution.py:21
  (58 shorter events, 21.1 us)
Async XLA Ops:
  0.6 8.3 %collective-permute-start = (bf16[256,256]{1,0:T(8,128)(2,1)}, bf16[256,256]{1,0:T(8,128)(2,1)S(1)}, u32[]{:S(2)}, u32[]{:S(2)}) collective-permute-start(bf16[256,256]{1,0:T(8,128)(2,1)} %param.7), channel_id=1, source_target_pairs={{0,8},{8,0},{16,24},{24,16},{1,9},{9,1},{17,25},{25,17},{2,10},{10... | collective-permute-start | bytes 393224 | tf_op jit(solution)/shard_map/ppermute | solution.py:21
  3.7 13.2 %collective-permute-start.1 = (bf16[256,256]{1,0:T(8,128)(2,1)}, bf16[256,256]{1,0:T(8,128)(2,1)S(1)}, u32[]{:S(2)}, u32[]{:S(2)}) collective-permute-start(bf16[256,256]{1,0:T(8,128)(2,1)} %param.7), channel_id=1, source_target_pairs={{0,16},{8,24},{16,0},{24,8},{1,17},{9,25},{17,1},{25,9},{2,18},{10... | collective-permute-start | bytes 393224 | tf_op jit(solution)/shard_map/ppermute | solution.py:21
  6.3 10.6 %collective-permute-start.2 = (bf16[256,256]{1,0:T(8,128)(2,1)}, bf16[256,256]{1,0:T(8,128)(2,1)S(1)}, u32[]{:S(2)}, u32[]{:S(2)}) collective-permute-start(bf16[256,256]{1,0:T(8,128)(2,1)} %param.7), channel_id=1, source_target_pairs={{0,24},{8,16},{16,8},{24,0},{1,25},{9,17},{17,9},{25,1},{2,26},{10... | collective-permute-start | bytes 393224 | tf_op jit(solution)/shard_map/ppermute | solution.py:21
  29.2 14.6 %copy-start.3 = (bf16[256,256]{1,0:T(8,128)(2,1)S(1)}, bf16[256,256]{1,0:T(8,128)(2,1)}, u32[]{:S(2)}) copy-start(bf16[256,256]{1,0:T(8,128)(2,1)} %param.13) | copy-start | bytes 393220
  29.2 2.1 %collective-permute-start.3 = (bf16[4,256,256]{2,1,0:T(8,128)(2,1)}, bf16[4,256,256]{2,1,0:T(8,128)(2,1)S(1)}, u32[]{:S(2)}, u32[]{:S(2)}) collective-permute-start(bf16[4,256,256]{2,1,0:T(8,128)(2,1)} %get-tuple-element.5), channel_id=1, source_target_pairs={{0,1},{1,0},{2,3},{3,2},{4,5},{5,4},{6,7},{7,6},{8,9},{9,8},{10,11... | collective-permute-start | bytes 1572872 | tf_op jit(solution)/shard_map/ppermute | solution.py:21
  32.7 8.4 %collective-permute-start.4 = (bf16[256,256]{1,0:T(8,128)(2,1)S(1)}, bf16[256,256]{1,0:T(8,128)(2,1)S(1)}, u32[]{:S(2)}, u32[]{:S(2)}) collective-permute-start(bf16[256,256]{1,0:T(8,128)(2,1)S(1)} %get-tuple-element.13), channel_id=1, source_target_pairs={{0,6},{2,4},{4,2},{6,0},{1,7},{3,5},{5,3},{7,1},{8,14},{10,12},{12... | collective-permute-start | bytes 393224 | tf_op jit(solution)/shard_map/ppermute | solution.py:21
  37.2 6.6 %collective-permute-start.5 = (bf16[256,256]{1,0:T(8,128)(2,1)S(1)}, bf16[256,256]{1,0:T(8,128)(2,1)S(1)}, u32[]{:S(2)}, u32[]{:S(2)}) collective-permute-start(bf16[256,256]{1,0:T(8,128)(2,1)S(1)} %get-tuple-element.15), channel_id=1, source_target_pairs={{0,4},{2,6},{4,0},{6,2},{1,5},{3,7},{5,1},{7,3},{8,12},{10,14},{12... | collective-permute-start | bytes 393224 | tf_op jit(solution)/shard_map/ppermute | solution.py:21
  37.2 6.6 %collective-permute-start.6 = (bf16[256,256]{1,0:T(8,128)(2,1)S(1)}, bf16[256,256]{1,0:T(8,128)(2,1)S(1)}, u32[]{:S(2)}, u32[]{:S(2)}) collective-permute-start(bf16[256,256]{1,0:T(8,128)(2,1)S(1)} %get-tuple-element.14), channel_id=1, source_target_pairs={{0,2},{2,0},{4,6},{6,4},{1,3},{3,1},{5,7},{7,5},{8,10},{10,8},{12,... | collective-permute-start | bytes 393224 | tf_op jit(solution)/shard_map/ppermute | solution.py:21
  44.7 6.2 %collective-permute-start.7 = (bf16[256,256]{1,0:T(8,128)(2,1)S(1)}, bf16[256,256]{1,0:T(8,128)(2,1)S(1)}, u32[]{:S(2)}, u32[]{:S(2)}) collective-permute-start(bf16[256,256]{1,0:T(8,128)(2,1)S(1)} %get-tuple-element.8), channel_id=1, source_target_pairs={{0,2},{2,0},{4,6},{6,4},{1,3},{3,1},{5,7},{7,5},{8,10},{10,8},{12,... | collective-permute-start | bytes 393224 | tf_op jit(solution)/shard_map/ppermute | solution.py:21
  46.4 7.4 %collective-permute-start.8 = (bf16[256,256]{1,0:T(8,128)(2,1)S(1)}, bf16[256,256]{1,0:T(8,128)(2,1)S(1)}, u32[]{:S(2)}, u32[]{:S(2)}) collective-permute-start(bf16[256,256]{1,0:T(8,128)(2,1)S(1)} %get-tuple-element.8), channel_id=1, source_target_pairs={{0,4},{2,6},{4,0},{6,2},{1,5},{3,7},{5,1},{7,3},{8,12},{10,14},{12... | collective-permute-start | bytes 393224 | tf_op jit(solution)/shard_map/ppermute | solution.py:21
  47.0 6.8 %collective-permute-start.9 = (bf16[256,256]{1,0:T(8,128)(2,1)S(1)}, bf16[256,256]{1,0:T(8,128)(2,1)S(1)}, u32[]{:S(2)}, u32[]{:S(2)}) collective-permute-start(bf16[256,256]{1,0:T(8,128)(2,1)S(1)} %get-tuple-element.8), channel_id=1, source_target_pairs={{0,6},{2,4},{4,2},{6,0},{1,7},{3,5},{5,3},{7,1},{8,14},{10,12},{12... | collective-permute-start | bytes 393224 | tf_op jit(solution)/shard_map/ppermute | solution.py:21
  54.5 14.6 %collective-permute-start.10 = (bf16[4,256,256]{2,1,0:T(8,128)(2,1)S(1)}, bf16[4,256,256]{2,1,0:T(8,128)(2,1)S(1)}, u32[]{:S(2)}, u32[]{:S(2)}) collective-permute-start(bf16[4,256,256]{2,1,0:T(8,128)(2,1)S(1)} %gather_fusion), channel_id=1, source_target_pairs={{0,1},{1,0},{2,3},{3,2},{4,5},{5,4},{6,7},{7,6},{8,9},{9,8},{10,11... | collective-permute-start | bytes 1572872 | tf_op jit(solution)/shard_map/ppermute | solution.py:21
  78.8 8.9 %collective-permute-start.11 = (bf16[384,256]{1,0:T(8,128)(2,1)S(1)}, bf16[384,256]{1,0:T(8,128)(2,1)S(1)}, u32[]{:S(2)}, u32[]{:S(2)}) collective-permute-start(bf16[384,256]{1,0:T(8,128)(2,1)S(1)} %get-tuple-element.10), channel_id=1, source_target_pairs={{0,6},{2,4},{4,2},{6,0},{1,7},{3,5},{5,3},{7,1},{8,14},{10,12},{12... | collective-permute-start | bytes 589832 | tf_op jit(solution)/shard_map/ppermute | solution.py:21
  82.3 10.0 %collective-permute-start.12 = (bf16[384,256]{1,0:T(8,128)(2,1)S(1)}, bf16[384,256]{1,0:T(8,128)(2,1)S(1)}, u32[]{:S(2)}, u32[]{:S(2)}) collective-permute-start(bf16[384,256]{1,0:T(8,128)(2,1)S(1)} %get-tuple-element.12), channel_id=1, source_target_pairs={{0,4},{2,6},{4,0},{6,2},{1,5},{3,7},{5,1},{7,3},{8,12},{10,14},{12... | collective-permute-start | bytes 589832 | tf_op jit(solution)/shard_map/ppermute | solution.py:21
  82.3 10.0 %collective-permute-start.13 = (bf16[384,256]{1,0:T(8,128)(2,1)S(1)}, bf16[384,256]{1,0:T(8,128)(2,1)S(1)}, u32[]{:S(2)}, u32[]{:S(2)}) collective-permute-start(bf16[384,256]{1,0:T(8,128)(2,1)S(1)} %get-tuple-element.11), channel_id=1, source_target_pairs={{0,2},{2,0},{4,6},{6,4},{1,3},{3,1},{5,7},{7,5},{8,10},{10,8},{12,... | collective-permute-start | bytes 589832 | tf_op jit(solution)/shard_map/ppermute | solution.py:21
  93.4 6.5 %collective-permute-start.14 = (bf16[96,256]{1,0:T(8,128)(2,1)S(1)}, bf16[96,256]{1,0:T(8,128)(2,1)S(1)}, u32[]{:S(2)}, u32[]{:S(2)}) collective-permute-start(bf16[96,256]{1,0:T(8,128)(2,1)S(1)} %get-tuple-element.16), channel_id=1, source_target_pairs={{0,24},{8,16},{16,8},{24,0},{1,25},{9,17},{17,9},{25,1},{2,26},{10... | collective-permute-start | bytes 147464 | tf_op jit(solution)/shard_map/ppermute | solution.py:21
  93.5 7.7 %collective-permute-start.15 = (bf16[96,256]{1,0:T(8,128)(2,1)S(1)}, bf16[96,256]{1,0:T(8,128)(2,1)S(1)}, u32[]{:S(2)}, u32[]{:S(2)}) collective-permute-start(bf16[96,256]{1,0:T(8,128)(2,1)S(1)} %get-tuple-element.18), channel_id=1, source_target_pairs={{0,16},{8,24},{16,0},{24,8},{1,17},{9,25},{17,1},{25,9},{2,18},{10... | collective-permute-start | bytes 147464 | tf_op jit(solution)/shard_map/ppermute | solution.py:21
  96.9 4.6 %collective-permute-start.16 = (bf16[96,256]{1,0:T(8,128)(2,1)S(1)}, bf16[96,256]{1,0:T(8,128)(2,1)S(1)}, u32[]{:S(2)}, u32[]{:S(2)}) collective-permute-start(bf16[96,256]{1,0:T(8,128)(2,1)S(1)} %get-tuple-element.17), channel_id=1, source_target_pairs={{0,8},{8,0},{16,24},{24,16},{1,9},{9,1},{17,25},{25,17},{2,10},{10... | collective-permute-start | bytes 147464 | tf_op jit(solution)/shard_map/ppermute | solution.py:21
  101.5 4.7 %collective-permute-start.17 = (bf16[96,256]{1,0:T(8,128)(2,1)S(1)}, bf16[96,256]{1,0:T(8,128)(2,1)S(1)}, u32[]{:S(2)}, u32[]{:S(2)}) collective-permute-start(bf16[96,256]{1,0:T(8,128)(2,1)S(1)} %fusion.8), channel_id=1, source_target_pairs={{0,8},{8,0},{16,24},{24,16},{1,9},{9,1},{17,25},{25,17},{2,10},{10... | collective-permute-start | bytes 147464 | tf_op jit(solution)/shard_map/ppermute | solution.py:21
  102.0 5.0 %collective-permute-start.18 = (bf16[96,256]{1,0:T(8,128)(2,1)S(1)}, bf16[96,256]{1,0:T(8,128)(2,1)S(1)}, u32[]{:S(2)}, u32[]{:S(2)}) collective-permute-start(bf16[96,256]{1,0:T(8,128)(2,1)S(1)} %fusion.8), channel_id=1, source_target_pairs={{0,16},{8,24},{16,0},{24,8},{1,17},{9,25},{17,1},{25,9},{2,18},{10... | collective-permute-start | bytes 147464 | tf_op jit(solution)/shard_map/ppermute | solution.py:21
  103.1 5.9 %collective-permute-start.19 = (bf16[96,256]{1,0:T(8,128)(2,1)S(1)}, bf16[96,256]{1,0:T(8,128)(2,1)S(1)}, u32[]{:S(2)}, u32[]{:S(2)}) collective-permute-start(bf16[96,256]{1,0:T(8,128)(2,1)S(1)} %fusion.8), channel_id=1, source_target_pairs={{0,24},{8,16},{16,8},{24,0},{1,25},{9,17},{17,9},{25,1},{2,26},{10... | collective-permute-start | bytes 147464 | tf_op jit(solution)/shard_map/ppermute | solution.py:21
  109.6 6.1 %collective-permute-start.20 = (bf16[384,256]{1,0:T(8,128)(2,1)S(1)}, bf16[384,256]{1,0:T(8,128)(2,1)S(1)}, u32[]{:S(2)}, u32[]{:S(2)}) collective-permute-start(bf16[384,256]{1,0:T(8,128)(2,1)S(1)} %bitcast.86), channel_id=1, source_target_pairs={{0,2},{2,0},{4,6},{6,4},{1,3},{3,1},{5,7},{7,5},{8,10},{10,8},{12,... | collective-permute-start | bytes 589832 | tf_op jit(solution)/shard_map/ppermute | solution.py:21
  110.7 8.2 %collective-permute-start.21 = (bf16[384,256]{1,0:T(8,128)(2,1)S(1)}, bf16[384,256]{1,0:T(8,128)(2,1)S(1)}, u32[]{:S(2)}, u32[]{:S(2)}) collective-permute-start(bf16[384,256]{1,0:T(8,128)(2,1)S(1)} %bitcast.87), channel_id=1, source_target_pairs={{0,4},{2,6},{4,0},{6,2},{1,5},{3,7},{5,1},{7,3},{8,12},{10,14},{12... | collective-permute-start | bytes 589832 | tf_op jit(solution)/shard_map/ppermute | solution.py:21
  111.5 7.4 %collective-permute-start.22 = (bf16[384,256]{1,0:T(8,128)(2,1)S(1)}, bf16[384,256]{1,0:T(8,128)(2,1)S(1)}, u32[]{:S(2)}, u32[]{:S(2)}) collective-permute-start(bf16[384,256]{1,0:T(8,128)(2,1)S(1)} %bitcast.88), channel_id=1, source_target_pairs={{0,6},{2,4},{4,2},{6,0},{1,7},{3,5},{5,3},{7,1},{8,14},{10,12},{12... | collective-permute-start | bytes 589832 | tf_op jit(solution)/shard_map/ppermute | solution.py:21
  (3 other events, 9.3 us)

commit v2 on v0

v2 whole, which is shorter than its diff:
```python
import functools
import math

import jax
import jax.numpy as jnp
from jax import lax
from jax.experimental import pallas as pl
from jax.experimental.pallas import tpu as pltpu
from jax.sharding import PartitionSpec as P

F32, BF16, I32 = jnp.float32, jnp.bfloat16, jnp.int32
WHOLE = pl.BlockSpec(memory_space=pltpu.VMEM)
SCALARS = pl.BlockSpec(memory_space=pltpu.SMEM)
UNROLL = 16


def vmem_for(*arrays):
    held = sum(math.prod(a.shape) * jnp.dtype(a.dtype).itemsize for a in arrays)
    return pltpu.CompilerParams(vmem_limit_bytes=held + held // 8 + 3 * 1024 * 1024)


def partner_pairs(size, mask):
    return [(i, i ^ mask) for i in range(size)]


def swap(value, axis, mask):
    return lax.ppermute(value, axis, partner_pairs(lax.axis_size(axis), mask))


def slot_of(places, partition, masked):
    return partition ^ places[0] if masked else partition


def for_entries(total, body):
    def step(i, carry):
        body([(jnp.minimum(i * UNROLL + u, total - 1), i * UNROLL + u < total) for u in range(UNROLL)])
        return carry

    lax.fori_loop(0, (total + UNROLL - 1) // UNROLL, step, 0)


def halo_block(places, chosen, halo_refs, i, first_slot, masked, tile):
    per_call = halo_refs[0].shape[0]
    first = pl.multiple_of(chosen[slot_of(places, i + first_slot, masked)] * tile, tile)
    return halo_refs[i // per_call][i % per_call, pl.ds(first, tile), :]


def forward_kernel(masked, tile, first_slot, halo_count, earlier, last, combine, *refs):
    places, chosen, table, count = refs[:4]
    halo_refs, refs = refs[4 : 4 + halo_count], refs[4 + halo_count :]
    weight, values, refs = refs[0], refs[1], refs[2:]
    before, refs = (refs[0], refs[1:]) if earlier else (None, refs)
    if last:
        keep, send, pre, projected, order = refs
    else:
        pre, projected, order = refs
    relations = weight.shape[0]
    slots = halo_count * halo_refs[0].shape[0]

    def pick(e, found):
        slot = slot_of(places, table[1, e], masked) - first_slot

        @pl.when((slot >= 0) & (slot < slots))
        def _():
            order[found] = e

        return found + ((slot >= 0) & (slot < slots)).astype(I32)

    total = lax.fori_loop(0, count[0], pick, jnp.int32(0))
    for i in range(slots):
        block = halo_block(places, chosen, halo_refs, i, first_slot, masked, tile)
        if combine:
            for r in range(relations):
                projected[i * relations + r] = jnp.dot(
                    block, weight[r], preferred_element_type=F32
                ).astype(BF16)
        else:
            projected[i] = block
    pre[...] = jnp.zeros_like(pre)
    spare = pre.shape[0] - 1

    def body(positions):
        terms = []
        for position, _ in positions:
            e = order[position]
            slot = slot_of(places, table[1, e], masked) - first_slot
            relation = table[2, e]
            if combine:
                term = jnp.dot(
                    values[e], projected[slot * relations + relation], preferred_element_type=F32
                )
            else:
                message = jnp.dot(values[e], projected[slot], preferred_element_type=F32)
                term = jnp.dot(message.astype(BF16), weight[relation], preferred_element_type=F32)
            terms.append(term)
        for (position, real), term in zip(positions, terms):
            target = jnp.where(real, table[0, order[position]], spare)
            pre[target] = pre[target] + term

    for_entries(total, body)
    if not last:
        return
    panels, per_owner = keep.shape[0], keep.shape[1] // tile
    groups = spare // (panels * per_owner)
    for distance in range(panels):
        panel = places[1] ^ distance
        for part in range(per_owner):
            rows = pl.ds(part * tile, tile)
            mine = (panel * groups + places[2]) * per_owner + part
            other = (panel * groups + (places[2] ^ 1)) * per_owner + part
            mine_rows, other_rows = pre[mine], pre[other]
            if earlier:
                mine_rows, other_rows = mine_rows + before[mine], other_rows + before[other]
            keep[distance, rows, :] = mine_rows
            send[distance, rows, :] = other_rows.astype(BF16)


def turn_kernel(masked, tile, halo_count, shares, places, chosen, *refs):
    halo_refs = refs[:halo_count]
    values, values_turned, halo_turned, scratch = refs[halo_count:]
    panels, parts = shares
    per_call = halo_refs[0].shape[0]
    features = scratch.shape[0]
    share = features // (panels * parts)
    for slot in range(halo_count * per_call):
        block = halo_block(places, chosen, halo_refs, slot, 0, masked, tile)
        scratch[...] = block.astype(F32).T
        for m in range(panels):
            for k in range(parts):
                part = (places[0] ^ k) if parts > 1 else 0
                start = pl.multiple_of(((places[1] ^ m) * parts + part) * share, share)
                halo_turned[pl.ds((m * parts + k) * share, share), pl.ds(slot * tile, tile)] = (
                    scratch[pl.ds(start, share), :].astype(BF16)
                )

    batch = 8

    def step(i, carry):
        for u in range(batch):
            values_turned[i * batch + u] = values[i * batch + u].T
        return carry

    lax.fori_loop(0, values.shape[0] // batch, step, 0)


def weight_kernel(masked, tile, shares, combine, places, table, count, *refs):
    panels, parts = shares
    values_turned, halo_turned = refs[:2]
    grad_refs, refs = refs[2 : 2 + 2 * panels], refs[2 + 2 * panels :]
    outs, (grads, sums) = refs[:panels], refs[panels:]
    features = halo_turned.shape[0]
    slots = halo_turned.shape[1] // tile
    relations = outs[0].shape[1]
    share = features // (panels * parts)
    own_rows = grad_refs[0].shape[0]
    per_owner = own_rows // tile
    for g in range(2):
        for m in range(panels):
            owner = (places[1] ^ m) * 2 + (places[2] ^ g)
            for part in range(per_owner):
                grads[owner * per_owner + part] = grad_refs[g * panels + m][
                    pl.ds(part * tile, tile), :
                ]
    sums[...] = jnp.zeros_like(sums)
    spare = sums.shape[0] - 1

    def body(positions):
        terms = []
        for e, _ in positions:
            term = jnp.dot(values_turned[e], grads[table[0, e]], preferred_element_type=F32)
            if not combine:
                slot = slot_of(places, table[1, e], masked)
                columns = pl.ds(pl.multiple_of(slot * tile, tile), tile)
                term = jnp.dot(
                    halo_turned[:, columns], term.astype(BF16), preferred_element_type=F32
                )
            terms.append(term)
        for (e, real), term in zip(positions, terms):
            place = table[2, e]
            if combine:
                place = place * slots + slot_of(places, table[1, e], masked)
            place = jnp.where(real, place, spare)
            sums[place] = sums[place] + term

    for_entries(count[0], body)
    for r in range(relations):
        if combine:
            stacked = sums[r * slots : (r + 1) * slots].reshape(slots * tile, features)
            grad = jnp.dot(halo_turned[...], stacked.astype(BF16), preferred_element_type=F32)
        else:
            grad = sums[r]
        for m in range(panels):
            for k in range(parts):
                rows = slice((m * parts + k) * share, (m * parts + k + 1) * share)
                outs[m][k, r] = grad[rows].astype(BF16)


def spread_kernel(shares, places, *refs):
    panels, parts = shares
    shares_in, out = refs[:panels], refs[panels]
    share = shares_in[0].shape[2]
    for m in range(panels):
        for k in range(parts):
            part = (places[0] ^ k) if parts > 1 else 0
            start = pl.multiple_of(((places[1] ^ m) * parts + part) * share, share)
            for r in range(out.shape[0]):
                out[r, pl.ds(start, share), :] = shares_in[m][k, r].astype(F32)


def silu_slope(pre_values):
    logistic = jax.nn.sigmoid(pre_values)
    return logistic * (1.0 + pre_values * (1.0 - logistic))


def exchange(pieces, axis):
    return [swap(pieces[m].astype(BF16), axis, m) for m in range(len(pieces) - 1, 0, -1)]


def added(own, arrived):
    total = own.astype(F32)
    for value in arrived:
        total = total + value.astype(F32)
    return total


def gather(value, axis):
    return [value] + [swap(value, axis, m) for m in range(1, lax.axis_size(axis))]


def local(source_feats, rel_weight, halo_pick, entry_index, entry_count, entry_values, cotangent):
    partitions, panels = lax.axis_size("dom"), lax.axis_size("src")
    groups = lax.axis_size("rel")
    tile = entry_values.shape[-1]
    own_rows, features = cotangent.shape
    relations = rel_weight.shape[0]
    values = entry_values.reshape(-1, tile, tile)
    table = entry_index.reshape(3, -1)
    entries = table.shape[1]
    count = entry_count.reshape(1)
    chosen = halo_pick.reshape(-1)
    places = jnp.stack([lax.axis_index(a) for a in ("dom", "src", "rel")]).astype(I32)
    targets = own_rows * panels * groups // tile
    direct = partitions <= 8
    parts = partitions if direct else 1
    shares = (panels, parts)
    share = features // (panels * parts)

    if direct:
        halo = gather(source_feats, "dom")
        halo = [h[None] for h in halo]
        calls = [halo[: partitions // 2], halo[partitions // 2 :]]
    else:
        halo = [lax.all_gather(source_feats, "dom", axis=0)]
        calls = [halo]
    slots = sum(h.shape[0] for h in halo)
    combine = slots * relations <= entries

    before, first_slot = [], 0
    for number, part in enumerate(calls):
        last = number == len(calls) - 1
        here = sum(h.shape[0] for h in part)
        sums = jax.ShapeDtypeStruct((targets + 1, tile, features), F32)
        projected = (here * relations if combine else here, tile, features)
        projected = jax.ShapeDtypeStruct(projected, BF16)
        scratch = [pltpu.VMEM(projected.shape, BF16), pltpu.SMEM((entries,), I32)]
        grant = vmem_for(sums, projected, *part, rel_weight, values, *before)
        if last:
            out_shape = (
                jax.ShapeDtypeStruct((panels, own_rows, features), F32),
                jax.ShapeDtypeStruct((panels, own_rows, features), BF16),
            )
            scratch = [pltpu.VMEM(sums.shape, F32)] + scratch
            grant = vmem_for(sums, projected, *part, rel_weight, values, *before, *out_shape)
        else:
            out_shape = (sums,)
        before = pl.pallas_call(
            functools.partial(
                forward_kernel, direct, tile, first_slot, len(part), bool(before), last, combine
            ),
            out_shape=out_shape,
            in_specs=[SCALARS] * 4 + [WHOLE] * (len(part) + 2 + len(before)),
            out_specs=(WHOLE,) * len(out_shape),
            scratch_shapes=scratch,
            compiler_params=grant,
            cost_estimate=pl.CostEstimate(
                flops=2 * entries * tile * tile * features * 4,
                bytes_accessed=values.size * 2,
                transcendentals=0,
            ),
            name="forward",
        )(places, chosen, table, count, *part, rel_weight, values, *before)
        first_slot += here
    keep, send = before

    chip_sum = keep + swap(send, "rel", 1).astype(F32)
    arrived = exchange([chip_sum[m] for m in range(panels)], "src")

    turned = (
        jax.ShapeDtypeStruct(values.shape, BF16),
        jax.ShapeDtypeStruct((features, slots * tile), BF16),
    )
    values_turned, halo_turned = pl.pallas_call(
        functools.partial(turn_kernel, direct, tile, len(halo), shares),
        out_shape=turned,
        in_specs=[SCALARS] * 2 + [WHOLE] * (len(halo) + 1),
        out_specs=(WHOLE, WHOLE),
        scratch_shapes=[pltpu.VMEM((features, tile), F32)],
        compiler_params=vmem_for(*turned, values, *halo),
        cost_estimate=pl.CostEstimate(
            flops=0, bytes_accessed=4 * values.size, transcendentals=0
        ),
        name="turn",
    )(places, chosen, *halo, values)
    arrived, values_turned, halo_turned = lax.optimization_barrier(
        (arrived, values_turned, halo_turned)
    )
    pre = added(chip_sum[0], arrived)

    out_feats = jax.nn.silu(pre).astype(BF16)
    local_grad = (cotangent.astype(F32) * silu_slope(pre)).astype(BF16)

    core_grads = gather(local_grad, "src")
    other_grads = [swap(value, "rel", 1) for value in core_grads]

    rows = shares[1], relations, share, features
    grads = jax.ShapeDtypeStruct((targets, tile, features), BF16)
    sums = jax.ShapeDtypeStruct(
        (relations * slots + 1, tile, features) if combine else (relations + 1, features, features),
        F32,
    )
    weight_shares = pl.pallas_call(
        functools.partial(weight_kernel, direct, tile, shares, combine),
        out_shape=(jax.ShapeDtypeStruct(rows, BF16),) * panels,
        in_specs=[SCALARS] * 3 + [WHOLE] * (2 + 2 * panels),
        out_specs=(WHOLE,) * panels,
        scratch_shapes=[pltpu.VMEM(grads.shape, BF16), pltpu.VMEM(sums.shape, F32)],
        compiler_params=vmem_for(grads, grads, sums, *turned, rel_weight),
        name="weight_terms",
    )(places, table, count, values_turned, halo_turned, *core_grads, *other_grads)

    panel_sum = added(weight_shares[0], exchange(weight_shares, "src"))
    if direct:
        part_sum = added(
            panel_sum[0], exchange([panel_sum[k] for k in range(parts)], "dom")
        ).astype(BF16)
        whole_sum = jnp.stack(gather(part_sum, "dom"))
    else:
        whole_sum = lax.psum(panel_sum, "dom").astype(BF16)
    total = jax.ShapeDtypeStruct((relations, features, features), F32)
    grad_rel = pl.pallas_call(
        functools.partial(spread_kernel, shares),
        out_shape=total,
        in_specs=[SCALARS] + [WHOLE] * panels,
        out_specs=WHOLE,
        compiler_params=vmem_for(total, rel_weight),
        name="spread",
    )(places, *gather(whole_sum, "src"))
    return (out_feats, grad_rel)


def solution(mesh):
    return jax.shard_map(
        local,
        mesh=mesh,
        in_specs=(
            P(("dom", "src", "rel"), None),
            P("rel", None, None),
            P("dom", "src", "rel", None),
            P("dom", "src", "rel", None, None),
            P("dom", "src", "rel"),
            P("dom", "src", "rel", None, None, None),
            P(("dom", "src", "rel"), None),
        ),
        out_specs=(P(("dom", "src", "rel"), None), P("rel", None, None)),
        check_vma=False,
    )
```

time: 268 us -> 85.8 us (0.32)
  waiting for transfers between devices: 186 us -> 38.8 us
  starting transfers between devices: 0.12 us -> 29.5 us
  matrix products: 24.5 us -> 0 us
  blocking collectives: 17.6 us -> 0 us
  local copies, waits for them, and re-layouts: 21.7 us -> 5.03 us
  between operations: 14.5 us -> 1.41 us
  Pallas kernels: 0 us -> 9.13 us
  other arithmetic: 3.91 us -> 1.23 us
    psum x1 -> x0, waiting for transfers between devices: 118 us -> none  [local(): grad_rel = lax.psum(weight_terms, ('dom', 'src'))]
    reduce_scatter x1 -> x0, waiting for transfers between devices: 43.1 us -> none  [local(): lax.psum_scatter(jnp.einsum('rtd,rde->te', relation_terms, rel_weight, pr...]
    ppermute x0 -> x26, waiting for transfers between devices: none -> 38.8 us  [swap(): return lax.ppermute(value, axis, partner_pairs(lax.axis_size(axis), mask))]
    ppermute x0 -> x26, starting transfers between devices: none -> 29.5 us  [swap(): return lax.ppermute(value, axis, partner_pairs(lax.axis_size(axis), mask))]
    dot_general x4 -> x0, matrix products: 24.5 us -> none  [the longest x1 8.46 us: local(): jnp.einsum('se,eid->sid', placement, messages, precision=lax.Precision.HI...]
    all_gather x1 -> x0, waiting for transfers between devices: 24.3 us -> none  [local(): grad_rows = lax.all_gather(local_grad, ('src', 'rel'), axis=0, tiled=True)]
    all_gather x1 -> x0, blocking collectives: 17.6 us -> none  [local(): everyone = lax.all_gather(source_feats, 'dom', axis=0, tiled=True)]
    dot_general x1 -> x0, local copies, waits for them, and re-layouts: 9.24 us -> none  [local(): jnp.einsum('eij,ejd->eid', values, picked, preferred_element_type=jnp.flo...]
  transfers between devices with their start and end apart: 3 -> 26, of which waited for: 3 -> 18; matrix products, arithmetic and copies ran while one was open for 0% -> 1% of each run, Pallas kernels for 0% -> 4%
where the time goes in v2:
time: 85.8 us; the launch traced here: 85.1 us
  waiting for transfers between devices  38.8 us (45%)
  starting transfers between devices  29.5 us (34%)
  Pallas kernels  9.13 us (11%)
  local copies, waits for them, and re-layouts  5.03 us (6%)
  between operations  1.41 us (2%)
  other arithmetic  1.23 us (1%)
    ppermute x26, waiting for transfers between devices, swap(): return lax.ppermute(value, axis, partner_pairs(lax.axis_size(axis), mask))  38.8 us
    ppermute x26, starting transfers between devices, swap(): return lax.ppermute(value, axis, partner_pairs(lax.axis_size(axis), mask))  29.5 us
    unnamed x19, local copies, waits for them, and re-layouts  4.99 us
    pallas_call x2, Pallas kernels, local(): pl.pallas_call(functools.partial(forward_kernel, direct, tile, first_slot...  3.76 us
    pallas_call x1, Pallas kernels, local(): pl.pallas_call(functools.partial(weight_kernel, direct, tile, shares, com...  1.88 us
    pallas_call x1, Pallas kernels, local(): pl.pallas_call(functools.partial(spread_kernel, shares), out_shape=total,...  1.79 us
  transfers between devices with their start and end apart: 26, of which 18 were waited for; matrix products, arithmetic and copies ran while one was open for 1% of the time, Pallas kernels for 4%

profile of v2, /device:TPU:0, one launch (start us, length us, event | category | flops | bytes accessed | tf_op | source)
XLA Modules:
  0.0 85.1 jit_solution(7679678878593191394)
XLA Ops:
  0.6 3.1 %collective-permute-start.2 = (bf16[256,256]{1,0:T(8,128)(2,1)}, bf16[256,256]{1,0:T(8,128)(2,1)S(1)}, u32[]{:S(2)}, u32[]{:S(2)}) collective-permute-start(bf16[256,256]{1,0:T(8,128)(2,1)} %param.7), channel_id=1, source_target_pairs={{0,8},{8,0},{16,24},{24,16},{1,9},{9,1},{17,25},{25,17},{2,10},{10... | collective-permute-start | bytes 393224 | tf_op jit(solution)/shard_map/ppermute | solution.py:27
  3.7 2.5 %collective-permute-start.1 = (bf16[256,256]{1,0:T(8,128)(2,1)}, bf16[256,256]{1,0:T(8,128)(2,1)S(1)}, u32[]{:S(2)}, u32[]{:S(2)}) collective-permute-start(bf16[256,256]{1,0:T(8,128)(2,1)} %param.7), channel_id=1, source_target_pairs={{0,24},{8,16},{16,8},{24,0},{1,25},{9,17},{17,9},{25,1},{2,26},{10... | collective-permute-start | bytes 393224 | tf_op jit(solution)/shard_map/ppermute | solution.py:27
  7.7 1.6 %copy-done = bf16[1,1,1,64,128,128]{5,4,3,2,1,0:T(8,128)(2,1)S(1)} copy-done((bf16[1,1,1,64,128,128]{5,4,3,2,1,0:T(8,128)(2,1)S(1)}, bf16[1,1,1,64,128,128]{5,4,3,2,1,0:T(8,128)(2,1)}, u32[]{:S(2)}) %copy-start) | copy-done | bytes 2097176
  12.0 1.7 %forward.2.refs_8_ = f32[17,128,256]{2,1,0:T(8,128)S(1)} custom-call(s32[3]{0:T(128)S(1)} %pad_add_fusion.refs_0_.places, s32[4]{0:T(128)S(1)} %bitcast.68, s32[3,64]{1,0:T(4,128)S(1)} %bitcast.65, s32[1]{0:T(128)} %bitcast.51.refs_3_, bf16[1,256,256]{2,1,0:T(8,128)(2,1)S(1)} %bitcast.57, bf16[1,256,256]{2,1,0:T(8,128)(2,1)S(1)} %bitcast.59, ...), custom_call_target="tpu_custom_call" | custom-call | flops 2147483648 | bytes 2097152 | tf_op jit(solution)/shard_map/forward/pallas_call | solution.py:276
  13.8 4.4 %collective-permute-done = bf16[256,256]{1,0:T(8,128)(2,1)S(1)} collective-permute-done((bf16[256,256]{1,0:T(8,128)(2,1)}, bf16[256,256]{1,0:T(8,128)(2,1)S(1)}, u32[]{:S(2)}, u32[]{:S(2)}) %collective-permute-start) | collective-permute-done | bytes 131104 | tf_op jit(solution)/shard_map/ppermute | solution.py:27
  18.2 2.0 %forward.3 = (f32[4,256,256]{2,1,0:T(8,128)S(1)}, bf16[4,256,256]{2,1,0:T(8,128)(2,1)S(1)}) custom-call(s32[3]{0:T(128)S(1)} %pad_add_fusion.refs_0_.places, s32[4]{0:T(128)S(1)} %bitcast.69, s32[3,64]{1,0:T(4,128)S(1)} %bitcast.66, s32[1]{0:T(128)} %bitcast.52.refs_3_, bf16[1,256,256]{2,1,0:T(8,128)(2,1)S(1)} %bitcast.63, ...), custom_call_target="tpu_custom_call" | custom-call | flops 2147483648 | bytes 2097152 | tf_op jit(solution)/shard_map/forward/pallas_call | solution.py:276
  20.3 1.9 %collective-permute-done.3 = bf16[4,256,256]{2,1,0:T(8,128)(2,1)S(1)} collective-permute-done((bf16[4,256,256]{2,1,0:T(8,128)(2,1)S(1)}, bf16[4,256,256]{2,1,0:T(8,128)(2,1)S(1)}, u32[]{:S(2)}, u32[]{:S(2)}) %collective-permute-start.3) | collective-permute-done | bytes 524320 | tf_op jit(solution)/shard_map/ppermute | solution.py:27
  23.8 2.7 %collective-permute-start.5 = (bf16[256,256]{1,0:T(8,128)(2,1)S(1)}, bf16[256,256]{1,0:T(8,128)(2,1)S(1)}, u32[]{:S(2)}, u32[]{:S(2)}) collective-permute-start(bf16[256,256]{1,0:T(8,128)(2,1)S(1)} %get-tuple-element.35), channel_id=1, source_target_pairs={{0,4},{2,6},{4,0},{6,2},{1,5},{3,7},{5,1},{7,3},{8,12},{10,14},{12... | collective-permute-start | bytes 393224 | tf_op jit(solution)/shard_map/ppermute | solution.py:27
  26.6 1.7 %turn.1 = (bf16[64,128,128]{2,1,0:T(8,128)(2,1)S(1)}, bf16[256,512]{1,0:T(8,128)(2,1)S(1)}) custom-call(s32[3]{0:T(128)S(1)} %pad_add_fusion.refs_0_.places, s32[4]{0:T(128)S(1)} %bitcast.70, bf16[1,256,256]{2,1,0:T(8,128)(2,1)S(1)} %bitcast.58, bf16[1,256,256]{2,1,0:T(8,128)(2,1)S(1)} %bitcast.60, bf16[1,256,256]{2,1,0:T(8,128)(2,1)S(1)} %bitcast.64, ...), custom_call_target="tpu_custom_call" | custom-call | bytes 4194304 | tf_op jit(solution)/shard_map/turn/pallas_call | solution.py:302
  28.3 4.6 %collective-permute-done.5 = bf16[256,256]{1,0:T(8,128)(2,1)S(1)} collective-permute-done((bf16[256,256]{1,0:T(8,128)(2,1)S(1)}, bf16[256,256]{1,0:T(8,128)(2,1)S(1)}, u32[]{:S(2)}, u32[]{:S(2)}) %collective-permute-start.5) | collective-permute-done | bytes 131104 | tf_op jit(solution)/shard_map/ppermute | solution.py:27
  33.7 1.5 %collective-permute-start.9 = (bf16[256,256]{1,0:T(8,128)(2,1)S(1)}, bf16[256,256]{1,0:T(8,128)(2,1)S(1)}, u32[]{:S(2)}, u32[]{:S(2)}) collective-permute-start(bf16[256,256]{1,0:T(8,128)(2,1)S(1)} %get-tuple-element.32.refs_2_), channel_id=1, source_target_pairs={{0,6},{2,4},{4,2},{6,0},{1,7},{3,5},{5,3},{7,1},{8,14},{10,12},{12... | collective-permute-start | bytes 393224 | tf_op jit(solution)/shard_map/ppermute | solution.py:27
  37.2 3.8 %collective-permute-done.9.refs_5_ = bf16[256,256]{1,0:T(8,128)(2,1)S(1)} collective-permute-done((bf16[256,256]{1,0:T(8,128)(2,1)S(1)}, bf16[256,256]{1,0:T(8,128)(2,1)S(1)}, u32[]{:S(2)}, u32[]{:S(2)}) %collective-permute-start.9) | collective-permute-done | bytes 131104 | tf_op jit(solution)/shard_map/ppermute | solution.py:27
  43.5 1.9 %weight_terms.1 = (bf16[4,6,16,256]{3,2,1,0:T(8,128)(2,1)S(1)}, bf16[4,6,16,256]{3,2,1,0:T(8,128)(2,1)S(1)}, bf16[4,6,16,256]{3,2,1,0:T(8,128)(2,1)S(1)}, bf16[4,6,16,256]{3,2,1,0:T(8,128)(2,1)S(1)}) custom-call(s32[3]{0:T(128)S(1)} %pad_add_fusion.refs_0_.places, s32[3,64]{1,0:T(4,128)S(1)} %bitcast.67, s32[1]{0:T(128)} %bitcast.53.count, ...), custom_call_target="tpu_custom_call" | custom-call | tf_op jit(solution)/shard_map/weight_terms/pallas_call | solution.py:331
  45.4 3.1 %collective-permute-start.14 = (bf16[4,6,16,256]{3,2,1,0:T(8,128)(2,1)S(1)}, bf16[4,6,16,256]{3,2,1,0:T(8,128)(2,1)S(1)}, u32[]{:S(2)}, u32[]{:S(2)}) collective-permute-start(bf16[4,6,16,256]{3,2,1,0:T(8,128)(2,1)S(1)} %get-tuple-element.25), channel_id=1, source_target_pairs={{0,6},{2,4},{4,2},{6,0},{1,7},{3,5},{5,3},{7,1},{8,14},{10,12},{12... | collective-permute-start | bytes 589832 | tf_op jit(solution)/shard_map/ppermute | solution.py:27
  49.1 5.1 %collective-permute-done.14 = bf16[4,6,16,256]{3,2,1,0:T(8,128)(2,1)S(1)} collective-permute-done((bf16[4,6,16,256]{3,2,1,0:T(8,128)(2,1)S(1)}, bf16[4,6,16,256]{3,2,1,0:T(8,128)(2,1)S(1)}, u32[]{:S(2)}, u32[]{:S(2)}) %collective-permute-start.14) | collective-permute-done | bytes 196640 | tf_op jit(solution)/shard_map/ppermute | solution.py:27
  54.3 3.4 %collective-permute-done.15 = bf16[4,6,16,256]{3,2,1,0:T(8,128)(2,1)S(1)} collective-permute-done((bf16[4,6,16,256]{3,2,1,0:T(8,128)(2,1)S(1)}, bf16[4,6,16,256]{3,2,1,0:T(8,128)(2,1)S(1)}, u32[]{:S(2)}, u32[]{:S(2)}) %collective-permute-start.15) | collective-permute-done | bytes 196640 | tf_op jit(solution)/shard_map/ppermute | solution.py:27
  59.7 3.8 %collective-permute-start.18 = (bf16[6,16,256]{2,1,0:T(8,128)(2,1)S(1)}, bf16[6,16,256]{2,1,0:T(8,128)(2,1)S(1)}, u32[]{:S(2)}, u32[]{:S(2)}) collective-permute-start(bf16[6,16,256]{2,1,0:T(8,128)(2,1)S(1)} %get-tuple-element.39), channel_id=1, source_target_pairs={{0,16},{8,24},{16,0},{24,8},{1,17},{9,25},{17,1},{25,9},{2,18},{10... | collective-permute-start | bytes 147464 | tf_op jit(solution)/shard_map/ppermute | solution.py:27
  63.5 2.0 %collective-permute-done.17 = bf16[6,16,256]{2,1,0:T(8,128)(2,1)S(1)} collective-permute-done((bf16[6,16,256]{2,1,0:T(8,128)(2,1)S(1)}, bf16[6,16,256]{2,1,0:T(8,128)(2,1)S(1)}, u32[]{:S(2)}, u32[]{:S(2)}) %collective-permute-start.17) | collective-permute-done | bytes 49184 | tf_op jit(solution)/shard_map/ppermute | solution.py:27
  66.6 1.7 %collective-permute-start.22 = (bf16[6,16,256]{2,1,0:T(8,128)(2,1)S(1)}, bf16[6,16,256]{2,1,0:T(8,128)(2,1)S(1)}, u32[]{:S(2)}, u32[]{:S(2)}) collective-permute-start(bf16[6,16,256]{2,1,0:T(8,128)(2,1)S(1)} %fusion.6), channel_id=1, source_target_pairs={{0,24},{8,16},{16,8},{24,0},{1,25},{9,17},{17,9},{25,1},{2,26},{10... | collective-permute-start | bytes 147464 | tf_op jit(solution)/shard_map/ppermute | solution.py:27
  68.7 2.4 %collective-permute-start.20 = (bf16[6,16,256]{2,1,0:T(8,128)(2,1)S(1)}, bf16[6,16,256]{2,1,0:T(8,128)(2,1)S(1)}, u32[]{:S(2)}, u32[]{:S(2)}) collective-permute-start(bf16[6,16,256]{2,1,0:T(8,128)(2,1)S(1)} %fusion.6), channel_id=1, source_target_pairs={{0,8},{8,0},{16,24},{24,16},{1,9},{9,1},{17,25},{25,17},{2,10},{10... | collective-permute-start | bytes 147464 | tf_op jit(solution)/shard_map/ppermute | solution.py:27
  73.9 1.8 %collective-permute-start.25 = (bf16[4,6,16,256]{3,2,1,0:T(8,128)(2,1)S(1)}, bf16[4,6,16,256]{3,2,1,0:T(8,128)(2,1)S(1)}, u32[]{:S(2)}, u32[]{:S(2)}) collective-permute-start(bf16[4,6,16,256]{3,2,1,0:T(8,128)(2,1)S(1)} %pad_maximum_fusion.refs_0_), channel_id=1, source_target_pairs={{0,6},{2,4},{4,2},{6,0},{1,7},{3,5},{5,3},{7,1},{8,14},{10,12},{12... | collective-permute-start | bytes 589832 | tf_op jit(solution)/shard_map/ppermute | solution.py:27
  77.5 4.3 %collective-permute-done.25.refs_3_ = bf16[4,6,16,256]{3,2,1,0:T(8,128)(2,1)S(1)} collective-permute-done((bf16[4,6,16,256]{3,2,1,0:T(8,128)(2,1)S(1)}, bf16[4,6,16,256]{3,2,1,0:T(8,128)(2,1)S(1)}, u32[]{:S(2)}, u32[]{:S(2)}) %collective-permute-start.25) | collective-permute-done | bytes 196640 | tf_op jit(solution)/shard_map/ppermute | solution.py:27
  81.8 1.5 %collective-permute-done.24.refs_2_ = bf16[4,6,16,256]{3,2,1,0:T(8,128)(2,1)S(1)} collective-permute-done((bf16[4,6,16,256]{3,2,1,0:T(8,128)(2,1)S(1)}, bf16[4,6,16,256]{3,2,1,0:T(8,128)(2,1)S(1)}, u32[]{:S(2)}, u32[]{:S(2)}) %collective-permute-start.24) | collective-permute-done | bytes 196640 | tf_op jit(solution)/shard_map/ppermute | solution.py:27
  83.3 1.8 %spread.1 = f32[6,256,256]{2,1,0:T(8,128)} custom-call(s32[3]{0:T(128)S(1)} %pad_add_fusion.refs_0_.places, bf16[4,6,16,256]{3,2,1,0:T(8,128)(2,1)S(1)} %pad_maximum_fusion.refs_0_, bf16[4,6,16,256]{3,2,1,0:T(8,128)(2,1)S(1)} %collective-permute-done.23.refs_1_, bf16[4,6,16,256]{3,2,1,0:T(8,128)(2,1)S(1)} %collective-permute-done.24.refs_2_, ...), custom_call_target="tpu_custom_call" | custom-call | tf_op jit(solution)/shard_map/spread/pallas_call | solution.py:350
  (60 shorter events, 19.2 us)
Async XLA Ops:
  0.6 7.1 %collective-permute-start.2 = (bf16[256,256]{1,0:T(8,128)(2,1)}, bf16[256,256]{1,0:T(8,128)(2,1)S(1)}, u32[]{:S(2)}, u32[]{:S(2)}) collective-permute-start(bf16[256,256]{1,0:T(8,128)(2,1)} %param.7), channel_id=1, source_target_pairs={{0,8},{8,0},{16,24},{24,16},{1,9},{9,1},{17,25},{25,17},{2,10},{10... | collective-permute-start | bytes 393224 | tf_op jit(solution)/shard_map/ppermute | solution.py:27
  3.7 10.0 %collective-permute-start.1 = (bf16[256,256]{1,0:T(8,128)(2,1)}, bf16[256,256]{1,0:T(8,128)(2,1)S(1)}, u32[]{:S(2)}, u32[]{:S(2)}) collective-permute-start(bf16[256,256]{1,0:T(8,128)(2,1)} %param.7), channel_id=1, source_target_pairs={{0,24},{8,16},{16,8},{24,0},{1,25},{9,17},{17,9},{25,1},{2,26},{10... | collective-permute-start | bytes 393224 | tf_op jit(solution)/shard_map/ppermute | solution.py:27
  6.2 12.0 %collective-permute-start = (bf16[256,256]{1,0:T(8,128)(2,1)}, bf16[256,256]{1,0:T(8,128)(2,1)S(1)}, u32[]{:S(2)}, u32[]{:S(2)}) collective-permute-start(bf16[256,256]{1,0:T(8,128)(2,1)} %param.7), channel_id=1, source_target_pairs={{0,16},{8,24},{16,0},{24,8},{1,17},{9,25},{17,1},{25,9},{2,18},{10... | collective-permute-start | bytes 393224 | tf_op jit(solution)/shard_map/ppermute | solution.py:27
  20.3 2.0 %collective-permute-start.3 = (bf16[4,256,256]{2,1,0:T(8,128)(2,1)S(1)}, bf16[4,256,256]{2,1,0:T(8,128)(2,1)S(1)}, u32[]{:S(2)}, u32[]{:S(2)}) collective-permute-start(bf16[4,256,256]{2,1,0:T(8,128)(2,1)S(1)} %get-tuple-element.16), channel_id=1, source_target_pairs={{0,1},{1,0},{2,3},{3,2},{4,5},{5,4},{6,7},{7,6},{8,9},{9,8},{10,11... | collective-permute-start | bytes 1572872 | tf_op jit(solution)/shard_map/ppermute | solution.py:27
  22.5 5.8 %collective-permute-start.6 = (bf16[256,256]{1,0:T(8,128)(2,1)S(1)}, bf16[256,256]{1,0:T(8,128)(2,1)S(1)}, u32[]{:S(2)}, u32[]{:S(2)}) collective-permute-start(bf16[256,256]{1,0:T(8,128)(2,1)S(1)} %get-tuple-element.34), channel_id=1, source_target_pairs={{0,2},{2,0},{4,6},{6,4},{1,3},{3,1},{5,7},{7,5},{8,10},{10,8},{12,... | collective-permute-start | bytes 393224 | tf_op jit(solution)/shard_map/ppermute | solution.py:27
  23.8 9.0 %collective-permute-start.5 = (bf16[256,256]{1,0:T(8,128)(2,1)S(1)}, bf16[256,256]{1,0:T(8,128)(2,1)S(1)}, u32[]{:S(2)}, u32[]{:S(2)}) collective-permute-start(bf16[256,256]{1,0:T(8,128)(2,1)S(1)} %get-tuple-element.35), channel_id=1, source_target_pairs={{0,4},{2,6},{4,0},{6,2},{1,5},{3,7},{5,1},{7,3},{8,12},{10,14},{12... | collective-permute-start | bytes 393224 | tf_op jit(solution)/shard_map/ppermute | solution.py:27
  26.5 6.3 %collective-permute-start.4 = (bf16[256,256]{1,0:T(8,128)(2,1)S(1)}, bf16[256,256]{1,0:T(8,128)(2,1)S(1)}, u32[]{:S(2)}, u32[]{:S(2)}) collective-permute-start(bf16[256,256]{1,0:T(8,128)(2,1)S(1)} %get-tuple-element.36), channel_id=1, source_target_pairs={{0,6},{2,4},{4,2},{6,0},{1,7},{3,5},{5,3},{7,1},{8,14},{10,12},{12... | collective-permute-start | bytes 393224 | tf_op jit(solution)/shard_map/ppermute | solution.py:27
  33.7 7.3 %collective-permute-start.9 = (bf16[256,256]{1,0:T(8,128)(2,1)S(1)}, bf16[256,256]{1,0:T(8,128)(2,1)S(1)}, u32[]{:S(2)}, u32[]{:S(2)}) collective-permute-start(bf16[256,256]{1,0:T(8,128)(2,1)S(1)} %get-tuple-element.32.refs_2_), channel_id=1, source_target_pairs={{0,6},{2,4},{4,2},{6,0},{1,7},{3,5},{5,3},{7,1},{8,14},{10,12},{12... | collective-permute-start | bytes 393224 | tf_op jit(solution)/shard_map/ppermute | solution.py:27
  35.2 6.2 %collective-permute-start.8 = (bf16[256,256]{1,0:T(8,128)(2,1)S(1)}, bf16[256,256]{1,0:T(8,128)(2,1)S(1)}, u32[]{:S(2)}, u32[]{:S(2)}) collective-permute-start(bf16[256,256]{1,0:T(8,128)(2,1)S(1)} %get-tuple-element.32.refs_2_), channel_id=1, source_target_pairs={{0,4},{2,6},{4,0},{6,2},{1,5},{3,7},{5,1},{7,3},{8,12},{10,14},{12... | collective-permute-start | bytes 393224 | tf_op jit(solution)/shard_map/ppermute | solution.py:27
  36.6 5.6 %collective-permute-start.7 = (bf16[256,256]{1,0:T(8,128)(2,1)S(1)}, bf16[256,256]{1,0:T(8,128)(2,1)S(1)}, u32[]{:S(2)}, u32[]{:S(2)}) collective-permute-start(bf16[256,256]{1,0:T(8,128)(2,1)S(1)} %get-tuple-element.32.refs_2_), channel_id=1, source_target_pairs={{0,2},{2,0},{4,6},{6,4},{1,3},{3,1},{5,7},{7,5},{8,10},{10,8},{12,... | collective-permute-start | bytes 393224 | tf_op jit(solution)/shard_map/ppermute | solution.py:27
  37.2 5.0 %collective-permute-start.10 = (bf16[256,256]{1,0:T(8,128)(2,1)S(1)}, bf16[256,256]{1,0:T(8,128)(2,1)S(1)}, u32[]{:S(2)}, u32[]{:S(2)}) collective-permute-start(bf16[256,256]{1,0:T(8,128)(2,1)S(1)} %get-tuple-element.32.refs_2_), channel_id=1, source_target_pairs={{0,1},{1,0},{2,3},{3,2},{4,5},{5,4},{6,7},{7,6},{8,9},{9,8},{10,11... | collective-permute-start | bytes 393224 | tf_op jit(solution)/shard_map/ppermute | solution.py:27
  41.0 1.3 %collective-permute-start.13 = (bf16[256,256]{1,0:T(8,128)(2,1)S(1)}, bf16[256,256]{1,0:T(8,128)(2,1)S(1)}, u32[]{:S(2)}, u32[]{:S(2)}) collective-permute-start(bf16[256,256]{1,0:T(8,128)(2,1)S(1)} %collective-permute-done.9.refs_5_), channel_id=1, source_target_pairs={{0,1},{1,0},{2,3},{3,2},{4,5},{5,4},{6,7},{7,6},{8,9},{9,8},{10,11... | collective-permute-start | bytes 393224 | tf_op jit(solution)/shard_map/ppermute | solution.py:27
  45.4 8.8 %collective-permute-start.14 = (bf16[4,6,16,256]{3,2,1,0:T(8,128)(2,1)S(1)}, bf16[4,6,16,256]{3,2,1,0:T(8,128)(2,1)S(1)}, u32[]{:S(2)}, u32[]{:S(2)}) collective-permute-start(bf16[4,6,16,256]{3,2,1,0:T(8,128)(2,1)S(1)} %get-tuple-element.25), channel_id=1, source_target_pairs={{0,6},{2,4},{4,2},{6,0},{1,7},{3,5},{5,3},{7,1},{8,14},{10,12},{12... | collective-permute-start | bytes 589832 | tf_op jit(solution)/shard_map/ppermute | solution.py:27
  48.5 9.2 %collective-permute-start.15 = (bf16[4,6,16,256]{3,2,1,0:T(8,128)(2,1)S(1)}, bf16[4,6,16,256]{3,2,1,0:T(8,128)(2,1)S(1)}, u32[]{:S(2)}, u32[]{:S(2)}) collective-permute-start(bf16[4,6,16,256]{3,2,1,0:T(8,128)(2,1)S(1)} %get-tuple-element.26), channel_id=1, source_target_pairs={{0,4},{2,6},{4,0},{6,2},{1,5},{3,7},{5,1},{7,3},{8,12},{10,14},{12... | collective-permute-start | bytes 589832 | tf_op jit(solution)/shard_map/ppermute | solution.py:27
  48.5 10.4 %collective-permute-start.16 = (bf16[4,6,16,256]{3,2,1,0:T(8,128)(2,1)S(1)}, bf16[4,6,16,256]{3,2,1,0:T(8,128)(2,1)S(1)}, u32[]{:S(2)}, u32[]{:S(2)}) collective-permute-start(bf16[4,6,16,256]{3,2,1,0:T(8,128)(2,1)S(1)} %get-tuple-element.27), channel_id=1, source_target_pairs={{0,2},{2,0},{4,6},{6,4},{1,3},{3,1},{5,7},{7,5},{8,10},{10,8},{12,... | collective-permute-start | bytes 589832 | tf_op jit(solution)/shard_map/ppermute | solution.py:27
  59.0 6.5 %collective-permute-start.17 = (bf16[6,16,256]{2,1,0:T(8,128)(2,1)S(1)}, bf16[6,16,256]{2,1,0:T(8,128)(2,1)S(1)}, u32[]{:S(2)}, u32[]{:S(2)}) collective-permute-start(bf16[6,16,256]{2,1,0:T(8,128)(2,1)S(1)} %get-tuple-element.37), channel_id=1, source_target_pairs={{0,24},{8,16},{16,8},{24,0},{1,25},{9,17},{17,9},{25,1},{2,26},{10... | collective-permute-start | bytes 147464 | tf_op jit(solution)/shard_map/ppermute | solution.py:27
  59.7 5.8 %collective-permute-start.19 = (bf16[6,16,256]{2,1,0:T(8,128)(2,1)S(1)}, bf16[6,16,256]{2,1,0:T(8,128)(2,1)S(1)}, u32[]{:S(2)}, u32[]{:S(2)}) collective-permute-start(bf16[6,16,256]{2,1,0:T(8,128)(2,1)S(1)} %get-tuple-element.38), channel_id=1, source_target_pairs={{0,8},{8,0},{16,24},{24,16},{1,9},{9,1},{17,25},{25,17},{2,10},{10... | collective-permute-start | bytes 147464 | tf_op jit(solution)/shard_map/ppermute | solution.py:27
  59.7 6.9 %collective-permute-start.18 = (bf16[6,16,256]{2,1,0:T(8,128)(2,1)S(1)}, bf16[6,16,256]{2,1,0:T(8,128)(2,1)S(1)}, u32[]{:S(2)}, u32[]{:S(2)}) collective-permute-start(bf16[6,16,256]{2,1,0:T(8,128)(2,1)S(1)} %get-tuple-element.39), channel_id=1, source_target_pairs={{0,16},{8,24},{16,0},{24,8},{1,17},{9,25},{17,1},{25,9},{2,18},{10... | collective-permute-start | bytes 147464 | tf_op jit(solution)/shard_map/ppermute | solution.py:27
  66.6 6.0 %collective-permute-start.22 = (bf16[6,16,256]{2,1,0:T(8,128)(2,1)S(1)}, bf16[6,16,256]{2,1,0:T(8,128)(2,1)S(1)}, u32[]{:S(2)}, u32[]{:S(2)}) collective-permute-start(bf16[6,16,256]{2,1,0:T(8,128)(2,1)S(1)} %fusion.6), channel_id=1, source_target_pairs={{0,24},{8,16},{16,8},{24,0},{1,25},{9,17},{17,9},{25,1},{2,26},{10... | collective-permute-start | bytes 147464 | tf_op jit(solution)/shard_map/ppermute | solution.py:27
  68.4 5.5 %collective-permute-start.21 = (bf16[6,16,256]{2,1,0:T(8,128)(2,1)S(1)}, bf16[6,16,256]{2,1,0:T(8,128)(2,1)S(1)}, u32[]{:S(2)}, u32[]{:S(2)}) collective-permute-start(bf16[6,16,256]{2,1,0:T(8,128)(2,1)S(1)} %fusion.6), channel_id=1, source_target_pairs={{0,16},{8,24},{16,0},{24,8},{1,17},{9,25},{17,1},{25,9},{2,18},{10... | collective-permute-start | bytes 147464 | tf_op jit(solution)/shard_map/ppermute | solution.py:27
  68.7 5.2 %collective-permute-start.20 = (bf16[6,16,256]{2,1,0:T(8,128)(2,1)S(1)}, bf16[6,16,256]{2,1,0:T(8,128)(2,1)S(1)}, u32[]{:S(2)}, u32[]{:S(2)}) collective-permute-start(bf16[6,16,256]{2,1,0:T(8,128)(2,1)S(1)} %fusion.6), channel_id=1, source_target_pairs={{0,8},{8,0},{16,24},{24,16},{1,9},{9,1},{17,25},{25,17},{2,10},{10... | collective-permute-start | bytes 147464 | tf_op jit(solution)/shard_map/ppermute | solution.py:27
  73.9 7.9 %collective-permute-start.25 = (bf16[4,6,16,256]{3,2,1,0:T(8,128)(2,1)S(1)}, bf16[4,6,16,256]{3,2,1,0:T(8,128)(2,1)S(1)}, u32[]{:S(2)}, u32[]{:S(2)}) collective-permute-start(bf16[4,6,16,256]{3,2,1,0:T(8,128)(2,1)S(1)} %pad_maximum_fusion.refs_0_), channel_id=1, source_target_pairs={{0,6},{2,4},{4,2},{6,0},{1,7},{3,5},{5,3},{7,1},{8,14},{10,12},{12... | collective-permute-start | bytes 589832 | tf_op jit(solution)/shard_map/ppermute | solution.py:27
  75.8 7.6 %collective-permute-start.24 = (bf16[4,6,16,256]{3,2,1,0:T(8,128)(2,1)S(1)}, bf16[4,6,16,256]{3,2,1,0:T(8,128)(2,1)S(1)}, u32[]{:S(2)}, u32[]{:S(2)}) collective-permute-start(bf16[4,6,16,256]{3,2,1,0:T(8,128)(2,1)S(1)} %pad_maximum_fusion.refs_0_), channel_id=1, source_target_pairs={{0,4},{2,6},{4,0},{6,2},{1,5},{3,7},{5,1},{7,3},{8,12},{10,14},{12... | collective-permute-start | bytes 589832 | tf_op jit(solution)/shard_map/ppermute | solution.py:27
  76.7 6.6 %collective-permute-start.23 = (bf16[4,6,16,256]{3,2,1,0:T(8,128)(2,1)S(1)}, bf16[4,6,16,256]{3,2,1,0:T(8,128)(2,1)S(1)}, u32[]{:S(2)}, u32[]{:S(2)}) collective-permute-start(bf16[4,6,16,256]{3,2,1,0:T(8,128)(2,1)S(1)} %pad_maximum_fusion.refs_0_), channel_id=1, source_target_pairs={{0,2},{2,0},{4,6},{6,4},{1,3},{3,1},{5,7},{7,5},{8,10},{10,8},{12,... | collective-permute-start | bytes 589832 | tf_op jit(solution)/shard_map/ppermute | solution.py:27
  (11 other events, 42.3 us)

commit v3 on v2

v3 whole, which is shorter than its diff:
```python
import functools
import math

import jax
import jax.numpy as jnp
from jax import lax
from jax.experimental import pallas as pl
from jax.experimental.pallas import tpu as pltpu
from jax.sharding import PartitionSpec as P

F32, BF16, I32 = jnp.float32, jnp.bfloat16, jnp.int32
WHOLE = pl.BlockSpec(memory_space=pltpu.VMEM)
SCALARS = pl.BlockSpec(memory_space=pltpu.SMEM)
ANYWHERE = pl.BlockSpec(memory_space=pl.ANY)
UNROLL = 16


def vmem_for(*arrays):
    held = sum(math.prod(a.shape) * jnp.dtype(a.dtype).itemsize for a in arrays)
    return pltpu.CompilerParams(vmem_limit_bytes=held + held // 8 + 3 * 1024 * 1024)


def partner_pairs(size, mask):
    return [(i, i ^ mask) for i in range(size)]


def swap(value, axis, mask):
    return lax.ppermute(value, axis, partner_pairs(lax.axis_size(axis), mask))


def slot_of(places, partition, masked):
    return partition ^ places[0] if masked else partition


def for_entries(total, body):
    def step(i, carry):
        body([(jnp.minimum(i * UNROLL + u, total - 1), i * UNROLL + u < total) for u in range(UNROLL)])
        return carry

    lax.fori_loop(0, (total + UNROLL - 1) // UNROLL, step, 0)


def halo_block(places, chosen, halo_refs, i, first_slot, masked, tile):
    per_call = halo_refs[0].shape[0]
    first = pl.multiple_of(chosen[slot_of(places, i + first_slot, masked)] * tile, tile)
    return halo_refs[i // per_call][i % per_call, pl.ds(first, tile), :]


def near_kernel(masked, tile, combine, near, bounds, places, chosen, table, count, *refs):
    halo_refs, refs = refs[:near], refs[near:]
    (weight, values, pre, others), lists, (projected, order) = refs[:4], refs[4:-2], refs[-2:]
    list_chunks(table, count, bounds, lists)
    entries = values.shape[0]

    def sort(e, found):
        mine = slot_of(places, table[1, e], masked) < near

        @pl.when(mine)
        def _():
            order[found] = e

        @pl.when(jnp.logical_not(mine))
        def _():
            others[e - found] = e

        return found + mine.astype(I32)

    total = lax.fori_loop(0, count[0], sort, jnp.int32(0))
    others[entries] = count[0] - total
    pre[...] = jnp.zeros_like(pre)
    project(masked, tile, combine, 0, places, chosen, halo_refs, weight, projected)
    add_entries(masked, combine, 0, places, table, values, weight, projected, order, total, pre)


def far_kernel(masked, tile, combine, near, places, chosen, table, order, *refs):
    halo_refs, refs = refs[:-7], refs[-7:]
    weight, values, before, pre, keep, send, projected = refs
    del before
    project(masked, tile, combine, near, places, chosen, halo_refs, weight, projected)
    total = order[values.shape[0]]
    add_entries(masked, combine, near, places, table, values, weight, projected, order, total, pre)
    hand_out(tile, places, pre, keep, send)


def all_kernel(masked, tile, combine, bounds, places, chosen, table, count, *refs):
    halo_refs, refs = refs[:1], refs[1:]
    (weight, values, keep, send), lists, (pre, projected, order) = refs[:4], refs[4:-3], refs[-3:]
    list_chunks(table, count, bounds, lists)

    def put(e, carry):
        order[e] = e
        return carry

    lax.fori_loop(0, count[0], put, 0)
    pre[...] = jnp.zeros_like(pre)
    project(masked, tile, combine, 0, places, chosen, halo_refs, weight, projected)
    add_entries(masked, combine, 0, places, table, values, weight, projected, order, count[0], pre)
    hand_out(tile, places, pre, keep, send)


def project(masked, tile, combine, first_slot, places, chosen, halo_refs, weight, projected):
    slots = len(halo_refs) * halo_refs[0].shape[0]
    relations = weight.shape[0]
    blocks = [
        halo_block(places, chosen, halo_refs, i, first_slot, masked, tile) for i in range(slots)
    ]
    if not combine:
        for i, block in enumerate(blocks):
            projected[i] = block
        return
    stacked = jnp.concatenate(blocks, axis=0)
    for r in range(relations):
        product = jnp.dot(stacked, weight[r], preferred_element_type=F32).astype(BF16)
        for i in range(slots):
            projected[i * relations + r] = product[i * tile : (i + 1) * tile]


def list_chunks(table, count, bounds, lists):
    def sort(e, found):
        relation = table[2, e]
        here = [(relation >= low) & (relation < high) for low, high in zip(bounds, bounds[1:])]
        for c, listed in enumerate(lists):

            @pl.when(here[c])
            def _():
                listed[found[c]] = e

        return tuple(f + h.astype(I32) for f, h in zip(found, here))

    found = lax.fori_loop(0, count[0], sort, (jnp.int32(0),) * len(lists))
    for listed, number in zip(lists, found):
        listed[listed.shape[0] - 1] = number


def add_entries(
    masked, combine, first_slot, places, table, values, weight, projected, order, total, pre
):
    relations = weight.shape[0]
    spare = pre.shape[0] - 1

    def body(positions):
        terms = []
        for position, _ in positions:
            e = order[position]
            slot = slot_of(places, table[1, e], masked) - first_slot
            relation = table[2, e]
            if combine:
                term = jnp.dot(
                    values[e], projected[slot * relations + relation], preferred_element_type=F32
                )
            else:
                message = jnp.dot(values[e], projected[slot], preferred_element_type=F32)
                term = jnp.dot(message.astype(BF16), weight[relation], preferred_element_type=F32)
            terms.append(term)
        for (position, real), term in zip(positions, terms):
            target = jnp.where(real, table[0, order[position]], spare)
            pre[target] = pre[target] + term

    for_entries(total, body)


def hand_out(tile, places, pre, keep, send):
    panels, per_owner = keep.shape[0], keep.shape[1] // tile
    groups = (pre.shape[0] - 1) // (panels * per_owner)
    for distance in range(panels):
        panel = places[1] ^ distance
        for part in range(per_owner):
            rows = pl.ds(part * tile, tile)
            mine = (panel * groups + places[2]) * per_owner + part
            other = (panel * groups + (places[2] ^ 1)) * per_owner + part
            send[distance, rows, :] = pre[other].astype(BF16)
            keep[distance, rows, :] = pre[mine]


def grad_kernel(own, first, second, third, cotangent, grad):
    pre = own[...] + first[...].astype(F32) + second[...].astype(F32) + third[...].astype(F32)
    grad[...] = (cotangent[...].astype(F32) * silu_slope(pre)).astype(BF16)


def turn_kernel(masked, tile, halo_count, panels, places, chosen, *refs):
    halo_refs, refs = refs[:halo_count], refs[halo_count:]
    values, values_turned, halo_turned, scratch = refs[0], refs[1], refs[2], refs[-1]
    entries = values.shape[0]
    for each in refs[3:-1]:
        each[...] = jnp.zeros_like(each)

    per_call = halo_refs[0].shape[0]
    features = scratch.shape[0]
    share = features // panels
    for slot in range(halo_count * per_call):
        block = halo_block(places, chosen, halo_refs, slot, 0, masked, tile)
        scratch[...] = block.astype(F32).T
        for m in range(panels):
            start = pl.multiple_of((places[1] ^ m) * share, share)
            halo_turned[pl.ds(m * share, share), pl.ds(slot * tile, tile)] = (
                scratch[pl.ds(start, share), :].astype(BF16)
            )

    batch = 8

    def step(i, carry):
        for u in range(batch):
            values_turned[i * batch + u] = values[i * batch + u].T
        return carry

    lax.fori_loop(0, entries // batch, step, 0)


def collect_kernel(tile, *refs):
    grad_refs, grads = refs[:-1], refs[-1]
    panels = len(grad_refs) // 2
    per_owner = grad_refs[0].shape[0] // tile
    for g in range(2):
        for m in range(panels):
            owner = (lax.axis_index("src") ^ m) * 2 + (lax.axis_index("rel") ^ g)
            for part in range(per_owner):
                grads[owner * per_owner + part] = grad_refs[g * panels + m][
                    pl.ds(part * tile, tile), :
                ]


def weight_kernel(masked, tile, first_relation, combine, places, table, listed, *refs):
    values_turned, halo_turned, grads = refs[:3]
    outs, sums = refs[4:-1], refs[-1]
    features = halo_turned.shape[0]
    slots = halo_turned.shape[1] // tile
    relations, share = outs[0].shape[0], outs[0].shape[1]
    spare = sums.shape[0] - 1

    def body(positions):
        terms = []
        for position, _ in positions:
            e = listed[position]
            term = jnp.dot(values_turned[e], grads[table[0, e]], preferred_element_type=F32)
            if not combine:
                slot = slot_of(places, table[1, e], masked)
                columns = pl.ds(pl.multiple_of(slot * tile, tile), tile)
                term = jnp.dot(
                    halo_turned[:, columns], term.astype(BF16), preferred_element_type=F32
                )
            terms.append(term)
        for (position, real), term in zip(positions, terms):
            e = listed[position]
            place = table[2, e] - first_relation
            if combine:
                place = place * slots + slot_of(places, table[1, e], masked)
            place = jnp.where(real, place, spare)
            sums[place] = sums[place] + term

    for_entries(listed[values_turned.shape[0]], body)
    for r in range(relations):
        if combine:
            stacked = sums[r * slots : (r + 1) * slots].reshape(slots * tile, features)
            grad = jnp.dot(halo_turned[...], stacked.astype(BF16), preferred_element_type=F32)
        else:
            grad = sums[r]
        for m, out in enumerate(outs):
            out[r] = grad[m * share : (m + 1) * share].astype(out.dtype)


def spread_kernel(first_relation, *refs):
    out, scratch, sems = refs[-3:]
    shares = refs[: scratch.shape[0]]
    relations, share = scratch.shape[1], scratch.shape[2]
    copies = []
    for m in reversed(range(len(shares))):
        scratch[m] = shares[m][...].astype(F32)
        panel = lax.axis_index("src") ^ m
        rows = pl.ds(pl.multiple_of(panel * share, share), share)
        copies.append(
            pltpu.make_async_copy(
                scratch.at[m],
                out.at[pl.ds(first_relation, relations), rows, :],
                sems.at[m],
            )
        )
        copies[-1].start()
    for copy in copies:
        copy.wait()


def spread(first_relation, shares, total, so_far):
    scratch = jax.ShapeDtypeStruct((len(shares), *shares[0].shape), F32)
    return pl.pallas_call(
        functools.partial(spread_kernel, first_relation),
        out_shape=total,
        in_specs=[WHOLE] * len(shares) + [ANYWHERE] * len(so_far),
        out_specs=ANYWHERE,
        scratch_shapes=[
            pltpu.VMEM(scratch.shape, F32),
            pltpu.SemaphoreType.DMA((len(shares),)),
        ],
        input_output_aliases={len(shares): 0} if so_far else {},
        compiler_params=vmem_for(scratch, *shares),
        name="spread",
    )(*shares, *so_far)


def sum_kernel(*refs):
    total = refs[0][...].astype(F32)
    for ref in refs[1:-1]:
        total = total + ref[...].astype(F32)
    refs[-1][...] = total.astype(refs[-1].dtype)


def summed(values, dtype=BF16):
    out = jax.ShapeDtypeStruct(values[0].shape, dtype)
    return pl.pallas_call(
        sum_kernel,
        out_shape=out,
        in_specs=[WHOLE] * len(values),
        out_specs=WHOLE,
        compiler_params=vmem_for(out, *values),
        name="sum",
    )(*values)


def silu_slope(pre_values):
    logistic = jax.nn.sigmoid(pre_values)
    return logistic * (1.0 + pre_values * (1.0 - logistic))


def exchange(pieces, axis):
    return [swap(pieces[m].astype(BF16), axis, m) for m in range(len(pieces) - 1, 0, -1)]


def added(own, arrived):
    total = own.astype(F32)
    for value in arrived:
        total = total + value.astype(F32)
    return total


def gather(value, axis):
    return [value] + [swap(value, axis, m) for m in range(1, lax.axis_size(axis))]


def local(source_feats, rel_weight, halo_pick, entry_index, entry_count, entry_values, cotangent):
    partitions, panels = lax.axis_size("dom"), lax.axis_size("src")
    groups = lax.axis_size("rel")
    tile = entry_values.shape[-1]
    own_rows, features = cotangent.shape
    relations = rel_weight.shape[0]
    values = entry_values.reshape(-1, tile, tile)
    table = entry_index.reshape(3, -1)
    entries = table.shape[1]
    count = entry_count.reshape(1)
    chosen = halo_pick.reshape(-1)
    places = jnp.stack([lax.axis_index(a) for a in ("dom", "src", "rel")]).astype(I32)
    targets = own_rows * panels * groups // tile
    direct = partitions <= 8
    share = features // panels
    bounds = tuple(sorted({0, relations // 2, relations}))
    chunks = len(bounds) - 1
    lists = (jax.ShapeDtypeStruct((entries + 1,), I32),) * chunks

    kept = (
        jax.ShapeDtypeStruct((panels, own_rows, features), F32),
        jax.ShapeDtypeStruct((panels, own_rows, features), BF16),
    )
    pre_sums = jax.ShapeDtypeStruct((targets + 1, tile, features), F32)
    if direct:
        halo = [h[None] for h in gather(source_feats, "dom")]
    else:
        halo = [lax.all_gather(source_feats, "dom", axis=0)]
    slots = sum(h.shape[0] for h in halo)
    combine = slots * relations <= entries
    near = partitions // 2
    projected = jax.ShapeDtypeStruct(
        ((near if direct else slots) * (relations if combine else 1), tile, features), BF16
    )
    cost = pl.CostEstimate(
        flops=4 * entries * tile * tile * features, bytes_accessed=values.size, transcendentals=0
    )
    if direct:
        before, others, *lists = pl.pallas_call(
            functools.partial(near_kernel, direct, tile, combine, near, bounds),
            out_shape=(pre_sums, lists[0], *lists),
            in_specs=[SCALARS] * 4 + [WHOLE] * (near + 2),
            out_specs=(WHOLE, SCALARS) + (SCALARS,) * chunks,
            scratch_shapes=[pltpu.VMEM(projected.shape, BF16), pltpu.SMEM((entries,), I32)],
            compiler_params=vmem_for(pre_sums, projected, *halo[:near], rel_weight, values),
            cost_estimate=cost,
            name="forward_near",
        )(places, chosen, table, count, *halo[:near], rel_weight, values)
        far = halo[near:]
        _, keep, send = pl.pallas_call(
            functools.partial(far_kernel, direct, tile, combine, near),
            out_shape=(pre_sums, *kept),
            in_specs=[SCALARS] * 4 + [WHOLE] * (len(far) + 3),
            out_specs=(WHOLE,) * 3,
            scratch_shapes=[pltpu.VMEM(projected.shape, BF16)],
            input_output_aliases={4 + len(far) + 2: 0},
            compiler_params=vmem_for(pre_sums, projected, *far, rel_weight, values, *kept),
            cost_estimate=cost,
            name="forward_far",
        )(places, chosen, table, others, *far, rel_weight, values, before)
    else:
        keep, send, *lists = pl.pallas_call(
            functools.partial(all_kernel, direct, tile, combine, bounds),
            out_shape=kept + lists,
            in_specs=[SCALARS] * 4 + [WHOLE] * (len(halo) + 2),
            out_specs=(WHOLE,) * 2 + (SCALARS,) * chunks,
            scratch_shapes=[
                pltpu.VMEM(pre_sums.shape, F32),
                pltpu.VMEM(projected.shape, BF16),
                pltpu.SMEM((entries,), I32),
            ],
            compiler_params=vmem_for(pre_sums, projected, *halo, rel_weight, values, *kept),
            cost_estimate=cost,
            name="forward_all",
        )(places, chosen, table, count, *halo, rel_weight, values)

    chip_sum = keep + swap(send, "rel", 1).astype(F32)
    leaving = [chip_sum[m] for m in range(panels)]
    leaving, values_then = lax.optimization_barrier((leaving, values))
    arrived = exchange(leaving, "src")

    sums = [
        jax.ShapeDtypeStruct(
            ((high - low) * slots + 1, tile, features)
            if combine
            else (high - low + 1, features, features),
            F32,
        )
        for low, high in zip(bounds, bounds[1:])
    ]
    turned = (
        jax.ShapeDtypeStruct(values.shape, BF16),
        jax.ShapeDtypeStruct((features, slots * tile), BF16),
    )
    prepared = pl.pallas_call(
        functools.partial(turn_kernel, direct, tile, len(halo), panels),
        out_shape=(*turned, *sums),
        in_specs=[SCALARS] * 2 + [WHOLE] * (len(halo) + 1),
        out_specs=(WHOLE,) * (2 + chunks),
        scratch_shapes=[pltpu.VMEM((features, tile), F32)],
        compiler_params=vmem_for(*turned, *sums, values, *halo),
        cost_estimate=pl.CostEstimate(
            flops=0, bytes_accessed=4 * values.size, transcendentals=0
        ),
        name="turn",
    )(places, chosen, *halo, values_then)
    arrived, prepared = lax.optimization_barrier((arrived, prepared))
    block = jax.ShapeDtypeStruct((own_rows, features), BF16)
    if len(arrived) == 3:
        local_grad = pl.pallas_call(
            grad_kernel,
            out_shape=block,
            in_specs=[WHOLE] * 5,
            out_specs=WHOLE,
            compiler_params=vmem_for(leaving[0], block, block, block, block, block),
            name="grad",
        )(leaving[0], *arrived, cotangent)
    else:
        local_grad = cotangent.astype(F32) * silu_slope(added(leaving[0], arrived))
        local_grad = local_grad.astype(BF16)
    out_feats = jax.nn.silu(added(leaving[0], arrived)).astype(BF16)

    core_grads = gather(local_grad, "src")
    other_grads = [swap(value, "rel", 1) for value in core_grads]

    by_target = jax.ShapeDtypeStruct((targets, tile, features), BF16)
    grads = pl.pallas_call(
        functools.partial(collect_kernel, tile),
        out_shape=by_target,
        in_specs=[WHOLE] * (2 * panels),
        out_specs=WHOLE,
        compiler_params=vmem_for(by_target, by_target),
        name="collect",
    )(*core_grads, *other_grads)

    total = jax.ShapeDtypeStruct((relations, features, features), F32)
    panel_sums, pieces, done = [], [], []
    for c in range(chunks):
        own_share = jax.ShapeDtypeStruct((bounds[c + 1] - bounds[c], share, features), F32)
        sent_share = jax.ShapeDtypeStruct(own_share.shape, BF16)
        *shares, _ = pl.pallas_call(
            functools.partial(weight_kernel, direct, tile, bounds[c], combine),
            out_shape=(own_share,) + (sent_share,) * (panels - 1) + (sums[c],),
            in_specs=[SCALARS] * 3 + [WHOLE] * 4,
            out_specs=(WHOLE,) * (panels + 1),
            input_output_aliases={6: panels},
            compiler_params=vmem_for(*(own_share,) * panels, sums[c], by_target, *turned),
            name="weight_terms",
        )(places, table, lists[c], *prepared[:2], grads, prepared[2 + c])
        panel_sums.append(
            summed([shares[0]] + exchange(shares, "src"), BF16 if direct else F32)
        )
    for panel_sum in panel_sums:
        if direct:
            mask = 1
            while mask < partitions:
                panel_sum = summed([panel_sum, swap(panel_sum, "dom", mask)])
                mask *= 2
        else:
            panel_sum = lax.psum(panel_sum, "dom").astype(BF16)
        pieces.append(gather(panel_sum, "src"))
    for c in range(chunks):
        done = [spread(bounds[c], pieces[c], total, done)]
    grad_rel = done[0]
    return (out_feats, grad_rel)


def solution(mesh):
    return jax.shard_map(
        local,
        mesh=mesh,
        in_specs=(
            P(("dom", "src", "rel"), None),
            P("rel", None, None),
            P("dom", "src", "rel", None),
            P("dom", "src", "rel", None, None),
            P("dom", "src", "rel"),
            P("dom", "src", "rel", None, None, None),
            P(("dom", "src", "rel"), None),
        ),
        out_specs=(P(("dom", "src", "rel"), None), P("rel", None, None)),
        check_vma=False,
    )
```

time: 85.8 us -> 80.7 us (0.941)
  waiting for transfers between devices: 38.8 us -> 27.9 us
  Pallas kernels: 9.13 us -> 14.2 us
  starting transfers between devices: 29.5 us -> 30.9 us
    ppermute x26 -> x30, waiting for transfers between devices: 38.8 us -> 27.9 us  [swap(): return lax.ppermute(value, axis, partner_pairs(lax.axis_size(axis), mask))]
    pallas_call x5 -> x15, Pallas kernels: 9.13 us -> 14.2 us  [the longest x1 4.27 us: local(): pl.pallas_call(functools.partial(near_kernel, direct, tile, combine, near...]
    ppermute x26 -> x30, starting transfers between devices: 29.5 us -> 30.9 us  [swap(): return lax.ppermute(value, axis, partner_pairs(lax.axis_size(axis), mask))]
  transfers between devices with their start and end apart: 26 -> 30, of which waited for: 18 -> 19; matrix products, arithmetic and copies ran while one was open for 1% -> 2% of each run, Pallas kernels for 4% -> 11%
where the time goes in v3:
time: 80.7 us; the launch traced here: 80.5 us
  starting transfers between devices  30.9 us (38%)
  waiting for transfers between devices  27.9 us (35%)
  Pallas kernels  14.2 us (18%)
  local copies, waits for them, and re-layouts  5.05 us (6%)
  between operations  1.45 us (2%)
  other arithmetic  0.98 us (1%)
    ppermute x30, starting transfers between devices, swap(): return lax.ppermute(value, axis, partner_pairs(lax.axis_size(axis), mask))  30.9 us
    ppermute x30, waiting for transfers between devices, swap(): return lax.ppermute(value, axis, partner_pairs(lax.axis_size(axis), mask))  27.9 us
    unnamed x19, local copies, waits for them, and re-layouts  4.99 us
    pallas_call x1, Pallas kernels, local(): pl.pallas_call(functools.partial(near_kernel, direct, tile, combine, near...  4.27 us
    pallas_call x2, Pallas kernels, local(): pl.pallas_call(functools.partial(weight_kernel, direct, tile, bounds[c],...  3.76 us
    pallas_call x1, Pallas kernels, local(): pl.pallas_call(functools.partial(far_kernel, direct, tile, combine, near)...  2.01 us
    pallas_call x1, Pallas kernels, local(): pl.pallas_call(functools.partial(turn_kernel, direct, tile, len(halo), pa...  1.89 us
    pallas_call x2, Pallas kernels, spread(): pl.pallas_call(functools.partial(spread_kernel, first_relation), out_shap...  1.84 us
  transfers between devices with their start and end apart: 30, of which 19 were waited for; matrix products, arithmetic and copies ran while one was open for 2% of the time, Pallas kernels for 11%

profile of v3, /device:TPU:0, one launch (start us, length us, event | category | flops | bytes accessed | tf_op | source)
XLA Modules:
  0.0 80.5 jit_solution(6038550606574082162)
XLA Ops:
  0.6 3.1 %collective-permute-start = (bf16[256,256]{1,0:T(8,128)(2,1)}, bf16[256,256]{1,0:T(8,128)(2,1)S(1)}, u32[]{:S(2)}, u32[]{:S(2)}) collective-permute-start(bf16[256,256]{1,0:T(8,128)(2,1)} %param.7), channel_id=1, source_target_pairs={{0,8},{8,0},{16,24},{24,16},{1,9},{9,1},{17,25},{25,17},{2,10},{10... | collective-permute-start | bytes 393224 | tf_op jit(solution)/shard_map/ppermute | solution.py:28
  3.7 2.5 %collective-permute-start.2 = (bf16[256,256]{1,0:T(8,128)(2,1)}, bf16[256,256]{1,0:T(8,128)(2,1)S(1)}, u32[]{:S(2)}, u32[]{:S(2)}) collective-permute-start(bf16[256,256]{1,0:T(8,128)(2,1)} %param.7), channel_id=1, source_target_pairs={{0,24},{8,16},{16,8},{24,0},{1,25},{9,17},{17,9},{25,1},{2,26},{10... | collective-permute-start | bytes 393224 | tf_op jit(solution)/shard_map/ppermute | solution.py:28
  7.7 1.6 %copy-done = bf16[1,1,1,64,128,128]{5,4,3,2,1,0:T(8,128)(2,1)S(1)} copy-done((bf16[1,1,1,64,128,128]{5,4,3,2,1,0:T(8,128)(2,1)S(1)}, bf16[1,1,1,64,128,128]{5,4,3,2,1,0:T(8,128)(2,1)}, u32[]{:S(2)}) %copy-start) | copy-done | bytes 2097176
  12.0 4.3 %forward_near.1 = (f32[17,128,256]{2,1,0:T(8,128)S(1)}, s32[65]{0:T(128)S(1)}, s32[65]{0:T(128)S(1)}, s32[65]{0:T(128)S(1)}) custom-call(s32[3]{0:T(128)S(1)} %pad_add_fusion.places, s32[4]{0:T(128)S(1)} %bitcast.37, s32[3,64]{1,0:T(4,128)S(1)} %bitcast.33, s32[1]{0:T(128)} %bitcast.21.count, bf16[1,256,256]{2,1,0:T(8,128)(2,1)S(1)} %bitcast.29, ...), custom_call_target="tpu_custom_call" | custom-call | flops 1073741824 | bytes 1048576 | tf_op jit(solution)/shard_map/forward_near/pallas_call | solution.py:376
  16.3 1.9 %collective-permute-done.1 = bf16[256,256]{1,0:T(8,128)(2,1)S(1)} collective-permute-done((bf16[256,256]{1,0:T(8,128)(2,1)}, bf16[256,256]{1,0:T(8,128)(2,1)S(1)}, u32[]{:S(2)}, u32[]{:S(2)}) %collective-permute-start.1) | collective-permute-done | bytes 131104 | tf_op jit(solution)/shard_map/ppermute | solution.py:28
  18.2 2.0 %forward_far.1 = (f32[17,128,256]{2,1,0:T(8,128)S(1)}, f32[4,256,256]{2,1,0:T(8,128)S(1)}, bf16[4,256,256]{2,1,0:T(8,128)(2,1)S(1)}) custom-call(s32[3]{0:T(128)S(1)} %pad_add_fusion.places, s32[4]{0:T(128)S(1)} %bitcast.38, s32[3,64]{1,0:T(4,128)S(1)} %bitcast.34, s32[65]{0:T(128)S(1)} %get-tuple-element.32.order, ...), custom_call_target="tpu_custom_call", output_to_operand_aliasing={{0}: (8, {})} | custom-call | flops 1073741824 | bytes 1048576 | tf_op jit(solution)/shard_map/forward_far/pallas_call | solution.py:387
  20.3 1.9 %collective-permute-done.3 = bf16[4,256,256]{2,1,0:T(8,128)(2,1)S(1)} collective-permute-done((bf16[4,256,256]{2,1,0:T(8,128)(2,1)S(1)}, bf16[4,256,256]{2,1,0:T(8,128)(2,1)S(1)}, u32[]{:S(2)}, u32[]{:S(2)}) %collective-permute-start.3) | collective-permute-done | bytes 524320 | tf_op jit(solution)/shard_map/ppermute | solution.py:28
  22.4 2.5 %collective-permute-start.4 = (bf16[256,256]{1,0:T(8,128)(2,1)S(1)}, bf16[256,256]{1,0:T(8,128)(2,1)S(1)}, u32[]{:S(2)}, u32[]{:S(2)}) collective-permute-start(bf16[256,256]{1,0:T(8,128)(2,1)S(1)} %get-tuple-element.37), channel_id=1, source_target_pairs={{0,6},{2,4},{4,2},{6,0},{1,7},{3,5},{5,3},{7,1},{8,14},{10,12},{12... | collective-permute-start | bytes 393224 | tf_op jit(solution)/shard_map/ppermute | solution.py:28
  26.0 1.9 %turn.1 = (bf16[64,128,128]{2,1,0:T(8,128)(2,1)S(1)}, bf16[256,512]{1,0:T(8,128)(2,1)S(1)}, f32[13,128,256]{2,1,0:T(8,128)S(1)}, f32[13,128,256]{2,1,0:T(8,128)S(1)}) custom-call(s32[3]{0:T(128)S(1)} %pad_add_fusion.places, s32[4]{0:T(128)S(1)} %bitcast.39, bf16[1,256,256]{2,1,0:T(8,128)(2,1)S(1)} %bitcast.30, bf16[1,256,256]{2,1,0:T(8,128)(2,1)S(1)} %bitcast.32, ...), custom_call_target="tpu_custom_call" | custom-call | bytes 4194304 | tf_op jit(solution)/shard_map/turn/pallas_call | solution.py:432
  27.9 1.3 %collective-permute-done.4.first = bf16[256,256]{1,0:T(8,128)(2,1)S(1)} collective-permute-done((bf16[256,256]{1,0:T(8,128)(2,1)S(1)}, bf16[256,256]{1,0:T(8,128)(2,1)S(1)}, u32[]{:S(2)}, u32[]{:S(2)}) %collective-permute-start.4) | collective-permute-done | bytes 131104 | tf_op jit(solution)/shard_map/ppermute | solution.py:28
  29.2 2.5 %collective-permute-done.5.second = bf16[256,256]{1,0:T(8,128)(2,1)S(1)} collective-permute-done((bf16[256,256]{1,0:T(8,128)(2,1)S(1)}, bf16[256,256]{1,0:T(8,128)(2,1)S(1)}, u32[]{:S(2)}, u32[]{:S(2)}) %collective-permute-start.5) | collective-permute-done | bytes 131104 | tf_op jit(solution)/shard_map/ppermute | solution.py:28
  31.9 1.8 %collective-permute-start.9 = (bf16[256,256]{1,0:T(8,128)(2,1)S(1)}, bf16[256,256]{1,0:T(8,128)(2,1)S(1)}, u32[]{:S(2)}, u32[]{:S(2)}) collective-permute-start(bf16[256,256]{1,0:T(8,128)(2,1)S(1)} %grad.1.refs_0_), channel_id=1, source_target_pairs={{0,6},{2,4},{4,2},{6,0},{1,7},{3,5},{5,3},{7,1},{8,14},{10,12},{12... | collective-permute-start | bytes 393224 | tf_op jit(solution)/shard_map/ppermute | solution.py:28
  35.4 3.8 %collective-permute-done.9.refs_3_ = bf16[256,256]{1,0:T(8,128)(2,1)S(1)} collective-permute-done((bf16[256,256]{1,0:T(8,128)(2,1)S(1)}, bf16[256,256]{1,0:T(8,128)(2,1)S(1)}, u32[]{:S(2)}, u32[]{:S(2)}) %collective-permute-start.9) | collective-permute-done | bytes 131104 | tf_op jit(solution)/shard_map/ppermute | solution.py:28
  39.3 1.7 %collective-permute-done.8.refs_2_ = bf16[256,256]{1,0:T(8,128)(2,1)S(1)} collective-permute-done((bf16[256,256]{1,0:T(8,128)(2,1)S(1)}, bf16[256,256]{1,0:T(8,128)(2,1)S(1)}, u32[]{:S(2)}, u32[]{:S(2)}) %collective-permute-start.8) | collective-permute-done | bytes 131104 | tf_op jit(solution)/shard_map/ppermute | solution.py:28
  42.5 1.9 %weight_terms.3 = (f32[3,64,256]{2,1,0:T(8,128)S(1)}, bf16[3,64,256]{2,1,0:T(8,128)(2,1)S(1)}, bf16[3,64,256]{2,1,0:T(8,128)(2,1)S(1)}, bf16[3,64,256]{2,1,0:T(8,128)(2,1)S(1)}, f32[13,128,256]{2,1,0:T(8,128)S(1)}) custom-call(s32[3]{0:T(128)S(1)} %pad_add_fusion.places, s32[3,64]{1,0:T(4,128)S(1)} %bitcast.35, ...), custom_call_target="tpu_custom_call", output_to_operand_aliasing={{4}: (6, {})} | custom-call | tf_op jit(solution)/shard_map/weight_terms/pallas_call | solution.py:478
  45.7 1.6 %collective-permute-start.23 = (bf16[3,64,256]{2,1,0:T(8,128)(2,1)S(1)}, bf16[3,64,256]{2,1,0:T(8,128)(2,1)S(1)}, u32[]{:S(2)}, u32[]{:S(2)}) collective-permute-start(bf16[3,64,256]{2,1,0:T(8,128)(2,1)S(1)} %get-tuple-element.60), channel_id=1, source_target_pairs={{0,4},{2,6},{4,0},{6,2},{1,5},{3,7},{5,1},{7,3},{8,12},{10,14},{12... | collective-permute-start | bytes 294920 | tf_op jit(solution)/shard_map/ppermute | solution.py:28
  48.0 1.9 %weight_terms.2 = (f32[3,64,256]{2,1,0:T(8,128)S(1)}, bf16[3,64,256]{2,1,0:T(8,128)(2,1)S(1)}, bf16[3,64,256]{2,1,0:T(8,128)(2,1)S(1)}, bf16[3,64,256]{2,1,0:T(8,128)(2,1)S(1)}, f32[13,128,256]{2,1,0:T(8,128)S(1)}) custom-call(s32[3]{0:T(128)S(1)} %pad_add_fusion.places, s32[3,64]{1,0:T(4,128)S(1)} %bitcast.36, ...), custom_call_target="tpu_custom_call", output_to_operand_aliasing={{4}: (6, {})} | custom-call | tf_op jit(solution)/shard_map/weight_terms/pallas_call | solution.py:478
  51.1 1.6 %collective-permute-start.15 = (bf16[3,64,256]{2,1,0:T(8,128)(2,1)S(1)}, bf16[3,64,256]{2,1,0:T(8,128)(2,1)S(1)}, u32[]{:S(2)}, u32[]{:S(2)}) collective-permute-start(bf16[3,64,256]{2,1,0:T(8,128)(2,1)S(1)} %get-tuple-element.54), channel_id=1, source_target_pairs={{0,4},{2,6},{4,0},{6,2},{1,5},{3,7},{5,1},{7,3},{8,12},{10,14},{12... | collective-permute-start | bytes 294920 | tf_op jit(solution)/shard_map/ppermute | solution.py:28
  53.6 2.5 %collective-permute-done.14.refs_1_ = bf16[3,64,256]{2,1,0:T(8,128)(2,1)S(1)} collective-permute-done((bf16[3,64,256]{2,1,0:T(8,128)(2,1)S(1)}, bf16[3,64,256]{2,1,0:T(8,128)(2,1)S(1)}, u32[]{:S(2)}, u32[]{:S(2)}) %collective-permute-start.14) | collective-permute-done | bytes 98336 | tf_op jit(solution)/shard_map/ppermute | solution.py:28
  58.2 2.3 %collective-permute-start.26 = (bf16[3,64,256]{2,1,0:T(8,128)(2,1)S(1)}, bf16[3,64,256]{2,1,0:T(8,128)(2,1)S(1)}, u32[]{:S(2)}, u32[]{:S(2)}) collective-permute-start(bf16[3,64,256]{2,1,0:T(8,128)(2,1)S(1)} %sum.10.refs_0_), channel_id=1, source_target_pairs={{0,16},{8,24},{16,0},{24,8},{1,17},{9,25},{17,1},{25,9},{2,18},{10... | collective-permute-start | bytes 294920 | tf_op jit(solution)/shard_map/ppermute | solution.py:28
  60.5 2.5 %collective-permute-done.17.refs_1_ = bf16[3,64,256]{2,1,0:T(8,128)(2,1)S(1)} collective-permute-done((bf16[3,64,256]{2,1,0:T(8,128)(2,1)S(1)}, bf16[3,64,256]{2,1,0:T(8,128)(2,1)S(1)}, u32[]{:S(2)}, u32[]{:S(2)}) %collective-permute-start.17) | collective-permute-done | bytes 98336 | tf_op jit(solution)/shard_map/ppermute | solution.py:28
  63.8 4.4 %collective-permute-done.26.refs_1_ = bf16[3,64,256]{2,1,0:T(8,128)(2,1)S(1)} collective-permute-done((bf16[3,64,256]{2,1,0:T(8,128)(2,1)S(1)}, bf16[3,64,256]{2,1,0:T(8,128)(2,1)S(1)}, u32[]{:S(2)}, u32[]{:S(2)}) %collective-permute-start.26) | collective-permute-done | bytes 98336 | tf_op jit(solution)/shard_map/ppermute | solution.py:28
  68.3 1.6 %collective-permute-start.29 = (bf16[3,64,256]{2,1,0:T(8,128)(2,1)S(1)}, bf16[3,64,256]{2,1,0:T(8,128)(2,1)S(1)}, u32[]{:S(2)}, u32[]{:S(2)}) collective-permute-start(bf16[3,64,256]{2,1,0:T(8,128)(2,1)S(1)} %sum.11.refs_0_), channel_id=1, source_target_pairs={{0,6},{2,4},{4,2},{6,0},{1,7},{3,5},{5,3},{7,1},{8,14},{10,12},{12... | collective-permute-start | bytes 294920 | tf_op jit(solution)/shard_map/ppermute | solution.py:28
  71.9 1.6 %collective-permute-start.21 = (bf16[3,64,256]{2,1,0:T(8,128)(2,1)S(1)}, bf16[3,64,256]{2,1,0:T(8,128)(2,1)S(1)}, u32[]{:S(2)}, u32[]{:S(2)}) collective-permute-start(bf16[3,64,256]{2,1,0:T(8,128)(2,1)S(1)} %sum.8.refs_0_), channel_id=1, source_target_pairs={{0,6},{2,4},{4,2},{6,0},{1,7},{3,5},{5,3},{7,1},{8,14},{10,12},{12... | collective-permute-start | bytes 294920 | tf_op jit(solution)/shard_map/ppermute | solution.py:28
  (75 shorter events, 24.4 us)
Async XLA Ops:
  0.6 7.1 %collective-permute-start = (bf16[256,256]{1,0:T(8,128)(2,1)}, bf16[256,256]{1,0:T(8,128)(2,1)S(1)}, u32[]{:S(2)}, u32[]{:S(2)}) collective-permute-start(bf16[256,256]{1,0:T(8,128)(2,1)} %param.7), channel_id=1, source_target_pairs={{0,8},{8,0},{16,24},{24,16},{1,9},{9,1},{17,25},{25,17},{2,10},{10... | collective-permute-start | bytes 393224 | tf_op jit(solution)/shard_map/ppermute | solution.py:28
  3.7 12.6 %collective-permute-start.2 = (bf16[256,256]{1,0:T(8,128)(2,1)}, bf16[256,256]{1,0:T(8,128)(2,1)S(1)}, u32[]{:S(2)}, u32[]{:S(2)}) collective-permute-start(bf16[256,256]{1,0:T(8,128)(2,1)} %param.7), channel_id=1, source_target_pairs={{0,24},{8,16},{16,8},{24,0},{1,25},{9,17},{17,9},{25,1},{2,26},{10... | collective-permute-start | bytes 393224 | tf_op jit(solution)/shard_map/ppermute | solution.py:28
  6.2 12.0 %collective-permute-start.1 = (bf16[256,256]{1,0:T(8,128)(2,1)}, bf16[256,256]{1,0:T(8,128)(2,1)S(1)}, u32[]{:S(2)}, u32[]{:S(2)}) collective-permute-start(bf16[256,256]{1,0:T(8,128)(2,1)} %param.7), channel_id=1, source_target_pairs={{0,16},{8,24},{16,0},{24,8},{1,17},{9,25},{17,1},{25,9},{2,18},{10... | collective-permute-start | bytes 393224 | tf_op jit(solution)/shard_map/ppermute | solution.py:28
  22.4 6.8 %collective-permute-start.4 = (bf16[256,256]{1,0:T(8,128)(2,1)S(1)}, bf16[256,256]{1,0:T(8,128)(2,1)S(1)}, u32[]{:S(2)}, u32[]{:S(2)}) collective-permute-start(bf16[256,256]{1,0:T(8,128)(2,1)S(1)} %get-tuple-element.37), channel_id=1, source_target_pairs={{0,6},{2,4},{4,2},{6,0},{1,7},{3,5},{5,3},{7,1},{8,14},{10,12},{12... | collective-permute-start | bytes 393224 | tf_op jit(solution)/shard_map/ppermute | solution.py:28
  24.9 6.8 %collective-permute-start.5 = (bf16[256,256]{1,0:T(8,128)(2,1)S(1)}, bf16[256,256]{1,0:T(8,128)(2,1)S(1)}, u32[]{:S(2)}, u32[]{:S(2)}) collective-permute-start(bf16[256,256]{1,0:T(8,128)(2,1)S(1)} %get-tuple-element.38), channel_id=1, source_target_pairs={{0,4},{2,6},{4,0},{6,2},{1,5},{3,7},{5,1},{7,3},{8,12},{10,14},{12... | collective-permute-start | bytes 393224 | tf_op jit(solution)/shard_map/ppermute | solution.py:28
  25.5 6.3 %collective-permute-start.6 = (bf16[256,256]{1,0:T(8,128)(2,1)S(1)}, bf16[256,256]{1,0:T(8,128)(2,1)S(1)}, u32[]{:S(2)}, u32[]{:S(2)}) collective-permute-start(bf16[256,256]{1,0:T(8,128)(2,1)S(1)} %get-tuple-element.39), channel_id=1, source_target_pairs={{0,2},{2,0},{4,6},{6,4},{1,3},{3,1},{5,7},{7,5},{8,10},{10,8},{12,... | collective-permute-start | bytes 393224 | tf_op jit(solution)/shard_map/ppermute | solution.py:28
  31.9 7.4 %collective-permute-start.9 = (bf16[256,256]{1,0:T(8,128)(2,1)S(1)}, bf16[256,256]{1,0:T(8,128)(2,1)S(1)}, u32[]{:S(2)}, u32[]{:S(2)}) collective-permute-start(bf16[256,256]{1,0:T(8,128)(2,1)S(1)} %grad.1.refs_0_), channel_id=1, source_target_pairs={{0,6},{2,4},{4,2},{6,0},{1,7},{3,5},{5,3},{7,1},{8,14},{10,12},{12... | collective-permute-start | bytes 393224 | tf_op jit(solution)/shard_map/ppermute | solution.py:28
  33.7 7.2 %collective-permute-start.8 = (bf16[256,256]{1,0:T(8,128)(2,1)S(1)}, bf16[256,256]{1,0:T(8,128)(2,1)S(1)}, u32[]{:S(2)}, u32[]{:S(2)}) collective-permute-start(bf16[256,256]{1,0:T(8,128)(2,1)S(1)} %grad.1.refs_0_), channel_id=1, source_target_pairs={{0,4},{2,6},{4,0},{6,2},{1,5},{3,7},{5,1},{7,3},{8,12},{10,14},{12... | collective-permute-start | bytes 393224 | tf_op jit(solution)/shard_map/ppermute | solution.py:28
  35.0 5.9 %collective-permute-start.7 = (bf16[256,256]{1,0:T(8,128)(2,1)S(1)}, bf16[256,256]{1,0:T(8,128)(2,1)S(1)}, u32[]{:S(2)}, u32[]{:S(2)}) collective-permute-start(bf16[256,256]{1,0:T(8,128)(2,1)S(1)} %grad.1.refs_0_), channel_id=1, source_target_pairs={{0,2},{2,0},{4,6},{6,4},{1,3},{3,1},{5,7},{7,5},{8,10},{10,8},{12,... | collective-permute-start | bytes 393224 | tf_op jit(solution)/shard_map/ppermute | solution.py:28
  35.4 6.0 %collective-permute-start.10 = (bf16[256,256]{1,0:T(8,128)(2,1)S(1)}, bf16[256,256]{1,0:T(8,128)(2,1)S(1)}, u32[]{:S(2)}, u32[]{:S(2)}) collective-permute-start(bf16[256,256]{1,0:T(8,128)(2,1)S(1)} %grad.1.refs_0_), channel_id=1, source_target_pairs={{0,1},{1,0},{2,3},{3,2},{4,5},{5,4},{6,7},{7,6},{8,9},{9,8},{10,11... | collective-permute-start | bytes 393224 | tf_op jit(solution)/shard_map/ppermute | solution.py:28
  44.4 8.3 %collective-permute-start.22 = (bf16[3,64,256]{2,1,0:T(8,128)(2,1)S(1)}, bf16[3,64,256]{2,1,0:T(8,128)(2,1)S(1)}, u32[]{:S(2)}, u32[]{:S(2)}) collective-permute-start(bf16[3,64,256]{2,1,0:T(8,128)(2,1)S(1)} %get-tuple-element.59), channel_id=1, source_target_pairs={{0,6},{2,4},{4,2},{6,0},{1,7},{3,5},{5,3},{7,1},{8,14},{10,12},{12... | collective-permute-start | bytes 294920 | tf_op jit(solution)/shard_map/ppermute | solution.py:28
  45.7 7.8 %collective-permute-start.23 = (bf16[3,64,256]{2,1,0:T(8,128)(2,1)S(1)}, bf16[3,64,256]{2,1,0:T(8,128)(2,1)S(1)}, u32[]{:S(2)}, u32[]{:S(2)}) collective-permute-start(bf16[3,64,256]{2,1,0:T(8,128)(2,1)S(1)} %get-tuple-element.60), channel_id=1, source_target_pairs={{0,4},{2,6},{4,0},{6,2},{1,5},{3,7},{5,1},{7,3},{8,12},{10,14},{12... | collective-permute-start | bytes 294920 | tf_op jit(solution)/shard_map/ppermute | solution.py:28
  47.3 6.1 %collective-permute-start.24 = (bf16[3,64,256]{2,1,0:T(8,128)(2,1)S(1)}, bf16[3,64,256]{2,1,0:T(8,128)(2,1)S(1)}, u32[]{:S(2)}, u32[]{:S(2)}) collective-permute-start(bf16[3,64,256]{2,1,0:T(8,128)(2,1)S(1)} %get-tuple-element.61), channel_id=1, source_target_pairs={{0,2},{2,0},{4,6},{6,4},{1,3},{3,1},{5,7},{7,5},{8,10},{10,8},{12,... | collective-permute-start | bytes 294920 | tf_op jit(solution)/shard_map/ppermute | solution.py:28
  49.9 6.2 %collective-permute-start.14 = (bf16[3,64,256]{2,1,0:T(8,128)(2,1)S(1)}, bf16[3,64,256]{2,1,0:T(8,128)(2,1)S(1)}, u32[]{:S(2)}, u32[]{:S(2)}) collective-permute-start(bf16[3,64,256]{2,1,0:T(8,128)(2,1)S(1)} %get-tuple-element.53), channel_id=1, source_target_pairs={{0,6},{2,4},{4,2},{6,0},{1,7},{3,5},{5,3},{7,1},{8,14},{10,12},{12... | collective-permute-start | bytes 294920 | tf_op jit(solution)/shard_map/ppermute | solution.py:28
  51.1 6.1 %collective-permute-start.15 = (bf16[3,64,256]{2,1,0:T(8,128)(2,1)S(1)}, bf16[3,64,256]{2,1,0:T(8,128)(2,1)S(1)}, u32[]{:S(2)}, u32[]{:S(2)}) collective-permute-start(bf16[3,64,256]{2,1,0:T(8,128)(2,1)S(1)} %get-tuple-element.54), channel_id=1, source_target_pairs={{0,4},{2,6},{4,0},{6,2},{1,5},{3,7},{5,1},{7,3},{8,12},{10,14},{12... | collective-permute-start | bytes 294920 | tf_op jit(solution)/shard_map/ppermute | solution.py:28
  53.5 4.7 %collective-permute-start.25 = (bf16[3,64,256]{2,1,0:T(8,128)(2,1)S(1)}, bf16[3,64,256]{2,1,0:T(8,128)(2,1)S(1)}, u32[]{:S(2)}, u32[]{:S(2)}) collective-permute-start(bf16[3,64,256]{2,1,0:T(8,128)(2,1)S(1)} %sum.9.refs_0_), channel_id=1, source_target_pairs={{0,8},{8,0},{16,24},{24,16},{1,9},{9,1},{17,25},{25,17},{2,10},{10... | collective-permute-start | bytes 294920 | tf_op jit(solution)/shard_map/ppermute | solution.py:28
  57.4 5.5 %collective-permute-start.17 = (bf16[3,64,256]{2,1,0:T(8,128)(2,1)S(1)}, bf16[3,64,256]{2,1,0:T(8,128)(2,1)S(1)}, u32[]{:S(2)}, u32[]{:S(2)}) collective-permute-start(bf16[3,64,256]{2,1,0:T(8,128)(2,1)S(1)} %sum.6.refs_0_), channel_id=1, source_target_pairs={{0,8},{8,0},{16,24},{24,16},{1,9},{9,1},{17,25},{25,17},{2,10},{10... | collective-permute-start | bytes 294920 | tf_op jit(solution)/shard_map/ppermute | solution.py:28
  58.2 10.0 %collective-permute-start.26 = (bf16[3,64,256]{2,1,0:T(8,128)(2,1)S(1)}, bf16[3,64,256]{2,1,0:T(8,128)(2,1)S(1)}, u32[]{:S(2)}, u32[]{:S(2)}) collective-permute-start(bf16[3,64,256]{2,1,0:T(8,128)(2,1)S(1)} %sum.10.refs_0_), channel_id=1, source_target_pairs={{0,16},{8,24},{16,0},{24,8},{1,17},{9,25},{17,1},{25,9},{2,18},{10... | collective-permute-start | bytes 294920 | tf_op jit(solution)/shard_map/ppermute | solution.py:28
  63.0 8.9 %collective-permute-start.18 = (bf16[3,64,256]{2,1,0:T(8,128)(2,1)S(1)}, bf16[3,64,256]{2,1,0:T(8,128)(2,1)S(1)}, u32[]{:S(2)}, u32[]{:S(2)}) collective-permute-start(bf16[3,64,256]{2,1,0:T(8,128)(2,1)S(1)} %sum.7.refs_0_), channel_id=1, source_target_pairs={{0,16},{8,24},{16,0},{24,8},{1,17},{9,25},{17,1},{25,9},{2,18},{10... | collective-permute-start | bytes 294920 | tf_op jit(solution)/shard_map/ppermute | solution.py:28
  68.3 6.6 %collective-permute-start.29 = (bf16[3,64,256]{2,1,0:T(8,128)(2,1)S(1)}, bf16[3,64,256]{2,1,0:T(8,128)(2,1)S(1)}, u32[]{:S(2)}, u32[]{:S(2)}) collective-permute-start(bf16[3,64,256]{2,1,0:T(8,128)(2,1)S(1)} %sum.11.refs_0_), channel_id=1, source_target_pairs={{0,6},{2,4},{4,2},{6,0},{1,7},{3,5},{5,3},{7,1},{8,14},{10,12},{12... | collective-permute-start | bytes 294920 | tf_op jit(solution)/shard_map/ppermute | solution.py:28
  69.9 6.9 %collective-permute-start.28 = (bf16[3,64,256]{2,1,0:T(8,128)(2,1)S(1)}, bf16[3,64,256]{2,1,0:T(8,128)(2,1)S(1)}, u32[]{:S(2)}, u32[]{:S(2)}) collective-permute-start(bf16[3,64,256]{2,1,0:T(8,128)(2,1)S(1)} %sum.11.refs_0_), channel_id=1, source_target_pairs={{0,4},{2,6},{4,0},{6,2},{1,5},{3,7},{5,1},{7,3},{8,12},{10,14},{12... | collective-permute-start | bytes 294920 | tf_op jit(solution)/shard_map/ppermute | solution.py:28
  70.8 6.0 %collective-permute-start.27 = (bf16[3,64,256]{2,1,0:T(8,128)(2,1)S(1)}, bf16[3,64,256]{2,1,0:T(8,128)(2,1)S(1)}, u32[]{:S(2)}, u32[]{:S(2)}) collective-permute-start(bf16[3,64,256]{2,1,0:T(8,128)(2,1)S(1)} %sum.11.refs_0_), channel_id=1, source_target_pairs={{0,2},{2,0},{4,6},{6,4},{1,3},{3,1},{5,7},{7,5},{8,10},{10,8},{12,... | collective-permute-start | bytes 294920 | tf_op jit(solution)/shard_map/ppermute | solution.py:28
  71.9 6.1 %collective-permute-start.21 = (bf16[3,64,256]{2,1,0:T(8,128)(2,1)S(1)}, bf16[3,64,256]{2,1,0:T(8,128)(2,1)S(1)}, u32[]{:S(2)}, u32[]{:S(2)}) collective-permute-start(bf16[3,64,256]{2,1,0:T(8,128)(2,1)S(1)} %sum.8.refs_0_), channel_id=1, source_target_pairs={{0,6},{2,4},{4,2},{6,0},{1,7},{3,5},{5,3},{7,1},{8,14},{10,12},{12... | collective-permute-start | bytes 294920 | tf_op jit(solution)/shard_map/ppermute | solution.py:28
  73.5 5.4 %collective-permute-start.20 = (bf16[3,64,256]{2,1,0:T(8,128)(2,1)S(1)}, bf16[3,64,256]{2,1,0:T(8,128)(2,1)S(1)}, u32[]{:S(2)}, u32[]{:S(2)}) collective-permute-start(bf16[3,64,256]{2,1,0:T(8,128)(2,1)S(1)} %sum.8.refs_0_), channel_id=1, source_target_pairs={{0,4},{2,6},{4,0},{6,2},{1,5},{3,7},{5,1},{7,3},{8,12},{10,14},{12... | collective-permute-start | bytes 294920 | tf_op jit(solution)/shard_map/ppermute | solution.py:28
  (15 other events, 52.3 us)

commit v4 on v3

v4 whole, which is shorter than its diff:
```python
import functools
import math

import jax
import jax.numpy as jnp
from jax import lax
from jax.experimental import pallas as pl
from jax.experimental.pallas import tpu as pltpu
from jax.sharding import PartitionSpec as P

F32, BF16, I32 = jnp.float32, jnp.bfloat16, jnp.int32
WHOLE = pl.BlockSpec(memory_space=pltpu.VMEM)
SCALARS = pl.BlockSpec(memory_space=pltpu.SMEM)
ANYWHERE = pl.BlockSpec(memory_space=pl.ANY)
UNROLL = 16


def vmem_for(*arrays):
    held = sum(math.prod(a.shape) * jnp.dtype(a.dtype).itemsize for a in arrays)
    return pltpu.CompilerParams(vmem_limit_bytes=held + held // 8 + 3 * 1024 * 1024)


def partner_pairs(size, mask):
    return [(i, i ^ mask) for i in range(size)]


def swap(value, axis, mask):
    return lax.ppermute(value, axis, partner_pairs(lax.axis_size(axis), mask))


def here():
    return [lax.axis_index(axis) for axis in ("dom", "src", "rel")]


def slot_of(places, partition, masked):
    return partition ^ places[0] if masked else partition


def packed(entries, targets, e, target, place):
    bits = (entries - 1).bit_length()
    return e | (target << bits) | (place << (bits + (targets - 1).bit_length()))


def unpacked(entries, targets, code):
    bits, more = (entries - 1).bit_length(), (targets - 1).bit_length()
    return code & ((1 << bits) - 1), (code >> bits) & ((1 << more) - 1), code >> (bits + more)


def for_entries(total, body):
    def step(i, carry):
        body([(jnp.minimum(i * UNROLL + u, total - 1), i * UNROLL + u < total) for u in range(UNROLL)])
        return carry

    lax.fori_loop(0, (total + UNROLL - 1) // UNROLL, step, 0)


def halo_block(first_block, halo_refs, i, tile):
    per_call = halo_refs[0].shape[0]
    rows = pl.ds(pl.multiple_of(first_block * tile, tile), tile)
    return halo_refs[i // per_call][i % per_call, rows, :]


def prepare_kernel(masked, combine, slot_bounds, bounds, targets, chosen, table, count, *refs):
    values, weight, values_here, weight_here, values_turned = refs[:5]
    by_slot = refs[5 : 4 + len(slot_bounds)]
    by_relation = refs[4 + len(slot_bounds) : 3 + len(slot_bounds) + len(bounds)]
    zeros, sems = refs[3 + len(slot_bounds) + len(bounds) : -1], refs[-1]
    entries, relations = values.shape[0], weight.shape[0]
    parts = sems.shape[0] - 1
    batch = entries // parts
    copies = [
        pltpu.make_async_copy(
            values.at[pl.ds(i * batch, batch)], values_here.at[pl.ds(i * batch, batch)], sems.at[i]
        )
        for i in range(parts)
    ]
    copies.append(pltpu.make_async_copy(weight, weight_here, sems.at[parts]))
    for copy in copies:
        copy.start()
    for each in zeros:
        each[...] = jnp.zeros_like(each)
    places = here()
    slots = slot_bounds[-1]

    def put(e, found):
        target, relation = table[0, e], table[2, e]
        slot = slot_of(places, table[1, e], masked)
        now = []
        for listed, low, high in zip(by_slot, slot_bounds, slot_bounds[1:]):
            place = (slot - low) * relations + relation
            listed[found[len(now)]] = packed(entries, targets, e, target, place)
            now.append((slot >= low) & (slot < high))
        for listed, low, high in zip(by_relation, bounds, bounds[1:]):
            place = (relation - low) * slots + slot
            listed[found[len(now)]] = packed(entries, targets, e, target, place)
            now.append((relation >= low) & (relation < high))
        return tuple(f + n.astype(I32) for f, n in zip(found, now))

    lists = (*by_slot, *by_relation)
    found = lax.fori_loop(0, count[0], put, (jnp.int32(0),) * len(lists))
    for listed, number in zip(lists, found):
        listed[entries] = number
    for listed, low, high in zip(by_slot, slot_bounds, slot_bounds[1:]):
        for i in range(low, high):
            listed[entries + 1 + i - low] = chosen[slot_of(places, i, masked)]

    for i, copy in enumerate(copies):
        copy.wait()
        if i < parts:

            def turn(j, carry):
                values_turned[i * batch + 2 * j] = values_here[i * batch + 2 * j].T
                values_turned[i * batch + 2 * j + 1] = values_here[i * batch + 2 * j + 1].T
                return carry

            lax.fori_loop(0, batch // 2, turn, 0, unroll=4)


def forward_kernel(tile, combine, halo_count, last, order, *refs):
    halo_refs, refs = refs[:halo_count], refs[halo_count:]
    weight, values, pre, outs, projected = refs[0], refs[1], refs[3], refs[4:-1], refs[-1]
    entries = values.shape[0]
    slots = halo_count * halo_refs[0].shape[0]
    firsts = [order[entries + 1 + i] for i in range(slots)]
    project(tile, combine, firsts, halo_refs, weight, projected)
    add_entries(combine, values, weight, projected, order, order[entries], pre)
    if last:
        hand_out(tile, here(), pre, outs)


def project(tile, combine, firsts, halo_refs, weight, projected):
    relations = weight.shape[0]
    blocks = [halo_block(first, halo_refs, i, tile) for i, first in enumerate(firsts)]
    if not combine:
        for i, block in enumerate(blocks):
            projected[i] = block
        return
    stacked = jnp.concatenate(blocks, axis=0)
    for r in range(relations):
        product = jnp.dot(stacked, weight[r], preferred_element_type=F32).astype(BF16)
        for i in range(len(blocks)):
            projected[i * relations + r] = product[i * tile : (i + 1) * tile]


def add_entries(combine, values, weight, projected, order, total, pre):
    entries, relations, spare = values.shape[0], weight.shape[0], pre.shape[0] - 1

    def body(positions):
        terms = []
        for position, real in positions:
            e, target, place = unpacked(entries, spare, order[position])
            if combine:
                term = jnp.dot(values[e], projected[place], preferred_element_type=F32)
            else:
                message = jnp.dot(
                    values[e], projected[place // relations], preferred_element_type=F32
                )
                term = jnp.dot(
                    message.astype(BF16), weight[place % relations], preferred_element_type=F32
                )
            terms.append((jnp.where(real, target, spare), term))
        for target, term in terms:
            pre[target] = pre[target] + term

    for_entries(total, body)


def hand_out(tile, places, pre, outs):
    keeps, sends = outs[:-2], outs[-2:]
    panels, per_owner = len(keeps), keeps[0].shape[0] // tile
    groups = (pre.shape[0] - 1) // (panels * per_owner)
    for distance in reversed(range(panels)):
        panel = places[1] ^ distance
        for part in range(per_owner):
            rows = pl.ds(part * tile, tile)
            mine = (panel * groups + places[2]) * per_owner + part
            other = (panel * groups + (places[2] ^ 1)) * per_owner + part
            if distance == panels - 1:
                sends[0][rows, :] = pre[other].astype(BF16)
            else:
                sends[1][distance, rows, :] = pre[other].astype(BF16)
            keeps[distance][rows, :] = pre[mine]


def chip_kernel(*refs):
    count = (len(refs) - 1) // 2
    keeps, arrived, outs = refs[:count], refs[count], refs[count + 1 :]
    for m in range(count):
        outs[m][...] = (keeps[m][...] + arrived[m].astype(F32)).astype(outs[m].dtype)


def grad_kernel(own, first, second, third, cotangent, grad):
    pre = own[...] + first[...].astype(F32) + second[...].astype(F32) + third[...].astype(F32)
    grad[...] = (cotangent[...].astype(F32) * silu_slope(pre)).astype(BF16)


def turn_kernel(masked, tile, panels, chosen, *refs):
    halo_refs, halo_turned, scratch = refs[:-2], refs[-2], refs[-1]
    places = here()
    share = scratch.shape[0] // panels
    for slot in range(len(halo_refs) * halo_refs[0].shape[0]):
        block = halo_block(chosen[slot_of(places, slot, masked)], halo_refs, slot, tile)
        scratch[...] = block.astype(F32).T
        for m in range(panels):
            start = pl.multiple_of((places[1] ^ m) * share, share)
            halo_turned[pl.ds(m * share, share), pl.ds(slot * tile, tile)] = (
                scratch[pl.ds(start, share), :].astype(BF16)
            )


def collect_kernel(tile, *refs):
    grad_refs, grads = refs[:-1], refs[-1]
    panels = len(grad_refs) // 2
    per_owner = grad_refs[0].shape[0] // tile
    for g in range(2):
        for m in range(panels):
            owner = (lax.axis_index("src") ^ m) * 2 + (lax.axis_index("rel") ^ g)
            for part in range(per_owner):
                grads[owner * per_owner + part] = grad_refs[g * panels + m][
                    pl.ds(part * tile, tile), :
                ]


def weight_kernel(tile, combine, listed, *refs):
    values_turned, halo_turned, grads = refs[:3]
    outs, sums = refs[4:-1], refs[-1]
    features = halo_turned.shape[0]
    slots = halo_turned.shape[1] // tile
    relations, share = outs[0].shape[0], outs[0].shape[1]
    entries, targets, spare = values_turned.shape[0], grads.shape[0], sums.shape[0] - 1

    def body(positions):
        terms = []
        for position, real in positions:
            e, target, place = unpacked(entries, targets, listed[position])
            term = jnp.dot(values_turned[e], grads[target], preferred_element_type=F32)
            if not combine:
                columns = pl.ds(pl.multiple_of(place % slots * tile, tile), tile)
                term = jnp.dot(
                    halo_turned[:, columns], term.astype(BF16), preferred_element_type=F32
                )
                place = place // slots
            terms.append((jnp.where(real, place, spare), term))
        for place, term in terms:
            sums[place] = sums[place] + term

    for_entries(listed[entries], body)
    for r in range(relations):
        if combine:
            stacked = sums[r * slots : (r + 1) * slots].reshape(slots * tile, features)
            grad = jnp.dot(halo_turned[...], stacked.astype(BF16), preferred_element_type=F32)
        else:
            grad = sums[r]
        for m, out in enumerate(outs):
            out[r] = grad[m * share : (m + 1) * share].astype(out.dtype)


def spread_kernel(first_relation, *refs):
    out, scratch, sems = refs[-3:]
    shares = refs[: scratch.shape[0]]
    relations, share = scratch.shape[1], scratch.shape[2]
    copies = []
    for m in reversed(range(len(shares))):
        scratch[m] = shares[m][...].astype(F32)
        panel = lax.axis_index("src") ^ m
        rows = pl.ds(pl.multiple_of(panel * share, share), share)
        copies.append(
            pltpu.make_async_copy(
                scratch.at[m],
                out.at[pl.ds(first_relation, relations), rows, :],
                sems.at[m],
            )
        )
        copies[-1].start()
    for copy in copies:
        copy.wait()


def spread(first_relation, shares, total, so_far):
    scratch = jax.ShapeDtypeStruct((len(shares), *shares[0].shape), F32)
    return pl.pallas_call(
        functools.partial(spread_kernel, first_relation),
        out_shape=total,
        in_specs=[WHOLE] * len(shares) + [ANYWHERE] * len(so_far),
        out_specs=ANYWHERE,
        scratch_shapes=[
            pltpu.VMEM(scratch.shape, F32),
            pltpu.SemaphoreType.DMA((len(shares),)),
        ],
        input_output_aliases={len(shares): 0} if so_far else {},
        compiler_params=vmem_for(scratch, *shares),
        name="spread",
    )(*shares, *so_far)


def sum_kernel(*refs):
    total = refs[0][...].astype(F32)
    for ref in refs[1:-1]:
        total = total + ref[...].astype(F32)
    refs[-1][...] = total.astype(refs[-1].dtype)


def summed(values, dtype=BF16):
    out = jax.ShapeDtypeStruct(values[0].shape, dtype)
    return pl.pallas_call(
        sum_kernel,
        out_shape=out,
        in_specs=[WHOLE] * len(values),
        out_specs=WHOLE,
        compiler_params=vmem_for(out, *values),
        name="sum",
    )(*values)


def silu_slope(pre_values):
    logistic = jax.nn.sigmoid(pre_values)
    return logistic * (1.0 + pre_values * (1.0 - logistic))


def exchange(pieces, axis):
    return [swap(pieces[m].astype(BF16), axis, m) for m in range(len(pieces) - 1, 0, -1)]


def added(own, arrived):
    total = own.astype(F32)
    for value in arrived:
        total = total + value.astype(F32)
    return total


def gather(value, axis):
    return [value] + [swap(value, axis, m) for m in range(1, lax.axis_size(axis))]


def local(source_feats, rel_weight, halo_pick, entry_index, entry_count, entry_values, cotangent):
    partitions, panels = lax.axis_size("dom"), lax.axis_size("src")
    groups = lax.axis_size("rel")
    tile = entry_values.shape[-1]
    own_rows, features = cotangent.shape
    relations = rel_weight.shape[0]
    values = entry_values.reshape(-1, tile, tile)
    table = entry_index.reshape(3, -1)
    entries = table.shape[1]
    count = entry_count.reshape(1)
    chosen = halo_pick.reshape(-1)
    targets = own_rows * panels * groups // tile
    direct = partitions <= 8
    share = features // panels
    bounds = tuple(sorted({0, relations // 2, relations}))
    chunks = len(bounds) - 1

    panel_f32 = jax.ShapeDtypeStruct((own_rows, features), F32)
    panel_bf16 = jax.ShapeDtypeStruct((own_rows, features), BF16)
    kept = (panel_f32,) * panels + (
        panel_bf16,
        jax.ShapeDtypeStruct((panels - 1, own_rows, features), BF16),
    )
    pre_sums = jax.ShapeDtypeStruct((targets + 1, tile, features), F32)
    if direct:
        halo = [h[None] for h in gather(source_feats, "dom")]
    else:
        halo = [lax.all_gather(source_feats, "dom", axis=0)]
    slots = sum(h.shape[0] for h in halo)
    combine = slots * relations <= entries
    near = partitions // 2
    slot_bounds = (0, near, slots) if direct else (0, slots)
    sums = [
        jax.ShapeDtypeStruct(
            ((high - low) * slots + 1, tile, features)
            if combine
            else (high - low + 1, features, features),
            F32,
        )
        for low, high in zip(bounds, bounds[1:])
    ]
    listings = [
        jax.ShapeDtypeStruct((entries + 1 + high - low,), I32)
        for low, high in zip(slot_bounds, slot_bounds[1:])
    ] + [jax.ShapeDtypeStruct((entries + 1,), I32)] * chunks
    held = [jax.ShapeDtypeStruct(v.shape, BF16) for v in (values, rel_weight, values)]
    values, rel_weight, values_turned, *others = pl.pallas_call(
        functools.partial(prepare_kernel, direct, combine, slot_bounds, bounds, targets),
        out_shape=(*held, *listings, pre_sums, *sums),
        in_specs=[SCALARS] * 3 + [ANYWHERE] * 2,
        out_specs=(WHOLE,) * 3 + (SCALARS,) * len(listings) + (WHOLE,) * (1 + chunks),
        scratch_shapes=[pltpu.SemaphoreType.DMA((5,))],
        compiler_params=vmem_for(*held, pre_sums, *sums),
        cost_estimate=pl.CostEstimate(
            flops=0, bytes_accessed=6 * values.size, transcendentals=0
        ),
        name="prepare",
    )(chosen, table, count, values, rel_weight)
    listings, pre, sums_in = others[: len(listings)], others[len(listings)], others[-chunks:]
    lists = listings[-chunks:]

    for call, (low, high) in enumerate(zip(slot_bounds, slot_bounds[1:])):
        last = high == slots
        blocks = halo[low:high] if direct else halo
        projected = jax.ShapeDtypeStruct(
            ((high - low) * (relations if combine else 1), tile, features), BF16
        )
        outs = (pre_sums, *kept) if last else (pre_sums,)
        pre, *given = pl.pallas_call(
            functools.partial(forward_kernel, tile, combine, len(blocks), last),
            out_shape=outs,
            in_specs=[SCALARS] + [WHOLE] * (len(blocks) + 3),
            out_specs=(WHOLE,) * len(outs),
            scratch_shapes=[pltpu.VMEM(projected.shape, BF16)],
            input_output_aliases={3 + len(blocks): 0},
            compiler_params=vmem_for(*outs, projected, *blocks, rel_weight, values),
            cost_estimate=pl.CostEstimate(
                flops=4 * entries * tile * tile * features,
                bytes_accessed=values.size,
                transcendentals=0,
            ),
            name="forward",
        )(listings[call], *blocks, rel_weight, values, pre)

    *keeps, farthest, rest = given
    farthest = summed([keeps[-1], swap(farthest, "rel", 1)])
    nearer = (panel_f32,) + (panel_bf16,) * (panels - 2)
    leaving = pl.pallas_call(
        chip_kernel,
        out_shape=nearer,
        in_specs=[WHOLE] * panels,
        out_specs=(WHOLE,) * (panels - 1),
        compiler_params=vmem_for(*nearer, *keeps, rest),
        name="chip",
    )(*keeps[:-1], swap(rest, "rel", 1))
    leaving = [*leaving, farthest]
    leaving, chosen_then = lax.optimization_barrier((leaving, chosen))
    arrived = exchange(leaving, "src")
    halo_turned = jax.ShapeDtypeStruct((features, slots * tile), BF16)
    turned = (values, halo_turned)
    halo_turned = pl.pallas_call(
        functools.partial(turn_kernel, direct, tile, panels),
        out_shape=halo_turned,
        in_specs=[SCALARS] + [WHOLE] * len(halo),
        out_specs=WHOLE,
        scratch_shapes=[pltpu.VMEM((features, tile), F32)],
        compiler_params=vmem_for(halo_turned, halo_turned, *halo),
        cost_estimate=pl.CostEstimate(
            flops=0, bytes_accessed=4 * halo_turned.size, transcendentals=0
        ),
        name="turn",
    )(chosen_then, *halo)
    arrived, halo_turned = lax.optimization_barrier((arrived, halo_turned))
    block = jax.ShapeDtypeStruct((own_rows, features), BF16)
    if len(arrived) == 3:
        local_grad = pl.pallas_call(
            grad_kernel,
            out_shape=block,
            in_specs=[WHOLE] * 5,
            out_specs=WHOLE,
            compiler_params=vmem_for(leaving[0], block, block, block, block, block),
            name="grad",
        )(leaving[0], *arrived, cotangent)
    else:
        local_grad = cotangent.astype(F32) * silu_slope(added(leaving[0], arrived))
        local_grad = local_grad.astype(BF16)
    out_feats = jax.nn.silu(added(leaving[0], arrived)).astype(BF16)

    core_grads = gather(local_grad, "src")
    other_grads = [swap(value, "rel", 1) for value in core_grads]

    by_target = jax.ShapeDtypeStruct((targets, tile, features), BF16)
    grads = pl.pallas_call(
        functools.partial(collect_kernel, tile),
        out_shape=by_target,
        in_specs=[WHOLE] * (2 * panels),
        out_specs=WHOLE,
        compiler_params=vmem_for(by_target, by_target),
        name="collect",
    )(*core_grads, *other_grads)

    total = jax.ShapeDtypeStruct((relations, features, features), F32)
    panel_sums, pieces, done = [], [], []
    for c in range(chunks):
        own_share = jax.ShapeDtypeStruct((bounds[c + 1] - bounds[c], share, features), F32)
        sent_share = jax.ShapeDtypeStruct(own_share.shape, BF16)
        *shares, _ = pl.pallas_call(
            functools.partial(weight_kernel, tile, combine),
            out_shape=(own_share,) + (sent_share,) * (panels - 1) + (sums[c],),
            in_specs=[SCALARS] + [WHOLE] * 4,
            out_specs=(WHOLE,) * (panels + 1),
            input_output_aliases={4: panels},
            compiler_params=vmem_for(*(own_share,) * panels, sums[c], by_target, *turned),
            name="weight_terms",
        )(lists[c], values_turned, halo_turned, grads, sums_in[c])
        panel_sums.append(
            summed([shares[0]] + exchange(shares, "src"), BF16 if direct else F32)
        )
    for c, panel_sum in enumerate(panel_sums):
        if direct:
            masks = [1 << i for i in range(partitions.bit_length() - 1)]
            for mask in masks if c % 2 else reversed(masks):
                panel_sum = summed([panel_sum, swap(panel_sum, "dom", mask)])
        else:
            panel_sum = lax.psum(panel_sum, "dom").astype(BF16)
        pieces.append(gather(panel_sum, "src"))
    for c in range(chunks):
        done = [spread(bounds[c], pieces[c], total, done)]
    grad_rel = done[0]
    return (out_feats, grad_rel)


def solution(mesh):
    return jax.shard_map(
        local,
        mesh=mesh,
        in_specs=(
            P(("dom", "src", "rel"), None),
            P("rel", None, None),
            P("dom", "src", "rel", None),
            P("dom", "src", "rel", None, None),
            P("dom", "src", "rel"),
            P("dom", "src", "rel", None, None, None),
            P(("dom", "src", "rel"), None),
        ),
        out_specs=(P(("dom", "src", "rel"), None), P("rel", None, None)),
        check_vma=False,
    )
```

time: 80.7 us -> 77.6 us (0.962)
  Pallas kernels: 14.2 us -> 13.1 us
  local copies, waits for them, and re-layouts: 5.05 us -> 4.07 us
    pallas_call x5 -> x7, Pallas kernels: 11.9 us -> 10.8 us  [the longest x1 3.4 us: local(): pl.pallas_call(functools.partial(prepare_kernel, direct, combine, slot_bo...]
    unnamed x19 -> x11, local copies, waits for them, and re-layouts: 4.99 us -> 4.07 us
    ppermute x30 -> x31, starting transfers between devices: 30.9 us -> 30.3 us  [swap(): return lax.ppermute(value, axis, partner_pairs(lax.axis_size(axis), mask))]
    ppermute x30 -> x31, waiting for transfers between devices: 27.9 us -> 27.6 us  [swap(): return lax.ppermute(value, axis, partner_pairs(lax.axis_size(axis), mask))]
  transfers between devices with their start and end apart: 30 -> 31, of which waited for: 19 -> 21; matrix products, arithmetic and copies ran while one was open for 2% -> 2% of each run, Pallas kernels for 11% -> 11%
where the time goes in v4:
time: 77.6 us; the launch traced here: 77.3 us
  starting transfers between devices  30.3 us (39%)
  waiting for transfers between devices  27.6 us (36%)
  Pallas kernels  13.1 us (17%)
  local copies, waits for them, and re-layouts  4.07 us (5%)
  between operations  1.47 us (2%)
    ppermute x31, starting transfers between devices, swap(): return lax.ppermute(value, axis, partner_pairs(lax.axis_size(axis), mask))  30.3 us
    ppermute x31, waiting for transfers between devices, swap(): return lax.ppermute(value, axis, partner_pairs(lax.axis_size(axis), mask))  27.6 us
    unnamed x11, local copies, waits for them, and re-layouts  4.07 us
    pallas_call x1, Pallas kernels, local(): pl.pallas_call(functools.partial(prepare_kernel, direct, combine, slot_bo...  3.4 us
    pallas_call x2, Pallas kernels, local(): pl.pallas_call(functools.partial(forward_kernel, tile, combine, len(block...  3.33 us
    pallas_call x2, Pallas kernels, local(): pl.pallas_call(functools.partial(weight_kernel, tile, combine), out_shape...  3.23 us
    pallas_call x2, Pallas kernels, spread(): pl.pallas_call(functools.partial(spread_kernel, first_relation), out_shap...  1.84 us
  transfers between devices with their start and end apart: 31, of which 21 were waited for; matrix products, arithmetic and copies ran while one was open for 2% of the time, Pallas kernels for 11%

profile of v4, /device:TPU:0, one launch (start us, length us, event | category | flops | bytes accessed | tf_op | source)
XLA Modules:
  0.0 77.3 jit_solution(11389722866773937186)
XLA Ops:
  0.6 3.1 %collective-permute-start.2 = (bf16[256,256]{1,0:T(8,128)(2,1)}, bf16[256,256]{1,0:T(8,128)(2,1)S(1)}, u32[]{:S(2)}, u32[]{:S(2)}) collective-permute-start(bf16[256,256]{1,0:T(8,128)(2,1)} %param.7), channel_id=1, source_target_pairs={{0,8},{8,0},{16,24},{24,16},{1,9},{9,1},{17,25},{25,17},{2,10},{10... | collective-permute-start | bytes 393224 | tf_op jit(solution)/shard_map/ppermute | solution.py:28
  3.7 2.5 %collective-permute-start.1 = (bf16[256,256]{1,0:T(8,128)(2,1)}, bf16[256,256]{1,0:T(8,128)(2,1)S(1)}, u32[]{:S(2)}, u32[]{:S(2)}) collective-permute-start(bf16[256,256]{1,0:T(8,128)(2,1)} %param.7), channel_id=1, source_target_pairs={{0,24},{8,16},{16,8},{24,0},{1,25},{9,17},{17,9},{25,1},{2,26},{10... | collective-permute-start | bytes 393224 | tf_op jit(solution)/shard_map/ppermute | solution.py:28
  7.6 1.6 %copy-done = bf16[1,1,1,64,128,128]{5,4,3,2,1,0:T(8,128)(2,1)S(1)} copy-done((bf16[1,1,1,64,128,128]{5,4,3,2,1,0:T(8,128)(2,1)S(1)}, bf16[1,1,1,64,128,128]{5,4,3,2,1,0:T(8,128)(2,1)}, u32[]{:S(2)}) %copy-start) | copy-done | bytes 2097176
  11.0 3.4 %prepare.1 = (bf16[64,128,128]{2,1,0:T(8,128)(2,1)S(1)}, bf16[6,256,256]{2,1,0:T(8,128)(2,1)S(1)}, bf16[64,128,128]{2,1,0:T(8,128)(2,1)S(1)}, s32[67]{0:T(128)S(...) custom-call(s32[4]{0:T(128)S(1)} %bitcast.21, ...), custom_call_target="tpu_custom_call" | custom-call | bytes 6291456 | tf_op jit(solution)/shard_map/prepare/pallas_call | solution.py:381
  14.5 1.8 %forward.2.refs_4_ = f32[17,128,256]{2,1,0:T(8,128)S(1)} custom-call(s32[67]{0:T(128)S(1)} %get-tuple-element.41.order, bf16[1,256,256]{2,1,0:T(8,128)(2,1)S(1)} %bitcast.12, bf16[1,256,256]{2,1,0:T(8,128)(2,1)S(1)} %bitcast.14, bf16[6,256,256]{2,1,0:T(8,128)(2,1)S(1)} %get-tuple-element.39.refs_2_, ...), custom_call_target="tpu_custom_call", output_to_operand_aliasing={{}: (5, {})} | custom-call | flops 1073741824 | bytes 1048576 | tf_op jit(solution)/shard_map/forward/pallas_call | solution.py:403
  16.3 1.9 %collective-permute-done = bf16[256,256]{1,0:T(8,128)(2,1)S(1)} collective-permute-done((bf16[256,256]{1,0:T(8,128)(2,1)}, bf16[256,256]{1,0:T(8,128)(2,1)S(1)}, u32[]{:S(2)}, u32[]{:S(2)}) %collective-permute-start) | collective-permute-done | bytes 131104 | tf_op jit(solution)/shard_map/ppermute | solution.py:28
  18.2 1.5 %forward.3 = (f32[17,128,256]{2,1,0:T(8,128)S(1)}, f32[256,256]{1,0:T(8,128)S(1)}, f32[256,256]{1,0:T(8,128)S(1)}, f32[256,256]{1,0:T(8,128)S(1)}, f32[256,256]{...) custom-call(s32[67]{0:T(128)S(1)} %get-tuple-element.38.order, ...), custom_call_target="tpu_custom_call", output_to_operand_aliasing={{0}: (5, {})} | custom-call | flops 1073741824 | bytes 1048576 | tf_op jit(solution)/shard_map/forward/pallas_call | solution.py:403
  20.3 1.4 %collective-permute-done.4.refs_1_ = bf16[256,256]{1,0:T(8,128)(2,1)S(1)} collective-permute-done((bf16[256,256]{1,0:T(8,128)(2,1)S(1)}, bf16[256,256]{1,0:T(8,128)(2,1)S(1)}, u32[]{:S(2)}, u32[]{:S(2)}) %collective-permute-start.4) | collective-permute-done | bytes 131104 | tf_op jit(solution)/shard_map/ppermute | solution.py:28
  21.8 2.5 %collective-permute-start.5 = (bf16[256,256]{1,0:T(8,128)(2,1)S(1)}, bf16[256,256]{1,0:T(8,128)(2,1)S(1)}, u32[]{:S(2)}, u32[]{:S(2)}) collective-permute-start(bf16[256,256]{1,0:T(8,128)(2,1)S(1)} %sum.7), channel_id=1, source_target_pairs={{0,6},{2,4},{4,2},{6,0},{1,7},{3,5},{5,3},{7,1},{8,14},{10,12},{12... | collective-permute-start | bytes 393224 | tf_op jit(solution)/shard_map/ppermute | solution.py:28
  26.1 2.5 %collective-permute-done.5.first = bf16[256,256]{1,0:T(8,128)(2,1)S(1)} collective-permute-done((bf16[256,256]{1,0:T(8,128)(2,1)S(1)}, bf16[256,256]{1,0:T(8,128)(2,1)S(1)}, u32[]{:S(2)}, u32[]{:S(2)}) %collective-permute-start.5) | collective-permute-done | bytes 131104 | tf_op jit(solution)/shard_map/ppermute | solution.py:28
  28.6 2.5 %collective-permute-done.6.second = bf16[256,256]{1,0:T(8,128)(2,1)S(1)} collective-permute-done((bf16[256,256]{1,0:T(8,128)(2,1)S(1)}, bf16[256,256]{1,0:T(8,128)(2,1)S(1)}, u32[]{:S(2)}, u32[]{:S(2)}) %collective-permute-start.6) | collective-permute-done | bytes 131104 | tf_op jit(solution)/shard_map/ppermute | solution.py:28
  31.8 1.5 %collective-permute-start.10 = (bf16[256,256]{1,0:T(8,128)(2,1)S(1)}, bf16[256,256]{1,0:T(8,128)(2,1)S(1)}, u32[]{:S(2)}, u32[]{:S(2)}) collective-permute-start(bf16[256,256]{1,0:T(8,128)(2,1)S(1)} %grad.1.refs_0_), channel_id=1, source_target_pairs={{0,6},{2,4},{4,2},{6,0},{1,7},{3,5},{5,3},{7,1},{8,14},{10,12},{12... | collective-permute-start | bytes 393224 | tf_op jit(solution)/shard_map/ppermute | solution.py:28
  33.3 1.4 %collective-permute-start.9 = (bf16[256,256]{1,0:T(8,128)(2,1)S(1)}, bf16[256,256]{1,0:T(8,128)(2,1)S(1)}, u32[]{:S(2)}, u32[]{:S(2)}) collective-permute-start(bf16[256,256]{1,0:T(8,128)(2,1)S(1)} %grad.1.refs_0_), channel_id=1, source_target_pairs={{0,4},{2,6},{4,0},{6,2},{1,5},{3,7},{5,1},{7,3},{8,12},{10,14},{12... | collective-permute-start | bytes 393224 | tf_op jit(solution)/shard_map/ppermute | solution.py:28
  35.4 3.6 %collective-permute-done.10.refs_3_ = bf16[256,256]{1,0:T(8,128)(2,1)S(1)} collective-permute-done((bf16[256,256]{1,0:T(8,128)(2,1)S(1)}, bf16[256,256]{1,0:T(8,128)(2,1)S(1)}, u32[]{:S(2)}, u32[]{:S(2)}) %collective-permute-start.10) | collective-permute-done | bytes 131104 | tf_op jit(solution)/shard_map/ppermute | solution.py:28
  38.9 1.5 %collective-permute-done.9.refs_2_ = bf16[256,256]{1,0:T(8,128)(2,1)S(1)} collective-permute-done((bf16[256,256]{1,0:T(8,128)(2,1)S(1)}, bf16[256,256]{1,0:T(8,128)(2,1)S(1)}, u32[]{:S(2)}, u32[]{:S(2)}) %collective-permute-start.9) | collective-permute-done | bytes 131104 | tf_op jit(solution)/shard_map/ppermute | solution.py:28
  42.4 1.8 %weight_terms.3 = (f32[3,64,256]{2,1,0:T(8,128)S(1)}, bf16[3,64,256]{2,1,0:T(8,128)(2,1)S(1)}, bf16[3,64,256]{2,1,0:T(8,128)(2,1)S(1)}, bf16[3,64,256]{2,1,0:T(8,128)(2,1)S(1)}, f32[13,128,256]{2,1,0:T(8,128)S(1)}) custom-call(s32[65]{0:T(128)S(1)} %get-tuple-element.68.listed, ...), custom_call_target="tpu_custom_call", output_to_operand_aliasing={{4}: (4, {})} | custom-call | tf_op jit(solution)/shard_map/weight_terms/pallas_call | solution.py:481
  45.3 2.1 %collective-permute-start.24 = (bf16[3,64,256]{2,1,0:T(8,128)(2,1)S(1)}, bf16[3,64,256]{2,1,0:T(8,128)(2,1)S(1)}, u32[]{:S(2)}, u32[]{:S(2)}) collective-permute-start(bf16[3,64,256]{2,1,0:T(8,128)(2,1)S(1)} %get-tuple-element.72), channel_id=1, source_target_pairs={{0,4},{2,6},{4,0},{6,2},{1,5},{3,7},{5,1},{7,3},{8,12},{10,14},{12... | collective-permute-start | bytes 294920 | tf_op jit(solution)/shard_map/ppermute | solution.py:28
  47.8 1.4 %weight_terms.2 = (f32[3,64,256]{2,1,0:T(8,128)S(1)}, bf16[3,64,256]{2,1,0:T(8,128)(2,1)S(1)}, bf16[3,64,256]{2,1,0:T(8,128)(2,1)S(1)}, bf16[3,64,256]{2,1,0:T(8,128)(2,1)S(1)}, f32[13,128,256]{2,1,0:T(8,128)S(1)}) custom-call(s32[65]{0:T(128)S(1)} %get-tuple-element.60.listed, ...), custom_call_target="tpu_custom_call", output_to_operand_aliasing={{4}: (4, {})} | custom-call | tf_op jit(solution)/shard_map/weight_terms/pallas_call | solution.py:481
  50.4 2.4 %collective-permute-start.16 = (bf16[3,64,256]{2,1,0:T(8,128)(2,1)S(1)}, bf16[3,64,256]{2,1,0:T(8,128)(2,1)S(1)}, u32[]{:S(2)}, u32[]{:S(2)}) collective-permute-start(bf16[3,64,256]{2,1,0:T(8,128)(2,1)S(1)} %get-tuple-element.66), channel_id=1, source_target_pairs={{0,4},{2,6},{4,0},{6,2},{1,5},{3,7},{5,1},{7,3},{8,12},{10,14},{12... | collective-permute-start | bytes 294920 | tf_op jit(solution)/shard_map/ppermute | solution.py:28
  57.6 2.2 %collective-permute-done.26.refs_1_ = bf16[3,64,256]{2,1,0:T(8,128)(2,1)S(1)} collective-permute-done((bf16[3,64,256]{2,1,0:T(8,128)(2,1)S(1)}, bf16[3,64,256]{2,1,0:T(8,128)(2,1)S(1)}, u32[]{:S(2)}, u32[]{:S(2)}) %collective-permute-start.26) | collective-permute-done | bytes 98336 | tf_op jit(solution)/shard_map/ppermute | solution.py:28
  59.8 3.0 %collective-permute-done.18.refs_1_ = bf16[3,64,256]{2,1,0:T(8,128)(2,1)S(1)} collective-permute-done((bf16[3,64,256]{2,1,0:T(8,128)(2,1)S(1)}, bf16[3,64,256]{2,1,0:T(8,128)(2,1)S(1)}, u32[]{:S(2)}, u32[]{:S(2)}) %collective-permute-start.18) | collective-permute-done | bytes 98336 | tf_op jit(solution)/shard_map/ppermute | solution.py:28
  64.8 1.7 %collective-permute-start.30 = (bf16[3,64,256]{2,1,0:T(8,128)(2,1)S(1)}, bf16[3,64,256]{2,1,0:T(8,128)(2,1)S(1)}, u32[]{:S(2)}, u32[]{:S(2)}) collective-permute-start(bf16[3,64,256]{2,1,0:T(8,128)(2,1)S(1)} %sum.13.refs_0_), channel_id=1, source_target_pairs={{0,6},{2,4},{4,2},{6,0},{1,7},{3,5},{5,3},{7,1},{8,14},{10,12},{12... | collective-permute-start | bytes 294920 | tf_op jit(solution)/shard_map/ppermute | solution.py:28
  68.8 1.5 %collective-permute-start.22 = (bf16[3,64,256]{2,1,0:T(8,128)(2,1)S(1)}, bf16[3,64,256]{2,1,0:T(8,128)(2,1)S(1)}, u32[]{:S(2)}, u32[]{:S(2)}) collective-permute-start(bf16[3,64,256]{2,1,0:T(8,128)(2,1)S(1)} %sum.10.refs_0_), channel_id=1, source_target_pairs={{0,6},{2,4},{4,2},{6,0},{1,7},{3,5},{5,3},{7,1},{8,14},{10,12},{12... | collective-permute-start | bytes 294920 | tf_op jit(solution)/shard_map/ppermute | solution.py:28
  70.3 1.4 %collective-permute-start.21 = (bf16[3,64,256]{2,1,0:T(8,128)(2,1)S(1)}, bf16[3,64,256]{2,1,0:T(8,128)(2,1)S(1)}, u32[]{:S(2)}, u32[]{:S(2)}) collective-permute-start(bf16[3,64,256]{2,1,0:T(8,128)(2,1)S(1)} %sum.10.refs_0_), channel_id=1, source_target_pairs={{0,4},{2,6},{4,0},{6,2},{1,5},{3,7},{5,1},{7,3},{8,12},{10,14},{12... | collective-permute-start | bytes 294920 | tf_op jit(solution)/shard_map/ppermute | solution.py:28
  (68 shorter events, 25.5 us)
Async XLA Ops:
  0.6 13.8 %collective-permute-start.2 = (bf16[256,256]{1,0:T(8,128)(2,1)}, bf16[256,256]{1,0:T(8,128)(2,1)S(1)}, u32[]{:S(2)}, u32[]{:S(2)}) collective-permute-start(bf16[256,256]{1,0:T(8,128)(2,1)} %param.7), channel_id=1, source_target_pairs={{0,8},{8,0},{16,24},{24,16},{1,9},{9,1},{17,25},{25,17},{2,10},{10... | collective-permute-start | bytes 393224 | tf_op jit(solution)/shard_map/ppermute | solution.py:28
  3.7 12.6 %collective-permute-start.1 = (bf16[256,256]{1,0:T(8,128)(2,1)}, bf16[256,256]{1,0:T(8,128)(2,1)S(1)}, u32[]{:S(2)}, u32[]{:S(2)}) collective-permute-start(bf16[256,256]{1,0:T(8,128)(2,1)} %param.7), channel_id=1, source_target_pairs={{0,24},{8,16},{16,8},{24,0},{1,25},{9,17},{17,9},{25,1},{2,26},{10... | collective-permute-start | bytes 393224 | tf_op jit(solution)/shard_map/ppermute | solution.py:28
  6.2 12.0 %collective-permute-start = (bf16[256,256]{1,0:T(8,128)(2,1)}, bf16[256,256]{1,0:T(8,128)(2,1)S(1)}, u32[]{:S(2)}, u32[]{:S(2)}) collective-permute-start(bf16[256,256]{1,0:T(8,128)(2,1)} %param.7), channel_id=1, source_target_pairs={{0,16},{8,24},{16,0},{24,8},{1,17},{9,25},{17,1},{25,9},{2,18},{10... | collective-permute-start | bytes 393224 | tf_op jit(solution)/shard_map/ppermute | solution.py:28
  21.8 6.8 %collective-permute-start.5 = (bf16[256,256]{1,0:T(8,128)(2,1)S(1)}, bf16[256,256]{1,0:T(8,128)(2,1)S(1)}, u32[]{:S(2)}, u32[]{:S(2)}) collective-permute-start(bf16[256,256]{1,0:T(8,128)(2,1)S(1)} %sum.7), channel_id=1, source_target_pairs={{0,6},{2,4},{4,2},{6,0},{1,7},{3,5},{5,3},{7,1},{8,14},{10,12},{12... | collective-permute-start | bytes 393224 | tf_op jit(solution)/shard_map/ppermute | solution.py:28
  24.3 6.8 %collective-permute-start.6 = (bf16[256,256]{1,0:T(8,128)(2,1)S(1)}, bf16[256,256]{1,0:T(8,128)(2,1)S(1)}, u32[]{:S(2)}, u32[]{:S(2)}) collective-permute-start(bf16[256,256]{1,0:T(8,128)(2,1)S(1)} %get-tuple-element.54), channel_id=1, source_target_pairs={{0,4},{2,6},{4,0},{6,2},{1,5},{3,7},{5,1},{7,3},{8,12},{10,14},{12... | collective-permute-start | bytes 393224 | tf_op jit(solution)/shard_map/ppermute | solution.py:28
  25.3 6.4 %collective-permute-start.7 = (bf16[256,256]{1,0:T(8,128)(2,1)S(1)}, bf16[256,256]{1,0:T(8,128)(2,1)S(1)}, u32[]{:S(2)}, u32[]{:S(2)}) collective-permute-start(bf16[256,256]{1,0:T(8,128)(2,1)S(1)} %get-tuple-element.55), channel_id=1, source_target_pairs={{0,2},{2,0},{4,6},{6,4},{1,3},{3,1},{5,7},{7,5},{8,10},{10,8},{12,... | collective-permute-start | bytes 393224 | tf_op jit(solution)/shard_map/ppermute | solution.py:28
  31.8 7.1 %collective-permute-start.10 = (bf16[256,256]{1,0:T(8,128)(2,1)S(1)}, bf16[256,256]{1,0:T(8,128)(2,1)S(1)}, u32[]{:S(2)}, u32[]{:S(2)}) collective-permute-start(bf16[256,256]{1,0:T(8,128)(2,1)S(1)} %grad.1.refs_0_), channel_id=1, source_target_pairs={{0,6},{2,4},{4,2},{6,0},{1,7},{3,5},{5,3},{7,1},{8,14},{10,12},{12... | collective-permute-start | bytes 393224 | tf_op jit(solution)/shard_map/ppermute | solution.py:28
  33.3 7.1 %collective-permute-start.9 = (bf16[256,256]{1,0:T(8,128)(2,1)S(1)}, bf16[256,256]{1,0:T(8,128)(2,1)S(1)}, u32[]{:S(2)}, u32[]{:S(2)}) collective-permute-start(bf16[256,256]{1,0:T(8,128)(2,1)S(1)} %grad.1.refs_0_), channel_id=1, source_target_pairs={{0,4},{2,6},{4,0},{6,2},{1,5},{3,7},{5,1},{7,3},{8,12},{10,14},{12... | collective-permute-start | bytes 393224 | tf_op jit(solution)/shard_map/ppermute | solution.py:28
  34.8 6.2 %collective-permute-start.8 = (bf16[256,256]{1,0:T(8,128)(2,1)S(1)}, bf16[256,256]{1,0:T(8,128)(2,1)S(1)}, u32[]{:S(2)}, u32[]{:S(2)}) collective-permute-start(bf16[256,256]{1,0:T(8,128)(2,1)S(1)} %grad.1.refs_0_), channel_id=1, source_target_pairs={{0,2},{2,0},{4,6},{6,4},{1,3},{3,1},{5,7},{7,5},{8,10},{10,8},{12,... | collective-permute-start | bytes 393224 | tf_op jit(solution)/shard_map/ppermute | solution.py:28
  35.4 5.6 %collective-permute-start.11 = (bf16[256,256]{1,0:T(8,128)(2,1)S(1)}, bf16[256,256]{1,0:T(8,128)(2,1)S(1)}, u32[]{:S(2)}, u32[]{:S(2)}) collective-permute-start(bf16[256,256]{1,0:T(8,128)(2,1)S(1)} %grad.1.refs_0_), channel_id=1, source_target_pairs={{0,1},{1,0},{2,3},{3,2},{4,5},{5,4},{6,7},{7,6},{8,9},{9,8},{10,11... | collective-permute-start | bytes 393224 | tf_op jit(solution)/shard_map/ppermute | solution.py:28
  44.3 8.5 %collective-permute-start.23 = (bf16[3,64,256]{2,1,0:T(8,128)(2,1)S(1)}, bf16[3,64,256]{2,1,0:T(8,128)(2,1)S(1)}, u32[]{:S(2)}, u32[]{:S(2)}) collective-permute-start(bf16[3,64,256]{2,1,0:T(8,128)(2,1)S(1)} %get-tuple-element.71), channel_id=1, source_target_pairs={{0,6},{2,4},{4,2},{6,0},{1,7},{3,5},{5,3},{7,1},{8,14},{10,12},{12... | collective-permute-start | bytes 294920 | tf_op jit(solution)/shard_map/ppermute | solution.py:28
  45.3 8.0 %collective-permute-start.24 = (bf16[3,64,256]{2,1,0:T(8,128)(2,1)S(1)}, bf16[3,64,256]{2,1,0:T(8,128)(2,1)S(1)}, u32[]{:S(2)}, u32[]{:S(2)}) collective-permute-start(bf16[3,64,256]{2,1,0:T(8,128)(2,1)S(1)} %get-tuple-element.72), channel_id=1, source_target_pairs={{0,4},{2,6},{4,0},{6,2},{1,5},{3,7},{5,1},{7,3},{8,12},{10,14},{12... | collective-permute-start | bytes 294920 | tf_op jit(solution)/shard_map/ppermute | solution.py:28
  47.4 5.9 %collective-permute-start.25 = (bf16[3,64,256]{2,1,0:T(8,128)(2,1)S(1)}, bf16[3,64,256]{2,1,0:T(8,128)(2,1)S(1)}, u32[]{:S(2)}, u32[]{:S(2)}) collective-permute-start(bf16[3,64,256]{2,1,0:T(8,128)(2,1)S(1)} %get-tuple-element.73), channel_id=1, source_target_pairs={{0,2},{2,0},{4,6},{6,4},{1,3},{3,1},{5,7},{7,5},{8,10},{10,8},{12,... | collective-permute-start | bytes 294920 | tf_op jit(solution)/shard_map/ppermute | solution.py:28
  49.2 6.4 %collective-permute-start.15 = (bf16[3,64,256]{2,1,0:T(8,128)(2,1)S(1)}, bf16[3,64,256]{2,1,0:T(8,128)(2,1)S(1)}, u32[]{:S(2)}, u32[]{:S(2)}) collective-permute-start(bf16[3,64,256]{2,1,0:T(8,128)(2,1)S(1)} %get-tuple-element.65), channel_id=1, source_target_pairs={{0,6},{2,4},{4,2},{6,0},{1,7},{3,5},{5,3},{7,1},{8,14},{10,12},{12... | collective-permute-start | bytes 294920 | tf_op jit(solution)/shard_map/ppermute | solution.py:28
  50.4 6.0 %collective-permute-start.16 = (bf16[3,64,256]{2,1,0:T(8,128)(2,1)S(1)}, bf16[3,64,256]{2,1,0:T(8,128)(2,1)S(1)}, u32[]{:S(2)}, u32[]{:S(2)}) collective-permute-start(bf16[3,64,256]{2,1,0:T(8,128)(2,1)S(1)} %get-tuple-element.66), channel_id=1, source_target_pairs={{0,4},{2,6},{4,0},{6,2},{1,5},{3,7},{5,1},{7,3},{8,12},{10,14},{12... | collective-permute-start | bytes 294920 | tf_op jit(solution)/shard_map/ppermute | solution.py:28
  53.4 6.4 %collective-permute-start.26 = (bf16[3,64,256]{2,1,0:T(8,128)(2,1)S(1)}, bf16[3,64,256]{2,1,0:T(8,128)(2,1)S(1)}, u32[]{:S(2)}, u32[]{:S(2)}) collective-permute-start(bf16[3,64,256]{2,1,0:T(8,128)(2,1)S(1)} %sum.11.refs_0_), channel_id=1, source_target_pairs={{0,16},{8,24},{16,0},{24,8},{1,17},{9,25},{17,1},{25,9},{2,18},{10... | collective-permute-start | bytes 294920 | tf_op jit(solution)/shard_map/ppermute | solution.py:28
  57.5 5.4 %collective-permute-start.18 = (bf16[3,64,256]{2,1,0:T(8,128)(2,1)S(1)}, bf16[3,64,256]{2,1,0:T(8,128)(2,1)S(1)}, u32[]{:S(2)}, u32[]{:S(2)}) collective-permute-start(bf16[3,64,256]{2,1,0:T(8,128)(2,1)S(1)} %sum.8.refs_0_), channel_id=1, source_target_pairs={{0,8},{8,0},{16,24},{24,16},{1,9},{9,1},{17,25},{25,17},{2,10},{10... | collective-permute-start | bytes 294920 | tf_op jit(solution)/shard_map/ppermute | solution.py:28
  59.7 5.0 %collective-permute-start.27 = (bf16[3,64,256]{2,1,0:T(8,128)(2,1)S(1)}, bf16[3,64,256]{2,1,0:T(8,128)(2,1)S(1)}, u32[]{:S(2)}, u32[]{:S(2)}) collective-permute-start(bf16[3,64,256]{2,1,0:T(8,128)(2,1)S(1)} %sum.12.refs_0_), channel_id=1, source_target_pairs={{0,8},{8,0},{16,24},{24,16},{1,9},{9,1},{17,25},{25,17},{2,10},{10... | collective-permute-start | bytes 294920 | tf_op jit(solution)/shard_map/ppermute | solution.py:28
  62.9 5.9 %collective-permute-start.19 = (bf16[3,64,256]{2,1,0:T(8,128)(2,1)S(1)}, bf16[3,64,256]{2,1,0:T(8,128)(2,1)S(1)}, u32[]{:S(2)}, u32[]{:S(2)}) collective-permute-start(bf16[3,64,256]{2,1,0:T(8,128)(2,1)S(1)} %sum.9.refs_0_), channel_id=1, source_target_pairs={{0,16},{8,24},{16,0},{24,8},{1,17},{9,25},{17,1},{25,9},{2,18},{10... | collective-permute-start | bytes 294920 | tf_op jit(solution)/shard_map/ppermute | solution.py:28
  64.8 6.9 %collective-permute-start.30 = (bf16[3,64,256]{2,1,0:T(8,128)(2,1)S(1)}, bf16[3,64,256]{2,1,0:T(8,128)(2,1)S(1)}, u32[]{:S(2)}, u32[]{:S(2)}) collective-permute-start(bf16[3,64,256]{2,1,0:T(8,128)(2,1)S(1)} %sum.13.refs_0_), channel_id=1, source_target_pairs={{0,6},{2,4},{4,2},{6,0},{1,7},{3,5},{5,3},{7,1},{8,14},{10,12},{12... | collective-permute-start | bytes 294920 | tf_op jit(solution)/shard_map/ppermute | solution.py:28
  66.5 7.0 %collective-permute-start.29 = (bf16[3,64,256]{2,1,0:T(8,128)(2,1)S(1)}, bf16[3,64,256]{2,1,0:T(8,128)(2,1)S(1)}, u32[]{:S(2)}, u32[]{:S(2)}) collective-permute-start(bf16[3,64,256]{2,1,0:T(8,128)(2,1)S(1)} %sum.13.refs_0_), channel_id=1, source_target_pairs={{0,4},{2,6},{4,0},{6,2},{1,5},{3,7},{5,1},{7,3},{8,12},{10,14},{12... | collective-permute-start | bytes 294920 | tf_op jit(solution)/shard_map/ppermute | solution.py:28
  67.8 5.8 %collective-permute-start.28 = (bf16[3,64,256]{2,1,0:T(8,128)(2,1)S(1)}, bf16[3,64,256]{2,1,0:T(8,128)(2,1)S(1)}, u32[]{:S(2)}, u32[]{:S(2)}) collective-permute-start(bf16[3,64,256]{2,1,0:T(8,128)(2,1)S(1)} %sum.13.refs_0_), channel_id=1, source_target_pairs={{0,2},{2,0},{4,6},{6,4},{1,3},{3,1},{5,7},{7,5},{8,10},{10,8},{12,... | collective-permute-start | bytes 294920 | tf_op jit(solution)/shard_map/ppermute | solution.py:28
  68.8 6.0 %collective-permute-start.22 = (bf16[3,64,256]{2,1,0:T(8,128)(2,1)S(1)}, bf16[3,64,256]{2,1,0:T(8,128)(2,1)S(1)}, u32[]{:S(2)}, u32[]{:S(2)}) collective-permute-start(bf16[3,64,256]{2,1,0:T(8,128)(2,1)S(1)} %sum.10.refs_0_), channel_id=1, source_target_pairs={{0,6},{2,4},{4,2},{6,0},{1,7},{3,5},{5,3},{7,1},{8,14},{10,12},{12... | collective-permute-start | bytes 294920 | tf_op jit(solution)/shard_map/ppermute | solution.py:28
  70.3 5.4 %collective-permute-start.21 = (bf16[3,64,256]{2,1,0:T(8,128)(2,1)S(1)}, bf16[3,64,256]{2,1,0:T(8,128)(2,1)S(1)}, u32[]{:S(2)}, u32[]{:S(2)}) collective-permute-start(bf16[3,64,256]{2,1,0:T(8,128)(2,1)S(1)} %sum.10.refs_0_), channel_id=1, source_target_pairs={{0,4},{2,6},{4,0},{6,2},{1,5},{3,7},{5,1},{7,3},{8,12},{10,14},{12... | collective-permute-start | bytes 294920 | tf_op jit(solution)/shard_map/ppermute | solution.py:28
  (12 other events, 36.7 us)

commit v5 on v4

--- a/solution.py
+++ b/solution.py
@@ -60,36 +60,32 @@
     return halo_refs[i // per_call][i % per_call, rows, :]
 
 
-def prepare_kernel(masked, combine, slot_bounds, bounds, targets, chosen, table, count, *refs):
-    values, weight, values_here, weight_here, values_turned = refs[:5]
-    by_slot = refs[5 : 4 + len(slot_bounds)]
-    by_relation = refs[4 + len(slot_bounds) : 3 + len(slot_bounds) + len(bounds)]
-    zeros, sems = refs[3 + len(slot_bounds) + len(bounds) : -1], refs[-1]
+def prepare_kernel(masked, owners, groups, bounds, targets, chosen, table, count, *refs):
+    values, weight, values_here, weight_here = refs[:4]
+    by_slot, refs = refs[4 : 4 + len(groups)], refs[4 + len(groups) :]
+    by_relation, (pre, sems) = refs[: len(bounds) - 1], refs[len(bounds) - 1 :]
     entries, relations = values.shape[0], weight.shape[0]
-    parts = sems.shape[0] - 1
-    batch = entries // parts
     copies = [
-        pltpu.make_async_copy(
-            values.at[pl.ds(i * batch, batch)], values_here.at[pl.ds(i * batch, batch)], sems.at[i]
-        )
-        for i in range(parts)
+        pltpu.make_async_copy(values, values_here, sems.at[0]),
+        pltpu.make_async_copy(weight, weight_here, sems.at[1]),
     ]
-    copies.append(pltpu.make_async_copy(weight, weight_here, sems.at[parts]))
     for copy in copies:
         copy.start()
-    for each in zeros:
-        each[...] = jnp.zeros_like(each)
+    pre[...] = jnp.zeros_like(pre)
     places = here()
-    slots = slot_bounds[-1]
+    cores, per_owner = owners
+    slots = groups[-1][1]
 
     def put(e, found):
         target, relation = table[0, e], table[2, e]
         slot = slot_of(places, table[1, e], masked)
+        own = (target >> (per_owner.bit_length() - 1)) & (cores - 1) == places[2]
         now = []
-        for listed, low, high in zip(by_slot, slot_bounds, slot_bounds[1:]):
+        for listed, (low, high, side) in zip(by_slot, groups):
             place = (slot - low) * relations + relation
             listed[found[len(now)]] = packed(entries, targets, e, target, place)
-            now.append((slot >= low) & (slot < high))
+            inside = (slot >= low) & (slot < high)
+            now.append(inside if side is None else inside & (own == side))
         for listed, low, high in zip(by_relation, bounds, bounds[1:]):
             place = (relation - low) * slots + slot
             listed[found[len(now)]] = packed(entries, targets, e, target, place)
@@ -100,32 +96,44 @@
     found = lax.fori_loop(0, count[0], put, (jnp.int32(0),) * len(lists))
     for listed, number in zip(lists, found):
         listed[entries] = number
-    for listed, low, high in zip(by_slot, slot_bounds, slot_bounds[1:]):
+    for listed, (low, high, _) in zip(by_slot, groups):
         for i in range(low, high):
             listed[entries + 1 + i - low] = chosen[slot_of(places, i, masked)]
 
-    for i, copy in enumerate(copies):
+    for copy in copies:
         copy.wait()
-        if i < parts:
-
-            def turn(j, carry):
-                values_turned[i * batch + 2 * j] = values_here[i * batch + 2 * j].T
-                values_turned[i * batch + 2 * j + 1] = values_here[i * batch + 2 * j + 1].T
-                return carry
-
-            lax.fori_loop(0, batch // 2, turn, 0, unroll=4)
-
-
-def forward_kernel(tile, combine, halo_count, last, order, *refs):
-    halo_refs, refs = refs[:halo_count], refs[halo_count:]
-    weight, values, pre, outs, projected = refs[0], refs[1], refs[3], refs[4:-1], refs[-1]
+
+
+def near_kernel(tile, combine, order, *refs):
+    *halo_refs, weight, values, before, pre, projected = refs
     entries = values.shape[0]
-    slots = halo_count * halo_refs[0].shape[0]
-    firsts = [order[entries + 1 + i] for i in range(slots)]
+    firsts = [order[entries + 1 + i] for i in range(order.shape[0] - entries - 1)]
     project(tile, combine, firsts, halo_refs, weight, projected)
     add_entries(combine, values, weight, projected, order, order[entries], pre)
-    if last:
-        hand_out(tile, here(), pre, outs)
+
+
+def theirs_kernel(tile, combine, owners, first, order, *refs):
+    near_kernel(tile, combine, order, *refs[:-2])
+    pre, sends = refs[-4], refs[-2:]
+    panels = sends[1].shape[0] + 1
+    others = [m for m in range(panels) if m != first]
+    for out, distance in ((sends[0], first), *((sends[1].at[i], m) for i, m in enumerate(others))):
+        for rows, block in blocks_of(tile, owners, here(), distance, 1):
+            out[rows, :] = pre[block].astype(BF16)
+
+
+def ours_kernel(tile, combine, owners, order, projected, weight, values, before, pre, *keeps):
+    del before
+    add_entries(combine, values, weight, projected, order, order[values.shape[0]], pre)
+    for distance, keep in enumerate(keeps):
+        for rows, block in blocks_of(tile, owners, here(), distance, 0):
+            keep[rows, :] = pre[block]
+
+
+def blocks_of(tile, owners, places, distance, other):
+    cores, per_owner = owners
+    owner = (places[1] ^ distance) * cores + (places[2] ^ other)
+    return [(pl.ds(i * tile, tile), owner * per_owner + i) for i in range(per_owner)]
 
 
 def project(tile, combine, firsts, halo_refs, weight, projected):
@@ -165,23 +173,6 @@
     for_entries(total, body)
 
 
-def hand_out(tile, places, pre, outs):
-    keeps, sends = outs[:-2], outs[-2:]
-    panels, per_owner = len(keeps), keeps[0].shape[0] // tile
-    groups = (pre.shape[0] - 1) // (panels * per_owner)
-    for distance in reversed(range(panels)):
-        panel = places[1] ^ distance
-        for part in range(per_owner):
-            rows = pl.ds(part * tile, tile)
-            mine = (panel * groups + places[2]) * per_owner + part
-            other = (panel * groups + (places[2] ^ 1)) * per_owner + part
-            if distance == panels - 1:
-                sends[0][rows, :] = pre[other].astype(BF16)
-            else:
-                sends[1][distance, rows, :] = pre[other].astype(BF16)
-            keeps[distance][rows, :] = pre[mine]
-
-
 def chip_kernel(*refs):
     count = (len(refs) - 1) // 2
     keeps, arrived, outs = refs[:count], refs[count], refs[count + 1 :]
@@ -194,9 +185,12 @@
     grad[...] = (cotangent[...].astype(F32) * silu_slope(pre)).astype(BF16)
 
 
-def turn_kernel(masked, tile, panels, chosen, *refs):
-    halo_refs, halo_turned, scratch = refs[:-2], refs[-2], refs[-1]
+def turn_kernel(masked, tile, panels, halo_count, chosen, values, *refs):
+    halo_refs, refs = refs[:halo_count], refs[halo_count:]
+    values_turned, halo_turned, zeros, scratch = refs[0], refs[1], refs[2:-1], refs[-1]
     places = here()
+    for each in zeros:
+        each[...] = jnp.zeros_like(each)
     share = scratch.shape[0] // panels
     for slot in range(len(halo_refs) * halo_refs[0].shape[0]):
         block = halo_block(chosen[slot_of(places, slot, masked)], halo_refs, slot, tile)
@@ -206,6 +200,15 @@
             halo_turned[pl.ds(m * share, share), pl.ds(slot * tile, tile)] = (
                 scratch[pl.ds(start, share), :].astype(BF16)
             )
+
+    batch = 8
+
+    def step(i, carry):
+        for u in range(batch):
+            values_turned[i * batch + u] = values[i * batch + u].T
+        return carry
+
+    lax.fori_loop(0, values.shape[0] // batch, step, 0)
 
 
 def collect_kernel(tile, *refs):
@@ -351,10 +354,6 @@
 
     panel_f32 = jax.ShapeDtypeStruct((own_rows, features), F32)
     panel_bf16 = jax.ShapeDtypeStruct((own_rows, features), BF16)
-    kept = (panel_f32,) * panels + (
-        panel_bf16,
-        jax.ShapeDtypeStruct((panels - 1, own_rows, features), BF16),
-    )
     pre_sums = jax.ShapeDtypeStruct((targets + 1, tile, features), F32)
     if direct:
         halo = [h[None] for h in gather(source_feats, "dom")]
@@ -363,7 +362,9 @@
     slots = sum(h.shape[0] for h in halo)
     combine = slots * relations <= entries
     near = partitions // 2
-    slot_bounds = (0, near, slots) if direct else (0, slots)
+    owners = groups, own_rows // tile
+    start = near if direct else 0
+    slot_groups = ((0, near, None),) * direct + ((start, slots, False), (start, slots, True))
     sums = [
         jax.ShapeDtypeStruct(
             ((high - low) * slots + 1, tile, features)
@@ -375,76 +376,88 @@
     ]
     listings = [
         jax.ShapeDtypeStruct((entries + 1 + high - low,), I32)
-        for low, high in zip(slot_bounds, slot_bounds[1:])
+        for low, high, _ in slot_groups
     ] + [jax.ShapeDtypeStruct((entries + 1,), I32)] * chunks
-    held = [jax.ShapeDtypeStruct(v.shape, BF16) for v in (values, rel_weight, values)]
-    values, rel_weight, values_turned, *others = pl.pallas_call(
-        functools.partial(prepare_kernel, direct, combine, slot_bounds, bounds, targets),
-        out_shape=(*held, *listings, pre_sums, *sums),
+    held = [jax.ShapeDtypeStruct(v.shape, BF16) for v in (values, rel_weight)]
+    values, rel_weight, *listings, pre = pl.pallas_call(
+        functools.partial(prepare_kernel, direct, owners, slot_groups, bounds, targets),
+        out_shape=(*held, *listings, pre_sums),
         in_specs=[SCALARS] * 3 + [ANYWHERE] * 2,
-        out_specs=(WHOLE,) * 3 + (SCALARS,) * len(listings) + (WHOLE,) * (1 + chunks),
-        scratch_shapes=[pltpu.SemaphoreType.DMA((5,))],
-        compiler_params=vmem_for(*held, pre_sums, *sums),
+        out_specs=(WHOLE,) * 2 + (SCALARS,) * len(listings) + (WHOLE,),
+        scratch_shapes=[pltpu.SemaphoreType.DMA((2,))],
+        compiler_params=vmem_for(*held, pre_sums),
         cost_estimate=pl.CostEstimate(
-            flops=0, bytes_accessed=6 * values.size, transcendentals=0
+            flops=0, bytes_accessed=4 * values.size, transcendentals=0
         ),
         name="prepare",
     )(chosen, table, count, values, rel_weight)
-    listings, pre, sums_in = others[: len(listings)], others[len(listings)], others[-chunks:]
     lists = listings[-chunks:]
 
-    for call, (low, high) in enumerate(zip(slot_bounds, slot_bounds[1:])):
-        last = high == slots
+    first = 1 if panels > 1 else 0
+    sends = (panel_bf16, jax.ShapeDtypeStruct((panels - 1, own_rows, features), BF16))
+    cost = pl.CostEstimate(
+        flops=4 * entries * tile * tile * features, bytes_accessed=values.size, transcendentals=0
+    )
+    for call, (low, high, _) in enumerate(slot_groups[:-1]):
+        last = call == len(slot_groups) - 2
         blocks = halo[low:high] if direct else halo
         projected = jax.ShapeDtypeStruct(
             ((high - low) * (relations if combine else 1), tile, features), BF16
         )
-        outs = (pre_sums, *kept) if last else (pre_sums,)
+        kernel = functools.partial(near_kernel, tile, combine)
+        if last:
+            kernel = functools.partial(theirs_kernel, tile, combine, owners, first)
+        outs = (pre_sums, projected, *sends) if last else (pre_sums,)
         pre, *given = pl.pallas_call(
-            functools.partial(forward_kernel, tile, combine, len(blocks), last),
+            kernel,
             out_shape=outs,
             in_specs=[SCALARS] + [WHOLE] * (len(blocks) + 3),
             out_specs=(WHOLE,) * len(outs),
-            scratch_shapes=[pltpu.VMEM(projected.shape, BF16)],
+            scratch_shapes=[] if last else [pltpu.VMEM(projected.shape, BF16)],
             input_output_aliases={3 + len(blocks): 0},
             compiler_params=vmem_for(*outs, projected, *blocks, rel_weight, values),
-            cost_estimate=pl.CostEstimate(
-                flops=4 * entries * tile * tile * features,
-                bytes_accessed=values.size,
-                transcendentals=0,
-            ),
+            cost_estimate=cost,
             name="forward",
         )(listings[call], *blocks, rel_weight, values, pre)
-
-    *keeps, farthest, rest = given
-    farthest = summed([keeps[-1], swap(farthest, "rel", 1)])
-    nearer = (panel_f32,) + (panel_bf16,) * (panels - 2)
+    projected, *given = given
+    _, *keeps = pl.pallas_call(
+        functools.partial(ours_kernel, tile, combine, owners),
+        out_shape=(pre_sums,) + (panel_f32,) * panels,
+        in_specs=[SCALARS] + [WHOLE] * 4,
+        out_specs=(WHOLE,) * (1 + panels),
+        input_output_aliases={4: 0},
+        compiler_params=vmem_for(pre_sums, pre_sums, projected, rel_weight, values),
+        cost_estimate=cost,
+        name="forward_ours",
+    )(listings[len(slot_groups) - 1], projected, rel_weight, values, pre)
+    first_sum = summed([keeps[first], swap(given[0], "rel", 1)])
+    rest = [m for m in range(panels) if m != first]
+    rest_sums = (panel_f32,) + (panel_bf16,) * (panels - 2)
     leaving = pl.pallas_call(
         chip_kernel,
-        out_shape=nearer,
+        out_shape=rest_sums,
         in_specs=[WHOLE] * panels,
         out_specs=(WHOLE,) * (panels - 1),
-        compiler_params=vmem_for(*nearer, *keeps, rest),
+        compiler_params=vmem_for(*rest_sums, *keeps, sends[1]),
         name="chip",
-    )(*keeps[:-1], swap(rest, "rel", 1))
-    leaving = [*leaving, farthest]
+    )(*(keeps[m] for m in rest), swap(given[1], "rel", 1))
+    leaving = [leaving[0], first_sum, *leaving[1:]]
     leaving, chosen_then = lax.optimization_barrier((leaving, chosen))
     arrived = exchange(leaving, "src")
-    halo_turned = jax.ShapeDtypeStruct((features, slots * tile), BF16)
-    turned = (values, halo_turned)
-    halo_turned = pl.pallas_call(
-        functools.partial(turn_kernel, direct, tile, panels),
-        out_shape=halo_turned,
-        in_specs=[SCALARS] + [WHOLE] * len(halo),
-        out_specs=WHOLE,
+    turned = (held[0], jax.ShapeDtypeStruct((features, slots * tile), BF16))
+    prepared = pl.pallas_call(
+        functools.partial(turn_kernel, direct, tile, panels, len(halo)),
+        out_shape=(*turned, *sums),
+        in_specs=[SCALARS] + [WHOLE] * (1 + len(halo)),
+        out_specs=(WHOLE,) * (2 + chunks),
         scratch_shapes=[pltpu.VMEM((features, tile), F32)],
-        compiler_params=vmem_for(halo_turned, halo_turned, *halo),
+        compiler_params=vmem_for(*turned, *sums, values, *halo),
         cost_estimate=pl.CostEstimate(
-            flops=0, bytes_accessed=4 * halo_turned.size, transcendentals=0
+            flops=0, bytes_accessed=4 * values.size, transcendentals=0
         ),
         name="turn",
-    )(chosen_then, *halo)
-    arrived, halo_turned = lax.optimization_barrier((arrived, halo_turned))
+    )(chosen_then, values, *halo)
+    arrived, prepared = lax.optimization_barrier((arrived, prepared))
     block = jax.ShapeDtypeStruct((own_rows, features), BF16)
     if len(arrived) == 3:
         local_grad = pl.pallas_call(
@@ -486,7 +499,7 @@
             input_output_aliases={4: panels},
             compiler_params=vmem_for(*(own_share,) * panels, sums[c], by_target, *turned),
             name="weight_terms",
-        )(lists[c], values_turned, halo_turned, grads, sums_in[c])
+        )(lists[c], *prepared[:2], grads, prepared[2 + c])
         panel_sums.append(
             summed([shares[0]] + exchange(shares, "src"), BF16 if direct else F32)
         )

time: 77.6 us -> 77.6 us (level)
  Pallas kernels: 13.1 us -> 16.2 us
  starting transfers between devices: 30.3 us -> 28.5 us
  waiting for transfers between devices: 27.6 us -> 26.5 us
    pallas_call x5 -> x6, Pallas kernels: 7.57 us -> 9.84 us  [the longest x2 3.22 us: local(): pl.pallas_call(kernel, out_shape=outs, in_specs=[SCALARS] + [WHOLE] * (le...]
    ppermute x31, starting transfers between devices: 30.3 us -> 28.5 us  [swap(): return lax.ppermute(value, axis, partner_pairs(lax.axis_size(axis), mask))]
    ppermute x31, waiting for transfers between devices: 27.6 us -> 26.5 us  [swap(): return lax.ppermute(value, axis, partner_pairs(lax.axis_size(axis), mask))]
    pallas_call x2, Pallas kernels: 3.23 us -> 4.05 us  [local(): pl.pallas_call(functools.partial(weight_kernel, tile, combine), out_shape...]
    unnamed x11 -> x13, local copies, waits for them, and re-layouts: 4.07 us -> 4.07 us
  transfers between devices with their start and end apart: 31 -> 31, of which waited for: 21 -> 20; matrix products, arithmetic and copies ran while one was open for 2% -> 2% of each run, Pallas kernels for 11% -> 15%
where the time goes in v5:
time: 77.6 us; the launch traced here: 77.5 us
  starting transfers between devices  28.5 us (37%)
  waiting for transfers between devices  26.5 us (34%)
  Pallas kernels  16.2 us (21%)
  local copies, waits for them, and re-layouts  4.07 us (5%)
  between operations  1.49 us (2%)
    ppermute x31, starting transfers between devices, swap(): return lax.ppermute(value, axis, partner_pairs(lax.axis_size(axis), mask))  28.5 us
    ppermute x31, waiting for transfers between devices, swap(): return lax.ppermute(value, axis, partner_pairs(lax.axis_size(axis), mask))  26.5 us
    unnamed x13, local copies, waits for them, and re-layouts  4.07 us
    pallas_call x2, Pallas kernels, local(): pl.pallas_call(functools.partial(weight_kernel, tile, combine), out_shape...  4.05 us
    pallas_call x2, Pallas kernels, local(): pl.pallas_call(kernel, out_shape=outs, in_specs=[SCALARS] + [WHOLE] * (le...  3.22 us
    pallas_call x1, Pallas kernels, local(): pl.pallas_call(functools.partial(prepare_kernel, direct, owners, slot_gro...  3.14 us
    pallas_call x1, Pallas kernels, local(): pl.pallas_call(functools.partial(turn_kernel, direct, tile, panels, len(h...  1.9 us
    pallas_call x2, Pallas kernels, spread(): pl.pallas_call(functools.partial(spread_kernel, first_relation), out_shap...  1.84 us
  transfers between devices with their start and end apart: 31, of which 20 were waited for; matrix products, arithmetic and copies ran while one was open for 2% of the time, Pallas kernels for 15%

profile of v5, /device:TPU:0, one launch (start us, length us, event | category | flops | bytes accessed | tf_op | source)
XLA Modules:
  0.0 77.5 jit_solution(10548438246207899482)
XLA Ops:
  0.6 3.1 %collective-permute-start.2 = (bf16[256,256]{1,0:T(8,128)(2,1)}, bf16[256,256]{1,0:T(8,128)(2,1)S(1)}, u32[]{:S(2)}, u32[]{:S(2)}) collective-permute-start(bf16[256,256]{1,0:T(8,128)(2,1)} %param.7), channel_id=1, source_target_pairs={{0,8},{8,0},{16,24},{24,16},{1,9},{9,1},{17,25},{25,17},{2,10},{10... | collective-permute-start | bytes 393224 | tf_op jit(solution)/shard_map/ppermute | solution.py:28
  3.7 2.5 %collective-permute-start.1 = (bf16[256,256]{1,0:T(8,128)(2,1)}, bf16[256,256]{1,0:T(8,128)(2,1)S(1)}, u32[]{:S(2)}, u32[]{:S(2)}) collective-permute-start(bf16[256,256]{1,0:T(8,128)(2,1)} %param.7), channel_id=1, source_target_pairs={{0,24},{8,16},{16,8},{24,0},{1,25},{9,17},{17,9},{25,1},{2,26},{10... | collective-permute-start | bytes 393224 | tf_op jit(solution)/shard_map/ppermute | solution.py:28
  7.6 1.6 %copy-done = bf16[1,1,1,64,128,128]{5,4,3,2,1,0:T(8,128)(2,1)S(1)} copy-done((bf16[1,1,1,64,128,128]{5,4,3,2,1,0:T(8,128)(2,1)S(1)}, bf16[1,1,1,64,128,128]{5,4,3,2,1,0:T(8,128)(2,1)}, u32[]{:S(2)}) %copy-start) | copy-done | bytes 2097176
  11.0 3.1 %prepare.1 = (bf16[64,128,128]{2,1,0:T(8,128)(2,1)S(1)}, bf16[6,256,256]{2,1,0:T(8,128)(2,1)S(1)}, s32[67]{0:T(128)S(1)}, s32[67]{0:T(128)S(1)}, s32[67]{0:T(128...) custom-call(s32[4]{0:T(128)S(1)} %bitcast.21, s32[3,64]{1,0:T(4,128)S(1)} %bitcast.20, ...), custom_call_target="tpu_custom_call" | custom-call | bytes 4194304 | tf_op jit(solution)/shard_map/prepare/pallas_call | solution.py:382
  14.2 1.8 %forward.2.refs_4_ = f32[17,128,256]{2,1,0:T(8,128)S(1)} custom-call(s32[67]{0:T(128)S(1)} %get-tuple-element.49.order, bf16[1,256,256]{2,1,0:T(8,128)(2,1)S(1)} %bitcast.12, bf16[1,256,256]{2,1,0:T(8,128)(2,1)S(1)} %bitcast.14, bf16[6,256,256]{2,1,0:T(8,128)(2,1)S(1)} %get-tuple-element.47.refs_2_.weight, ...), custom_call_target="tpu_custom_call", output_to_operand_aliasing={{}: (5, {})} | custom-call | flops 1073741824 | bytes 1048576 | tf_op jit(solution)/shard_map/forward/pallas_call | solution.py:411
  16.0 2.2 %collective-permute-done = bf16[256,256]{1,0:T(8,128)(2,1)S(1)} collective-permute-done((bf16[256,256]{1,0:T(8,128)(2,1)}, bf16[256,256]{1,0:T(8,128)(2,1)S(1)}, u32[]{:S(2)}, u32[]{:S(2)}) %collective-permute-start) | collective-permute-done | bytes 131104 | tf_op jit(solution)/shard_map/ppermute | solution.py:28
  20.2 1.5 %forward_ours.1 = (f32[17,128,256]{2,1,0:T(8,128)S(1)}, f32[256,256]{1,0:T(8,128)S(1)}, f32[256,256]{1,0:T(8,128)S(1)}, f32[256,256]{1,0:T(8,128)S(1)}, f32[256,256]{1,0:T(8,128)S(1)}) custom-call(s32[67]{0:T(128)S(1)} %get-tuple-element.45.order, bf16[12,128,256]{2,1,0:T(8,128)(2,1)S(1)} %get-tuple-element.51.projected, ...), custom_call_target="tpu_custom_call", output_to_operand_aliasing={{0}: (4, {})} | custom-call | flops 1073741824 | bytes 1048576 | tf_op jit(solution)/shard_map/forward_ours/pallas_call | solution.py:423
  21.8 2.4 %collective-permute-start.5 = (bf16[256,256]{1,0:T(8,128)(2,1)S(1)}, bf16[256,256]{1,0:T(8,128)(2,1)S(1)}, u32[]{:S(2)}, u32[]{:S(2)}) collective-permute-start(bf16[256,256]{1,0:T(8,128)(2,1)S(1)} %get-tuple-element.63), channel_id=1, source_target_pairs={{0,6},{2,4},{4,2},{6,0},{1,7},{3,5},{5,3},{7,1},{8,14},{10,12},{12... | collective-permute-start | bytes 393224 | tf_op jit(solution)/shard_map/ppermute | solution.py:28
  25.4 1.9 %turn.1 = (bf16[64,128,128]{2,1,0:T(8,128)(2,1)S(1)}, bf16[256,512]{1,0:T(8,128)(2,1)S(1)}, f32[13,128,256]{2,1,0:T(8,128)S(1)}, f32[13,128,256]{2,1,0:T(8,128)S(1)}) custom-call(s32[4]{0:T(128)S(1)} %bitcast.22, bf16[64,128,128]{2,1,0:T(8,128)(2,1)S(1)} %get-tuple-element.48.refs_3_.values, bf16[1,256,256]{2,1,0:T(8,128)(2,1)S(1)} %bitcast.13, ...), custom_call_target="tpu_custom_call" | custom-call | bytes 4194304 | tf_op jit(solution)/shard_map/turn/pallas_call | solution.py:448
  28.5 2.5 %collective-permute-done.6.second = bf16[256,256]{1,0:T(8,128)(2,1)S(1)} collective-permute-done((bf16[256,256]{1,0:T(8,128)(2,1)S(1)}, bf16[256,256]{1,0:T(8,128)(2,1)S(1)}, u32[]{:S(2)}, u32[]{:S(2)}) %collective-permute-start.6) | collective-permute-done | bytes 131104 | tf_op jit(solution)/shard_map/ppermute | solution.py:28
  31.7 1.5 %collective-permute-start.10 = (bf16[256,256]{1,0:T(8,128)(2,1)S(1)}, bf16[256,256]{1,0:T(8,128)(2,1)S(1)}, u32[]{:S(2)}, u32[]{:S(2)}) collective-permute-start(bf16[256,256]{1,0:T(8,128)(2,1)S(1)} %grad.1.refs_0_), channel_id=1, source_target_pairs={{0,6},{2,4},{4,2},{6,0},{1,7},{3,5},{5,3},{7,1},{8,14},{10,12},{12... | collective-permute-start | bytes 393224 | tf_op jit(solution)/shard_map/ppermute | solution.py:28
  33.2 1.4 %collective-permute-start.9 = (bf16[256,256]{1,0:T(8,128)(2,1)S(1)}, bf16[256,256]{1,0:T(8,128)(2,1)S(1)}, u32[]{:S(2)}, u32[]{:S(2)}) collective-permute-start(bf16[256,256]{1,0:T(8,128)(2,1)S(1)} %grad.1.refs_0_), channel_id=1, source_target_pairs={{0,4},{2,6},{4,0},{6,2},{1,5},{3,7},{5,1},{7,3},{8,12},{10,14},{12... | collective-permute-start | bytes 393224 | tf_op jit(solution)/shard_map/ppermute | solution.py:28
  35.2 3.6 %collective-permute-done.10.refs_3_ = bf16[256,256]{1,0:T(8,128)(2,1)S(1)} collective-permute-done((bf16[256,256]{1,0:T(8,128)(2,1)S(1)}, bf16[256,256]{1,0:T(8,128)(2,1)S(1)}, u32[]{:S(2)}, u32[]{:S(2)}) %collective-permute-start.10) | collective-permute-done | bytes 131104 | tf_op jit(solution)/shard_map/ppermute | solution.py:28
  38.8 1.5 %collective-permute-done.9.refs_2_ = bf16[256,256]{1,0:T(8,128)(2,1)S(1)} collective-permute-done((bf16[256,256]{1,0:T(8,128)(2,1)S(1)}, bf16[256,256]{1,0:T(8,128)(2,1)S(1)}, u32[]{:S(2)}, u32[]{:S(2)}) %collective-permute-start.9) | collective-permute-done | bytes 131104 | tf_op jit(solution)/shard_map/ppermute | solution.py:28
  42.3 1.8 %weight_terms.3 = (f32[3,64,256]{2,1,0:T(8,128)S(1)}, bf16[3,64,256]{2,1,0:T(8,128)(2,1)S(1)}, bf16[3,64,256]{2,1,0:T(8,128)(2,1)S(1)}, bf16[3,64,256]{2,1,0:T(8,128)(2,1)S(1)}, f32[13,128,256]{2,1,0:T(8,128)S(1)}) custom-call(s32[65]{0:T(128)S(1)} %get-tuple-element.82.listed, ...), custom_call_target="tpu_custom_call", output_to_operand_aliasing={{4}: (4, {})} | custom-call | tf_op jit(solution)/shard_map/weight_terms/pallas_call | solution.py:494
  45.2 2.5 %collective-permute-start.24 = (bf16[3,64,256]{2,1,0:T(8,128)(2,1)S(1)}, bf16[3,64,256]{2,1,0:T(8,128)(2,1)S(1)}, u32[]{:S(2)}, u32[]{:S(2)}) collective-permute-start(bf16[3,64,256]{2,1,0:T(8,128)(2,1)S(1)} %get-tuple-element.86), channel_id=1, source_target_pairs={{0,4},{2,6},{4,0},{6,2},{1,5},{3,7},{5,1},{7,3},{8,12},{10,14},{12... | collective-permute-start | bytes 294920 | tf_op jit(solution)/shard_map/ppermute | solution.py:28
  47.7 2.2 %weight_terms.2 = (f32[3,64,256]{2,1,0:T(8,128)S(1)}, bf16[3,64,256]{2,1,0:T(8,128)(2,1)S(1)}, bf16[3,64,256]{2,1,0:T(8,128)(2,1)S(1)}, bf16[3,64,256]{2,1,0:T(8,128)(2,1)S(1)}, f32[13,128,256]{2,1,0:T(8,128)S(1)}) custom-call(s32[65]{0:T(128)S(1)} %get-tuple-element.74.listed, ...), custom_call_target="tpu_custom_call", output_to_operand_aliasing={{4}: (4, {})} | custom-call | tf_op jit(solution)/shard_map/weight_terms/pallas_call | solution.py:494
  51.0 2.0 %collective-permute-start.16 = (bf16[3,64,256]{2,1,0:T(8,128)(2,1)S(1)}, bf16[3,64,256]{2,1,0:T(8,128)(2,1)S(1)}, u32[]{:S(2)}, u32[]{:S(2)}) collective-permute-start(bf16[3,64,256]{2,1,0:T(8,128)(2,1)S(1)} %get-tuple-element.80), channel_id=1, source_target_pairs={{0,4},{2,6},{4,0},{6,2},{1,5},{3,7},{5,1},{7,3},{8,12},{10,14},{12... | collective-permute-start | bytes 294920 | tf_op jit(solution)/shard_map/ppermute | solution.py:28
  53.6 2.4 %collective-permute-done.15.refs_1_ = bf16[3,64,256]{2,1,0:T(8,128)(2,1)S(1)} collective-permute-done((bf16[3,64,256]{2,1,0:T(8,128)(2,1)S(1)}, bf16[3,64,256]{2,1,0:T(8,128)(2,1)S(1)}, u32[]{:S(2)}, u32[]{:S(2)}) %collective-permute-start.15) | collective-permute-done | bytes 98336 | tf_op jit(solution)/shard_map/ppermute | solution.py:28
  57.8 1.8 %collective-permute-done.26.refs_1_ = bf16[3,64,256]{2,1,0:T(8,128)(2,1)S(1)} collective-permute-done((bf16[3,64,256]{2,1,0:T(8,128)(2,1)S(1)}, bf16[3,64,256]{2,1,0:T(8,128)(2,1)S(1)}, u32[]{:S(2)}, u32[]{:S(2)}) %collective-permute-start.26) | collective-permute-done | bytes 98336 | tf_op jit(solution)/shard_map/ppermute | solution.py:28
  59.9 2.8 %collective-permute-done.18.refs_1_ = bf16[3,64,256]{2,1,0:T(8,128)(2,1)S(1)} collective-permute-done((bf16[3,64,256]{2,1,0:T(8,128)(2,1)S(1)}, bf16[3,64,256]{2,1,0:T(8,128)(2,1)S(1)}, u32[]{:S(2)}, u32[]{:S(2)}) %collective-permute-start.18) | collective-permute-done | bytes 98336 | tf_op jit(solution)/shard_map/ppermute | solution.py:28
  63.2 1.5 %collective-permute-done.27.refs_1_ = bf16[3,64,256]{2,1,0:T(8,128)(2,1)S(1)} collective-permute-done((bf16[3,64,256]{2,1,0:T(8,128)(2,1)S(1)}, bf16[3,64,256]{2,1,0:T(8,128)(2,1)S(1)}, u32[]{:S(2)}, u32[]{:S(2)}) %collective-permute-start.27) | collective-permute-done | bytes 98336 | tf_op jit(solution)/shard_map/ppermute | solution.py:28
  64.7 1.9 %collective-permute-start.30 = (bf16[3,64,256]{2,1,0:T(8,128)(2,1)S(1)}, bf16[3,64,256]{2,1,0:T(8,128)(2,1)S(1)}, u32[]{:S(2)}, u32[]{:S(2)}) collective-permute-start(bf16[3,64,256]{2,1,0:T(8,128)(2,1)S(1)} %sum.13.refs_0_), channel_id=1, source_target_pairs={{0,6},{2,4},{4,2},{6,0},{1,7},{3,5},{5,3},{7,1},{8,14},{10,12},{12... | collective-permute-start | bytes 294920 | tf_op jit(solution)/shard_map/ppermute | solution.py:28
  68.8 2.3 %collective-permute-start.22 = (bf16[3,64,256]{2,1,0:T(8,128)(2,1)S(1)}, bf16[3,64,256]{2,1,0:T(8,128)(2,1)S(1)}, u32[]{:S(2)}, u32[]{:S(2)}) collective-permute-start(bf16[3,64,256]{2,1,0:T(8,128)(2,1)S(1)} %sum.10.refs_0_), channel_id=1, source_target_pairs={{0,6},{2,4},{4,2},{6,0},{1,7},{3,5},{5,3},{7,1},{8,14},{10,12},{12... | collective-permute-start | bytes 294920 | tf_op jit(solution)/shard_map/ppermute | solution.py:28
  (71 shorter events, 24.1 us)
Async XLA Ops:
  0.6 13.6 %collective-permute-start.2 = (bf16[256,256]{1,0:T(8,128)(2,1)}, bf16[256,256]{1,0:T(8,128)(2,1)S(1)}, u32[]{:S(2)}, u32[]{:S(2)}) collective-permute-start(bf16[256,256]{1,0:T(8,128)(2,1)} %param.7), channel_id=1, source_target_pairs={{0,8},{8,0},{16,24},{24,16},{1,9},{9,1},{17,25},{25,17},{2,10},{10... | collective-permute-start | bytes 393224 | tf_op jit(solution)/shard_map/ppermute | solution.py:28
  3.7 12.3 %collective-permute-start.1 = (bf16[256,256]{1,0:T(8,128)(2,1)}, bf16[256,256]{1,0:T(8,128)(2,1)S(1)}, u32[]{:S(2)}, u32[]{:S(2)}) collective-permute-start(bf16[256,256]{1,0:T(8,128)(2,1)} %param.7), channel_id=1, source_target_pairs={{0,24},{8,16},{16,8},{24,0},{1,25},{9,17},{17,9},{25,1},{2,26},{10... | collective-permute-start | bytes 393224 | tf_op jit(solution)/shard_map/ppermute | solution.py:28
  6.2 12.0 %collective-permute-start = (bf16[256,256]{1,0:T(8,128)(2,1)}, bf16[256,256]{1,0:T(8,128)(2,1)S(1)}, u32[]{:S(2)}, u32[]{:S(2)}) collective-permute-start(bf16[256,256]{1,0:T(8,128)(2,1)} %param.7), channel_id=1, source_target_pairs={{0,16},{8,24},{16,0},{24,8},{1,17},{9,25},{17,1},{25,9},{2,18},{10... | collective-permute-start | bytes 393224 | tf_op jit(solution)/shard_map/ppermute | solution.py:28
  21.8 6.7 %collective-permute-start.5 = (bf16[256,256]{1,0:T(8,128)(2,1)S(1)}, bf16[256,256]{1,0:T(8,128)(2,1)S(1)}, u32[]{:S(2)}, u32[]{:S(2)}) collective-permute-start(bf16[256,256]{1,0:T(8,128)(2,1)S(1)} %get-tuple-element.63), channel_id=1, source_target_pairs={{0,6},{2,4},{4,2},{6,0},{1,7},{3,5},{5,3},{7,1},{8,14},{10,12},{12... | collective-permute-start | bytes 393224 | tf_op jit(solution)/shard_map/ppermute | solution.py:28
  24.2 6.8 %collective-permute-start.6 = (bf16[256,256]{1,0:T(8,128)(2,1)S(1)}, bf16[256,256]{1,0:T(8,128)(2,1)S(1)}, u32[]{:S(2)}, u32[]{:S(2)}) collective-permute-start(bf16[256,256]{1,0:T(8,128)(2,1)S(1)} %get-tuple-element.64), channel_id=1, source_target_pairs={{0,4},{2,6},{4,0},{6,2},{1,5},{3,7},{5,1},{7,3},{8,12},{10,14},{12... | collective-permute-start | bytes 393224 | tf_op jit(solution)/shard_map/ppermute | solution.py:28
  25.2 6.4 %collective-permute-start.7 = (bf16[256,256]{1,0:T(8,128)(2,1)S(1)}, bf16[256,256]{1,0:T(8,128)(2,1)S(1)}, u32[]{:S(2)}, u32[]{:S(2)}) collective-permute-start(bf16[256,256]{1,0:T(8,128)(2,1)S(1)} %sum.7), channel_id=1, source_target_pairs={{0,2},{2,0},{4,6},{6,4},{1,3},{3,1},{5,7},{7,5},{8,10},{10,8},{12,... | collective-permute-start | bytes 393224 | tf_op jit(solution)/shard_map/ppermute | solution.py:28
  31.7 7.1 %collective-permute-start.10 = (bf16[256,256]{1,0:T(8,128)(2,1)S(1)}, bf16[256,256]{1,0:T(8,128)(2,1)S(1)}, u32[]{:S(2)}, u32[]{:S(2)}) collective-permute-start(bf16[256,256]{1,0:T(8,128)(2,1)S(1)} %grad.1.refs_0_), channel_id=1, source_target_pairs={{0,6},{2,4},{4,2},{6,0},{1,7},{3,5},{5,3},{7,1},{8,14},{10,12},{12... | collective-permute-start | bytes 393224 | tf_op jit(solution)/shard_map/ppermute | solution.py:28
  33.2 7.2 %collective-permute-start.9 = (bf16[256,256]{1,0:T(8,128)(2,1)S(1)}, bf16[256,256]{1,0:T(8,128)(2,1)S(1)}, u32[]{:S(2)}, u32[]{:S(2)}) collective-permute-start(bf16[256,256]{1,0:T(8,128)(2,1)S(1)} %grad.1.refs_0_), channel_id=1, source_target_pairs={{0,4},{2,6},{4,0},{6,2},{1,5},{3,7},{5,1},{7,3},{8,12},{10,14},{12... | collective-permute-start | bytes 393224 | tf_op jit(solution)/shard_map/ppermute | solution.py:28
  34.6 6.2 %collective-permute-start.8 = (bf16[256,256]{1,0:T(8,128)(2,1)S(1)}, bf16[256,256]{1,0:T(8,128)(2,1)S(1)}, u32[]{:S(2)}, u32[]{:S(2)}) collective-permute-start(bf16[256,256]{1,0:T(8,128)(2,1)S(1)} %grad.1.refs_0_), channel_id=1, source_target_pairs={{0,2},{2,0},{4,6},{6,4},{1,3},{3,1},{5,7},{7,5},{8,10},{10,8},{12,... | collective-permute-start | bytes 393224 | tf_op jit(solution)/shard_map/ppermute | solution.py:28
  35.2 5.6 %collective-permute-start.11 = (bf16[256,256]{1,0:T(8,128)(2,1)S(1)}, bf16[256,256]{1,0:T(8,128)(2,1)S(1)}, u32[]{:S(2)}, u32[]{:S(2)}) collective-permute-start(bf16[256,256]{1,0:T(8,128)(2,1)S(1)} %grad.1.refs_0_), channel_id=1, source_target_pairs={{0,1},{1,0},{2,3},{3,2},{4,5},{5,4},{6,7},{7,6},{8,9},{9,8},{10,11... | collective-permute-start | bytes 393224 | tf_op jit(solution)/shard_map/ppermute | solution.py:28
  44.1 8.9 %collective-permute-start.23 = (bf16[3,64,256]{2,1,0:T(8,128)(2,1)S(1)}, bf16[3,64,256]{2,1,0:T(8,128)(2,1)S(1)}, u32[]{:S(2)}, u32[]{:S(2)}) collective-permute-start(bf16[3,64,256]{2,1,0:T(8,128)(2,1)S(1)} %get-tuple-element.85), channel_id=1, source_target_pairs={{0,6},{2,4},{4,2},{6,0},{1,7},{3,5},{5,3},{7,1},{8,14},{10,12},{12... | collective-permute-start | bytes 294920 | tf_op jit(solution)/shard_map/ppermute | solution.py:28
  45.2 8.3 %collective-permute-start.24 = (bf16[3,64,256]{2,1,0:T(8,128)(2,1)S(1)}, bf16[3,64,256]{2,1,0:T(8,128)(2,1)S(1)}, u32[]{:S(2)}, u32[]{:S(2)}) collective-permute-start(bf16[3,64,256]{2,1,0:T(8,128)(2,1)S(1)} %get-tuple-element.86), channel_id=1, source_target_pairs={{0,4},{2,6},{4,0},{6,2},{1,5},{3,7},{5,1},{7,3},{8,12},{10,14},{12... | collective-permute-start | bytes 294920 | tf_op jit(solution)/shard_map/ppermute | solution.py:28
  47.7 5.8 %collective-permute-start.25 = (bf16[3,64,256]{2,1,0:T(8,128)(2,1)S(1)}, bf16[3,64,256]{2,1,0:T(8,128)(2,1)S(1)}, u32[]{:S(2)}, u32[]{:S(2)}) collective-permute-start(bf16[3,64,256]{2,1,0:T(8,128)(2,1)S(1)} %get-tuple-element.87), channel_id=1, source_target_pairs={{0,2},{2,0},{4,6},{6,4},{1,3},{3,1},{5,7},{7,5},{8,10},{10,8},{12,... | collective-permute-start | bytes 294920 | tf_op jit(solution)/shard_map/ppermute | solution.py:28
  49.9 6.1 %collective-permute-start.15 = (bf16[3,64,256]{2,1,0:T(8,128)(2,1)S(1)}, bf16[3,64,256]{2,1,0:T(8,128)(2,1)S(1)}, u32[]{:S(2)}, u32[]{:S(2)}) collective-permute-start(bf16[3,64,256]{2,1,0:T(8,128)(2,1)S(1)} %get-tuple-element.79), channel_id=1, source_target_pairs={{0,6},{2,4},{4,2},{6,0},{1,7},{3,5},{5,3},{7,1},{8,14},{10,12},{12... | collective-permute-start | bytes 294920 | tf_op jit(solution)/shard_map/ppermute | solution.py:28
  51.0 5.6 %collective-permute-start.16 = (bf16[3,64,256]{2,1,0:T(8,128)(2,1)S(1)}, bf16[3,64,256]{2,1,0:T(8,128)(2,1)S(1)}, u32[]{:S(2)}, u32[]{:S(2)}) collective-permute-start(bf16[3,64,256]{2,1,0:T(8,128)(2,1)S(1)} %get-tuple-element.80), channel_id=1, source_target_pairs={{0,4},{2,6},{4,0},{6,2},{1,5},{3,7},{5,1},{7,3},{8,12},{10,14},{12... | collective-permute-start | bytes 294920 | tf_op jit(solution)/shard_map/ppermute | solution.py:28
  53.6 6.1 %collective-permute-start.26 = (bf16[3,64,256]{2,1,0:T(8,128)(2,1)S(1)}, bf16[3,64,256]{2,1,0:T(8,128)(2,1)S(1)}, u32[]{:S(2)}, u32[]{:S(2)}) collective-permute-start(bf16[3,64,256]{2,1,0:T(8,128)(2,1)S(1)} %sum.11.refs_0_), channel_id=1, source_target_pairs={{0,16},{8,24},{16,0},{24,8},{1,17},{9,25},{17,1},{25,9},{2,18},{10... | collective-permute-start | bytes 294920 | tf_op jit(solution)/shard_map/ppermute | solution.py:28
  57.7 5.0 %collective-permute-start.18 = (bf16[3,64,256]{2,1,0:T(8,128)(2,1)S(1)}, bf16[3,64,256]{2,1,0:T(8,128)(2,1)S(1)}, u32[]{:S(2)}, u32[]{:S(2)}) collective-permute-start(bf16[3,64,256]{2,1,0:T(8,128)(2,1)S(1)} %sum.8.refs_0_), channel_id=1, source_target_pairs={{0,8},{8,0},{16,24},{24,16},{1,9},{9,1},{17,25},{25,17},{2,10},{10... | collective-permute-start | bytes 294920 | tf_op jit(solution)/shard_map/ppermute | solution.py:28
  59.7 5.0 %collective-permute-start.27 = (bf16[3,64,256]{2,1,0:T(8,128)(2,1)S(1)}, bf16[3,64,256]{2,1,0:T(8,128)(2,1)S(1)}, u32[]{:S(2)}, u32[]{:S(2)}) collective-permute-start(bf16[3,64,256]{2,1,0:T(8,128)(2,1)S(1)} %sum.12.refs_0_), channel_id=1, source_target_pairs={{0,8},{8,0},{16,24},{24,16},{1,9},{9,1},{17,25},{25,17},{2,10},{10... | collective-permute-start | bytes 294920 | tf_op jit(solution)/shard_map/ppermute | solution.py:28
  62.7 6.0 %collective-permute-start.19 = (bf16[3,64,256]{2,1,0:T(8,128)(2,1)S(1)}, bf16[3,64,256]{2,1,0:T(8,128)(2,1)S(1)}, u32[]{:S(2)}, u32[]{:S(2)}) collective-permute-start(bf16[3,64,256]{2,1,0:T(8,128)(2,1)S(1)} %sum.9.refs_0_), channel_id=1, source_target_pairs={{0,16},{8,24},{16,0},{24,8},{1,17},{9,25},{17,1},{25,9},{2,18},{10... | collective-permute-start | bytes 294920 | tf_op jit(solution)/shard_map/ppermute | solution.py:28
  64.7 7.2 %collective-permute-start.30 = (bf16[3,64,256]{2,1,0:T(8,128)(2,1)S(1)}, bf16[3,64,256]{2,1,0:T(8,128)(2,1)S(1)}, u32[]{:S(2)}, u32[]{:S(2)}) collective-permute-start(bf16[3,64,256]{2,1,0:T(8,128)(2,1)S(1)} %sum.13.refs_0_), channel_id=1, source_target_pairs={{0,6},{2,4},{4,2},{6,0},{1,7},{3,5},{5,3},{7,1},{8,14},{10,12},{12... | collective-permute-start | bytes 294920 | tf_op jit(solution)/shard_map/ppermute | solution.py:28
  66.6 6.5 %collective-permute-start.29 = (bf16[3,64,256]{2,1,0:T(8,128)(2,1)S(1)}, bf16[3,64,256]{2,1,0:T(8,128)(2,1)S(1)}, u32[]{:S(2)}, u32[]{:S(2)}) collective-permute-start(bf16[3,64,256]{2,1,0:T(8,128)(2,1)S(1)} %sum.13.refs_0_), channel_id=1, source_target_pairs={{0,4},{2,6},{4,0},{6,2},{1,5},{3,7},{5,1},{7,3},{8,12},{10,14},{12... | collective-permute-start | bytes 294920 | tf_op jit(solution)/shard_map/ppermute | solution.py:28
  67.8 5.5 %collective-permute-start.28 = (bf16[3,64,256]{2,1,0:T(8,128)(2,1)S(1)}, bf16[3,64,256]{2,1,0:T(8,128)(2,1)S(1)}, u32[]{:S(2)}, u32[]{:S(2)}) collective-permute-start(bf16[3,64,256]{2,1,0:T(8,128)(2,1)S(1)} %sum.13.refs_0_), channel_id=1, source_target_pairs={{0,2},{2,0},{4,6},{6,4},{1,3},{3,1},{5,7},{7,5},{8,10},{10,8},{12,... | collective-permute-start | bytes 294920 | tf_op jit(solution)/shard_map/ppermute | solution.py:28
  68.8 6.5 %collective-permute-start.22 = (bf16[3,64,256]{2,1,0:T(8,128)(2,1)S(1)}, bf16[3,64,256]{2,1,0:T(8,128)(2,1)S(1)}, u32[]{:S(2)}, u32[]{:S(2)}) collective-permute-start(bf16[3,64,256]{2,1,0:T(8,128)(2,1)S(1)} %sum.10.refs_0_), channel_id=1, source_target_pairs={{0,6},{2,4},{4,2},{6,0},{1,7},{3,5},{5,3},{7,1},{8,14},{10,12},{12... | collective-permute-start | bytes 294920 | tf_op jit(solution)/shard_map/ppermute | solution.py:28
  71.1 5.0 %collective-permute-start.21 = (bf16[3,64,256]{2,1,0:T(8,128)(2,1)S(1)}, bf16[3,64,256]{2,1,0:T(8,128)(2,1)S(1)}, u32[]{:S(2)}, u32[]{:S(2)}) collective-permute-start(bf16[3,64,256]{2,1,0:T(8,128)(2,1)S(1)} %sum.10.refs_0_), channel_id=1, source_target_pairs={{0,4},{2,6},{4,0},{6,2},{1,5},{3,7},{5,1},{7,3},{8,12},{10,14},{12... | collective-permute-start | bytes 294920 | tf_op jit(solution)/shard_map/ppermute | solution.py:28
  (13 other events, 39.8 us)

commit v6 on v5

--- a/solution.py
+++ b/solution.py
@@ -12,7 +12,7 @@
 WHOLE = pl.BlockSpec(memory_space=pltpu.VMEM)
 SCALARS = pl.BlockSpec(memory_space=pltpu.SMEM)
 ANYWHERE = pl.BlockSpec(memory_space=pl.ANY)
-UNROLL = 16
+UNROLL = 20
 
 
 def vmem_for(*arrays):
@@ -136,6 +136,11 @@
     return [(pl.ds(i * tile, tile), owner * per_owner + i) for i in range(per_owner)]
 
 
+def halves(value):
+    high = value.astype(BF16)
+    return high, (value - high.astype(F32)).astype(BF16)
+
+
 def project(tile, combine, firsts, halo_refs, weight, projected):
     relations = weight.shape[0]
     blocks = [halo_block(first, halo_refs, i, tile) for i, first in enumerate(firsts)]
@@ -145,9 +150,11 @@
         return
     stacked = jnp.concatenate(blocks, axis=0)
     for r in range(relations):
-        product = jnp.dot(stacked, weight[r], preferred_element_type=F32).astype(BF16)
+        high, low = halves(jnp.dot(stacked, weight[r], preferred_element_type=F32))
         for i in range(len(blocks)):
-            projected[i * relations + r] = product[i * tile : (i + 1) * tile]
+            rows = slice(i * tile, (i + 1) * tile)
+            projected[i * relations + r, :tile, :] = high[rows]
+            projected[i * relations + r, tile:, :] = low[rows]
 
 
 def add_entries(combine, values, weight, projected, order, total, pre):
@@ -158,7 +165,8 @@
         for position, real in positions:
             e, target, place = unpacked(entries, spare, order[position])
             if combine:
-                term = jnp.dot(values[e], projected[place], preferred_element_type=F32)
+                twice = jnp.concatenate([values[e], values[e]], axis=1)
+                term = jnp.dot(twice, projected[place], preferred_element_type=F32)
             else:
                 message = jnp.dot(
                     values[e], projected[place // relations], preferred_element_type=F32
@@ -251,7 +259,9 @@
     for r in range(relations):
         if combine:
             stacked = sums[r * slots : (r + 1) * slots].reshape(slots * tile, features)
-            grad = jnp.dot(halo_turned[...], stacked.astype(BF16), preferred_element_type=F32)
+            high, low = halves(stacked)
+            grad = jnp.dot(halo_turned[...], high, preferred_element_type=F32)
+            grad = grad + jnp.dot(halo_turned[...], low, preferred_element_type=F32)
         else:
             grad = sums[r]
         for m, out in enumerate(outs):
@@ -402,7 +412,10 @@
         last = call == len(slot_groups) - 2
         blocks = halo[low:high] if direct else halo
         projected = jax.ShapeDtypeStruct(
-            ((high - low) * (relations if combine else 1), tile, features), BF16
+            ((high - low) * relations, 2 * tile, features)
+            if combine
+            else (high - low, tile, features),
+            BF16,
         )
         kernel = functools.partial(near_kernel, tile, combine)
         if last:

time: 77.6 us -> 77.7 us (level)
  starting transfers between devices: 28.5 us -> 30.9 us
  Pallas kernels: 16.2 us -> 14.1 us
    ppermute x31, starting transfers between devices: 28.5 us -> 30.9 us  [swap(): return lax.ppermute(value, axis, partner_pairs(lax.axis_size(axis), mask))]
    pallas_call x1, Pallas kernels: 3.14 us -> 2.33 us  [local(): pl.pallas_call(functools.partial(prepare_kernel, direct, owners, slot_gro...]
  transfers between devices with their start and end apart: 31 -> 31, of which waited for: 20 -> 21; matrix products, arithmetic and copies ran while one was open for 2% -> 2% of each run, Pallas kernels for 15% -> 13%
where the time goes in v6:
time: 77.7 us; the launch traced here: 77.4 us
  starting transfers between devices  30.9 us (40%)
  waiting for transfers between devices  26.1 us (34%)
  Pallas kernels  14.1 us (18%)
  local copies, waits for them, and re-layouts  4.07 us (5%)
  between operations  1.47 us (2%)
    ppermute x31, starting transfers between devices, swap(): return lax.ppermute(value, axis, partner_pairs(lax.axis_size(axis), mask))  30.9 us
    ppermute x31, waiting for transfers between devices, swap(): return lax.ppermute(value, axis, partner_pairs(lax.axis_size(axis), mask))  26.1 us
    unnamed x13, local copies, waits for them, and re-layouts  4.07 us
    pallas_call x2, Pallas kernels, local(): pl.pallas_call(functools.partial(weight_kernel, tile, combine), out_shape...  3.3 us
    pallas_call x2, Pallas kernels, local(): pl.pallas_call(kernel, out_shape=outs, in_specs=[SCALARS] + [WHOLE] * (le...  3.04 us
    pallas_call x1, Pallas kernels, local(): pl.pallas_call(functools.partial(prepare_kernel, direct, owners, slot_gro...  2.33 us
    pallas_call x1, Pallas kernels, local(): pl.pallas_call(functools.partial(turn_kernel, direct, tile, panels, len(h...  1.9 us
    pallas_call x2, Pallas kernels, spread(): pl.pallas_call(functools.partial(spread_kernel, first_relation), out_shap...  1.84 us
  transfers between devices with their start and end apart: 31, of which 21 were waited for; matrix products, arithmetic and copies ran while one was open for 2% of the time, Pallas kernels for 13%

profile of v6, /device:TPU:0, one launch (start us, length us, event | category | flops | bytes accessed | tf_op | source)
XLA Modules:
  0.0 77.4 jit_solution(8835945579831508309)
XLA Ops:
  0.6 3.1 %collective-permute-start.2 = (bf16[256,256]{1,0:T(8,128)(2,1)}, bf16[256,256]{1,0:T(8,128)(2,1)S(1)}, u32[]{:S(2)}, u32[]{:S(2)}) collective-permute-start(bf16[256,256]{1,0:T(8,128)(2,1)} %param.7), channel_id=1, source_target_pairs={{0,8},{8,0},{16,24},{24,16},{1,9},{9,1},{17,25},{25,17},{2,10},{10... | collective-permute-start | bytes 393224 | tf_op jit(solution)/shard_map/ppermute | solution.py:28
  3.7 2.5 %collective-permute-start.1 = (bf16[256,256]{1,0:T(8,128)(2,1)}, bf16[256,256]{1,0:T(8,128)(2,1)S(1)}, u32[]{:S(2)}, u32[]{:S(2)}) collective-permute-start(bf16[256,256]{1,0:T(8,128)(2,1)} %param.7), channel_id=1, source_target_pairs={{0,24},{8,16},{16,8},{24,0},{1,25},{9,17},{17,9},{25,1},{2,26},{10... | collective-permute-start | bytes 393224 | tf_op jit(solution)/shard_map/ppermute | solution.py:28
  7.6 1.6 %copy-done = bf16[1,1,1,64,128,128]{5,4,3,2,1,0:T(8,128)(2,1)S(1)} copy-done((bf16[1,1,1,64,128,128]{5,4,3,2,1,0:T(8,128)(2,1)S(1)}, bf16[1,1,1,64,128,128]{5,4,3,2,1,0:T(8,128)(2,1)}, u32[]{:S(2)}) %copy-start) | copy-done | bytes 2097176
  11.0 2.3 %prepare.1 = (bf16[64,128,128]{2,1,0:T(8,128)(2,1)S(1)}, bf16[6,256,256]{2,1,0:T(8,128)(2,1)S(1)}, s32[67]{0:T(128)S(1)}, s32[67]{0:T(128)S(1)}, s32[67]{0:T(128...) custom-call(s32[4]{0:T(128)S(1)} %bitcast.21, s32[3,64]{1,0:T(4,128)S(1)} %bitcast.20, ...), custom_call_target="tpu_custom_call" | custom-call | bytes 4194304 | tf_op jit(solution)/shard_map/prepare/pallas_call | solution.py:392
  13.4 1.5 %forward.2.refs_4_ = f32[17,128,256]{2,1,0:T(8,128)S(1)} custom-call(s32[67]{0:T(128)S(1)} %get-tuple-element.49.order, bf16[1,256,256]{2,1,0:T(8,128)(2,1)S(1)} %bitcast.12, bf16[1,256,256]{2,1,0:T(8,128)(2,1)S(1)} %bitcast.14, bf16[6,256,256]{2,1,0:T(8,128)(2,1)S(1)} %get-tuple-element.47.refs_2_.weight, ...), custom_call_target="tpu_custom_call", output_to_operand_aliasing={{}: (5, {})} | custom-call | flops 1073741824 | bytes 1048576 | tf_op jit(solution)/shard_map/forward/pallas_call | solution.py:424
  14.9 3.3 %collective-permute-done = bf16[256,256]{1,0:T(8,128)(2,1)S(1)} collective-permute-done((bf16[256,256]{1,0:T(8,128)(2,1)}, bf16[256,256]{1,0:T(8,128)(2,1)S(1)}, u32[]{:S(2)}, u32[]{:S(2)}) %collective-permute-start) | collective-permute-done | bytes 131104 | tf_op jit(solution)/shard_map/ppermute | solution.py:28
  18.2 1.5 %forward.3 = (f32[17,128,256]{2,1,0:T(8,128)S(1)}, bf16[12,256,256]{2,1,0:T(8,128)(2,1)S(1)}, bf16[256,256]{1,0:T(8,128)(2,1)S(1)}, bf16[3,256,256]{2,1,0:T(8,128)(2,1)S(1)}) custom-call(s32[67]{0:T(128)S(1)} %get-tuple-element.46.order, bf16[1,256,256]{2,1,0:T(8,128)(2,1)S(1)} %bitcast.18, ...), custom_call_target="tpu_custom_call", output_to_operand_aliasing={{0}: (5, {})} | custom-call | flops 1073741824 | bytes 1048576 | tf_op jit(solution)/shard_map/forward/pallas_call | solution.py:424
  21.9 2.5 %collective-permute-start.5 = (bf16[256,256]{1,0:T(8,128)(2,1)S(1)}, bf16[256,256]{1,0:T(8,128)(2,1)S(1)}, u32[]{:S(2)}, u32[]{:S(2)}) collective-permute-start(bf16[256,256]{1,0:T(8,128)(2,1)S(1)} %get-tuple-element.63), channel_id=1, source_target_pairs={{0,6},{2,4},{4,2},{6,0},{1,7},{3,5},{5,3},{7,1},{8,14},{10,12},{12... | collective-permute-start | bytes 393224 | tf_op jit(solution)/shard_map/ppermute | solution.py:28
  25.4 1.9 %turn.1 = (bf16[64,128,128]{2,1,0:T(8,128)(2,1)S(1)}, bf16[256,512]{1,0:T(8,128)(2,1)S(1)}, f32[13,128,256]{2,1,0:T(8,128)S(1)}, f32[13,128,256]{2,1,0:T(8,128)S(1)}) custom-call(s32[4]{0:T(128)S(1)} %bitcast.22, bf16[64,128,128]{2,1,0:T(8,128)(2,1)S(1)} %get-tuple-element.48.refs_3_.values, bf16[1,256,256]{2,1,0:T(8,128)(2,1)S(1)} %bitcast.13, ...), custom_call_target="tpu_custom_call" | custom-call | bytes 4194304 | tf_op jit(solution)/shard_map/turn/pallas_call | solution.py:461
  27.3 1.3 %collective-permute-done.5.first = bf16[256,256]{1,0:T(8,128)(2,1)S(1)} collective-permute-done((bf16[256,256]{1,0:T(8,128)(2,1)S(1)}, bf16[256,256]{1,0:T(8,128)(2,1)S(1)}, u32[]{:S(2)}, u32[]{:S(2)}) %collective-permute-start.5) | collective-permute-done | bytes 131104 | tf_op jit(solution)/shard_map/ppermute | solution.py:28
  28.6 2.5 %collective-permute-done.6.second = bf16[256,256]{1,0:T(8,128)(2,1)S(1)} collective-permute-done((bf16[256,256]{1,0:T(8,128)(2,1)S(1)}, bf16[256,256]{1,0:T(8,128)(2,1)S(1)}, u32[]{:S(2)}, u32[]{:S(2)}) %collective-permute-start.6) | collective-permute-done | bytes 131104 | tf_op jit(solution)/shard_map/ppermute | solution.py:28
  31.4 1.7 %collective-permute-start.10 = (bf16[256,256]{1,0:T(8,128)(2,1)S(1)}, bf16[256,256]{1,0:T(8,128)(2,1)S(1)}, u32[]{:S(2)}, u32[]{:S(2)}) collective-permute-start(bf16[256,256]{1,0:T(8,128)(2,1)S(1)} %grad.1.refs_0_), channel_id=1, source_target_pairs={{0,6},{2,4},{4,2},{6,0},{1,7},{3,5},{5,3},{7,1},{8,14},{10,12},{12... | collective-permute-start | bytes 393224 | tf_op jit(solution)/shard_map/ppermute | solution.py:28
  34.9 3.8 %collective-permute-done.10.refs_3_ = bf16[256,256]{1,0:T(8,128)(2,1)S(1)} collective-permute-done((bf16[256,256]{1,0:T(8,128)(2,1)S(1)}, bf16[256,256]{1,0:T(8,128)(2,1)S(1)}, u32[]{:S(2)}, u32[]{:S(2)}) %collective-permute-start.10) | collective-permute-done | bytes 131104 | tf_op jit(solution)/shard_map/ppermute | solution.py:28
  38.8 1.7 %collective-permute-done.9.refs_2_ = bf16[256,256]{1,0:T(8,128)(2,1)S(1)} collective-permute-done((bf16[256,256]{1,0:T(8,128)(2,1)S(1)}, bf16[256,256]{1,0:T(8,128)(2,1)S(1)}, u32[]{:S(2)}, u32[]{:S(2)}) %collective-permute-start.9) | collective-permute-done | bytes 131104 | tf_op jit(solution)/shard_map/ppermute | solution.py:28
  42.1 1.7 %weight_terms.3 = (f32[3,64,256]{2,1,0:T(8,128)S(1)}, bf16[3,64,256]{2,1,0:T(8,128)(2,1)S(1)}, bf16[3,64,256]{2,1,0:T(8,128)(2,1)S(1)}, bf16[3,64,256]{2,1,0:T(8,128)(2,1)S(1)}, f32[13,128,256]{2,1,0:T(8,128)S(1)}) custom-call(s32[65]{0:T(128)S(1)} %get-tuple-element.82.listed, ...), custom_call_target="tpu_custom_call", output_to_operand_aliasing={{4}: (4, {})} | custom-call | tf_op jit(solution)/shard_map/weight_terms/pallas_call | solution.py:507
  43.8 1.9 %collective-permute-start.23 = (bf16[3,64,256]{2,1,0:T(8,128)(2,1)S(1)}, bf16[3,64,256]{2,1,0:T(8,128)(2,1)S(1)}, u32[]{:S(2)}, u32[]{:S(2)}) collective-permute-start(bf16[3,64,256]{2,1,0:T(8,128)(2,1)S(1)} %get-tuple-element.85), channel_id=1, source_target_pairs={{0,6},{2,4},{4,2},{6,0},{1,7},{3,5},{5,3},{7,1},{8,14},{10,12},{12... | collective-permute-start | bytes 294920 | tf_op jit(solution)/shard_map/ppermute | solution.py:28
  47.3 1.6 %weight_terms.2 = (f32[3,64,256]{2,1,0:T(8,128)S(1)}, bf16[3,64,256]{2,1,0:T(8,128)(2,1)S(1)}, bf16[3,64,256]{2,1,0:T(8,128)(2,1)S(1)}, bf16[3,64,256]{2,1,0:T(8,128)(2,1)S(1)}, f32[13,128,256]{2,1,0:T(8,128)S(1)}) custom-call(s32[65]{0:T(128)S(1)} %get-tuple-element.74.listed, ...), custom_call_target="tpu_custom_call", output_to_operand_aliasing={{4}: (4, {})} | custom-call | tf_op jit(solution)/shard_map/weight_terms/pallas_call | solution.py:507
  49.0 2.4 %collective-permute-start.15 = (bf16[3,64,256]{2,1,0:T(8,128)(2,1)S(1)}, bf16[3,64,256]{2,1,0:T(8,128)(2,1)S(1)}, u32[]{:S(2)}, u32[]{:S(2)}) collective-permute-start(bf16[3,64,256]{2,1,0:T(8,128)(2,1)S(1)} %get-tuple-element.79), channel_id=1, source_target_pairs={{0,6},{2,4},{4,2},{6,0},{1,7},{3,5},{5,3},{7,1},{8,14},{10,12},{12... | collective-permute-start | bytes 294920 | tf_op jit(solution)/shard_map/ppermute | solution.py:28
  52.6 1.6 %collective-permute-start.26 = (bf16[3,64,256]{2,1,0:T(8,128)(2,1)S(1)}, bf16[3,64,256]{2,1,0:T(8,128)(2,1)S(1)}, u32[]{:S(2)}, u32[]{:S(2)}) collective-permute-start(bf16[3,64,256]{2,1,0:T(8,128)(2,1)S(1)} %sum.11.refs_0_), channel_id=1, source_target_pairs={{0,16},{8,24},{16,0},{24,8},{1,17},{9,25},{17,1},{25,9},{2,18},{10... | collective-permute-start | bytes 294920 | tf_op jit(solution)/shard_map/ppermute | solution.py:28
  54.9 1.7 %collective-permute-done.16.refs_2_ = bf16[3,64,256]{2,1,0:T(8,128)(2,1)S(1)} collective-permute-done((bf16[3,64,256]{2,1,0:T(8,128)(2,1)S(1)}, bf16[3,64,256]{2,1,0:T(8,128)(2,1)S(1)}, u32[]{:S(2)}, u32[]{:S(2)}) %collective-permute-start.16) | collective-permute-done | bytes 98336 | tf_op jit(solution)/shard_map/ppermute | solution.py:28
  57.5 2.2 %collective-permute-done.26.refs_1_ = bf16[3,64,256]{2,1,0:T(8,128)(2,1)S(1)} collective-permute-done((bf16[3,64,256]{2,1,0:T(8,128)(2,1)S(1)}, bf16[3,64,256]{2,1,0:T(8,128)(2,1)S(1)}, u32[]{:S(2)}, u32[]{:S(2)}) %collective-permute-start.26) | collective-permute-done | bytes 98336 | tf_op jit(solution)/shard_map/ppermute | solution.py:28
  59.9 2.5 %collective-permute-done.18.refs_1_ = bf16[3,64,256]{2,1,0:T(8,128)(2,1)S(1)} collective-permute-done((bf16[3,64,256]{2,1,0:T(8,128)(2,1)S(1)}, bf16[3,64,256]{2,1,0:T(8,128)(2,1)S(1)}, u32[]{:S(2)}, u32[]{:S(2)}) %collective-permute-start.18) | collective-permute-done | bytes 98336 | tf_op jit(solution)/shard_map/ppermute | solution.py:28
  64.8 1.5 %collective-permute-start.30 = (bf16[3,64,256]{2,1,0:T(8,128)(2,1)S(1)}, bf16[3,64,256]{2,1,0:T(8,128)(2,1)S(1)}, u32[]{:S(2)}, u32[]{:S(2)}) collective-permute-start(bf16[3,64,256]{2,1,0:T(8,128)(2,1)S(1)} %sum.13.refs_0_), channel_id=1, source_target_pairs={{0,6},{2,4},{4,2},{6,0},{1,7},{3,5},{5,3},{7,1},{8,14},{10,12},{12... | collective-permute-start | bytes 294920 | tf_op jit(solution)/shard_map/ppermute | solution.py:28
  68.5 1.8 %collective-permute-start.22 = (bf16[3,64,256]{2,1,0:T(8,128)(2,1)S(1)}, bf16[3,64,256]{2,1,0:T(8,128)(2,1)S(1)}, u32[]{:S(2)}, u32[]{:S(2)}) collective-permute-start(bf16[3,64,256]{2,1,0:T(8,128)(2,1)S(1)} %sum.10.refs_0_), channel_id=1, source_target_pairs={{0,6},{2,4},{4,2},{6,0},{1,7},{3,5},{5,3},{7,1},{8,14},{10,12},{12... | collective-permute-start | bytes 294920 | tf_op jit(solution)/shard_map/ppermute | solution.py:28
  (71 shorter events, 25.6 us)
Async XLA Ops:
  0.6 12.7 %collective-permute-start.2 = (bf16[256,256]{1,0:T(8,128)(2,1)}, bf16[256,256]{1,0:T(8,128)(2,1)S(1)}, u32[]{:S(2)}, u32[]{:S(2)}) collective-permute-start(bf16[256,256]{1,0:T(8,128)(2,1)} %param.7), channel_id=1, source_target_pairs={{0,8},{8,0},{16,24},{24,16},{1,9},{9,1},{17,25},{25,17},{2,10},{10... | collective-permute-start | bytes 393224 | tf_op jit(solution)/shard_map/ppermute | solution.py:28
  3.7 11.2 %collective-permute-start.1 = (bf16[256,256]{1,0:T(8,128)(2,1)}, bf16[256,256]{1,0:T(8,128)(2,1)S(1)}, u32[]{:S(2)}, u32[]{:S(2)}) collective-permute-start(bf16[256,256]{1,0:T(8,128)(2,1)} %param.7), channel_id=1, source_target_pairs={{0,24},{8,16},{16,8},{24,0},{1,25},{9,17},{17,9},{25,1},{2,26},{10... | collective-permute-start | bytes 393224 | tf_op jit(solution)/shard_map/ppermute | solution.py:28
  6.2 12.0 %collective-permute-start = (bf16[256,256]{1,0:T(8,128)(2,1)}, bf16[256,256]{1,0:T(8,128)(2,1)S(1)}, u32[]{:S(2)}, u32[]{:S(2)}) collective-permute-start(bf16[256,256]{1,0:T(8,128)(2,1)} %param.7), channel_id=1, source_target_pairs={{0,16},{8,24},{16,0},{24,8},{1,17},{9,25},{17,1},{25,9},{2,18},{10... | collective-permute-start | bytes 393224 | tf_op jit(solution)/shard_map/ppermute | solution.py:28
  21.9 6.8 %collective-permute-start.5 = (bf16[256,256]{1,0:T(8,128)(2,1)S(1)}, bf16[256,256]{1,0:T(8,128)(2,1)S(1)}, u32[]{:S(2)}, u32[]{:S(2)}) collective-permute-start(bf16[256,256]{1,0:T(8,128)(2,1)S(1)} %get-tuple-element.63), channel_id=1, source_target_pairs={{0,6},{2,4},{4,2},{6,0},{1,7},{3,5},{5,3},{7,1},{8,14},{10,12},{12... | collective-permute-start | bytes 393224 | tf_op jit(solution)/shard_map/ppermute | solution.py:28
  24.4 6.8 %collective-permute-start.6 = (bf16[256,256]{1,0:T(8,128)(2,1)S(1)}, bf16[256,256]{1,0:T(8,128)(2,1)S(1)}, u32[]{:S(2)}, u32[]{:S(2)}) collective-permute-start(bf16[256,256]{1,0:T(8,128)(2,1)S(1)} %get-tuple-element.64), channel_id=1, source_target_pairs={{0,4},{2,6},{4,0},{6,2},{1,5},{3,7},{5,1},{7,3},{8,12},{10,14},{12... | collective-permute-start | bytes 393224 | tf_op jit(solution)/shard_map/ppermute | solution.py:28
  24.9 6.4 %collective-permute-start.7 = (bf16[256,256]{1,0:T(8,128)(2,1)S(1)}, bf16[256,256]{1,0:T(8,128)(2,1)S(1)}, u32[]{:S(2)}, u32[]{:S(2)}) collective-permute-start(bf16[256,256]{1,0:T(8,128)(2,1)S(1)} %sum.7), channel_id=1, source_target_pairs={{0,2},{2,0},{4,6},{6,4},{1,3},{3,1},{5,7},{7,5},{8,10},{10,8},{12,... | collective-permute-start | bytes 393224 | tf_op jit(solution)/shard_map/ppermute | solution.py:28
  31.4 7.4 %collective-permute-start.10 = (bf16[256,256]{1,0:T(8,128)(2,1)S(1)}, bf16[256,256]{1,0:T(8,128)(2,1)S(1)}, u32[]{:S(2)}, u32[]{:S(2)}) collective-permute-start(bf16[256,256]{1,0:T(8,128)(2,1)S(1)} %grad.1.refs_0_), channel_id=1, source_target_pairs={{0,6},{2,4},{4,2},{6,0},{1,7},{3,5},{5,3},{7,1},{8,14},{10,12},{12... | collective-permute-start | bytes 393224 | tf_op jit(solution)/shard_map/ppermute | solution.py:28
  33.1 7.4 %collective-permute-start.9 = (bf16[256,256]{1,0:T(8,128)(2,1)S(1)}, bf16[256,256]{1,0:T(8,128)(2,1)S(1)}, u32[]{:S(2)}, u32[]{:S(2)}) collective-permute-start(bf16[256,256]{1,0:T(8,128)(2,1)S(1)} %grad.1.refs_0_), channel_id=1, source_target_pairs={{0,4},{2,6},{4,0},{6,2},{1,5},{3,7},{5,1},{7,3},{8,12},{10,14},{12... | collective-permute-start | bytes 393224 | tf_op jit(solution)/shard_map/ppermute | solution.py:28
  34.4 6.1 %collective-permute-start.8 = (bf16[256,256]{1,0:T(8,128)(2,1)S(1)}, bf16[256,256]{1,0:T(8,128)(2,1)S(1)}, u32[]{:S(2)}, u32[]{:S(2)}) collective-permute-start(bf16[256,256]{1,0:T(8,128)(2,1)S(1)} %grad.1.refs_0_), channel_id=1, source_target_pairs={{0,2},{2,0},{4,6},{6,4},{1,3},{3,1},{5,7},{7,5},{8,10},{10,8},{12,... | collective-permute-start | bytes 393224 | tf_op jit(solution)/shard_map/ppermute | solution.py:28
  34.9 6.1 %collective-permute-start.11 = (bf16[256,256]{1,0:T(8,128)(2,1)S(1)}, bf16[256,256]{1,0:T(8,128)(2,1)S(1)}, u32[]{:S(2)}, u32[]{:S(2)}) collective-permute-start(bf16[256,256]{1,0:T(8,128)(2,1)S(1)} %grad.1.refs_0_), channel_id=1, source_target_pairs={{0,1},{1,0},{2,3},{3,2},{4,5},{5,4},{6,7},{7,6},{8,9},{9,8},{10,11... | collective-permute-start | bytes 393224 | tf_op jit(solution)/shard_map/ppermute | solution.py:28
  43.8 8.2 %collective-permute-start.23 = (bf16[3,64,256]{2,1,0:T(8,128)(2,1)S(1)}, bf16[3,64,256]{2,1,0:T(8,128)(2,1)S(1)}, u32[]{:S(2)}, u32[]{:S(2)}) collective-permute-start(bf16[3,64,256]{2,1,0:T(8,128)(2,1)S(1)} %get-tuple-element.85), channel_id=1, source_target_pairs={{0,6},{2,4},{4,2},{6,0},{1,7},{3,5},{5,3},{7,1},{8,14},{10,12},{12... | collective-permute-start | bytes 294920 | tf_op jit(solution)/shard_map/ppermute | solution.py:28
  45.7 6.9 %collective-permute-start.24 = (bf16[3,64,256]{2,1,0:T(8,128)(2,1)S(1)}, bf16[3,64,256]{2,1,0:T(8,128)(2,1)S(1)}, u32[]{:S(2)}, u32[]{:S(2)}) collective-permute-start(bf16[3,64,256]{2,1,0:T(8,128)(2,1)S(1)} %get-tuple-element.86), channel_id=1, source_target_pairs={{0,4},{2,6},{4,0},{6,2},{1,5},{3,7},{5,1},{7,3},{8,12},{10,14},{12... | collective-permute-start | bytes 294920 | tf_op jit(solution)/shard_map/ppermute | solution.py:28
  46.8 5.8 %collective-permute-start.25 = (bf16[3,64,256]{2,1,0:T(8,128)(2,1)S(1)}, bf16[3,64,256]{2,1,0:T(8,128)(2,1)S(1)}, u32[]{:S(2)}, u32[]{:S(2)}) collective-permute-start(bf16[3,64,256]{2,1,0:T(8,128)(2,1)S(1)} %get-tuple-element.87), channel_id=1, source_target_pairs={{0,2},{2,0},{4,6},{6,4},{1,3},{3,1},{5,7},{7,5},{8,10},{10,8},{12,... | collective-permute-start | bytes 294920 | tf_op jit(solution)/shard_map/ppermute | solution.py:28
  49.0 5.9 %collective-permute-start.15 = (bf16[3,64,256]{2,1,0:T(8,128)(2,1)S(1)}, bf16[3,64,256]{2,1,0:T(8,128)(2,1)S(1)}, u32[]{:S(2)}, u32[]{:S(2)}) collective-permute-start(bf16[3,64,256]{2,1,0:T(8,128)(2,1)S(1)} %get-tuple-element.79), channel_id=1, source_target_pairs={{0,6},{2,4},{4,2},{6,0},{1,7},{3,5},{5,3},{7,1},{8,14},{10,12},{12... | collective-permute-start | bytes 294920 | tf_op jit(solution)/shard_map/ppermute | solution.py:28
  51.4 5.2 %collective-permute-start.16 = (bf16[3,64,256]{2,1,0:T(8,128)(2,1)S(1)}, bf16[3,64,256]{2,1,0:T(8,128)(2,1)S(1)}, u32[]{:S(2)}, u32[]{:S(2)}) collective-permute-start(bf16[3,64,256]{2,1,0:T(8,128)(2,1)S(1)} %get-tuple-element.80), channel_id=1, source_target_pairs={{0,4},{2,6},{4,0},{6,2},{1,5},{3,7},{5,1},{7,3},{8,12},{10,14},{12... | collective-permute-start | bytes 294920 | tf_op jit(solution)/shard_map/ppermute | solution.py:28
  52.0 5.4 %collective-permute-start.17 = (bf16[3,64,256]{2,1,0:T(8,128)(2,1)S(1)}, bf16[3,64,256]{2,1,0:T(8,128)(2,1)S(1)}, u32[]{:S(2)}, u32[]{:S(2)}) collective-permute-start(bf16[3,64,256]{2,1,0:T(8,128)(2,1)S(1)} %get-tuple-element.81), channel_id=1, source_target_pairs={{0,2},{2,0},{4,6},{6,4},{1,3},{3,1},{5,7},{7,5},{8,10},{10,8},{12,... | collective-permute-start | bytes 294920 | tf_op jit(solution)/shard_map/ppermute | solution.py:28
  52.6 7.1 %collective-permute-start.26 = (bf16[3,64,256]{2,1,0:T(8,128)(2,1)S(1)}, bf16[3,64,256]{2,1,0:T(8,128)(2,1)S(1)}, u32[]{:S(2)}, u32[]{:S(2)}) collective-permute-start(bf16[3,64,256]{2,1,0:T(8,128)(2,1)S(1)} %sum.11.refs_0_), channel_id=1, source_target_pairs={{0,16},{8,24},{16,0},{24,8},{1,17},{9,25},{17,1},{25,9},{2,18},{10... | collective-permute-start | bytes 294920 | tf_op jit(solution)/shard_map/ppermute | solution.py:28
  59.8 5.0 %collective-permute-start.27 = (bf16[3,64,256]{2,1,0:T(8,128)(2,1)S(1)}, bf16[3,64,256]{2,1,0:T(8,128)(2,1)S(1)}, u32[]{:S(2)}, u32[]{:S(2)}) collective-permute-start(bf16[3,64,256]{2,1,0:T(8,128)(2,1)S(1)} %sum.12.refs_0_), channel_id=1, source_target_pairs={{0,8},{8,0},{16,24},{24,16},{1,9},{9,1},{17,25},{25,17},{2,10},{10... | collective-permute-start | bytes 294920 | tf_op jit(solution)/shard_map/ppermute | solution.py:28
  62.4 6.1 %collective-permute-start.19 = (bf16[3,64,256]{2,1,0:T(8,128)(2,1)S(1)}, bf16[3,64,256]{2,1,0:T(8,128)(2,1)S(1)}, u32[]{:S(2)}, u32[]{:S(2)}) collective-permute-start(bf16[3,64,256]{2,1,0:T(8,128)(2,1)S(1)} %sum.9.refs_0_), channel_id=1, source_target_pairs={{0,16},{8,24},{16,0},{24,8},{1,17},{9,25},{17,1},{25,9},{2,18},{10... | collective-permute-start | bytes 294920 | tf_op jit(solution)/shard_map/ppermute | solution.py:28
  64.8 6.9 %collective-permute-start.30 = (bf16[3,64,256]{2,1,0:T(8,128)(2,1)S(1)}, bf16[3,64,256]{2,1,0:T(8,128)(2,1)S(1)}, u32[]{:S(2)}, u32[]{:S(2)}) collective-permute-start(bf16[3,64,256]{2,1,0:T(8,128)(2,1)S(1)} %sum.13.refs_0_), channel_id=1, source_target_pairs={{0,6},{2,4},{4,2},{6,0},{1,7},{3,5},{5,3},{7,1},{8,14},{10,12},{12... | collective-permute-start | bytes 294920 | tf_op jit(solution)/shard_map/ppermute | solution.py:28
  66.3 6.8 %collective-permute-start.29 = (bf16[3,64,256]{2,1,0:T(8,128)(2,1)S(1)}, bf16[3,64,256]{2,1,0:T(8,128)(2,1)S(1)}, u32[]{:S(2)}, u32[]{:S(2)}) collective-permute-start(bf16[3,64,256]{2,1,0:T(8,128)(2,1)S(1)} %sum.13.refs_0_), channel_id=1, source_target_pairs={{0,4},{2,6},{4,0},{6,2},{1,5},{3,7},{5,1},{7,3},{8,12},{10,14},{12... | collective-permute-start | bytes 294920 | tf_op jit(solution)/shard_map/ppermute | solution.py:28
  67.5 5.6 %collective-permute-start.28 = (bf16[3,64,256]{2,1,0:T(8,128)(2,1)S(1)}, bf16[3,64,256]{2,1,0:T(8,128)(2,1)S(1)}, u32[]{:S(2)}, u32[]{:S(2)}) collective-permute-start(bf16[3,64,256]{2,1,0:T(8,128)(2,1)S(1)} %sum.13.refs_0_), channel_id=1, source_target_pairs={{0,2},{2,0},{4,6},{6,4},{1,3},{3,1},{5,7},{7,5},{8,10},{10,8},{12,... | collective-permute-start | bytes 294920 | tf_op jit(solution)/shard_map/ppermute | solution.py:28
  68.5 6.7 %collective-permute-start.22 = (bf16[3,64,256]{2,1,0:T(8,128)(2,1)S(1)}, bf16[3,64,256]{2,1,0:T(8,128)(2,1)S(1)}, u32[]{:S(2)}, u32[]{:S(2)}) collective-permute-start(bf16[3,64,256]{2,1,0:T(8,128)(2,1)S(1)} %sum.10.refs_0_), channel_id=1, source_target_pairs={{0,6},{2,4},{4,2},{6,0},{1,7},{3,5},{5,3},{7,1},{8,14},{10,12},{12... | collective-permute-start | bytes 294920 | tf_op jit(solution)/shard_map/ppermute | solution.py:28
  70.4 5.3 %collective-permute-start.21 = (bf16[3,64,256]{2,1,0:T(8,128)(2,1)S(1)}, bf16[3,64,256]{2,1,0:T(8,128)(2,1)S(1)}, u32[]{:S(2)}, u32[]{:S(2)}) collective-permute-start(bf16[3,64,256]{2,1,0:T(8,128)(2,1)S(1)} %sum.10.refs_0_), channel_id=1, source_target_pairs={{0,4},{2,6},{4,0},{6,2},{1,5},{3,7},{5,1},{7,3},{8,12},{10,14},{12... | collective-permute-start | bytes 294920 | tf_op jit(solution)/shard_map/ppermute | solution.py:28
  (13 other events, 39.1 us)

commit v7 on v6

--- a/solution.py
+++ b/solution.py
@@ -403,7 +403,7 @@
     )(chosen, table, count, values, rel_weight)
     lists = listings[-chunks:]
 
-    first = 1 if panels > 1 else 0
+    first = panels - 1
     sends = (panel_bf16, jax.ShapeDtypeStruct((panels - 1, own_rows, features), BF16))
     cost = pl.CostEstimate(
         flops=4 * entries * tile * tile * features, bytes_accessed=values.size, transcendentals=0
@@ -454,7 +454,7 @@
         compiler_params=vmem_for(*rest_sums, *keeps, sends[1]),
         name="chip",
     )(*(keeps[m] for m in rest), swap(given[1], "rel", 1))
-    leaving = [leaving[0], first_sum, *leaving[1:]]
+    leaving = [*leaving, first_sum]
     leaving, chosen_then = lax.optimization_barrier((leaving, chosen))
     arrived = exchange(leaving, "src")
     turned = (held[0], jax.ShapeDtypeStruct((features, slots * tile), BF16))

time: 77.7 us -> 77.2 us (level)
  starting transfers between devices: 30.9 us -> 30.1 us
  waiting for transfers between devices: 26.1 us -> 26.9 us
    ppermute x31, waiting for transfers between devices: 26.1 us -> 26.9 us  [swap(): return lax.ppermute(value, axis, partner_pairs(lax.axis_size(axis), mask))]
    ppermute x31, starting transfers between devices: 30.9 us -> 30.1 us  [swap(): return lax.ppermute(value, axis, partner_pairs(lax.axis_size(axis), mask))]
  transfers between devices with their start and end apart: 31 -> 31, of which waited for: 21 -> 20; matrix products, arithmetic and copies ran while one was open for 2% -> 2% of each run, Pallas kernels for 13% -> 12%
where the time goes in v7:
time: 77.2 us; the launch traced here: 76.9 us
  starting transfers between devices  30.1 us (39%)
  waiting for transfers between devices  26.9 us (35%)
  Pallas kernels  13.6 us (18%)
  local copies, waits for them, and re-layouts  4.07 us (5%)
  between operations  1.47 us (2%)
    ppermute x31, starting transfers between devices, swap(): return lax.ppermute(value, axis, partner_pairs(lax.axis_size(axis), mask))  30.1 us
    ppermute x31, waiting for transfers between devices, swap(): return lax.ppermute(value, axis, partner_pairs(lax.axis_size(axis), mask))  26.9 us
    unnamed x13, local copies, waits for them, and re-layouts  4.07 us
    pallas_call x2, Pallas kernels, local(): pl.pallas_call(functools.partial(weight_kernel, tile, combine), out_shape...  3.3 us
    pallas_call x2, Pallas kernels, local(): pl.pallas_call(kernel, out_shape=outs, in_specs=[SCALARS] + [WHOLE] * (le...  3.04 us
    pallas_call x1, Pallas kernels, local(): pl.pallas_call(functools.partial(turn_kernel, direct, tile, panels, len(h...  1.9 us
    pallas_call x2, Pallas kernels, spread(): pl.pallas_call(functools.partial(spread_kernel, first_relation), out_shap...  1.84 us
    pallas_call x1, Pallas kernels, local(): pl.pallas_call(functools.partial(prepare_kernel, direct, owners, slot_gro...  1.81 us
  transfers between devices with their start and end apart: 31, of which 20 were waited for; matrix products, arithmetic and copies ran while one was open for 2% of the time, Pallas kernels for 12%

profile of v7, /device:TPU:0, one launch (start us, length us, event | category | flops | bytes accessed | tf_op | source)
XLA Modules:
  0.0 76.9 jit_solution(17970931544756775997)
XLA Ops:
  0.6 3.1 %collective-permute-start.2 = (bf16[256,256]{1,0:T(8,128)(2,1)}, bf16[256,256]{1,0:T(8,128)(2,1)S(1)}, u32[]{:S(2)}, u32[]{:S(2)}) collective-permute-start(bf16[256,256]{1,0:T(8,128)(2,1)} %param.7), channel_id=1, source_target_pairs={{0,8},{8,0},{16,24},{24,16},{1,9},{9,1},{17,25},{25,17},{2,10},{10... | collective-permute-start | bytes 393224 | tf_op jit(solution)/shard_map/ppermute | solution.py:28
  3.7 2.5 %collective-permute-start.1 = (bf16[256,256]{1,0:T(8,128)(2,1)}, bf16[256,256]{1,0:T(8,128)(2,1)S(1)}, u32[]{:S(2)}, u32[]{:S(2)}) collective-permute-start(bf16[256,256]{1,0:T(8,128)(2,1)} %param.7), channel_id=1, source_target_pairs={{0,24},{8,16},{16,8},{24,0},{1,25},{9,17},{17,9},{25,1},{2,26},{10... | collective-permute-start | bytes 393224 | tf_op jit(solution)/shard_map/ppermute | solution.py:28
  7.6 1.6 %copy-done = bf16[1,1,1,64,128,128]{5,4,3,2,1,0:T(8,128)(2,1)S(1)} copy-done((bf16[1,1,1,64,128,128]{5,4,3,2,1,0:T(8,128)(2,1)S(1)}, bf16[1,1,1,64,128,128]{5,4,3,2,1,0:T(8,128)(2,1)}, u32[]{:S(2)}) %copy-start) | copy-done | bytes 2097176
  11.0 1.8 %prepare.1 = (bf16[64,128,128]{2,1,0:T(8,128)(2,1)S(1)}, bf16[6,256,256]{2,1,0:T(8,128)(2,1)S(1)}, s32[67]{0:T(128)S(1)}, s32[67]{0:T(128)S(1)}, s32[67]{0:T(128...) custom-call(s32[4]{0:T(128)S(1)} %bitcast.21, s32[3,64]{1,0:T(4,128)S(1)} %bitcast.20, ...), custom_call_target="tpu_custom_call" | custom-call | bytes 4194304 | tf_op jit(solution)/shard_map/prepare/pallas_call | solution.py:392
  12.9 1.5 %forward.2.refs_4_ = f32[17,128,256]{2,1,0:T(8,128)S(1)} custom-call(s32[67]{0:T(128)S(1)} %get-tuple-element.49.order, bf16[1,256,256]{2,1,0:T(8,128)(2,1)S(1)} %bitcast.12, bf16[1,256,256]{2,1,0:T(8,128)(2,1)S(1)} %bitcast.14, bf16[6,256,256]{2,1,0:T(8,128)(2,1)S(1)} %get-tuple-element.47.refs_2_.weight, ...), custom_call_target="tpu_custom_call", output_to_operand_aliasing={{}: (5, {})} | custom-call | flops 1073741824 | bytes 1048576 | tf_op jit(solution)/shard_map/forward/pallas_call | solution.py:424
  14.4 3.8 %collective-permute-done = bf16[256,256]{1,0:T(8,128)(2,1)S(1)} collective-permute-done((bf16[256,256]{1,0:T(8,128)(2,1)}, bf16[256,256]{1,0:T(8,128)(2,1)S(1)}, u32[]{:S(2)}, u32[]{:S(2)}) %collective-permute-start) | collective-permute-done | bytes 131104 | tf_op jit(solution)/shard_map/ppermute | solution.py:28
  18.2 1.5 %forward.3 = (f32[17,128,256]{2,1,0:T(8,128)S(1)}, bf16[12,256,256]{2,1,0:T(8,128)(2,1)S(1)}, bf16[256,256]{1,0:T(8,128)(2,1)S(1)}, bf16[3,256,256]{2,1,0:T(8,128)(2,1)S(1)}) custom-call(s32[67]{0:T(128)S(1)} %get-tuple-element.46.order, bf16[1,256,256]{2,1,0:T(8,128)(2,1)S(1)} %bitcast.18, ...), custom_call_target="tpu_custom_call", output_to_operand_aliasing={{0}: (5, {})} | custom-call | flops 1073741824 | bytes 1048576 | tf_op jit(solution)/shard_map/forward/pallas_call | solution.py:424
  21.8 2.5 %collective-permute-start.5 = (bf16[256,256]{1,0:T(8,128)(2,1)S(1)}, bf16[256,256]{1,0:T(8,128)(2,1)S(1)}, u32[]{:S(2)}, u32[]{:S(2)}) collective-permute-start(bf16[256,256]{1,0:T(8,128)(2,1)S(1)} %sum.7), channel_id=1, source_target_pairs={{0,6},{2,4},{4,2},{6,0},{1,7},{3,5},{5,3},{7,1},{8,14},{10,12},{12... | collective-permute-start | bytes 393224 | tf_op jit(solution)/shard_map/ppermute | solution.py:28
  25.4 1.9 %turn.1 = (bf16[64,128,128]{2,1,0:T(8,128)(2,1)S(1)}, bf16[256,512]{1,0:T(8,128)(2,1)S(1)}, f32[13,128,256]{2,1,0:T(8,128)S(1)}, f32[13,128,256]{2,1,0:T(8,128)S(1)}) custom-call(s32[4]{0:T(128)S(1)} %bitcast.22, bf16[64,128,128]{2,1,0:T(8,128)(2,1)S(1)} %get-tuple-element.48.refs_3_.values, bf16[1,256,256]{2,1,0:T(8,128)(2,1)S(1)} %bitcast.13, ...), custom_call_target="tpu_custom_call" | custom-call | bytes 4194304 | tf_op jit(solution)/shard_map/turn/pallas_call | solution.py:461
  28.6 2.5 %collective-permute-done.6.second = bf16[256,256]{1,0:T(8,128)(2,1)S(1)} collective-permute-done((bf16[256,256]{1,0:T(8,128)(2,1)S(1)}, bf16[256,256]{1,0:T(8,128)(2,1)S(1)}, u32[]{:S(2)}, u32[]{:S(2)}) %collective-permute-start.6) | collective-permute-done | bytes 131104 | tf_op jit(solution)/shard_map/ppermute | solution.py:28
  31.4 1.7 %collective-permute-start.10 = (bf16[256,256]{1,0:T(8,128)(2,1)S(1)}, bf16[256,256]{1,0:T(8,128)(2,1)S(1)}, u32[]{:S(2)}, u32[]{:S(2)}) collective-permute-start(bf16[256,256]{1,0:T(8,128)(2,1)S(1)} %grad.1.refs_0_), channel_id=1, source_target_pairs={{0,6},{2,4},{4,2},{6,0},{1,7},{3,5},{5,3},{7,1},{8,14},{10,12},{12... | collective-permute-start | bytes 393224 | tf_op jit(solution)/shard_map/ppermute | solution.py:28
  34.9 3.8 %collective-permute-done.10.refs_3_ = bf16[256,256]{1,0:T(8,128)(2,1)S(1)} collective-permute-done((bf16[256,256]{1,0:T(8,128)(2,1)S(1)}, bf16[256,256]{1,0:T(8,128)(2,1)S(1)}, u32[]{:S(2)}, u32[]{:S(2)}) %collective-permute-start.10) | collective-permute-done | bytes 131104 | tf_op jit(solution)/shard_map/ppermute | solution.py:28
  38.7 1.7 %collective-permute-done.9.refs_2_ = bf16[256,256]{1,0:T(8,128)(2,1)S(1)} collective-permute-done((bf16[256,256]{1,0:T(8,128)(2,1)S(1)}, bf16[256,256]{1,0:T(8,128)(2,1)S(1)}, u32[]{:S(2)}, u32[]{:S(2)}) %collective-permute-start.9) | collective-permute-done | bytes 131104 | tf_op jit(solution)/shard_map/ppermute | solution.py:28
  42.1 1.7 %weight_terms.3 = (f32[3,64,256]{2,1,0:T(8,128)S(1)}, bf16[3,64,256]{2,1,0:T(8,128)(2,1)S(1)}, bf16[3,64,256]{2,1,0:T(8,128)(2,1)S(1)}, bf16[3,64,256]{2,1,0:T(8,128)(2,1)S(1)}, f32[13,128,256]{2,1,0:T(8,128)S(1)}) custom-call(s32[65]{0:T(128)S(1)} %get-tuple-element.82.listed, ...), custom_call_target="tpu_custom_call", output_to_operand_aliasing={{4}: (4, {})} | custom-call | tf_op jit(solution)/shard_map/weight_terms/pallas_call | solution.py:507
  45.1 1.7 %collective-permute-start.24 = (bf16[3,64,256]{2,1,0:T(8,128)(2,1)S(1)}, bf16[3,64,256]{2,1,0:T(8,128)(2,1)S(1)}, u32[]{:S(2)}, u32[]{:S(2)}) collective-permute-start(bf16[3,64,256]{2,1,0:T(8,128)(2,1)S(1)} %get-tuple-element.86), channel_id=1, source_target_pairs={{0,4},{2,6},{4,0},{6,2},{1,5},{3,7},{5,1},{7,3},{8,12},{10,14},{12... | collective-permute-start | bytes 294920 | tf_op jit(solution)/shard_map/ppermute | solution.py:28
  47.3 1.6 %weight_terms.2 = (f32[3,64,256]{2,1,0:T(8,128)S(1)}, bf16[3,64,256]{2,1,0:T(8,128)(2,1)S(1)}, bf16[3,64,256]{2,1,0:T(8,128)(2,1)S(1)}, bf16[3,64,256]{2,1,0:T(8,128)(2,1)S(1)}, f32[13,128,256]{2,1,0:T(8,128)S(1)}) custom-call(s32[65]{0:T(128)S(1)} %get-tuple-element.74.listed, ...), custom_call_target="tpu_custom_call", output_to_operand_aliasing={{4}: (4, {})} | custom-call | tf_op jit(solution)/shard_map/weight_terms/pallas_call | solution.py:507
  49.0 1.5 %collective-permute-start.15 = (bf16[3,64,256]{2,1,0:T(8,128)(2,1)S(1)}, bf16[3,64,256]{2,1,0:T(8,128)(2,1)S(1)}, u32[]{:S(2)}, u32[]{:S(2)}) collective-permute-start(bf16[3,64,256]{2,1,0:T(8,128)(2,1)S(1)} %get-tuple-element.79), channel_id=1, source_target_pairs={{0,6},{2,4},{4,2},{6,0},{1,7},{3,5},{5,3},{7,1},{8,14},{10,12},{12... | collective-permute-start | bytes 294920 | tf_op jit(solution)/shard_map/ppermute | solution.py:28
  53.2 2.0 %collective-permute-done.15.refs_1_ = bf16[3,64,256]{2,1,0:T(8,128)(2,1)S(1)} collective-permute-done((bf16[3,64,256]{2,1,0:T(8,128)(2,1)S(1)}, bf16[3,64,256]{2,1,0:T(8,128)(2,1)S(1)}, u32[]{:S(2)}, u32[]{:S(2)}) %collective-permute-start.15) | collective-permute-done | bytes 98336 | tf_op jit(solution)/shard_map/ppermute | solution.py:28
  55.1 1.6 %collective-permute-done.16.refs_2_ = bf16[3,64,256]{2,1,0:T(8,128)(2,1)S(1)} collective-permute-done((bf16[3,64,256]{2,1,0:T(8,128)(2,1)S(1)}, bf16[3,64,256]{2,1,0:T(8,128)(2,1)S(1)}, u32[]{:S(2)}, u32[]{:S(2)}) %collective-permute-start.16) | collective-permute-done | bytes 98336 | tf_op jit(solution)/shard_map/ppermute | solution.py:28
  57.2 2.6 %collective-permute-done.26.refs_1_ = bf16[3,64,256]{2,1,0:T(8,128)(2,1)S(1)} collective-permute-done((bf16[3,64,256]{2,1,0:T(8,128)(2,1)S(1)}, bf16[3,64,256]{2,1,0:T(8,128)(2,1)S(1)}, u32[]{:S(2)}, u32[]{:S(2)}) %collective-permute-start.26) | collective-permute-done | bytes 98336 | tf_op jit(solution)/shard_map/ppermute | solution.py:28
  59.9 2.0 %collective-permute-done.18.refs_1_ = bf16[3,64,256]{2,1,0:T(8,128)(2,1)S(1)} collective-permute-done((bf16[3,64,256]{2,1,0:T(8,128)(2,1)S(1)}, bf16[3,64,256]{2,1,0:T(8,128)(2,1)S(1)}, u32[]{:S(2)}, u32[]{:S(2)}) %collective-permute-start.18) | collective-permute-done | bytes 98336 | tf_op jit(solution)/shard_map/ppermute | solution.py:28
  62.8 1.7 %collective-permute-done.27.refs_1_ = bf16[3,64,256]{2,1,0:T(8,128)(2,1)S(1)} collective-permute-done((bf16[3,64,256]{2,1,0:T(8,128)(2,1)S(1)}, bf16[3,64,256]{2,1,0:T(8,128)(2,1)S(1)}, u32[]{:S(2)}, u32[]{:S(2)}) %collective-permute-start.27) | collective-permute-done | bytes 98336 | tf_op jit(solution)/shard_map/ppermute | solution.py:28
  64.5 1.6 %collective-permute-start.30 = (bf16[3,64,256]{2,1,0:T(8,128)(2,1)S(1)}, bf16[3,64,256]{2,1,0:T(8,128)(2,1)S(1)}, u32[]{:S(2)}, u32[]{:S(2)}) collective-permute-start(bf16[3,64,256]{2,1,0:T(8,128)(2,1)S(1)} %sum.13.refs_0_), channel_id=1, source_target_pairs={{0,6},{2,4},{4,2},{6,0},{1,7},{3,5},{5,3},{7,1},{8,14},{10,12},{12... | collective-permute-start | bytes 294920 | tf_op jit(solution)/shard_map/ppermute | solution.py:28
  68.7 1.6 %collective-permute-start.22 = (bf16[3,64,256]{2,1,0:T(8,128)(2,1)S(1)}, bf16[3,64,256]{2,1,0:T(8,128)(2,1)S(1)}, u32[]{:S(2)}, u32[]{:S(2)}) collective-permute-start(bf16[3,64,256]{2,1,0:T(8,128)(2,1)S(1)} %sum.10.refs_0_), channel_id=1, source_target_pairs={{0,6},{2,4},{4,2},{6,0},{1,7},{3,5},{5,3},{7,1},{8,14},{10,12},{12... | collective-permute-start | bytes 294920 | tf_op jit(solution)/shard_map/ppermute | solution.py:28
  (71 shorter events, 25.9 us)
Async XLA Ops:
  0.6 12.2 %collective-permute-start.2 = (bf16[256,256]{1,0:T(8,128)(2,1)}, bf16[256,256]{1,0:T(8,128)(2,1)S(1)}, u32[]{:S(2)}, u32[]{:S(2)}) collective-permute-start(bf16[256,256]{1,0:T(8,128)(2,1)} %param.7), channel_id=1, source_target_pairs={{0,8},{8,0},{16,24},{24,16},{1,9},{9,1},{17,25},{25,17},{2,10},{10... | collective-permute-start | bytes 393224 | tf_op jit(solution)/shard_map/ppermute | solution.py:28
  3.7 10.7 %collective-permute-start.1 = (bf16[256,256]{1,0:T(8,128)(2,1)}, bf16[256,256]{1,0:T(8,128)(2,1)S(1)}, u32[]{:S(2)}, u32[]{:S(2)}) collective-permute-start(bf16[256,256]{1,0:T(8,128)(2,1)} %param.7), channel_id=1, source_target_pairs={{0,24},{8,16},{16,8},{24,0},{1,25},{9,17},{17,9},{25,1},{2,26},{10... | collective-permute-start | bytes 393224 | tf_op jit(solution)/shard_map/ppermute | solution.py:28
  6.2 12.0 %collective-permute-start = (bf16[256,256]{1,0:T(8,128)(2,1)}, bf16[256,256]{1,0:T(8,128)(2,1)S(1)}, u32[]{:S(2)}, u32[]{:S(2)}) collective-permute-start(bf16[256,256]{1,0:T(8,128)(2,1)} %param.7), channel_id=1, source_target_pairs={{0,16},{8,24},{16,0},{24,8},{1,17},{9,25},{17,1},{25,9},{2,18},{10... | collective-permute-start | bytes 393224 | tf_op jit(solution)/shard_map/ppermute | solution.py:28
  21.8 6.8 %collective-permute-start.5 = (bf16[256,256]{1,0:T(8,128)(2,1)S(1)}, bf16[256,256]{1,0:T(8,128)(2,1)S(1)}, u32[]{:S(2)}, u32[]{:S(2)}) collective-permute-start(bf16[256,256]{1,0:T(8,128)(2,1)S(1)} %sum.7), channel_id=1, source_target_pairs={{0,6},{2,4},{4,2},{6,0},{1,7},{3,5},{5,3},{7,1},{8,14},{10,12},{12... | collective-permute-start | bytes 393224 | tf_op jit(solution)/shard_map/ppermute | solution.py:28
  24.3 6.8 %collective-permute-start.6 = (bf16[256,256]{1,0:T(8,128)(2,1)S(1)}, bf16[256,256]{1,0:T(8,128)(2,1)S(1)}, u32[]{:S(2)}, u32[]{:S(2)}) collective-permute-start(bf16[256,256]{1,0:T(8,128)(2,1)S(1)} %get-tuple-element.64), channel_id=1, source_target_pairs={{0,4},{2,6},{4,0},{6,2},{1,5},{3,7},{5,1},{7,3},{8,12},{10,14},{12... | collective-permute-start | bytes 393224 | tf_op jit(solution)/shard_map/ppermute | solution.py:28
  24.9 6.4 %collective-permute-start.7 = (bf16[256,256]{1,0:T(8,128)(2,1)S(1)}, bf16[256,256]{1,0:T(8,128)(2,1)S(1)}, u32[]{:S(2)}, u32[]{:S(2)}) collective-permute-start(bf16[256,256]{1,0:T(8,128)(2,1)S(1)} %get-tuple-element.65), channel_id=1, source_target_pairs={{0,2},{2,0},{4,6},{6,4},{1,3},{3,1},{5,7},{7,5},{8,10},{10,8},{12,... | collective-permute-start | bytes 393224 | tf_op jit(solution)/shard_map/ppermute | solution.py:28
  31.4 7.4 %collective-permute-start.10 = (bf16[256,256]{1,0:T(8,128)(2,1)S(1)}, bf16[256,256]{1,0:T(8,128)(2,1)S(1)}, u32[]{:S(2)}, u32[]{:S(2)}) collective-permute-start(bf16[256,256]{1,0:T(8,128)(2,1)S(1)} %grad.1.refs_0_), channel_id=1, source_target_pairs={{0,6},{2,4},{4,2},{6,0},{1,7},{3,5},{5,3},{7,1},{8,14},{10,12},{12... | collective-permute-start | bytes 393224 | tf_op jit(solution)/shard_map/ppermute | solution.py:28
  33.1 7.4 %collective-permute-start.9 = (bf16[256,256]{1,0:T(8,128)(2,1)S(1)}, bf16[256,256]{1,0:T(8,128)(2,1)S(1)}, u32[]{:S(2)}, u32[]{:S(2)}) collective-permute-start(bf16[256,256]{1,0:T(8,128)(2,1)S(1)} %grad.1.refs_0_), channel_id=1, source_target_pairs={{0,4},{2,6},{4,0},{6,2},{1,5},{3,7},{5,1},{7,3},{8,12},{10,14},{12... | collective-permute-start | bytes 393224 | tf_op jit(solution)/shard_map/ppermute | solution.py:28
  34.4 6.1 %collective-permute-start.8 = (bf16[256,256]{1,0:T(8,128)(2,1)S(1)}, bf16[256,256]{1,0:T(8,128)(2,1)S(1)}, u32[]{:S(2)}, u32[]{:S(2)}) collective-permute-start(bf16[256,256]{1,0:T(8,128)(2,1)S(1)} %grad.1.refs_0_), channel_id=1, source_target_pairs={{0,2},{2,0},{4,6},{6,4},{1,3},{3,1},{5,7},{7,5},{8,10},{10,8},{12,... | collective-permute-start | bytes 393224 | tf_op jit(solution)/shard_map/ppermute | solution.py:28
  34.9 6.1 %collective-permute-start.11 = (bf16[256,256]{1,0:T(8,128)(2,1)S(1)}, bf16[256,256]{1,0:T(8,128)(2,1)S(1)}, u32[]{:S(2)}, u32[]{:S(2)}) collective-permute-start(bf16[256,256]{1,0:T(8,128)(2,1)S(1)} %grad.1.refs_0_), channel_id=1, source_target_pairs={{0,1},{1,0},{2,3},{3,2},{4,5},{5,4},{6,7},{7,6},{8,9},{9,8},{10,11... | collective-permute-start | bytes 393224 | tf_op jit(solution)/shard_map/ppermute | solution.py:28
  43.8 7.9 %collective-permute-start.23 = (bf16[3,64,256]{2,1,0:T(8,128)(2,1)S(1)}, bf16[3,64,256]{2,1,0:T(8,128)(2,1)S(1)}, u32[]{:S(2)}, u32[]{:S(2)}) collective-permute-start(bf16[3,64,256]{2,1,0:T(8,128)(2,1)S(1)} %get-tuple-element.85), channel_id=1, source_target_pairs={{0,6},{2,4},{4,2},{6,0},{1,7},{3,5},{5,3},{7,1},{8,14},{10,12},{12... | collective-permute-start | bytes 294920 | tf_op jit(solution)/shard_map/ppermute | solution.py:28
  45.1 7.9 %collective-permute-start.24 = (bf16[3,64,256]{2,1,0:T(8,128)(2,1)S(1)}, bf16[3,64,256]{2,1,0:T(8,128)(2,1)S(1)}, u32[]{:S(2)}, u32[]{:S(2)}) collective-permute-start(bf16[3,64,256]{2,1,0:T(8,128)(2,1)S(1)} %get-tuple-element.86), channel_id=1, source_target_pairs={{0,4},{2,6},{4,0},{6,2},{1,5},{3,7},{5,1},{7,3},{8,12},{10,14},{12... | collective-permute-start | bytes 294920 | tf_op jit(solution)/shard_map/ppermute | solution.py:28
  46.8 6.3 %collective-permute-start.25 = (bf16[3,64,256]{2,1,0:T(8,128)(2,1)S(1)}, bf16[3,64,256]{2,1,0:T(8,128)(2,1)S(1)}, u32[]{:S(2)}, u32[]{:S(2)}) collective-permute-start(bf16[3,64,256]{2,1,0:T(8,128)(2,1)S(1)} %get-tuple-element.87), channel_id=1, source_target_pairs={{0,2},{2,0},{4,6},{6,4},{1,3},{3,1},{5,7},{7,5},{8,10},{10,8},{12,... | collective-permute-start | bytes 294920 | tf_op jit(solution)/shard_map/ppermute | solution.py:28
  49.0 6.2 %collective-permute-start.15 = (bf16[3,64,256]{2,1,0:T(8,128)(2,1)S(1)}, bf16[3,64,256]{2,1,0:T(8,128)(2,1)S(1)}, u32[]{:S(2)}, u32[]{:S(2)}) collective-permute-start(bf16[3,64,256]{2,1,0:T(8,128)(2,1)S(1)} %get-tuple-element.79), channel_id=1, source_target_pairs={{0,6},{2,4},{4,2},{6,0},{1,7},{3,5},{5,3},{7,1},{8,14},{10,12},{12... | collective-permute-start | bytes 294920 | tf_op jit(solution)/shard_map/ppermute | solution.py:28
  50.5 6.2 %collective-permute-start.16 = (bf16[3,64,256]{2,1,0:T(8,128)(2,1)S(1)}, bf16[3,64,256]{2,1,0:T(8,128)(2,1)S(1)}, u32[]{:S(2)}, u32[]{:S(2)}) collective-permute-start(bf16[3,64,256]{2,1,0:T(8,128)(2,1)S(1)} %get-tuple-element.80), channel_id=1, source_target_pairs={{0,4},{2,6},{4,0},{6,2},{1,5},{3,7},{5,1},{7,3},{8,12},{10,14},{12... | collective-permute-start | bytes 294920 | tf_op jit(solution)/shard_map/ppermute | solution.py:28
  51.7 5.1 %collective-permute-start.17 = (bf16[3,64,256]{2,1,0:T(8,128)(2,1)S(1)}, bf16[3,64,256]{2,1,0:T(8,128)(2,1)S(1)}, u32[]{:S(2)}, u32[]{:S(2)}) collective-permute-start(bf16[3,64,256]{2,1,0:T(8,128)(2,1)S(1)} %get-tuple-element.81), channel_id=1, source_target_pairs={{0,2},{2,0},{4,6},{6,4},{1,3},{3,1},{5,7},{7,5},{8,10},{10,8},{12,... | collective-permute-start | bytes 294920 | tf_op jit(solution)/shard_map/ppermute | solution.py:28
  53.1 6.7 %collective-permute-start.26 = (bf16[3,64,256]{2,1,0:T(8,128)(2,1)S(1)}, bf16[3,64,256]{2,1,0:T(8,128)(2,1)S(1)}, u32[]{:S(2)}, u32[]{:S(2)}) collective-permute-start(bf16[3,64,256]{2,1,0:T(8,128)(2,1)S(1)} %sum.11.refs_0_), channel_id=1, source_target_pairs={{0,16},{8,24},{16,0},{24,8},{1,17},{9,25},{17,1},{25,9},{2,18},{10... | collective-permute-start | bytes 294920 | tf_op jit(solution)/shard_map/ppermute | solution.py:28
  56.8 5.1 %collective-permute-start.18 = (bf16[3,64,256]{2,1,0:T(8,128)(2,1)S(1)}, bf16[3,64,256]{2,1,0:T(8,128)(2,1)S(1)}, u32[]{:S(2)}, u32[]{:S(2)}) collective-permute-start(bf16[3,64,256]{2,1,0:T(8,128)(2,1)S(1)} %sum.8.refs_0_), channel_id=1, source_target_pairs={{0,8},{8,0},{16,24},{24,16},{1,9},{9,1},{17,25},{25,17},{2,10},{10... | collective-permute-start | bytes 294920 | tf_op jit(solution)/shard_map/ppermute | solution.py:28
  61.9 6.8 %collective-permute-start.19 = (bf16[3,64,256]{2,1,0:T(8,128)(2,1)S(1)}, bf16[3,64,256]{2,1,0:T(8,128)(2,1)S(1)}, u32[]{:S(2)}, u32[]{:S(2)}) collective-permute-start(bf16[3,64,256]{2,1,0:T(8,128)(2,1)S(1)} %sum.9.refs_0_), channel_id=1, source_target_pairs={{0,16},{8,24},{16,0},{24,8},{1,17},{9,25},{17,1},{25,9},{2,18},{10... | collective-permute-start | bytes 294920 | tf_op jit(solution)/shard_map/ppermute | solution.py:28
  64.5 6.5 %collective-permute-start.30 = (bf16[3,64,256]{2,1,0:T(8,128)(2,1)S(1)}, bf16[3,64,256]{2,1,0:T(8,128)(2,1)S(1)}, u32[]{:S(2)}, u32[]{:S(2)}) collective-permute-start(bf16[3,64,256]{2,1,0:T(8,128)(2,1)S(1)} %sum.13.refs_0_), channel_id=1, source_target_pairs={{0,6},{2,4},{4,2},{6,0},{1,7},{3,5},{5,3},{7,1},{8,14},{10,12},{12... | collective-permute-start | bytes 294920 | tf_op jit(solution)/shard_map/ppermute | solution.py:28
  66.1 7.0 %collective-permute-start.29 = (bf16[3,64,256]{2,1,0:T(8,128)(2,1)S(1)}, bf16[3,64,256]{2,1,0:T(8,128)(2,1)S(1)}, u32[]{:S(2)}, u32[]{:S(2)}) collective-permute-start(bf16[3,64,256]{2,1,0:T(8,128)(2,1)S(1)} %sum.13.refs_0_), channel_id=1, source_target_pairs={{0,4},{2,6},{4,0},{6,2},{1,5},{3,7},{5,1},{7,3},{8,12},{10,14},{12... | collective-permute-start | bytes 294920 | tf_op jit(solution)/shard_map/ppermute | solution.py:28
  67.3 6.1 %collective-permute-start.28 = (bf16[3,64,256]{2,1,0:T(8,128)(2,1)S(1)}, bf16[3,64,256]{2,1,0:T(8,128)(2,1)S(1)}, u32[]{:S(2)}, u32[]{:S(2)}) collective-permute-start(bf16[3,64,256]{2,1,0:T(8,128)(2,1)S(1)} %sum.13.refs_0_), channel_id=1, source_target_pairs={{0,2},{2,0},{4,6},{6,4},{1,3},{3,1},{5,7},{7,5},{8,10},{10,8},{12,... | collective-permute-start | bytes 294920 | tf_op jit(solution)/shard_map/ppermute | solution.py:28
  68.7 6.7 %collective-permute-start.22 = (bf16[3,64,256]{2,1,0:T(8,128)(2,1)S(1)}, bf16[3,64,256]{2,1,0:T(8,128)(2,1)S(1)}, u32[]{:S(2)}, u32[]{:S(2)}) collective-permute-start(bf16[3,64,256]{2,1,0:T(8,128)(2,1)S(1)} %sum.10.refs_0_), channel_id=1, source_target_pairs={{0,6},{2,4},{4,2},{6,0},{1,7},{3,5},{5,3},{7,1},{8,14},{10,12},{12... | collective-permute-start | bytes 294920 | tf_op jit(solution)/shard_map/ppermute | solution.py:28
  70.3 5.4 %collective-permute-start.21 = (bf16[3,64,256]{2,1,0:T(8,128)(2,1)S(1)}, bf16[3,64,256]{2,1,0:T(8,128)(2,1)S(1)}, u32[]{:S(2)}, u32[]{:S(2)}) collective-permute-start(bf16[3,64,256]{2,1,0:T(8,128)(2,1)S(1)} %sum.10.refs_0_), channel_id=1, source_target_pairs={{0,4},{2,6},{4,0},{6,2},{1,5},{3,7},{5,1},{7,3},{8,12},{10,14},{12... | collective-permute-start | bytes 294920 | tf_op jit(solution)/shard_map/ppermute | solution.py:28
  (13 other events, 38.4 us)

commit v8 on v7

--- a/solution.py
+++ b/solution.py
@@ -112,14 +112,12 @@
     add_entries(combine, values, weight, projected, order, order[entries], pre)
 
 
-def theirs_kernel(tile, combine, owners, first, order, *refs):
-    near_kernel(tile, combine, order, *refs[:-2])
-    pre, sends = refs[-4], refs[-2:]
-    panels = sends[1].shape[0] + 1
-    others = [m for m in range(panels) if m != first]
-    for out, distance in ((sends[0], first), *((sends[1].at[i], m) for i, m in enumerate(others))):
+def theirs_kernel(tile, combine, owners, order, *refs):
+    near_kernel(tile, combine, order, *refs[:-1])
+    pre, sends = refs[-3], refs[-1]
+    for distance in range(sends.shape[0]):
         for rows, block in blocks_of(tile, owners, here(), distance, 1):
-            out[rows, :] = pre[block].astype(BF16)
+            sends[distance, rows, :] = pre[block].astype(BF16)
 
 
 def ours_kernel(tile, combine, owners, order, projected, weight, values, before, pre, *keeps):
@@ -403,8 +401,7 @@
     )(chosen, table, count, values, rel_weight)
     lists = listings[-chunks:]
 
-    first = panels - 1
-    sends = (panel_bf16, jax.ShapeDtypeStruct((panels - 1, own_rows, features), BF16))
+    sends = (jax.ShapeDtypeStruct((panels, own_rows, features), BF16),)
     cost = pl.CostEstimate(
         flops=4 * entries * tile * tile * features, bytes_accessed=values.size, transcendentals=0
     )
@@ -419,7 +416,7 @@
         )
         kernel = functools.partial(near_kernel, tile, combine)
         if last:
-            kernel = functools.partial(theirs_kernel, tile, combine, owners, first)
+            kernel = functools.partial(theirs_kernel, tile, combine, owners)
         outs = (pre_sums, projected, *sends) if last else (pre_sums,)
         pre, *given = pl.pallas_call(
             kernel,
@@ -443,18 +440,15 @@
         cost_estimate=cost,
         name="forward_ours",
     )(listings[len(slot_groups) - 1], projected, rel_weight, values, pre)
-    first_sum = summed([keeps[first], swap(given[0], "rel", 1)])
-    rest = [m for m in range(panels) if m != first]
-    rest_sums = (panel_f32,) + (panel_bf16,) * (panels - 2)
+    panel_sums = (panel_f32,) + (panel_bf16,) * (panels - 1)
     leaving = pl.pallas_call(
         chip_kernel,
-        out_shape=rest_sums,
-        in_specs=[WHOLE] * panels,
-        out_specs=(WHOLE,) * (panels - 1),
-        compiler_params=vmem_for(*rest_sums, *keeps, sends[1]),
+        out_shape=panel_sums,
+        in_specs=[WHOLE] * (panels + 1),
+        out_specs=(WHOLE,) * panels,
+        compiler_params=vmem_for(*panel_sums, *keeps, *sends),
         name="chip",
-    )(*(keeps[m] for m in rest), swap(given[1], "rel", 1))
-    leaving = [*leaving, first_sum]
+    )(*keeps, swap(given[0], "rel", 1))
     leaving, chosen_then = lax.optimization_barrier((leaving, chosen))
     arrived = exchange(leaving, "src")
     turned = (held[0], jax.ShapeDtypeStruct((features, slots * tile), BF16))

time: 77.2 us -> 77.6 us (level)
  waiting for transfers between devices: 26.9 us -> 28.1 us
    ppermute x31 -> x30, waiting for transfers between devices: 26.9 us -> 28.1 us  [swap(): return lax.ppermute(value, axis, partner_pairs(lax.axis_size(axis), mask))]
    ppermute x31 -> x30, starting transfers between devices: 30.1 us -> 29.4 us  [swap(): return lax.ppermute(value, axis, partner_pairs(lax.axis_size(axis), mask))]
  transfers between devices with their start and end apart: 31 -> 30, of which waited for: 20 -> 18; matrix products, arithmetic and copies ran while one was open for 2% -> 2% of each run, Pallas kernels for 12% -> 12%
where the time goes in v8:
time: 77.6 us; the launch traced here: 77.3 us
  starting transfers between devices  29.4 us (38%)
  waiting for transfers between devices  28.1 us (36%)
  Pallas kernels  13.5 us (17%)
  local copies, waits for them, and re-layouts  4.07 us (5%)
  between operations  1.46 us (2%)
    ppermute x30, starting transfers between devices, swap(): return lax.ppermute(value, axis, partner_pairs(lax.axis_size(axis), mask))  29.4 us
    ppermute x30, waiting for transfers between devices, swap(): return lax.ppermute(value, axis, partner_pairs(lax.axis_size(axis), mask))  28.1 us
    unnamed x13, local copies, waits for them, and re-layouts  4.07 us
    pallas_call x2, Pallas kernels, local(): pl.pallas_call(functools.partial(weight_kernel, tile, combine), out_shape...  3.3 us
    pallas_call x2, Pallas kernels, local(): pl.pallas_call(kernel, out_shape=outs, in_specs=[SCALARS] + [WHOLE] * (le...  3.04 us
    pallas_call x1, Pallas kernels, local(): pl.pallas_call(functools.partial(turn_kernel, direct, tile, panels, len(h...  1.9 us
    pallas_call x2, Pallas kernels, spread(): pl.pallas_call(functools.partial(spread_kernel, first_relation), out_shap...  1.84 us
    pallas_call x1, Pallas kernels, local(): pl.pallas_call(functools.partial(prepare_kernel, direct, owners, slot_gro...  1.71 us
  transfers between devices with their start and end apart: 30, of which 18 were waited for; matrix products, arithmetic and copies ran while one was open for 2% of the time, Pallas kernels for 12%

profile of v8, /device:TPU:0, one launch (start us, length us, event | category | flops | bytes accessed | tf_op | source)
XLA Modules:
  0.0 77.3 jit_solution(1377678701190694915)
XLA Ops:
  0.6 3.1 %collective-permute-start.2 = (bf16[256,256]{1,0:T(8,128)(2,1)}, bf16[256,256]{1,0:T(8,128)(2,1)S(1)}, u32[]{:S(2)}, u32[]{:S(2)}) collective-permute-start(bf16[256,256]{1,0:T(8,128)(2,1)} %param.7), channel_id=1, source_target_pairs={{0,8},{8,0},{16,24},{24,16},{1,9},{9,1},{17,25},{25,17},{2,10},{10... | collective-permute-start | bytes 393224 | tf_op jit(solution)/shard_map/ppermute | solution.py:28
  3.7 2.5 %collective-permute-start.1 = (bf16[256,256]{1,0:T(8,128)(2,1)}, bf16[256,256]{1,0:T(8,128)(2,1)S(1)}, u32[]{:S(2)}, u32[]{:S(2)}) collective-permute-start(bf16[256,256]{1,0:T(8,128)(2,1)} %param.7), channel_id=1, source_target_pairs={{0,24},{8,16},{16,8},{24,0},{1,25},{9,17},{17,9},{25,1},{2,26},{10... | collective-permute-start | bytes 393224 | tf_op jit(solution)/shard_map/ppermute | solution.py:28
  7.6 1.6 %copy-done = bf16[1,1,1,64,128,128]{5,4,3,2,1,0:T(8,128)(2,1)S(1)} copy-done((bf16[1,1,1,64,128,128]{5,4,3,2,1,0:T(8,128)(2,1)S(1)}, bf16[1,1,1,64,128,128]{5,4,3,2,1,0:T(8,128)(2,1)}, u32[]{:S(2)}) %copy-start) | copy-done | bytes 2097176
  11.0 1.7 %prepare.1 = (bf16[64,128,128]{2,1,0:T(8,128)(2,1)S(1)}, bf16[6,256,256]{2,1,0:T(8,128)(2,1)S(1)}, s32[67]{0:T(128)S(1)}, s32[67]{0:T(128)S(1)}, s32[67]{0:T(128...) custom-call(s32[4]{0:T(128)S(1)} %bitcast.21, s32[3,64]{1,0:T(4,128)S(1)} %bitcast.20, ...), custom_call_target="tpu_custom_call" | custom-call | bytes 4194304 | tf_op jit(solution)/shard_map/prepare/pallas_call | solution.py:390
  12.8 1.5 %forward.2.refs_4_ = f32[17,128,256]{2,1,0:T(8,128)S(1)} custom-call(s32[67]{0:T(128)S(1)} %get-tuple-element.49.order, bf16[1,256,256]{2,1,0:T(8,128)(2,1)S(1)} %bitcast.12, bf16[1,256,256]{2,1,0:T(8,128)(2,1)S(1)} %bitcast.14, bf16[6,256,256]{2,1,0:T(8,128)(2,1)S(1)} %get-tuple-element.47.refs_2_.weight, ...), custom_call_target="tpu_custom_call", output_to_operand_aliasing={{}: (5, {})} | custom-call | flops 1073741824 | bytes 1048576 | tf_op jit(solution)/shard_map/forward/pallas_call | solution.py:421
  14.3 3.9 %collective-permute-done = bf16[256,256]{1,0:T(8,128)(2,1)S(1)} collective-permute-done((bf16[256,256]{1,0:T(8,128)(2,1)}, bf16[256,256]{1,0:T(8,128)(2,1)S(1)}, u32[]{:S(2)}, u32[]{:S(2)}) %collective-permute-start) | collective-permute-done | bytes 131104 | tf_op jit(solution)/shard_map/ppermute | solution.py:28
  18.2 1.5 %forward.3 = (f32[17,128,256]{2,1,0:T(8,128)S(1)}, bf16[12,256,256]{2,1,0:T(8,128)(2,1)S(1)}, bf16[4,256,256]{2,1,0:T(8,128)(2,1)S(1)}) custom-call(s32[67]{0:T(128)S(1)} %get-tuple-element.46.order, bf16[1,256,256]{2,1,0:T(8,128)(2,1)S(1)} %bitcast.18, bf16[1,256,256]{2,1,0:T(8,128)(2,1)S(1)} %bitcast.16, ...), custom_call_target="tpu_custom_call", output_to_operand_aliasing={{0}: (5, {})} | custom-call | flops 1073741824 | bytes 1048576 | tf_op jit(solution)/shard_map/forward/pallas_call | solution.py:421
  21.8 3.1 %collective-permute-start.4 = (bf16[256,256]{1,0:T(8,128)(2,1)S(1)}, bf16[256,256]{1,0:T(8,128)(2,1)S(1)}, u32[]{:S(2)}, u32[]{:S(2)}) collective-permute-start(bf16[256,256]{1,0:T(8,128)(2,1)S(1)} %get-tuple-element.63), channel_id=1, source_target_pairs={{0,6},{2,4},{4,2},{6,0},{1,7},{3,5},{5,3},{7,1},{8,14},{10,12},{12... | collective-permute-start | bytes 393224 | tf_op jit(solution)/shard_map/ppermute | solution.py:28
  25.5 1.9 %turn.1 = (bf16[64,128,128]{2,1,0:T(8,128)(2,1)S(1)}, bf16[256,512]{1,0:T(8,128)(2,1)S(1)}, f32[13,128,256]{2,1,0:T(8,128)S(1)}, f32[13,128,256]{2,1,0:T(8,128)S(1)}) custom-call(s32[4]{0:T(128)S(1)} %bitcast.22, bf16[64,128,128]{2,1,0:T(8,128)(2,1)S(1)} %get-tuple-element.48.refs_3_.values, bf16[1,256,256]{2,1,0:T(8,128)(2,1)S(1)} %bitcast.13, ...), custom_call_target="tpu_custom_call" | custom-call | bytes 4194304 | tf_op jit(solution)/shard_map/turn/pallas_call | solution.py:455
  27.4 1.4 %collective-permute-done.4.first = bf16[256,256]{1,0:T(8,128)(2,1)S(1)} collective-permute-done((bf16[256,256]{1,0:T(8,128)(2,1)S(1)}, bf16[256,256]{1,0:T(8,128)(2,1)S(1)}, u32[]{:S(2)}, u32[]{:S(2)}) %collective-permute-start.4) | collective-permute-done | bytes 131104 | tf_op jit(solution)/shard_map/ppermute | solution.py:28
  28.8 2.7 %collective-permute-done.5.second = bf16[256,256]{1,0:T(8,128)(2,1)S(1)} collective-permute-done((bf16[256,256]{1,0:T(8,128)(2,1)S(1)}, bf16[256,256]{1,0:T(8,128)(2,1)S(1)}, u32[]{:S(2)}, u32[]{:S(2)}) %collective-permute-start.5) | collective-permute-done | bytes 131104 | tf_op jit(solution)/shard_map/ppermute | solution.py:28
  31.6 1.9 %collective-permute-start.9 = (bf16[256,256]{1,0:T(8,128)(2,1)S(1)}, bf16[256,256]{1,0:T(8,128)(2,1)S(1)}, u32[]{:S(2)}, u32[]{:S(2)}) collective-permute-start(bf16[256,256]{1,0:T(8,128)(2,1)S(1)} %grad.1.refs_0_), channel_id=1, source_target_pairs={{0,6},{2,4},{4,2},{6,0},{1,7},{3,5},{5,3},{7,1},{8,14},{10,12},{12... | collective-permute-start | bytes 393224 | tf_op jit(solution)/shard_map/ppermute | solution.py:28
  33.5 1.4 %collective-permute-start.8 = (bf16[256,256]{1,0:T(8,128)(2,1)S(1)}, bf16[256,256]{1,0:T(8,128)(2,1)S(1)}, u32[]{:S(2)}, u32[]{:S(2)}) collective-permute-start(bf16[256,256]{1,0:T(8,128)(2,1)S(1)} %grad.1.refs_0_), channel_id=1, source_target_pairs={{0,4},{2,6},{4,0},{6,2},{1,5},{3,7},{5,1},{7,3},{8,12},{10,14},{12... | collective-permute-start | bytes 393224 | tf_op jit(solution)/shard_map/ppermute | solution.py:28
  35.2 3.8 %collective-permute-done.9.refs_3_ = bf16[256,256]{1,0:T(8,128)(2,1)S(1)} collective-permute-done((bf16[256,256]{1,0:T(8,128)(2,1)S(1)}, bf16[256,256]{1,0:T(8,128)(2,1)S(1)}, u32[]{:S(2)}, u32[]{:S(2)}) %collective-permute-start.9) | collective-permute-done | bytes 131104 | tf_op jit(solution)/shard_map/ppermute | solution.py:28
  39.0 1.8 %collective-permute-done.8.refs_2_ = bf16[256,256]{1,0:T(8,128)(2,1)S(1)} collective-permute-done((bf16[256,256]{1,0:T(8,128)(2,1)S(1)}, bf16[256,256]{1,0:T(8,128)(2,1)S(1)}, u32[]{:S(2)}, u32[]{:S(2)}) %collective-permute-start.8) | collective-permute-done | bytes 131104 | tf_op jit(solution)/shard_map/ppermute | solution.py:28
  42.4 1.7 %weight_terms.3 = (f32[3,64,256]{2,1,0:T(8,128)S(1)}, bf16[3,64,256]{2,1,0:T(8,128)(2,1)S(1)}, bf16[3,64,256]{2,1,0:T(8,128)(2,1)S(1)}, bf16[3,64,256]{2,1,0:T(8,128)(2,1)S(1)}, f32[13,128,256]{2,1,0:T(8,128)S(1)}) custom-call(s32[65]{0:T(128)S(1)} %get-tuple-element.82.listed, ...), custom_call_target="tpu_custom_call", output_to_operand_aliasing={{4}: (4, {})} | custom-call | tf_op jit(solution)/shard_map/weight_terms/pallas_call | solution.py:501
  44.0 1.8 %collective-permute-start.22 = (bf16[3,64,256]{2,1,0:T(8,128)(2,1)S(1)}, bf16[3,64,256]{2,1,0:T(8,128)(2,1)S(1)}, u32[]{:S(2)}, u32[]{:S(2)}) collective-permute-start(bf16[3,64,256]{2,1,0:T(8,128)(2,1)S(1)} %get-tuple-element.85), channel_id=1, source_target_pairs={{0,6},{2,4},{4,2},{6,0},{1,7},{3,5},{5,3},{7,1},{8,14},{10,12},{12... | collective-permute-start | bytes 294920 | tf_op jit(solution)/shard_map/ppermute | solution.py:28
  45.8 1.5 %collective-permute-start.23 = (bf16[3,64,256]{2,1,0:T(8,128)(2,1)S(1)}, bf16[3,64,256]{2,1,0:T(8,128)(2,1)S(1)}, u32[]{:S(2)}, u32[]{:S(2)}) collective-permute-start(bf16[3,64,256]{2,1,0:T(8,128)(2,1)S(1)} %get-tuple-element.86), channel_id=1, source_target_pairs={{0,4},{2,6},{4,0},{6,2},{1,5},{3,7},{5,1},{7,3},{8,12},{10,14},{12... | collective-permute-start | bytes 294920 | tf_op jit(solution)/shard_map/ppermute | solution.py:28
  47.6 1.6 %weight_terms.2 = (f32[3,64,256]{2,1,0:T(8,128)S(1)}, bf16[3,64,256]{2,1,0:T(8,128)(2,1)S(1)}, bf16[3,64,256]{2,1,0:T(8,128)(2,1)S(1)}, bf16[3,64,256]{2,1,0:T(8,128)(2,1)S(1)}, f32[13,128,256]{2,1,0:T(8,128)S(1)}) custom-call(s32[65]{0:T(128)S(1)} %get-tuple-element.74.listed, ...), custom_call_target="tpu_custom_call", output_to_operand_aliasing={{4}: (4, {})} | custom-call | tf_op jit(solution)/shard_map/weight_terms/pallas_call | solution.py:501
  49.2 2.3 %collective-permute-start.14 = (bf16[3,64,256]{2,1,0:T(8,128)(2,1)S(1)}, bf16[3,64,256]{2,1,0:T(8,128)(2,1)S(1)}, u32[]{:S(2)}, u32[]{:S(2)}) collective-permute-start(bf16[3,64,256]{2,1,0:T(8,128)(2,1)S(1)} %get-tuple-element.79), channel_id=1, source_target_pairs={{0,6},{2,4},{4,2},{6,0},{1,7},{3,5},{5,3},{7,1},{8,14},{10,12},{12... | collective-permute-start | bytes 294920 | tf_op jit(solution)/shard_map/ppermute | solution.py:28
  52.9 2.9 %collective-permute-done.14.refs_1_ = bf16[3,64,256]{2,1,0:T(8,128)(2,1)S(1)} collective-permute-done((bf16[3,64,256]{2,1,0:T(8,128)(2,1)S(1)}, bf16[3,64,256]{2,1,0:T(8,128)(2,1)S(1)}, u32[]{:S(2)}, u32[]{:S(2)}) %collective-permute-start.14) | collective-permute-done | bytes 98336 | tf_op jit(solution)/shard_map/ppermute | solution.py:28
  57.7 2.0 %collective-permute-done.25.refs_1_ = bf16[3,64,256]{2,1,0:T(8,128)(2,1)S(1)} collective-permute-done((bf16[3,64,256]{2,1,0:T(8,128)(2,1)S(1)}, bf16[3,64,256]{2,1,0:T(8,128)(2,1)S(1)}, u32[]{:S(2)}, u32[]{:S(2)}) %collective-permute-start.25) | collective-permute-done | bytes 98336 | tf_op jit(solution)/shard_map/ppermute | solution.py:28
  59.8 3.0 %collective-permute-done.17.refs_1_ = bf16[3,64,256]{2,1,0:T(8,128)(2,1)S(1)} collective-permute-done((bf16[3,64,256]{2,1,0:T(8,128)(2,1)S(1)}, bf16[3,64,256]{2,1,0:T(8,128)(2,1)S(1)}, u32[]{:S(2)}, u32[]{:S(2)}) %collective-permute-start.17) | collective-permute-done | bytes 98336 | tf_op jit(solution)/shard_map/ppermute | solution.py:28
  64.7 1.7 %collective-permute-start.29 = (bf16[3,64,256]{2,1,0:T(8,128)(2,1)S(1)}, bf16[3,64,256]{2,1,0:T(8,128)(2,1)S(1)}, u32[]{:S(2)}, u32[]{:S(2)}) collective-permute-start(bf16[3,64,256]{2,1,0:T(8,128)(2,1)S(1)} %sum.11.refs_0_), channel_id=1, source_target_pairs={{0,6},{2,4},{4,2},{6,0},{1,7},{3,5},{5,3},{7,1},{8,14},{10,12},{12... | collective-permute-start | bytes 294920 | tf_op jit(solution)/shard_map/ppermute | solution.py:28
  (68 shorter events, 23.8 us)
Async XLA Ops:
  0.6 12.1 %collective-permute-start.2 = (bf16[256,256]{1,0:T(8,128)(2,1)}, bf16[256,256]{1,0:T(8,128)(2,1)S(1)}, u32[]{:S(2)}, u32[]{:S(2)}) collective-permute-start(bf16[256,256]{1,0:T(8,128)(2,1)} %param.7), channel_id=1, source_target_pairs={{0,8},{8,0},{16,24},{24,16},{1,9},{9,1},{17,25},{25,17},{2,10},{10... | collective-permute-start | bytes 393224 | tf_op jit(solution)/shard_map/ppermute | solution.py:28
  3.7 10.6 %collective-permute-start.1 = (bf16[256,256]{1,0:T(8,128)(2,1)}, bf16[256,256]{1,0:T(8,128)(2,1)S(1)}, u32[]{:S(2)}, u32[]{:S(2)}) collective-permute-start(bf16[256,256]{1,0:T(8,128)(2,1)} %param.7), channel_id=1, source_target_pairs={{0,24},{8,16},{16,8},{24,0},{1,25},{9,17},{17,9},{25,1},{2,26},{10... | collective-permute-start | bytes 393224 | tf_op jit(solution)/shard_map/ppermute | solution.py:28
  6.2 12.0 %collective-permute-start = (bf16[256,256]{1,0:T(8,128)(2,1)}, bf16[256,256]{1,0:T(8,128)(2,1)S(1)}, u32[]{:S(2)}, u32[]{:S(2)}) collective-permute-start(bf16[256,256]{1,0:T(8,128)(2,1)} %param.7), channel_id=1, source_target_pairs={{0,16},{8,24},{16,0},{24,8},{1,17},{9,25},{17,1},{25,9},{2,18},{10... | collective-permute-start | bytes 393224 | tf_op jit(solution)/shard_map/ppermute | solution.py:28
  21.8 7.0 %collective-permute-start.4 = (bf16[256,256]{1,0:T(8,128)(2,1)S(1)}, bf16[256,256]{1,0:T(8,128)(2,1)S(1)}, u32[]{:S(2)}, u32[]{:S(2)}) collective-permute-start(bf16[256,256]{1,0:T(8,128)(2,1)S(1)} %get-tuple-element.63), channel_id=1, source_target_pairs={{0,6},{2,4},{4,2},{6,0},{1,7},{3,5},{5,3},{7,1},{8,14},{10,12},{12... | collective-permute-start | bytes 393224 | tf_op jit(solution)/shard_map/ppermute | solution.py:28
  24.9 6.6 %collective-permute-start.5 = (bf16[256,256]{1,0:T(8,128)(2,1)S(1)}, bf16[256,256]{1,0:T(8,128)(2,1)S(1)}, u32[]{:S(2)}, u32[]{:S(2)}) collective-permute-start(bf16[256,256]{1,0:T(8,128)(2,1)S(1)} %get-tuple-element.64), channel_id=1, source_target_pairs={{0,4},{2,6},{4,0},{6,2},{1,5},{3,7},{5,1},{7,3},{8,12},{10,14},{12... | collective-permute-start | bytes 393224 | tf_op jit(solution)/shard_map/ppermute | solution.py:28
  24.9 6.6 %collective-permute-start.6 = (bf16[256,256]{1,0:T(8,128)(2,1)S(1)}, bf16[256,256]{1,0:T(8,128)(2,1)S(1)}, u32[]{:S(2)}, u32[]{:S(2)}) collective-permute-start(bf16[256,256]{1,0:T(8,128)(2,1)S(1)} %get-tuple-element.65), channel_id=1, source_target_pairs={{0,2},{2,0},{4,6},{6,4},{1,3},{3,1},{5,7},{7,5},{8,10},{10,8},{12,... | collective-permute-start | bytes 393224 | tf_op jit(solution)/shard_map/ppermute | solution.py:28
  31.6 7.4 %collective-permute-start.9 = (bf16[256,256]{1,0:T(8,128)(2,1)S(1)}, bf16[256,256]{1,0:T(8,128)(2,1)S(1)}, u32[]{:S(2)}, u32[]{:S(2)}) collective-permute-start(bf16[256,256]{1,0:T(8,128)(2,1)S(1)} %grad.1.refs_0_), channel_id=1, source_target_pairs={{0,6},{2,4},{4,2},{6,0},{1,7},{3,5},{5,3},{7,1},{8,14},{10,12},{12... | collective-permute-start | bytes 393224 | tf_op jit(solution)/shard_map/ppermute | solution.py:28
  33.5 7.3 %collective-permute-start.8 = (bf16[256,256]{1,0:T(8,128)(2,1)S(1)}, bf16[256,256]{1,0:T(8,128)(2,1)S(1)}, u32[]{:S(2)}, u32[]{:S(2)}) collective-permute-start(bf16[256,256]{1,0:T(8,128)(2,1)S(1)} %grad.1.refs_0_), channel_id=1, source_target_pairs={{0,4},{2,6},{4,0},{6,2},{1,5},{3,7},{5,1},{7,3},{8,12},{10,14},{12... | collective-permute-start | bytes 393224 | tf_op jit(solution)/shard_map/ppermute | solution.py:28
  34.9 5.8 %collective-permute-start.7 = (bf16[256,256]{1,0:T(8,128)(2,1)S(1)}, bf16[256,256]{1,0:T(8,128)(2,1)S(1)}, u32[]{:S(2)}, u32[]{:S(2)}) collective-permute-start(bf16[256,256]{1,0:T(8,128)(2,1)S(1)} %grad.1.refs_0_), channel_id=1, source_target_pairs={{0,2},{2,0},{4,6},{6,4},{1,3},{3,1},{5,7},{7,5},{8,10},{10,8},{12,... | collective-permute-start | bytes 393224 | tf_op jit(solution)/shard_map/ppermute | solution.py:28
  35.2 6.1 %collective-permute-start.10 = (bf16[256,256]{1,0:T(8,128)(2,1)S(1)}, bf16[256,256]{1,0:T(8,128)(2,1)S(1)}, u32[]{:S(2)}, u32[]{:S(2)}) collective-permute-start(bf16[256,256]{1,0:T(8,128)(2,1)S(1)} %grad.1.refs_0_), channel_id=1, source_target_pairs={{0,1},{1,0},{2,3},{3,2},{4,5},{5,4},{6,7},{7,6},{8,9},{9,8},{10,11... | collective-permute-start | bytes 393224 | tf_op jit(solution)/shard_map/ppermute | solution.py:28
  44.0 8.4 %collective-permute-start.22 = (bf16[3,64,256]{2,1,0:T(8,128)(2,1)S(1)}, bf16[3,64,256]{2,1,0:T(8,128)(2,1)S(1)}, u32[]{:S(2)}, u32[]{:S(2)}) collective-permute-start(bf16[3,64,256]{2,1,0:T(8,128)(2,1)S(1)} %get-tuple-element.85), channel_id=1, source_target_pairs={{0,6},{2,4},{4,2},{6,0},{1,7},{3,5},{5,3},{7,1},{8,14},{10,12},{12... | collective-permute-start | bytes 294920 | tf_op jit(solution)/shard_map/ppermute | solution.py:28
  45.8 7.0 %collective-permute-start.23 = (bf16[3,64,256]{2,1,0:T(8,128)(2,1)S(1)}, bf16[3,64,256]{2,1,0:T(8,128)(2,1)S(1)}, u32[]{:S(2)}, u32[]{:S(2)}) collective-permute-start(bf16[3,64,256]{2,1,0:T(8,128)(2,1)S(1)} %get-tuple-element.86), channel_id=1, source_target_pairs={{0,4},{2,6},{4,0},{6,2},{1,5},{3,7},{5,1},{7,3},{8,12},{10,14},{12... | collective-permute-start | bytes 294920 | tf_op jit(solution)/shard_map/ppermute | solution.py:28
  47.3 5.6 %collective-permute-start.24 = (bf16[3,64,256]{2,1,0:T(8,128)(2,1)S(1)}, bf16[3,64,256]{2,1,0:T(8,128)(2,1)S(1)}, u32[]{:S(2)}, u32[]{:S(2)}) collective-permute-start(bf16[3,64,256]{2,1,0:T(8,128)(2,1)S(1)} %get-tuple-element.87), channel_id=1, source_target_pairs={{0,2},{2,0},{4,6},{6,4},{1,3},{3,1},{5,7},{7,5},{8,10},{10,8},{12,... | collective-permute-start | bytes 294920 | tf_op jit(solution)/shard_map/ppermute | solution.py:28
  49.2 6.6 %collective-permute-start.14 = (bf16[3,64,256]{2,1,0:T(8,128)(2,1)S(1)}, bf16[3,64,256]{2,1,0:T(8,128)(2,1)S(1)}, u32[]{:S(2)}, u32[]{:S(2)}) collective-permute-start(bf16[3,64,256]{2,1,0:T(8,128)(2,1)S(1)} %get-tuple-element.79), channel_id=1, source_target_pairs={{0,6},{2,4},{4,2},{6,0},{1,7},{3,5},{5,3},{7,1},{8,14},{10,12},{12... | collective-permute-start | bytes 294920 | tf_op jit(solution)/shard_map/ppermute | solution.py:28
  51.5 5.3 %collective-permute-start.15 = (bf16[3,64,256]{2,1,0:T(8,128)(2,1)S(1)}, bf16[3,64,256]{2,1,0:T(8,128)(2,1)S(1)}, u32[]{:S(2)}, u32[]{:S(2)}) collective-permute-start(bf16[3,64,256]{2,1,0:T(8,128)(2,1)S(1)} %get-tuple-element.80), channel_id=1, source_target_pairs={{0,4},{2,6},{4,0},{6,2},{1,5},{3,7},{5,1},{7,3},{8,12},{10,14},{12... | collective-permute-start | bytes 294920 | tf_op jit(solution)/shard_map/ppermute | solution.py:28
  52.9 6.8 %collective-permute-start.25 = (bf16[3,64,256]{2,1,0:T(8,128)(2,1)S(1)}, bf16[3,64,256]{2,1,0:T(8,128)(2,1)S(1)}, u32[]{:S(2)}, u32[]{:S(2)}) collective-permute-start(bf16[3,64,256]{2,1,0:T(8,128)(2,1)S(1)} %sum.9.refs_0_), channel_id=1, source_target_pairs={{0,16},{8,24},{16,0},{24,8},{1,17},{9,25},{17,1},{25,9},{2,18},{10... | collective-permute-start | bytes 294920 | tf_op jit(solution)/shard_map/ppermute | solution.py:28
  57.4 5.4 %collective-permute-start.17 = (bf16[3,64,256]{2,1,0:T(8,128)(2,1)S(1)}, bf16[3,64,256]{2,1,0:T(8,128)(2,1)S(1)}, u32[]{:S(2)}, u32[]{:S(2)}) collective-permute-start(bf16[3,64,256]{2,1,0:T(8,128)(2,1)S(1)} %sum.6.refs_0_), channel_id=1, source_target_pairs={{0,8},{8,0},{16,24},{24,16},{1,9},{9,1},{17,25},{25,17},{2,10},{10... | collective-permute-start | bytes 294920 | tf_op jit(solution)/shard_map/ppermute | solution.py:28
  59.7 5.0 %collective-permute-start.26 = (bf16[3,64,256]{2,1,0:T(8,128)(2,1)S(1)}, bf16[3,64,256]{2,1,0:T(8,128)(2,1)S(1)}, u32[]{:S(2)}, u32[]{:S(2)}) collective-permute-start(bf16[3,64,256]{2,1,0:T(8,128)(2,1)S(1)} %sum.10.refs_0_), channel_id=1, source_target_pairs={{0,8},{8,0},{16,24},{24,16},{1,9},{9,1},{17,25},{25,17},{2,10},{10... | collective-permute-start | bytes 294920 | tf_op jit(solution)/shard_map/ppermute | solution.py:28
  62.8 6.5 %collective-permute-start.18 = (bf16[3,64,256]{2,1,0:T(8,128)(2,1)S(1)}, bf16[3,64,256]{2,1,0:T(8,128)(2,1)S(1)}, u32[]{:S(2)}, u32[]{:S(2)}) collective-permute-start(bf16[3,64,256]{2,1,0:T(8,128)(2,1)S(1)} %sum.7.refs_0_), channel_id=1, source_target_pairs={{0,16},{8,24},{16,0},{24,8},{1,17},{9,25},{17,1},{25,9},{2,18},{10... | collective-permute-start | bytes 294920 | tf_op jit(solution)/shard_map/ppermute | solution.py:28
  64.7 7.1 %collective-permute-start.29 = (bf16[3,64,256]{2,1,0:T(8,128)(2,1)S(1)}, bf16[3,64,256]{2,1,0:T(8,128)(2,1)S(1)}, u32[]{:S(2)}, u32[]{:S(2)}) collective-permute-start(bf16[3,64,256]{2,1,0:T(8,128)(2,1)S(1)} %sum.11.refs_0_), channel_id=1, source_target_pairs={{0,6},{2,4},{4,2},{6,0},{1,7},{3,5},{5,3},{7,1},{8,14},{10,12},{12... | collective-permute-start | bytes 294920 | tf_op jit(solution)/shard_map/ppermute | solution.py:28
  66.4 7.3 %collective-permute-start.28 = (bf16[3,64,256]{2,1,0:T(8,128)(2,1)S(1)}, bf16[3,64,256]{2,1,0:T(8,128)(2,1)S(1)}, u32[]{:S(2)}, u32[]{:S(2)}) collective-permute-start(bf16[3,64,256]{2,1,0:T(8,128)(2,1)S(1)} %sum.11.refs_0_), channel_id=1, source_target_pairs={{0,4},{2,6},{4,0},{6,2},{1,5},{3,7},{5,1},{7,3},{8,12},{10,14},{12... | collective-permute-start | bytes 294920 | tf_op jit(solution)/shard_map/ppermute | solution.py:28
  67.7 6.1 %collective-permute-start.27 = (bf16[3,64,256]{2,1,0:T(8,128)(2,1)S(1)}, bf16[3,64,256]{2,1,0:T(8,128)(2,1)S(1)}, u32[]{:S(2)}, u32[]{:S(2)}) collective-permute-start(bf16[3,64,256]{2,1,0:T(8,128)(2,1)S(1)} %sum.11.refs_0_), channel_id=1, source_target_pairs={{0,2},{2,0},{4,6},{6,4},{1,3},{3,1},{5,7},{7,5},{8,10},{10,8},{12,... | collective-permute-start | bytes 294920 | tf_op jit(solution)/shard_map/ppermute | solution.py:28
  69.4 5.7 %collective-permute-start.21 = (bf16[3,64,256]{2,1,0:T(8,128)(2,1)S(1)}, bf16[3,64,256]{2,1,0:T(8,128)(2,1)S(1)}, u32[]{:S(2)}, u32[]{:S(2)}) collective-permute-start(bf16[3,64,256]{2,1,0:T(8,128)(2,1)S(1)} %sum.8.refs_0_), channel_id=1, source_target_pairs={{0,6},{2,4},{4,2},{6,0},{1,7},{3,5},{5,3},{7,1},{8,14},{10,12},{12... | collective-permute-start | bytes 294920 | tf_op jit(solution)/shard_map/ppermute | solution.py:28
  70.5 5.5 %collective-permute-start.20 = (bf16[3,64,256]{2,1,0:T(8,128)(2,1)S(1)}, bf16[3,64,256]{2,1,0:T(8,128)(2,1)S(1)}, u32[]{:S(2)}, u32[]{:S(2)}) collective-permute-start(bf16[3,64,256]{2,1,0:T(8,128)(2,1)S(1)} %sum.8.refs_0_), channel_id=1, source_target_pairs={{0,4},{2,6},{4,0},{6,2},{1,5},{3,7},{5,1},{7,3},{8,12},{10,14},{12... | collective-permute-start | bytes 294920 | tf_op jit(solution)/shard_map/ppermute | solution.py:28
  (12 other events, 37.2 us)

commit v9 on v8

--- a/solution.py
+++ b/solution.py
@@ -369,7 +369,7 @@
         halo = [lax.all_gather(source_feats, "dom", axis=0)]
     slots = sum(h.shape[0] for h in halo)
     combine = slots * relations <= entries
-    near = partitions // 2
+    near = 1
     owners = groups, own_rows // tile
     start = near if direct else 0
     slot_groups = ((0, near, None),) * direct + ((start, slots, False), (start, slots, True))

time: 77.6 us -> 76.9 us (level)
  waiting for transfers between devices: 28.1 us -> 18 us
  starting transfers between devices: 29.4 us -> 38.1 us
    ppermute x30, waiting for transfers between devices: 28.1 us -> 18 us  [swap(): return lax.ppermute(value, axis, partner_pairs(lax.axis_size(axis), mask))]
    ppermute x30, starting transfers between devices: 29.4 us -> 38.1 us  [swap(): return lax.ppermute(value, axis, partner_pairs(lax.axis_size(axis), mask))]
  transfers between devices with their start and end apart: 30 -> 30, of which waited for: 18 -> 15; matrix products, arithmetic and copies ran while one was open for 2% -> 2% of each run, Pallas kernels for 12% -> 12%
where the time goes in v9:
time: 76.9 us; the launch traced here: 76.5 us
  starting transfers between devices  38.1 us (50%)
  waiting for transfers between devices  18 us (23%)
  Pallas kernels  14.1 us (18%)
  local copies, waits for them, and re-layouts  4.07 us (5%)
  between operations  1.48 us (2%)
    ppermute x30, starting transfers between devices, swap(): return lax.ppermute(value, axis, partner_pairs(lax.axis_size(axis), mask))  38.1 us
    ppermute x30, waiting for transfers between devices, swap(): return lax.ppermute(value, axis, partner_pairs(lax.axis_size(axis), mask))  18 us
    unnamed x13, local copies, waits for them, and re-layouts  4.07 us
    pallas_call x2, Pallas kernels, local(): pl.pallas_call(functools.partial(weight_kernel, tile, combine), out_shape...  3.31 us
    pallas_call x2, Pallas kernels, local(): pl.pallas_call(kernel, out_shape=outs, in_specs=[SCALARS] + [WHOLE] * (le...  3.04 us
    pallas_call x1, Pallas kernels, local(): pl.pallas_call(functools.partial(prepare_kernel, direct, owners, slot_gro...  2.25 us
    pallas_call x1, Pallas kernels, local(): pl.pallas_call(functools.partial(turn_kernel, direct, tile, panels, len(h...  1.9 us
    pallas_call x2, Pallas kernels, spread(): pl.pallas_call(functools.partial(spread_kernel, first_relation), out_shap...  1.84 us
  transfers between devices with their start and end apart: 30, of which 15 were waited for; matrix products, arithmetic and copies ran while one was open for 2% of the time, Pallas kernels for 12%

profile of v9, /device:TPU:0, one launch (start us, length us, event | category | flops | bytes accessed | tf_op | source)
XLA Modules:
  0.0 76.5 jit_solution(7695710100364387581)
XLA Ops:
  0.6 4.1 %collective-permute-start.1 = (bf16[256,256]{1,0:T(8,128)(2,1)}, bf16[256,256]{1,0:T(8,128)(2,1)S(1)}, u32[]{:S(2)}, u32[]{:S(2)}) collective-permute-start(bf16[256,256]{1,0:T(8,128)(2,1)} %param.7), channel_id=1, source_target_pairs={{0,16},{8,24},{16,0},{24,8},{1,17},{9,25},{17,1},{25,9},{2,18},{10... | collective-permute-start | bytes 393224 | tf_op jit(solution)/shard_map/ppermute | solution.py:28
  4.7 1.6 %collective-permute-start = (bf16[256,256]{1,0:T(8,128)(2,1)}, bf16[256,256]{1,0:T(8,128)(2,1)S(1)}, u32[]{:S(2)}, u32[]{:S(2)}) collective-permute-start(bf16[256,256]{1,0:T(8,128)(2,1)} %param.7), channel_id=1, source_target_pairs={{0,8},{8,0},{16,24},{24,16},{1,9},{9,1},{17,25},{25,17},{2,10},{10... | collective-permute-start | bytes 393224 | tf_op jit(solution)/shard_map/ppermute | solution.py:28
  7.6 1.6 %copy-done = bf16[1,1,1,64,128,128]{5,4,3,2,1,0:T(8,128)(2,1)S(1)} copy-done((bf16[1,1,1,64,128,128]{5,4,3,2,1,0:T(8,128)(2,1)S(1)}, bf16[1,1,1,64,128,128]{5,4,3,2,1,0:T(8,128)(2,1)}, u32[]{:S(2)}) %copy-start) | copy-done | bytes 2097176
  11.0 2.3 %prepare.1 = (bf16[64,128,128]{2,1,0:T(8,128)(2,1)S(1)}, bf16[6,256,256]{2,1,0:T(8,128)(2,1)S(1)}, s32[66]{0:T(128)S(1)}, s32[68]{0:T(128)S(1)}, s32[68]{0:T(128...) custom-call(s32[4]{0:T(128)S(1)} %bitcast.21, s32[3,64]{1,0:T(4,128)S(1)} %bitcast.20, ...), custom_call_target="tpu_custom_call" | custom-call | bytes 4194304 | tf_op jit(solution)/shard_map/prepare/pallas_call | solution.py:390
  15.3 1.6 %forward.3 = (f32[17,128,256]{2,1,0:T(8,128)S(1)}, bf16[18,256,256]{2,1,0:T(8,128)(2,1)S(1)}, bf16[4,256,256]{2,1,0:T(8,128)(2,1)S(1)}) custom-call(s32[68]{0:T(128)S(1)} %get-tuple-element.46.order, bf16[1,256,256]{2,1,0:T(8,128)(2,1)S(1)} %bitcast.16, bf16[1,256,256]{2,1,0:T(8,128)(2,1)S(1)} %bitcast.14, ...), custom_call_target="tpu_custom_call", output_to_operand_aliasing={{0}: (6, {})} | custom-call | flops 1073741824 | bytes 1048576 | tf_op jit(solution)/shard_map/forward/pallas_call | solution.py:421
  19.0 2.5 %collective-permute-start.4 = (bf16[256,256]{1,0:T(8,128)(2,1)S(1)}, bf16[256,256]{1,0:T(8,128)(2,1)S(1)}, u32[]{:S(2)}, u32[]{:S(2)}) collective-permute-start(bf16[256,256]{1,0:T(8,128)(2,1)S(1)} %get-tuple-element.63), channel_id=1, source_target_pairs={{0,6},{2,4},{4,2},{6,0},{1,7},{3,5},{5,3},{7,1},{8,14},{10,12},{12... | collective-permute-start | bytes 393224 | tf_op jit(solution)/shard_map/ppermute | solution.py:28
  22.6 1.9 %turn.1 = (bf16[64,128,128]{2,1,0:T(8,128)(2,1)S(1)}, bf16[256,512]{1,0:T(8,128)(2,1)S(1)}, f32[13,128,256]{2,1,0:T(8,128)S(1)}, f32[13,128,256]{2,1,0:T(8,128)S(1)}) custom-call(s32[4]{0:T(128)S(1)} %bitcast.22, bf16[64,128,128]{2,1,0:T(8,128)(2,1)S(1)} %get-tuple-element.48.refs_2_.refs_4_.values, bf16[1,256,256]{2,1,0:T(8,128)(2,1)S(1)} %bitcast.13, ...), custom_call_target="tpu_custom_call" | custom-call | bytes 4194304 | tf_op jit(solution)/shard_map/turn/pallas_call | solution.py:455
  25.8 2.5 %collective-permute-done.5.second = bf16[256,256]{1,0:T(8,128)(2,1)S(1)} collective-permute-done((bf16[256,256]{1,0:T(8,128)(2,1)S(1)}, bf16[256,256]{1,0:T(8,128)(2,1)S(1)}, u32[]{:S(2)}, u32[]{:S(2)}) %collective-permute-start.5) | collective-permute-done | bytes 131104 | tf_op jit(solution)/shard_map/ppermute | solution.py:28
  28.6 1.7 %collective-permute-start.9 = (bf16[256,256]{1,0:T(8,128)(2,1)S(1)}, bf16[256,256]{1,0:T(8,128)(2,1)S(1)}, u32[]{:S(2)}, u32[]{:S(2)}) collective-permute-start(bf16[256,256]{1,0:T(8,128)(2,1)S(1)} %grad.1.refs_0_), channel_id=1, source_target_pairs={{0,6},{2,4},{4,2},{6,0},{1,7},{3,5},{5,3},{7,1},{8,14},{10,12},{12... | collective-permute-start | bytes 393224 | tf_op jit(solution)/shard_map/ppermute | solution.py:28
  32.2 3.8 %collective-permute-done.9.refs_3_ = bf16[256,256]{1,0:T(8,128)(2,1)S(1)} collective-permute-done((bf16[256,256]{1,0:T(8,128)(2,1)S(1)}, bf16[256,256]{1,0:T(8,128)(2,1)S(1)}, u32[]{:S(2)}, u32[]{:S(2)}) %collective-permute-start.9) | collective-permute-done | bytes 131104 | tf_op jit(solution)/shard_map/ppermute | solution.py:28
  36.0 1.7 %collective-permute-done.8.refs_2_ = bf16[256,256]{1,0:T(8,128)(2,1)S(1)} collective-permute-done((bf16[256,256]{1,0:T(8,128)(2,1)S(1)}, bf16[256,256]{1,0:T(8,128)(2,1)S(1)}, u32[]{:S(2)}, u32[]{:S(2)}) %collective-permute-start.8) | collective-permute-done | bytes 131104 | tf_op jit(solution)/shard_map/ppermute | solution.py:28
  39.3 1.7 %weight_terms.3 = (f32[3,64,256]{2,1,0:T(8,128)S(1)}, bf16[3,64,256]{2,1,0:T(8,128)(2,1)S(1)}, bf16[3,64,256]{2,1,0:T(8,128)(2,1)S(1)}, bf16[3,64,256]{2,1,0:T(8,128)(2,1)S(1)}, f32[13,128,256]{2,1,0:T(8,128)S(1)}) custom-call(s32[65]{0:T(128)S(1)} %get-tuple-element.82.listed, ...), custom_call_target="tpu_custom_call", output_to_operand_aliasing={{4}: (4, {})} | custom-call | tf_op jit(solution)/shard_map/weight_terms/pallas_call | solution.py:501
  40.9 1.6 %collective-permute-start.22 = (bf16[3,64,256]{2,1,0:T(8,128)(2,1)S(1)}, bf16[3,64,256]{2,1,0:T(8,128)(2,1)S(1)}, u32[]{:S(2)}, u32[]{:S(2)}) collective-permute-start(bf16[3,64,256]{2,1,0:T(8,128)(2,1)S(1)} %get-tuple-element.85), channel_id=1, source_target_pairs={{0,6},{2,4},{4,2},{6,0},{1,7},{3,5},{5,3},{7,1},{8,14},{10,12},{12... | collective-permute-start | bytes 294920 | tf_op jit(solution)/shard_map/ppermute | solution.py:28
  42.5 2.1 %collective-permute-start.23 = (bf16[3,64,256]{2,1,0:T(8,128)(2,1)S(1)}, bf16[3,64,256]{2,1,0:T(8,128)(2,1)S(1)}, u32[]{:S(2)}, u32[]{:S(2)}) collective-permute-start(bf16[3,64,256]{2,1,0:T(8,128)(2,1)S(1)} %get-tuple-element.86), channel_id=1, source_target_pairs={{0,4},{2,6},{4,0},{6,2},{1,5},{3,7},{5,1},{7,3},{8,12},{10,14},{12... | collective-permute-start | bytes 294920 | tf_op jit(solution)/shard_map/ppermute | solution.py:28
  44.7 1.6 %weight_terms.2 = (f32[3,64,256]{2,1,0:T(8,128)S(1)}, bf16[3,64,256]{2,1,0:T(8,128)(2,1)S(1)}, bf16[3,64,256]{2,1,0:T(8,128)(2,1)S(1)}, bf16[3,64,256]{2,1,0:T(8,128)(2,1)S(1)}, f32[13,128,256]{2,1,0:T(8,128)S(1)}) custom-call(s32[65]{0:T(128)S(1)} %get-tuple-element.74.listed, ...), custom_call_target="tpu_custom_call", output_to_operand_aliasing={{4}: (4, {})} | custom-call | tf_op jit(solution)/shard_map/weight_terms/pallas_call | solution.py:501
  46.3 1.5 %collective-permute-start.14 = (bf16[3,64,256]{2,1,0:T(8,128)(2,1)S(1)}, bf16[3,64,256]{2,1,0:T(8,128)(2,1)S(1)}, u32[]{:S(2)}, u32[]{:S(2)}) collective-permute-start(bf16[3,64,256]{2,1,0:T(8,128)(2,1)S(1)} %get-tuple-element.79), channel_id=1, source_target_pairs={{0,6},{2,4},{4,2},{6,0},{1,7},{3,5},{5,3},{7,1},{8,14},{10,12},{12... | collective-permute-start | bytes 294920 | tf_op jit(solution)/shard_map/ppermute | solution.py:28
  47.9 2.5 %collective-permute-start.15 = (bf16[3,64,256]{2,1,0:T(8,128)(2,1)S(1)}, bf16[3,64,256]{2,1,0:T(8,128)(2,1)S(1)}, u32[]{:S(2)}, u32[]{:S(2)}) collective-permute-start(bf16[3,64,256]{2,1,0:T(8,128)(2,1)S(1)} %get-tuple-element.80), channel_id=1, source_target_pairs={{0,4},{2,6},{4,0},{6,2},{1,5},{3,7},{5,1},{7,3},{8,12},{10,14},{12... | collective-permute-start | bytes 294920 | tf_op jit(solution)/shard_map/ppermute | solution.py:28
  50.5 5.0 %collective-permute-start.25 = (bf16[3,64,256]{2,1,0:T(8,128)(2,1)S(1)}, bf16[3,64,256]{2,1,0:T(8,128)(2,1)S(1)}, u32[]{:S(2)}, u32[]{:S(2)}) collective-permute-start(bf16[3,64,256]{2,1,0:T(8,128)(2,1)S(1)} %sum.9.refs_0_), channel_id=1, source_target_pairs={{0,16},{8,24},{16,0},{24,8},{1,17},{9,25},{17,1},{25,9},{2,18},{10... | collective-permute-start | bytes 294920 | tf_op jit(solution)/shard_map/ppermute | solution.py:28
  55.5 1.7 %collective-permute-start.17 = (bf16[3,64,256]{2,1,0:T(8,128)(2,1)S(1)}, bf16[3,64,256]{2,1,0:T(8,128)(2,1)S(1)}, u32[]{:S(2)}, u32[]{:S(2)}) collective-permute-start(bf16[3,64,256]{2,1,0:T(8,128)(2,1)S(1)} %sum.6.refs_0_), channel_id=1, source_target_pairs={{0,8},{8,0},{16,24},{24,16},{1,9},{9,1},{17,25},{25,17},{2,10},{10... | collective-permute-start | bytes 294920 | tf_op jit(solution)/shard_map/ppermute | solution.py:28
  57.2 1.9 %collective-permute-done.25.refs_1_ = bf16[3,64,256]{2,1,0:T(8,128)(2,1)S(1)} collective-permute-done((bf16[3,64,256]{2,1,0:T(8,128)(2,1)S(1)}, bf16[3,64,256]{2,1,0:T(8,128)(2,1)S(1)}, u32[]{:S(2)}, u32[]{:S(2)}) %collective-permute-start.25) | collective-permute-done | bytes 98336 | tf_op jit(solution)/shard_map/ppermute | solution.py:28
  59.2 2.0 %collective-permute-done.17.refs_1_ = bf16[3,64,256]{2,1,0:T(8,128)(2,1)S(1)} collective-permute-done((bf16[3,64,256]{2,1,0:T(8,128)(2,1)S(1)}, bf16[3,64,256]{2,1,0:T(8,128)(2,1)S(1)}, u32[]{:S(2)}, u32[]{:S(2)}) %collective-permute-start.17) | collective-permute-done | bytes 98336 | tf_op jit(solution)/shard_map/ppermute | solution.py:28
  61.2 2.5 %collective-permute-start.18 = (bf16[3,64,256]{2,1,0:T(8,128)(2,1)S(1)}, bf16[3,64,256]{2,1,0:T(8,128)(2,1)S(1)}, u32[]{:S(2)}, u32[]{:S(2)}) collective-permute-start(bf16[3,64,256]{2,1,0:T(8,128)(2,1)S(1)} %sum.7.refs_0_), channel_id=1, source_target_pairs={{0,16},{8,24},{16,0},{24,8},{1,17},{9,25},{17,1},{25,9},{2,18},{10... | collective-permute-start | bytes 294920 | tf_op jit(solution)/shard_map/ppermute | solution.py:28
  64.6 1.9 %collective-permute-start.29 = (bf16[3,64,256]{2,1,0:T(8,128)(2,1)S(1)}, bf16[3,64,256]{2,1,0:T(8,128)(2,1)S(1)}, u32[]{:S(2)}, u32[]{:S(2)}) collective-permute-start(bf16[3,64,256]{2,1,0:T(8,128)(2,1)S(1)} %sum.11.refs_0_), channel_id=1, source_target_pairs={{0,6},{2,4},{4,2},{6,0},{1,7},{3,5},{5,3},{7,1},{8,14},{10,12},{12... | collective-permute-start | bytes 294920 | tf_op jit(solution)/shard_map/ppermute | solution.py:28
  68.2 1.9 %collective-permute-start.21 = (bf16[3,64,256]{2,1,0:T(8,128)(2,1)S(1)}, bf16[3,64,256]{2,1,0:T(8,128)(2,1)S(1)}, u32[]{:S(2)}, u32[]{:S(2)}) collective-permute-start(bf16[3,64,256]{2,1,0:T(8,128)(2,1)S(1)} %sum.8.refs_0_), channel_id=1, source_target_pairs={{0,6},{2,4},{4,2},{6,0},{1,7},{3,5},{5,3},{7,1},{8,14},{10,12},{12... | collective-permute-start | bytes 294920 | tf_op jit(solution)/shard_map/ppermute | solution.py:28
  (68 shorter events, 22.0 us)
Async XLA Ops:
  0.6 14.1 %collective-permute-start.1 = (bf16[256,256]{1,0:T(8,128)(2,1)}, bf16[256,256]{1,0:T(8,128)(2,1)S(1)}, u32[]{:S(2)}, u32[]{:S(2)}) collective-permute-start(bf16[256,256]{1,0:T(8,128)(2,1)} %param.7), channel_id=1, source_target_pairs={{0,16},{8,24},{16,0},{24,8},{1,17},{9,25},{17,1},{25,9},{2,18},{10... | collective-permute-start | bytes 393224 | tf_op jit(solution)/shard_map/ppermute | solution.py:28
  4.7 10.0 %collective-permute-start = (bf16[256,256]{1,0:T(8,128)(2,1)}, bf16[256,256]{1,0:T(8,128)(2,1)S(1)}, u32[]{:S(2)}, u32[]{:S(2)}) collective-permute-start(bf16[256,256]{1,0:T(8,128)(2,1)} %param.7), channel_id=1, source_target_pairs={{0,8},{8,0},{16,24},{24,16},{1,9},{9,1},{17,25},{25,17},{2,10},{10... | collective-permute-start | bytes 393224 | tf_op jit(solution)/shard_map/ppermute | solution.py:28
  6.3 9.0 %collective-permute-start.2 = (bf16[256,256]{1,0:T(8,128)(2,1)}, bf16[256,256]{1,0:T(8,128)(2,1)S(1)}, u32[]{:S(2)}, u32[]{:S(2)}) collective-permute-start(bf16[256,256]{1,0:T(8,128)(2,1)} %param.7), channel_id=1, source_target_pairs={{0,24},{8,16},{16,8},{24,0},{1,25},{9,17},{17,9},{25,1},{2,26},{10... | collective-permute-start | bytes 393224 | tf_op jit(solution)/shard_map/ppermute | solution.py:28
  19.0 6.8 %collective-permute-start.4 = (bf16[256,256]{1,0:T(8,128)(2,1)S(1)}, bf16[256,256]{1,0:T(8,128)(2,1)S(1)}, u32[]{:S(2)}, u32[]{:S(2)}) collective-permute-start(bf16[256,256]{1,0:T(8,128)(2,1)S(1)} %get-tuple-element.63), channel_id=1, source_target_pairs={{0,6},{2,4},{4,2},{6,0},{1,7},{3,5},{5,3},{7,1},{8,14},{10,12},{12... | collective-permute-start | bytes 393224 | tf_op jit(solution)/shard_map/ppermute | solution.py:28
  21.5 6.8 %collective-permute-start.5 = (bf16[256,256]{1,0:T(8,128)(2,1)S(1)}, bf16[256,256]{1,0:T(8,128)(2,1)S(1)}, u32[]{:S(2)}, u32[]{:S(2)}) collective-permute-start(bf16[256,256]{1,0:T(8,128)(2,1)S(1)} %get-tuple-element.64), channel_id=1, source_target_pairs={{0,4},{2,6},{4,0},{6,2},{1,5},{3,7},{5,1},{7,3},{8,12},{10,14},{12... | collective-permute-start | bytes 393224 | tf_op jit(solution)/shard_map/ppermute | solution.py:28
  22.2 6.3 %collective-permute-start.6 = (bf16[256,256]{1,0:T(8,128)(2,1)S(1)}, bf16[256,256]{1,0:T(8,128)(2,1)S(1)}, u32[]{:S(2)}, u32[]{:S(2)}) collective-permute-start(bf16[256,256]{1,0:T(8,128)(2,1)S(1)} %get-tuple-element.65), channel_id=1, source_target_pairs={{0,2},{2,0},{4,6},{6,4},{1,3},{3,1},{5,7},{7,5},{8,10},{10,8},{12,... | collective-permute-start | bytes 393224 | tf_op jit(solution)/shard_map/ppermute | solution.py:28
  28.6 7.3 %collective-permute-start.9 = (bf16[256,256]{1,0:T(8,128)(2,1)S(1)}, bf16[256,256]{1,0:T(8,128)(2,1)S(1)}, u32[]{:S(2)}, u32[]{:S(2)}) collective-permute-start(bf16[256,256]{1,0:T(8,128)(2,1)S(1)} %grad.1.refs_0_), channel_id=1, source_target_pairs={{0,6},{2,4},{4,2},{6,0},{1,7},{3,5},{5,3},{7,1},{8,14},{10,12},{12... | collective-permute-start | bytes 393224 | tf_op jit(solution)/shard_map/ppermute | solution.py:28
  30.3 7.4 %collective-permute-start.8 = (bf16[256,256]{1,0:T(8,128)(2,1)S(1)}, bf16[256,256]{1,0:T(8,128)(2,1)S(1)}, u32[]{:S(2)}, u32[]{:S(2)}) collective-permute-start(bf16[256,256]{1,0:T(8,128)(2,1)S(1)} %grad.1.refs_0_), channel_id=1, source_target_pairs={{0,4},{2,6},{4,0},{6,2},{1,5},{3,7},{5,1},{7,3},{8,12},{10,14},{12... | collective-permute-start | bytes 393224 | tf_op jit(solution)/shard_map/ppermute | solution.py:28
  31.7 6.1 %collective-permute-start.7 = (bf16[256,256]{1,0:T(8,128)(2,1)S(1)}, bf16[256,256]{1,0:T(8,128)(2,1)S(1)}, u32[]{:S(2)}, u32[]{:S(2)}) collective-permute-start(bf16[256,256]{1,0:T(8,128)(2,1)S(1)} %grad.1.refs_0_), channel_id=1, source_target_pairs={{0,2},{2,0},{4,6},{6,4},{1,3},{3,1},{5,7},{7,5},{8,10},{10,8},{12,... | collective-permute-start | bytes 393224 | tf_op jit(solution)/shard_map/ppermute | solution.py:28
  32.2 6.0 %collective-permute-start.10 = (bf16[256,256]{1,0:T(8,128)(2,1)S(1)}, bf16[256,256]{1,0:T(8,128)(2,1)S(1)}, u32[]{:S(2)}, u32[]{:S(2)}) collective-permute-start(bf16[256,256]{1,0:T(8,128)(2,1)S(1)} %grad.1.refs_0_), channel_id=1, source_target_pairs={{0,1},{1,0},{2,3},{3,2},{4,5},{5,4},{6,7},{7,6},{8,9},{9,8},{10,11... | collective-permute-start | bytes 393224 | tf_op jit(solution)/shard_map/ppermute | solution.py:28
  40.9 9.4 %collective-permute-start.22 = (bf16[3,64,256]{2,1,0:T(8,128)(2,1)S(1)}, bf16[3,64,256]{2,1,0:T(8,128)(2,1)S(1)}, u32[]{:S(2)}, u32[]{:S(2)}) collective-permute-start(bf16[3,64,256]{2,1,0:T(8,128)(2,1)S(1)} %get-tuple-element.85), channel_id=1, source_target_pairs={{0,6},{2,4},{4,2},{6,0},{1,7},{3,5},{5,3},{7,1},{8,14},{10,12},{12... | collective-permute-start | bytes 294920 | tf_op jit(solution)/shard_map/ppermute | solution.py:28
  42.5 7.9 %collective-permute-start.23 = (bf16[3,64,256]{2,1,0:T(8,128)(2,1)S(1)}, bf16[3,64,256]{2,1,0:T(8,128)(2,1)S(1)}, u32[]{:S(2)}, u32[]{:S(2)}) collective-permute-start(bf16[3,64,256]{2,1,0:T(8,128)(2,1)S(1)} %get-tuple-element.86), channel_id=1, source_target_pairs={{0,4},{2,6},{4,0},{6,2},{1,5},{3,7},{5,1},{7,3},{8,12},{10,14},{12... | collective-permute-start | bytes 294920 | tf_op jit(solution)/shard_map/ppermute | solution.py:28
  44.7 5.7 %collective-permute-start.24 = (bf16[3,64,256]{2,1,0:T(8,128)(2,1)S(1)}, bf16[3,64,256]{2,1,0:T(8,128)(2,1)S(1)}, u32[]{:S(2)}, u32[]{:S(2)}) collective-permute-start(bf16[3,64,256]{2,1,0:T(8,128)(2,1)S(1)} %get-tuple-element.87), channel_id=1, source_target_pairs={{0,2},{2,0},{4,6},{6,4},{1,3},{3,1},{5,7},{7,5},{8,10},{10,8},{12,... | collective-permute-start | bytes 294920 | tf_op jit(solution)/shard_map/ppermute | solution.py:28
  46.3 9.2 %collective-permute-start.14 = (bf16[3,64,256]{2,1,0:T(8,128)(2,1)S(1)}, bf16[3,64,256]{2,1,0:T(8,128)(2,1)S(1)}, u32[]{:S(2)}, u32[]{:S(2)}) collective-permute-start(bf16[3,64,256]{2,1,0:T(8,128)(2,1)S(1)} %get-tuple-element.79), channel_id=1, source_target_pairs={{0,6},{2,4},{4,2},{6,0},{1,7},{3,5},{5,3},{7,1},{8,14},{10,12},{12... | collective-permute-start | bytes 294920 | tf_op jit(solution)/shard_map/ppermute | solution.py:28
  47.9 7.6 %collective-permute-start.15 = (bf16[3,64,256]{2,1,0:T(8,128)(2,1)S(1)}, bf16[3,64,256]{2,1,0:T(8,128)(2,1)S(1)}, u32[]{:S(2)}, u32[]{:S(2)}) collective-permute-start(bf16[3,64,256]{2,1,0:T(8,128)(2,1)S(1)} %get-tuple-element.80), channel_id=1, source_target_pairs={{0,4},{2,6},{4,0},{6,2},{1,5},{3,7},{5,1},{7,3},{8,12},{10,14},{12... | collective-permute-start | bytes 294920 | tf_op jit(solution)/shard_map/ppermute | solution.py:28
  50.4 5.1 %collective-permute-start.16 = (bf16[3,64,256]{2,1,0:T(8,128)(2,1)S(1)}, bf16[3,64,256]{2,1,0:T(8,128)(2,1)S(1)}, u32[]{:S(2)}, u32[]{:S(2)}) collective-permute-start(bf16[3,64,256]{2,1,0:T(8,128)(2,1)S(1)} %get-tuple-element.81), channel_id=1, source_target_pairs={{0,2},{2,0},{4,6},{6,4},{1,3},{3,1},{5,7},{7,5},{8,10},{10,8},{12,... | collective-permute-start | bytes 294920 | tf_op jit(solution)/shard_map/ppermute | solution.py:28
  50.5 8.7 %collective-permute-start.25 = (bf16[3,64,256]{2,1,0:T(8,128)(2,1)S(1)}, bf16[3,64,256]{2,1,0:T(8,128)(2,1)S(1)}, u32[]{:S(2)}, u32[]{:S(2)}) collective-permute-start(bf16[3,64,256]{2,1,0:T(8,128)(2,1)S(1)} %sum.9.refs_0_), channel_id=1, source_target_pairs={{0,16},{8,24},{16,0},{24,8},{1,17},{9,25},{17,1},{25,9},{2,18},{10... | collective-permute-start | bytes 294920 | tf_op jit(solution)/shard_map/ppermute | solution.py:28
  55.5 5.7 %collective-permute-start.17 = (bf16[3,64,256]{2,1,0:T(8,128)(2,1)S(1)}, bf16[3,64,256]{2,1,0:T(8,128)(2,1)S(1)}, u32[]{:S(2)}, u32[]{:S(2)}) collective-permute-start(bf16[3,64,256]{2,1,0:T(8,128)(2,1)S(1)} %sum.6.refs_0_), channel_id=1, source_target_pairs={{0,8},{8,0},{16,24},{24,16},{1,9},{9,1},{17,25},{25,17},{2,10},{10... | collective-permute-start | bytes 294920 | tf_op jit(solution)/shard_map/ppermute | solution.py:28
  59.1 5.4 %collective-permute-start.26 = (bf16[3,64,256]{2,1,0:T(8,128)(2,1)S(1)}, bf16[3,64,256]{2,1,0:T(8,128)(2,1)S(1)}, u32[]{:S(2)}, u32[]{:S(2)}) collective-permute-start(bf16[3,64,256]{2,1,0:T(8,128)(2,1)S(1)} %sum.10.refs_0_), channel_id=1, source_target_pairs={{0,8},{8,0},{16,24},{24,16},{1,9},{9,1},{17,25},{25,17},{2,10},{10... | collective-permute-start | bytes 294920 | tf_op jit(solution)/shard_map/ppermute | solution.py:28
  61.2 6.9 %collective-permute-start.18 = (bf16[3,64,256]{2,1,0:T(8,128)(2,1)S(1)}, bf16[3,64,256]{2,1,0:T(8,128)(2,1)S(1)}, u32[]{:S(2)}, u32[]{:S(2)}) collective-permute-start(bf16[3,64,256]{2,1,0:T(8,128)(2,1)S(1)} %sum.7.refs_0_), channel_id=1, source_target_pairs={{0,16},{8,24},{16,0},{24,8},{1,17},{9,25},{17,1},{25,9},{2,18},{10... | collective-permute-start | bytes 294920 | tf_op jit(solution)/shard_map/ppermute | solution.py:28
  64.6 6.4 %collective-permute-start.29 = (bf16[3,64,256]{2,1,0:T(8,128)(2,1)S(1)}, bf16[3,64,256]{2,1,0:T(8,128)(2,1)S(1)}, u32[]{:S(2)}, u32[]{:S(2)}) collective-permute-start(bf16[3,64,256]{2,1,0:T(8,128)(2,1)S(1)} %sum.11.refs_0_), channel_id=1, source_target_pairs={{0,6},{2,4},{4,2},{6,0},{1,7},{3,5},{5,3},{7,1},{8,14},{10,12},{12... | collective-permute-start | bytes 294920 | tf_op jit(solution)/shard_map/ppermute | solution.py:28
  66.5 6.8 %collective-permute-start.28 = (bf16[3,64,256]{2,1,0:T(8,128)(2,1)S(1)}, bf16[3,64,256]{2,1,0:T(8,128)(2,1)S(1)}, u32[]{:S(2)}, u32[]{:S(2)}) collective-permute-start(bf16[3,64,256]{2,1,0:T(8,128)(2,1)S(1)} %sum.11.refs_0_), channel_id=1, source_target_pairs={{0,4},{2,6},{4,0},{6,2},{1,5},{3,7},{5,1},{7,3},{8,12},{10,14},{12... | collective-permute-start | bytes 294920 | tf_op jit(solution)/shard_map/ppermute | solution.py:28
  67.4 5.9 %collective-permute-start.27 = (bf16[3,64,256]{2,1,0:T(8,128)(2,1)S(1)}, bf16[3,64,256]{2,1,0:T(8,128)(2,1)S(1)}, u32[]{:S(2)}, u32[]{:S(2)}) collective-permute-start(bf16[3,64,256]{2,1,0:T(8,128)(2,1)S(1)} %sum.11.refs_0_), channel_id=1, source_target_pairs={{0,2},{2,0},{4,6},{6,4},{1,3},{3,1},{5,7},{7,5},{8,10},{10,8},{12,... | collective-permute-start | bytes 294920 | tf_op jit(solution)/shard_map/ppermute | solution.py:28
  68.2 6.0 %collective-permute-start.21 = (bf16[3,64,256]{2,1,0:T(8,128)(2,1)S(1)}, bf16[3,64,256]{2,1,0:T(8,128)(2,1)S(1)}, u32[]{:S(2)}, u32[]{:S(2)}) collective-permute-start(bf16[3,64,256]{2,1,0:T(8,128)(2,1)S(1)} %sum.8.refs_0_), channel_id=1, source_target_pairs={{0,6},{2,4},{4,2},{6,0},{1,7},{3,5},{5,3},{7,1},{8,14},{10,12},{12... | collective-permute-start | bytes 294920 | tf_op jit(solution)/shard_map/ppermute | solution.py:28
  (12 other events, 37.1 us)

commit v10 on v9

--- a/solution.py
+++ b/solution.py
@@ -46,12 +46,12 @@
     return code & ((1 << bits) - 1), (code >> bits) & ((1 << more) - 1), code >> (bits + more)
 
 
-def for_entries(total, body):
+def for_entries(total, body, unroll=UNROLL):
     def step(i, carry):
-        body([(jnp.minimum(i * UNROLL + u, total - 1), i * UNROLL + u < total) for u in range(UNROLL)])
+        body([(jnp.minimum(i * unroll + u, total - 1), i * unroll + u < total) for u in range(unroll)])
         return carry
 
-    lax.fori_loop(0, (total + UNROLL - 1) // UNROLL, step, 0)
+    lax.fori_loop(0, (total + unroll - 1) // unroll, step, 0)
 
 
 def halo_block(first_block, halo_refs, i, tile):
@@ -176,7 +176,7 @@
         for target, term in terms:
             pre[target] = pre[target] + term
 
-    for_entries(total, body)
+    for_entries(total, body, 16 if order.shape[0] == entries + 2 else 28)
 
 
 def chip_kernel(*refs):

time: 76.9 us -> 77 us (level)
  Pallas kernels: 14.1 us -> 13.3 us
  transfers between devices with their start and end apart: 30 -> 30, of which waited for: 15 -> 15; matrix products, arithmetic and copies ran while one was open for 2% -> 2% of each run, Pallas kernels for 12% -> 11%
where the time goes in v10:
time: 77 us; the launch traced here: 76.7 us
  starting transfers between devices  38.7 us (50%)
  waiting for transfers between devices  18.5 us (24%)
  Pallas kernels  13.3 us (17%)
  local copies, waits for them, and re-layouts  4.07 us (5%)
  between operations  1.46 us (2%)
    ppermute x30, starting transfers between devices, swap(): return lax.ppermute(value, axis, partner_pairs(lax.axis_size(axis), mask))  38.7 us
    ppermute x30, waiting for transfers between devices, swap(): return lax.ppermute(value, axis, partner_pairs(lax.axis_size(axis), mask))  18.5 us
    unnamed x13, local copies, waits for them, and re-layouts  4.07 us
    pallas_call x2, Pallas kernels, local(): pl.pallas_call(functools.partial(weight_kernel, tile, combine), out_shape...  3.31 us
    pallas_call x2, Pallas kernels, local(): pl.pallas_call(kernel, out_shape=outs, in_specs=[SCALARS] + [WHOLE] * (le...  2.65 us
    pallas_call x1, Pallas kernels, local(): pl.pallas_call(functools.partial(turn_kernel, direct, tile, panels, len(h...  1.9 us
    pallas_call x2, Pallas kernels, spread(): pl.pallas_call(functools.partial(spread_kernel, first_relation), out_shap...  1.84 us
    pallas_call x1, Pallas kernels, local(): pl.pallas_call(functools.partial(prepare_kernel, direct, owners, slot_gro...  1.66 us
  transfers between devices with their start and end apart: 30, of which 15 were waited for; matrix products, arithmetic and copies ran while one was open for 2% of the time, Pallas kernels for 11%

profile of v10, /device:TPU:0, one launch (start us, length us, event | category | flops | bytes accessed | tf_op | source)
XLA Modules:
  0.0 76.7 jit_solution(12625688029264929830)
XLA Ops:
  0.6 4.1 %collective-permute-start.1 = (bf16[256,256]{1,0:T(8,128)(2,1)}, bf16[256,256]{1,0:T(8,128)(2,1)S(1)}, u32[]{:S(2)}, u32[]{:S(2)}) collective-permute-start(bf16[256,256]{1,0:T(8,128)(2,1)} %param.7), channel_id=1, source_target_pairs={{0,16},{8,24},{16,0},{24,8},{1,17},{9,25},{17,1},{25,9},{2,18},{10... | collective-permute-start | bytes 393224 | tf_op jit(solution)/shard_map/ppermute | solution.py:28
  4.7 1.6 %collective-permute-start = (bf16[256,256]{1,0:T(8,128)(2,1)}, bf16[256,256]{1,0:T(8,128)(2,1)S(1)}, u32[]{:S(2)}, u32[]{:S(2)}) collective-permute-start(bf16[256,256]{1,0:T(8,128)(2,1)} %param.7), channel_id=1, source_target_pairs={{0,8},{8,0},{16,24},{24,16},{1,9},{9,1},{17,25},{25,17},{2,10},{10... | collective-permute-start | bytes 393224 | tf_op jit(solution)/shard_map/ppermute | solution.py:28
  7.6 1.6 %copy-done = bf16[1,1,1,64,128,128]{5,4,3,2,1,0:T(8,128)(2,1)S(1)} copy-done((bf16[1,1,1,64,128,128]{5,4,3,2,1,0:T(8,128)(2,1)S(1)}, bf16[1,1,1,64,128,128]{5,4,3,2,1,0:T(8,128)(2,1)}, u32[]{:S(2)}) %copy-start) | copy-done | bytes 2097176
  11.0 1.7 %prepare.1 = (bf16[64,128,128]{2,1,0:T(8,128)(2,1)S(1)}, bf16[6,256,256]{2,1,0:T(8,128)(2,1)S(1)}, s32[66]{0:T(128)S(1)}, s32[68]{0:T(128)S(1)}, s32[68]{0:T(128...) custom-call(s32[4]{0:T(128)S(1)} %bitcast.21, s32[3,64]{1,0:T(4,128)S(1)} %bitcast.20, ...), custom_call_target="tpu_custom_call" | custom-call | bytes 4194304 | tf_op jit(solution)/shard_map/prepare/pallas_call | solution.py:390
  13.6 1.7 %collective-permute-done.2 = bf16[256,256]{1,0:T(8,128)(2,1)S(1)} collective-permute-done((bf16[256,256]{1,0:T(8,128)(2,1)}, bf16[256,256]{1,0:T(8,128)(2,1)S(1)}, u32[]{:S(2)}, u32[]{:S(2)}) %collective-permute-start.2) | collective-permute-done | bytes 131104 | tf_op jit(solution)/shard_map/ppermute | solution.py:28
  15.3 1.8 %forward.3 = (f32[17,128,256]{2,1,0:T(8,128)S(1)}, bf16[18,256,256]{2,1,0:T(8,128)(2,1)S(1)}, bf16[4,256,256]{2,1,0:T(8,128)(2,1)S(1)}) custom-call(s32[68]{0:T(128)S(1)} %get-tuple-element.46.order, bf16[1,256,256]{2,1,0:T(8,128)(2,1)S(1)} %bitcast.16, bf16[1,256,256]{2,1,0:T(8,128)(2,1)S(1)} %bitcast.14, ...), custom_call_target="tpu_custom_call", output_to_operand_aliasing={{0}: (6, {})} | custom-call | flops 1073741824 | bytes 1048576 | tf_op jit(solution)/shard_map/forward/pallas_call | solution.py:421
  17.2 1.4 %forward_ours.1 = (f32[17,128,256]{2,1,0:T(8,128)S(1)}, f32[256,256]{1,0:T(8,128)S(1)}, f32[256,256]{1,0:T(8,128)S(1)}, f32[256,256]{1,0:T(8,128)S(1)}, f32[256,256]{1,0:T(8,128)S(1)}) custom-call(s32[68]{0:T(128)S(1)} %get-tuple-element.45.order, bf16[18,256,256]{2,1,0:T(8,128)(2,1)S(1)} %get-tuple-element.51.projected, ...), custom_call_target="tpu_custom_call", output_to_operand_aliasing={{0}: (4, {})} | custom-call | flops 1073741824 | bytes 1048576 | tf_op jit(solution)/shard_map/forward_ours/pallas_call | solution.py:433
  19.2 1.8 %collective-permute-start.4 = (bf16[256,256]{1,0:T(8,128)(2,1)S(1)}, bf16[256,256]{1,0:T(8,128)(2,1)S(1)}, u32[]{:S(2)}, u32[]{:S(2)}) collective-permute-start(bf16[256,256]{1,0:T(8,128)(2,1)S(1)} %get-tuple-element.63), channel_id=1, source_target_pairs={{0,6},{2,4},{4,2},{6,0},{1,7},{3,5},{5,3},{7,1},{8,14},{10,12},{12... | collective-permute-start | bytes 393224 | tf_op jit(solution)/shard_map/ppermute | solution.py:28
  23.0 1.9 %turn.1 = (bf16[64,128,128]{2,1,0:T(8,128)(2,1)S(1)}, bf16[256,512]{1,0:T(8,128)(2,1)S(1)}, f32[13,128,256]{2,1,0:T(8,128)S(1)}, f32[13,128,256]{2,1,0:T(8,128)S(1)}) custom-call(s32[4]{0:T(128)S(1)} %bitcast.22, bf16[64,128,128]{2,1,0:T(8,128)(2,1)S(1)} %get-tuple-element.48.refs_2_.refs_4_.values, bf16[1,256,256]{2,1,0:T(8,128)(2,1)S(1)} %bitcast.13, ...), custom_call_target="tpu_custom_call" | custom-call | bytes 4194304 | tf_op jit(solution)/shard_map/turn/pallas_call | solution.py:455
  24.9 1.6 %collective-permute-done.4.first = bf16[256,256]{1,0:T(8,128)(2,1)S(1)} collective-permute-done((bf16[256,256]{1,0:T(8,128)(2,1)S(1)}, bf16[256,256]{1,0:T(8,128)(2,1)S(1)}, u32[]{:S(2)}, u32[]{:S(2)}) %collective-permute-start.4) | collective-permute-done | bytes 131104 | tf_op jit(solution)/shard_map/ppermute | solution.py:28
  26.5 2.0 %collective-permute-done.5.second = bf16[256,256]{1,0:T(8,128)(2,1)S(1)} collective-permute-done((bf16[256,256]{1,0:T(8,128)(2,1)S(1)}, bf16[256,256]{1,0:T(8,128)(2,1)S(1)}, u32[]{:S(2)}, u32[]{:S(2)}) %collective-permute-start.5) | collective-permute-done | bytes 131104 | tf_op jit(solution)/shard_map/ppermute | solution.py:28
  32.8 3.4 %collective-permute-done.9.refs_3_ = bf16[256,256]{1,0:T(8,128)(2,1)S(1)} collective-permute-done((bf16[256,256]{1,0:T(8,128)(2,1)S(1)}, bf16[256,256]{1,0:T(8,128)(2,1)S(1)}, u32[]{:S(2)}, u32[]{:S(2)}) %collective-permute-start.9) | collective-permute-done | bytes 131104 | tf_op jit(solution)/shard_map/ppermute | solution.py:28
  36.2 1.6 %collective-permute-done.8.refs_2_ = bf16[256,256]{1,0:T(8,128)(2,1)S(1)} collective-permute-done((bf16[256,256]{1,0:T(8,128)(2,1)S(1)}, bf16[256,256]{1,0:T(8,128)(2,1)S(1)}, u32[]{:S(2)}, u32[]{:S(2)}) %collective-permute-start.8) | collective-permute-done | bytes 131104 | tf_op jit(solution)/shard_map/ppermute | solution.py:28
  39.5 1.7 %weight_terms.3 = (f32[3,64,256]{2,1,0:T(8,128)S(1)}, bf16[3,64,256]{2,1,0:T(8,128)(2,1)S(1)}, bf16[3,64,256]{2,1,0:T(8,128)(2,1)S(1)}, bf16[3,64,256]{2,1,0:T(8,128)(2,1)S(1)}, f32[13,128,256]{2,1,0:T(8,128)S(1)}) custom-call(s32[65]{0:T(128)S(1)} %get-tuple-element.82.listed, ...), custom_call_target="tpu_custom_call", output_to_operand_aliasing={{4}: (4, {})} | custom-call | tf_op jit(solution)/shard_map/weight_terms/pallas_call | solution.py:501
  41.1 1.8 %collective-permute-start.22 = (bf16[3,64,256]{2,1,0:T(8,128)(2,1)S(1)}, bf16[3,64,256]{2,1,0:T(8,128)(2,1)S(1)}, u32[]{:S(2)}, u32[]{:S(2)}) collective-permute-start(bf16[3,64,256]{2,1,0:T(8,128)(2,1)S(1)} %get-tuple-element.85), channel_id=1, source_target_pairs={{0,6},{2,4},{4,2},{6,0},{1,7},{3,5},{5,3},{7,1},{8,14},{10,12},{12... | collective-permute-start | bytes 294920 | tf_op jit(solution)/shard_map/ppermute | solution.py:28
  44.7 1.6 %weight_terms.2 = (f32[3,64,256]{2,1,0:T(8,128)S(1)}, bf16[3,64,256]{2,1,0:T(8,128)(2,1)S(1)}, bf16[3,64,256]{2,1,0:T(8,128)(2,1)S(1)}, bf16[3,64,256]{2,1,0:T(8,128)(2,1)S(1)}, f32[13,128,256]{2,1,0:T(8,128)S(1)}) custom-call(s32[65]{0:T(128)S(1)} %get-tuple-element.74.listed, ...), custom_call_target="tpu_custom_call", output_to_operand_aliasing={{4}: (4, {})} | custom-call | tf_op jit(solution)/shard_map/weight_terms/pallas_call | solution.py:501
  46.4 1.8 %collective-permute-start.14 = (bf16[3,64,256]{2,1,0:T(8,128)(2,1)S(1)}, bf16[3,64,256]{2,1,0:T(8,128)(2,1)S(1)}, u32[]{:S(2)}, u32[]{:S(2)}) collective-permute-start(bf16[3,64,256]{2,1,0:T(8,128)(2,1)S(1)} %get-tuple-element.79), channel_id=1, source_target_pairs={{0,6},{2,4},{4,2},{6,0},{1,7},{3,5},{5,3},{7,1},{8,14},{10,12},{12... | collective-permute-start | bytes 294920 | tf_op jit(solution)/shard_map/ppermute | solution.py:28
  50.5 4.8 %collective-permute-start.25 = (bf16[3,64,256]{2,1,0:T(8,128)(2,1)S(1)}, bf16[3,64,256]{2,1,0:T(8,128)(2,1)S(1)}, u32[]{:S(2)}, u32[]{:S(2)}) collective-permute-start(bf16[3,64,256]{2,1,0:T(8,128)(2,1)S(1)} %sum.9.refs_0_), channel_id=1, source_target_pairs={{0,16},{8,24},{16,0},{24,8},{1,17},{9,25},{17,1},{25,9},{2,18},{10... | collective-permute-start | bytes 294920 | tf_op jit(solution)/shard_map/ppermute | solution.py:28
  56.7 2.2 %collective-permute-done.25.refs_1_ = bf16[3,64,256]{2,1,0:T(8,128)(2,1)S(1)} collective-permute-done((bf16[3,64,256]{2,1,0:T(8,128)(2,1)S(1)}, bf16[3,64,256]{2,1,0:T(8,128)(2,1)S(1)}, u32[]{:S(2)}, u32[]{:S(2)}) %collective-permute-start.25) | collective-permute-done | bytes 98336 | tf_op jit(solution)/shard_map/ppermute | solution.py:28
  59.0 1.6 %collective-permute-done.17.refs_1_ = bf16[3,64,256]{2,1,0:T(8,128)(2,1)S(1)} collective-permute-done((bf16[3,64,256]{2,1,0:T(8,128)(2,1)S(1)}, bf16[3,64,256]{2,1,0:T(8,128)(2,1)S(1)}, u32[]{:S(2)}, u32[]{:S(2)}) %collective-permute-start.17) | collective-permute-done | bytes 98336 | tf_op jit(solution)/shard_map/ppermute | solution.py:28
  60.6 2.6 %collective-permute-start.18 = (bf16[3,64,256]{2,1,0:T(8,128)(2,1)S(1)}, bf16[3,64,256]{2,1,0:T(8,128)(2,1)S(1)}, u32[]{:S(2)}, u32[]{:S(2)}) collective-permute-start(bf16[3,64,256]{2,1,0:T(8,128)(2,1)S(1)} %sum.7.refs_0_), channel_id=1, source_target_pairs={{0,16},{8,24},{16,0},{24,8},{1,17},{9,25},{17,1},{25,9},{2,18},{10... | collective-permute-start | bytes 294920 | tf_op jit(solution)/shard_map/ppermute | solution.py:28
  63.6 1.7 %collective-permute-start.29 = (bf16[3,64,256]{2,1,0:T(8,128)(2,1)S(1)}, bf16[3,64,256]{2,1,0:T(8,128)(2,1)S(1)}, u32[]{:S(2)}, u32[]{:S(2)}) collective-permute-start(bf16[3,64,256]{2,1,0:T(8,128)(2,1)S(1)} %sum.11.refs_0_), channel_id=1, source_target_pairs={{0,6},{2,4},{4,2},{6,0},{1,7},{3,5},{5,3},{7,1},{8,14},{10,12},{12... | collective-permute-start | bytes 294920 | tf_op jit(solution)/shard_map/ppermute | solution.py:28
  65.3 2.3 %collective-permute-start.28 = (bf16[3,64,256]{2,1,0:T(8,128)(2,1)S(1)}, bf16[3,64,256]{2,1,0:T(8,128)(2,1)S(1)}, u32[]{:S(2)}, u32[]{:S(2)}) collective-permute-start(bf16[3,64,256]{2,1,0:T(8,128)(2,1)S(1)} %sum.11.refs_0_), channel_id=1, source_target_pairs={{0,4},{2,6},{4,0},{6,2},{1,5},{3,7},{5,1},{7,3},{8,12},{10,14},{12... | collective-permute-start | bytes 294920 | tf_op jit(solution)/shard_map/ppermute | solution.py:28
  67.6 2.2 %collective-permute-start.21 = (bf16[3,64,256]{2,1,0:T(8,128)(2,1)S(1)}, bf16[3,64,256]{2,1,0:T(8,128)(2,1)S(1)}, u32[]{:S(2)}, u32[]{:S(2)}) collective-permute-start(bf16[3,64,256]{2,1,0:T(8,128)(2,1)S(1)} %sum.8.refs_0_), channel_id=1, source_target_pairs={{0,6},{2,4},{4,2},{6,0},{1,7},{3,5},{5,3},{7,1},{8,14},{10,12},{12... | collective-permute-start | bytes 294920 | tf_op jit(solution)/shard_map/ppermute | solution.py:28
  (68 shorter events, 24.8 us)
Async XLA Ops:
  0.6 12.9 %collective-permute-start.1 = (bf16[256,256]{1,0:T(8,128)(2,1)}, bf16[256,256]{1,0:T(8,128)(2,1)S(1)}, u32[]{:S(2)}, u32[]{:S(2)}) collective-permute-start(bf16[256,256]{1,0:T(8,128)(2,1)} %param.7), channel_id=1, source_target_pairs={{0,16},{8,24},{16,0},{24,8},{1,17},{9,25},{17,1},{25,9},{2,18},{10... | collective-permute-start | bytes 393224 | tf_op jit(solution)/shard_map/ppermute | solution.py:28
  4.7 8.8 %collective-permute-start = (bf16[256,256]{1,0:T(8,128)(2,1)}, bf16[256,256]{1,0:T(8,128)(2,1)S(1)}, u32[]{:S(2)}, u32[]{:S(2)}) collective-permute-start(bf16[256,256]{1,0:T(8,128)(2,1)} %param.7), channel_id=1, source_target_pairs={{0,8},{8,0},{16,24},{24,16},{1,9},{9,1},{17,25},{25,17},{2,10},{10... | collective-permute-start | bytes 393224 | tf_op jit(solution)/shard_map/ppermute | solution.py:28
  6.3 9.0 %collective-permute-start.2 = (bf16[256,256]{1,0:T(8,128)(2,1)}, bf16[256,256]{1,0:T(8,128)(2,1)S(1)}, u32[]{:S(2)}, u32[]{:S(2)}) collective-permute-start(bf16[256,256]{1,0:T(8,128)(2,1)} %param.7), channel_id=1, source_target_pairs={{0,24},{8,16},{16,8},{24,0},{1,25},{9,17},{17,9},{25,1},{2,26},{10... | collective-permute-start | bytes 393224 | tf_op jit(solution)/shard_map/ppermute | solution.py:28
  19.2 7.3 %collective-permute-start.4 = (bf16[256,256]{1,0:T(8,128)(2,1)S(1)}, bf16[256,256]{1,0:T(8,128)(2,1)S(1)}, u32[]{:S(2)}, u32[]{:S(2)}) collective-permute-start(bf16[256,256]{1,0:T(8,128)(2,1)S(1)} %get-tuple-element.63), channel_id=1, source_target_pairs={{0,6},{2,4},{4,2},{6,0},{1,7},{3,5},{5,3},{7,1},{8,14},{10,12},{12... | collective-permute-start | bytes 393224 | tf_op jit(solution)/shard_map/ppermute | solution.py:28
  21.0 7.6 %collective-permute-start.5 = (bf16[256,256]{1,0:T(8,128)(2,1)S(1)}, bf16[256,256]{1,0:T(8,128)(2,1)S(1)}, u32[]{:S(2)}, u32[]{:S(2)}) collective-permute-start(bf16[256,256]{1,0:T(8,128)(2,1)S(1)} %get-tuple-element.64), channel_id=1, source_target_pairs={{0,4},{2,6},{4,0},{6,2},{1,5},{3,7},{5,1},{7,3},{8,12},{10,14},{12... | collective-permute-start | bytes 393224 | tf_op jit(solution)/shard_map/ppermute | solution.py:28
  22.2 6.9 %collective-permute-start.6 = (bf16[256,256]{1,0:T(8,128)(2,1)S(1)}, bf16[256,256]{1,0:T(8,128)(2,1)S(1)}, u32[]{:S(2)}, u32[]{:S(2)}) collective-permute-start(bf16[256,256]{1,0:T(8,128)(2,1)S(1)} %get-tuple-element.65), channel_id=1, source_target_pairs={{0,2},{2,0},{4,6},{6,4},{1,3},{3,1},{5,7},{7,5},{8,10},{10,8},{12,... | collective-permute-start | bytes 393224 | tf_op jit(solution)/shard_map/ppermute | solution.py:28
  29.2 7.0 %collective-permute-start.9 = (bf16[256,256]{1,0:T(8,128)(2,1)S(1)}, bf16[256,256]{1,0:T(8,128)(2,1)S(1)}, u32[]{:S(2)}, u32[]{:S(2)}) collective-permute-start(bf16[256,256]{1,0:T(8,128)(2,1)S(1)} %grad.1.refs_0_), channel_id=1, source_target_pairs={{0,6},{2,4},{4,2},{6,0},{1,7},{3,5},{5,3},{7,1},{8,14},{10,12},{12... | collective-permute-start | bytes 393224 | tf_op jit(solution)/shard_map/ppermute | solution.py:28
  30.6 7.3 %collective-permute-start.8 = (bf16[256,256]{1,0:T(8,128)(2,1)S(1)}, bf16[256,256]{1,0:T(8,128)(2,1)S(1)}, u32[]{:S(2)}, u32[]{:S(2)}) collective-permute-start(bf16[256,256]{1,0:T(8,128)(2,1)S(1)} %grad.1.refs_0_), channel_id=1, source_target_pairs={{0,4},{2,6},{4,0},{6,2},{1,5},{3,7},{5,1},{7,3},{8,12},{10,14},{12... | collective-permute-start | bytes 393224 | tf_op jit(solution)/shard_map/ppermute | solution.py:28
  31.7 6.2 %collective-permute-start.7 = (bf16[256,256]{1,0:T(8,128)(2,1)S(1)}, bf16[256,256]{1,0:T(8,128)(2,1)S(1)}, u32[]{:S(2)}, u32[]{:S(2)}) collective-permute-start(bf16[256,256]{1,0:T(8,128)(2,1)S(1)} %grad.1.refs_0_), channel_id=1, source_target_pairs={{0,2},{2,0},{4,6},{6,4},{1,3},{3,1},{5,7},{7,5},{8,10},{10,8},{12,... | collective-permute-start | bytes 393224 | tf_op jit(solution)/shard_map/ppermute | solution.py:28
  32.8 5.6 %collective-permute-start.10 = (bf16[256,256]{1,0:T(8,128)(2,1)S(1)}, bf16[256,256]{1,0:T(8,128)(2,1)S(1)}, u32[]{:S(2)}, u32[]{:S(2)}) collective-permute-start(bf16[256,256]{1,0:T(8,128)(2,1)S(1)} %grad.1.refs_0_), channel_id=1, source_target_pairs={{0,1},{1,0},{2,3},{3,2},{4,5},{5,4},{6,7},{7,6},{8,9},{9,8},{10,11... | collective-permute-start | bytes 393224 | tf_op jit(solution)/shard_map/ppermute | solution.py:28
  41.1 8.2 %collective-permute-start.22 = (bf16[3,64,256]{2,1,0:T(8,128)(2,1)S(1)}, bf16[3,64,256]{2,1,0:T(8,128)(2,1)S(1)}, u32[]{:S(2)}, u32[]{:S(2)}) collective-permute-start(bf16[3,64,256]{2,1,0:T(8,128)(2,1)S(1)} %get-tuple-element.85), channel_id=1, source_target_pairs={{0,6},{2,4},{4,2},{6,0},{1,7},{3,5},{5,3},{7,1},{8,14},{10,12},{12... | collective-permute-start | bytes 294920 | tf_op jit(solution)/shard_map/ppermute | solution.py:28
  43.0 7.5 %collective-permute-start.23 = (bf16[3,64,256]{2,1,0:T(8,128)(2,1)S(1)}, bf16[3,64,256]{2,1,0:T(8,128)(2,1)S(1)}, u32[]{:S(2)}, u32[]{:S(2)}) collective-permute-start(bf16[3,64,256]{2,1,0:T(8,128)(2,1)S(1)} %get-tuple-element.86), channel_id=1, source_target_pairs={{0,4},{2,6},{4,0},{6,2},{1,5},{3,7},{5,1},{7,3},{8,12},{10,14},{12... | collective-permute-start | bytes 294920 | tf_op jit(solution)/shard_map/ppermute | solution.py:28
  44.1 6.3 %collective-permute-start.24 = (bf16[3,64,256]{2,1,0:T(8,128)(2,1)S(1)}, bf16[3,64,256]{2,1,0:T(8,128)(2,1)S(1)}, u32[]{:S(2)}, u32[]{:S(2)}) collective-permute-start(bf16[3,64,256]{2,1,0:T(8,128)(2,1)S(1)} %get-tuple-element.87), channel_id=1, source_target_pairs={{0,2},{2,0},{4,6},{6,4},{1,3},{3,1},{5,7},{7,5},{8,10},{10,8},{12,... | collective-permute-start | bytes 294920 | tf_op jit(solution)/shard_map/ppermute | solution.py:28
  46.4 8.9 %collective-permute-start.14 = (bf16[3,64,256]{2,1,0:T(8,128)(2,1)S(1)}, bf16[3,64,256]{2,1,0:T(8,128)(2,1)S(1)}, u32[]{:S(2)}, u32[]{:S(2)}) collective-permute-start(bf16[3,64,256]{2,1,0:T(8,128)(2,1)S(1)} %get-tuple-element.79), channel_id=1, source_target_pairs={{0,6},{2,4},{4,2},{6,0},{1,7},{3,5},{5,3},{7,1},{8,14},{10,12},{12... | collective-permute-start | bytes 294920 | tf_op jit(solution)/shard_map/ppermute | solution.py:28
  48.2 7.1 %collective-permute-start.15 = (bf16[3,64,256]{2,1,0:T(8,128)(2,1)S(1)}, bf16[3,64,256]{2,1,0:T(8,128)(2,1)S(1)}, u32[]{:S(2)}, u32[]{:S(2)}) collective-permute-start(bf16[3,64,256]{2,1,0:T(8,128)(2,1)S(1)} %get-tuple-element.80), channel_id=1, source_target_pairs={{0,4},{2,6},{4,0},{6,2},{1,5},{3,7},{5,1},{7,3},{8,12},{10,14},{12... | collective-permute-start | bytes 294920 | tf_op jit(solution)/shard_map/ppermute | solution.py:28
  49.4 5.9 %collective-permute-start.16 = (bf16[3,64,256]{2,1,0:T(8,128)(2,1)S(1)}, bf16[3,64,256]{2,1,0:T(8,128)(2,1)S(1)}, u32[]{:S(2)}, u32[]{:S(2)}) collective-permute-start(bf16[3,64,256]{2,1,0:T(8,128)(2,1)S(1)} %get-tuple-element.81), channel_id=1, source_target_pairs={{0,2},{2,0},{4,6},{6,4},{1,3},{3,1},{5,7},{7,5},{8,10},{10,8},{12,... | collective-permute-start | bytes 294920 | tf_op jit(solution)/shard_map/ppermute | solution.py:28
  50.5 8.4 %collective-permute-start.25 = (bf16[3,64,256]{2,1,0:T(8,128)(2,1)S(1)}, bf16[3,64,256]{2,1,0:T(8,128)(2,1)S(1)}, u32[]{:S(2)}, u32[]{:S(2)}) collective-permute-start(bf16[3,64,256]{2,1,0:T(8,128)(2,1)S(1)} %sum.9.refs_0_), channel_id=1, source_target_pairs={{0,16},{8,24},{16,0},{24,8},{1,17},{9,25},{17,1},{25,9},{2,18},{10... | collective-permute-start | bytes 294920 | tf_op jit(solution)/shard_map/ppermute | solution.py:28
  55.3 5.3 %collective-permute-start.17 = (bf16[3,64,256]{2,1,0:T(8,128)(2,1)S(1)}, bf16[3,64,256]{2,1,0:T(8,128)(2,1)S(1)}, u32[]{:S(2)}, u32[]{:S(2)}) collective-permute-start(bf16[3,64,256]{2,1,0:T(8,128)(2,1)S(1)} %sum.6.refs_0_), channel_id=1, source_target_pairs={{0,8},{8,0},{16,24},{24,16},{1,9},{9,1},{17,25},{25,17},{2,10},{10... | collective-permute-start | bytes 294920 | tf_op jit(solution)/shard_map/ppermute | solution.py:28
  60.6 7.0 %collective-permute-start.18 = (bf16[3,64,256]{2,1,0:T(8,128)(2,1)S(1)}, bf16[3,64,256]{2,1,0:T(8,128)(2,1)S(1)}, u32[]{:S(2)}, u32[]{:S(2)}) collective-permute-start(bf16[3,64,256]{2,1,0:T(8,128)(2,1)S(1)} %sum.7.refs_0_), channel_id=1, source_target_pairs={{0,16},{8,24},{16,0},{24,8},{1,17},{9,25},{17,1},{25,9},{2,18},{10... | collective-permute-start | bytes 294920 | tf_op jit(solution)/shard_map/ppermute | solution.py:28
  63.6 7.6 %collective-permute-start.29 = (bf16[3,64,256]{2,1,0:T(8,128)(2,1)S(1)}, bf16[3,64,256]{2,1,0:T(8,128)(2,1)S(1)}, u32[]{:S(2)}, u32[]{:S(2)}) collective-permute-start(bf16[3,64,256]{2,1,0:T(8,128)(2,1)S(1)} %sum.11.refs_0_), channel_id=1, source_target_pairs={{0,6},{2,4},{4,2},{6,0},{1,7},{3,5},{5,3},{7,1},{8,14},{10,12},{12... | collective-permute-start | bytes 294920 | tf_op jit(solution)/shard_map/ppermute | solution.py:28
  65.3 7.7 %collective-permute-start.28 = (bf16[3,64,256]{2,1,0:T(8,128)(2,1)S(1)}, bf16[3,64,256]{2,1,0:T(8,128)(2,1)S(1)}, u32[]{:S(2)}, u32[]{:S(2)}) collective-permute-start(bf16[3,64,256]{2,1,0:T(8,128)(2,1)S(1)} %sum.11.refs_0_), channel_id=1, source_target_pairs={{0,4},{2,6},{4,0},{6,2},{1,5},{3,7},{5,1},{7,3},{8,12},{10,14},{12... | collective-permute-start | bytes 294920 | tf_op jit(solution)/shard_map/ppermute | solution.py:28
  67.6 5.5 %collective-permute-start.27 = (bf16[3,64,256]{2,1,0:T(8,128)(2,1)S(1)}, bf16[3,64,256]{2,1,0:T(8,128)(2,1)S(1)}, u32[]{:S(2)}, u32[]{:S(2)}) collective-permute-start(bf16[3,64,256]{2,1,0:T(8,128)(2,1)S(1)} %sum.11.refs_0_), channel_id=1, source_target_pairs={{0,2},{2,0},{4,6},{6,4},{1,3},{3,1},{5,7},{7,5},{8,10},{10,8},{12,... | collective-permute-start | bytes 294920 | tf_op jit(solution)/shard_map/ppermute | solution.py:28
  67.6 6.4 %collective-permute-start.21 = (bf16[3,64,256]{2,1,0:T(8,128)(2,1)S(1)}, bf16[3,64,256]{2,1,0:T(8,128)(2,1)S(1)}, u32[]{:S(2)}, u32[]{:S(2)}) collective-permute-start(bf16[3,64,256]{2,1,0:T(8,128)(2,1)S(1)} %sum.8.refs_0_), channel_id=1, source_target_pairs={{0,6},{2,4},{4,2},{6,0},{1,7},{3,5},{5,3},{7,1},{8,14},{10,12},{12... | collective-permute-start | bytes 294920 | tf_op jit(solution)/shard_map/ppermute | solution.py:28
  69.8 5.5 %collective-permute-start.20 = (bf16[3,64,256]{2,1,0:T(8,128)(2,1)S(1)}, bf16[3,64,256]{2,1,0:T(8,128)(2,1)S(1)}, u32[]{:S(2)}, u32[]{:S(2)}) collective-permute-start(bf16[3,64,256]{2,1,0:T(8,128)(2,1)S(1)} %sum.8.refs_0_), channel_id=1, source_target_pairs={{0,4},{2,6},{4,0},{6,2},{1,5},{3,7},{5,1},{7,3},{8,12},{10,14},{12... | collective-permute-start | bytes 294920 | tf_op jit(solution)/shard_map/ppermute | solution.py:28
  (12 other events, 37.1 us)
